TPU v7x, 512 devices: a whole 4x8x8 slice. The times are simulated.
512 devices in a mesh: batch: 8 (over z), pair: 2 (over core), ctx: 32 (over y, x).
Axes of the slice: x: 4, y: 8, z: 8, core: 2. Of those that a mesh axis runs over, the one named last changes fastest.
Arguments:
- prompt_keys: bfloat16 [8, 2048, 512], P('batch', 'ctx', 'pair'), may hold values from -6 to 6
- prompt_values: bfloat16 [8, 2048, 512], P('batch', 'ctx', 'pair'), may hold values from -6 to 6
- queries: bfloat16 [8, 2, 1024, 4096], P('batch', 'pair', 'ctx'), may hold values from -6 to 6
- resp_keys: bfloat16 [8, 2, 1024, 512], P('batch', 'pair', 'ctx'), may hold values from -6 to 6
- resp_values: bfloat16 [8, 2, 1024, 512], P('batch', 'pair', 'ctx'), may hold values from -6 to 6
- resp_grads: bfloat16 [8, 2, 1024, 4096], P('batch', 'pair', 'ctx'), may hold values from -640 to 640
- resp_lse: bfloat16 [8, 2, 1024, 32], P('batch', 'pair', 'ctx'), may hold values from 6 to 9
- resp_delta: bfloat16 [8, 2, 1024, 32], P('batch', 'pair', 'ctx'), may hold values from -6144 to 6144
- logratio: float32 [8, 2, 1024], P('batch', None, 'ctx'), may hold values from -4 to 4
- lengths: int32 [8, 3], P('batch'), may hold values from 256 to 2048, as said below
Outputs:
- prompt_key_grad: bfloat16 [8, 2048, 512], P('batch', 'ctx', 'pair')
- prompt_value_grad: bfloat16 [8, 2048, 512], P('batch', 'ctx', 'pair')
- query_grad: bfloat16 [8, 2, 1024, 4096], P('batch', None, 'ctx', 'pair')
- key_grad: bfloat16 [8, 2, 1024, 512], P('batch', None, 'ctx', 'pair')
- value_grad: bfloat16 [8, 2, 1024, 512], P('batch', None, 'ctx', 'pair')
- pair_gate: float32 [8], P('batch')
Inputs may be any that keep to these rules, and one draw needn't show every extreme that they name: `lengths`: column 0 holds 512 to 2048, and 2048 in some pair; columns 1 and 2 hold 256 to 1024, and 1024 in some response.
All inputs are finite; a program needn't handle non-finite values.
Results may differ from a plain program's by a relative error of at most 0.02.
Values may be sent and summed in bfloat16 or wider, within the bound.
No kernel may reach another device: no remote copies, remote signals or barrier semaphores. Data moves between devices by JAX's collectives and lax.ppermute only.
A program may use at most 128 MiB of HBM per device.

v0:
```python
import jax
import jax.numpy as jnp
from jax import lax
from jax.sharding import PartitionSpec as P

beta_coef = 0.1


def group_count(shards, shard_rows, upper):
    limit = max(1, min(upper, 1024 // shard_rows))
    return max(
        (divisor for divisor in range(1, shards + 1) if shards % divisor == 0 and divisor <= limit)
    )


def fold_pieces(step_fn, shard_rows):

    def fold_piece(loop_carry_state, pieces, first_row):
        key_piece, value_piece = pieces
        row_axis = key_piece.ndim - 2
        total_rows = key_piece.shape[row_axis]
        shards = total_rows // shard_rows
        per_turn = group_count(shards, shard_rows, shards) * shard_rows

        def one_turn(turn_index, inner):
            offset_row = turn_index * per_turn
            key_block = lax.dynamic_slice_in_dim(key_piece, offset_row, per_turn, row_axis)
            value_block = lax.dynamic_slice_in_dim(value_piece, offset_row, per_turn, row_axis)
            return step_fn(inner, key_block, value_block, offset_row)

        return lax.fori_loop(0, total_rows // per_turn, one_turn, loop_carry_state)

    return fold_piece


def per_device(
    prompt_keys,
    prompt_values,
    queries,
    resp_keys,
    resp_values,
    resp_grads,
    resp_lse,
    resp_delta,
    logratio,
    lengths,
):
    pair_count = lax.axis_size("pair")
    ctx_count = lax.axis_size("ctx")
    ctx_index = lax.axis_index("ctx")
    side_index = lax.axis_index("pair")
    resp_rows = queries.shape[2]
    prompt_rows = prompt_keys.shape[1]
    head_count = resp_lse.shape[3]
    head_size = queries.shape[3] // head_count
    kv_heads = resp_keys.shape[3] // head_size
    kv_local = kv_heads // pair_count
    group_size = head_count // kv_heads
    scale_factor = head_size ** (-0.5)
    row_groups = resp_rows * group_size
    flat_rows = pair_count * row_groups
    prompt_total = prompt_rows * ctx_count
    resp_total = resp_rows * ctx_count
    signed_grads = jnp.where(side_index == 0, -resp_grads[0, 0], resp_grads[0, 0])
    signed_delta = jnp.where(side_index == 0, -resp_delta[0, 0], resp_delta[0, 0])

    def owner_layout(values):
        return values.reshape(resp_rows, pair_count, values.shape[1] // pair_count)

    moved = (
        lax.all_to_all(
            owner_layout(queries[0, 0]), "pair", split_axis=1, concat_axis=0, tiled=True
        ),
        lax.all_to_all(owner_layout(signed_grads), "pair", split_axis=1, concat_axis=0, tiled=True),
        lax.all_to_all(
            owner_layout(resp_keys[0, 0]), "pair", split_axis=1, concat_axis=0, tiled=True
        ),
        lax.all_to_all(
            owner_layout(resp_values[0, 0]), "pair", split_axis=1, concat_axis=0, tiled=True
        ),
        lax.all_to_all(
            owner_layout(resp_lse[0, 0]), "pair", split_axis=1, concat_axis=0, tiled=True
        ),
        lax.all_to_all(owner_layout(signed_delta), "pair", split_axis=1, concat_axis=0, tiled=True),
    )

    def head_major(values):
        shaped = values.reshape(pair_count, resp_rows, kv_local, group_size, head_size)
        return shaped.transpose(2, 0, 1, 3, 4).reshape(kv_local, pair_count, row_groups, head_size)

    def stat_major(values):
        shaped = values.reshape(pair_count, resp_rows, kv_local, group_size)
        return shaped.transpose(2, 0, 1, 3).reshape(kv_local, pair_count, row_groups)

    query_heads = head_major(moved[0])
    grad_heads = head_major(moved[1])
    resp_key_own = moved[2].reshape(pair_count, resp_rows, kv_local * head_size)
    resp_value_own = moved[3].reshape(pair_count, resp_rows, kv_local * head_size)
    lse_low = stat_major(moved[4])
    delta_low = stat_major(moved[5])
    lse_heads = lse_low.astype(jnp.float32)
    delta_heads = delta_low.astype(jnp.float32)
    row_position = ctx_index * resp_rows + jnp.arange(row_groups, dtype=jnp.int32) // group_size
    row_live = row_position[None, :] < lengths[0, 1:3][:, None]
    prompt_length = lengths[0, 0]
    query_flat = query_heads.reshape(kv_local, flat_rows, head_size)
    grad_flat = grad_heads.reshape(kv_local, flat_rows, head_size)
    lse_flat = lse_heads.reshape(kv_local, flat_rows)
    delta_flat = delta_heads.reshape(kv_local, flat_rows)
    live_flat = row_live.reshape(flat_rows)

    def make_prompt_step():

        def prompt_step(loop_carry_state, key_block, value_block, first_row):
            query_acc = loop_carry_state[0]
            row_count = key_block.shape[1]
            key_rows = key_block[0].reshape(row_count, kv_local, head_size)
            value_rows = value_block[0].reshape(row_count, kv_local, head_size)
            scores = scale_factor * jnp.einsum(
                "kad,amd->kam", key_rows, query_flat, preferred_element_type=jnp.float32
            )
            key_live = first_row + jnp.arange(row_count, dtype=jnp.int32) < prompt_length
            allowed = key_live[:, None, None] & live_flat[None, None, :]
            weights = jnp.where(allowed, jnp.exp(scores - lse_flat[None]), 0.0)
            weight_grads = jnp.einsum(
                "kad,amd->kam", value_rows, grad_flat, preferred_element_type=jnp.float32
            )
            score_grads = (weights * (weight_grads - delta_flat[None])).astype(jnp.bfloat16)
            query_acc = query_acc + scale_factor * jnp.einsum(
                "kam,kad->amd", score_grads, key_rows, preferred_element_type=jnp.float32
            )
            weight_lower_precision = weights.astype(jnp.bfloat16)
            key_part = scale_factor * jnp.einsum(
                "kam,amd->kad", score_grads, query_flat, preferred_element_type=jnp.float32
            )
            value_part = jnp.einsum(
                "kam,amd->kad",
                weight_lower_precision,
                grad_flat,
                preferred_element_type=jnp.float32,
            )
            key_buffer = lax.dynamic_update_slice_in_dim(
                loop_carry_state[1], key_part, first_row, 0
            )
            value_buffer = lax.dynamic_update_slice_in_dim(
                loop_carry_state[2], value_part, first_row, 0
            )
            return (query_acc, key_buffer, value_buffer)

        return prompt_step

    def resp_step(loop_carry_state, key_block, value_block, first_row):
        query_acc, key_buffer, value_buffer = loop_carry_state
        row_count = key_block.shape[1]
        key_rows = key_block.reshape(pair_count, row_count, kv_local, head_size)
        value_rows = value_block.reshape(pair_count, row_count, kv_local, head_size)
        scores = scale_factor * jnp.einsum(
            "skad,asnd->askn", key_rows, query_heads, preferred_element_type=jnp.float32
        )
        key_position = first_row + jnp.arange(row_count, dtype=jnp.int32)
        causal = key_position[:, None] <= row_position[None, :]
        allowed = causal[None, None, :, :] & row_live[None, :, None, :]
        weights = jnp.where(allowed, jnp.exp(scores - lse_heads[:, :, None, :]), 0.0)
        weight_grads = jnp.einsum(
            "skad,asnd->askn", value_rows, grad_heads, preferred_element_type=jnp.float32
        )
        score_grads = (weights * (weight_grads - delta_heads[:, :, None, :])).astype(jnp.bfloat16)
        weight_lower_precision = weights.astype(jnp.bfloat16)
        query_acc = query_acc + scale_factor * jnp.einsum(
            "askn,skad->asnd", score_grads, key_rows, preferred_element_type=jnp.float32
        )
        key_part = scale_factor * jnp.einsum(
            "askn,asnd->ksad", score_grads, query_heads, preferred_element_type=jnp.float32
        )
        value_part = jnp.einsum(
            "askn,asnd->ksad",
            weight_lower_precision,
            grad_heads,
            preferred_element_type=jnp.float32,
        )
        key_buffer = key_part
        value_buffer = value_part
        return (query_acc, key_buffer, value_buffer)

    query_zero = jnp.zeros((kv_local, flat_rows, head_size), jnp.float32)
    prompt_fn = fold_pieces(make_prompt_step(), prompt_rows)
    prompt_init = (
        query_zero,
        jnp.zeros((prompt_total, kv_local, head_size), jnp.float32),
        jnp.zeros((prompt_total, kv_local, head_size), jnp.float32),
    )
    prompt_carry = prompt_fn(
        prompt_init,
        (
            lax.all_gather(prompt_keys, "ctx", axis=1, tiled=True),
            lax.all_gather(prompt_values, "ctx", axis=1, tiled=True),
        ),
        jnp.int32(0),
    )
    resp_zero = jnp.zeros((resp_total, pair_count, kv_local, head_size), jnp.float32)
    resp_init = (
        jnp.zeros((kv_local, pair_count, row_groups, head_size), jnp.float32),
        resp_zero,
        resp_zero,
    )
    resp_carry = fold_pieces(resp_step, resp_rows)(
        resp_init,
        (
            lax.all_gather(resp_key_own, "ctx", axis=1, tiled=True),
            lax.all_gather(resp_value_own, "ctx", axis=1, tiled=True),
        ),
        jnp.int32(0),
    )
    positions = ctx_index * resp_rows + jnp.arange(resp_rows, dtype=jnp.int32)
    chosen = jnp.sum(jnp.where(positions < lengths[0, 1], logratio[0, 0], 0.0))
    rejected = jnp.sum(jnp.where(positions < lengths[0, 2], logratio[0, 1], 0.0))
    margin = lax.psum(chosen - rejected, "ctx")
    gate = beta_coef * jax.nn.sigmoid(-beta_coef * margin)
    summed = (
        lax.psum_scatter(
            prompt_carry[1].astype(jnp.bfloat16), "ctx", scatter_dimension=0, tiled=True
        ).astype(jnp.float32),
        lax.psum_scatter(
            prompt_carry[2].astype(jnp.bfloat16), "ctx", scatter_dimension=0, tiled=True
        ).astype(jnp.float32),
        lax.psum_scatter(
            resp_carry[1].astype(jnp.bfloat16), "ctx", scatter_dimension=0, tiled=True
        ).astype(jnp.float32),
        lax.psum_scatter(
            resp_carry[2].astype(jnp.bfloat16), "ctx", scatter_dimension=0, tiled=True
        ).astype(jnp.float32),
    )
    prompt_key_grad = (
        (gate * summed[0]).reshape(1, prompt_rows, kv_local * head_size).astype(jnp.bfloat16)
    )
    prompt_value_grad = (
        (gate * summed[1]).reshape(1, prompt_rows, kv_local * head_size).astype(jnp.bfloat16)
    )

    def side_major(values):
        return values.transpose(1, 0, 2, 3).reshape(1, pair_count, resp_rows, kv_local * head_size)

    key_grad = side_major(gate * summed[2]).astype(jnp.bfloat16)
    value_grad = side_major(gate * summed[3]).astype(jnp.bfloat16)
    query_gradient_total = (
        prompt_carry[0].reshape(kv_local, pair_count, row_groups, head_size) + resp_carry[0]
    )
    query_gradient_total = query_gradient_total.reshape(
        kv_local, pair_count, resp_rows, group_size, head_size
    ).transpose(1, 2, 0, 3, 4)
    query_grad = (
        gate
        * query_gradient_total.reshape(1, pair_count, resp_rows, kv_local * group_size * head_size)
    ).astype(jnp.bfloat16)
    pair_gate = jnp.reshape(gate, (1,))
    return (prompt_key_grad, prompt_value_grad, query_grad, key_grad, value_grad, pair_gate)


def solution(mesh):
    placed = (
        P("batch", "ctx", "pair"),
        P("batch", "ctx", "pair"),
        P("batch", "pair", "ctx", None),
        P("batch", "pair", "ctx", None),
        P("batch", "pair", "ctx", None),
        P("batch", "pair", "ctx", None),
        P("batch", "pair", "ctx", None),
        P("batch", "pair", "ctx", None),
        P("batch", None, "ctx"),
        P("batch", None),
    )
    return jax.shard_map(
        per_device,
        mesh=mesh,
        in_specs=placed,
        out_specs=(
            P("batch", "ctx", "pair"),
            P("batch", "ctx", "pair"),
            P("batch", None, "ctx", "pair"),
            P("batch", None, "ctx", "pair"),
            P("batch", None, "ctx", "pair"),
            P("batch"),
        ),
        check_vma=False,
    )
```

profile of v0, /device:TPU:6, one launch (start us, length us, event | category | flops | bytes accessed | tf_op | source)
XLA Modules:
  0.0 1246.2 jit_solution(5610604232332728598)
XLA Ops:
  7.2 0.7 all-gather.7.cloned.1.call-update
  8.0 0.7 all-gather.9.cloned.1.call-update
  8.7 0.8 reshape_squeeze.14
  9.5 3.7 all_to_all.84
  13.9 0.8 reshape_squeeze.15
  15.3 3.3 all-to-all-start.5
  18.6 1.1 reshape_squeeze.12
  19.7 0.8 copy.133
  20.5 3.4 all-to-all-start
  24.7 1.4 fusion.73
  26.1 0.7 slice_bitcast_fusion
  26.9 0.8 copy.135
  27.6 0.7 reshape.287
  28.3 3.2 all-to-all-start.1
  31.6 0.7 copy-done.4
  32.3 1.1 squeeze.42
  33.5 0.9 negate_select_fusion
  34.4 3.4 all-to-all-start.2
  38.2 0.7 reshape.289
  39.4 3.2 all-to-all-start.3
  42.7 0.7 copy-done.6
  43.4 0.7 copy.227
  44.4 51.7 %all-gather.7.cloned.1.call-done = bf16[1,2048,256]{2,1,0:T(8,128)(2,1)} async-done(((bf16[1,64,256]{2,1,0:T(8,128)(2,1)}), bf16[1,2048,256]{2,1,0:T(8,128)(2,1)}) %all-gather.7.cloned.1.call-update) | async-done | bytes 1048592 | tf_op jit(solution)/shard_map/all_gather | solution.py:195
  96.2 82.6 %all-gather.9.cloned.1.call-done = bf16[1,2048,256]{2,1,0:T(8,128)(2,1)} async-done(((bf16[1,64,256]{2,1,0:T(8,128)(2,1)}), bf16[1,2048,256]{2,1,0:T(8,128)(2,1)}) %all-gather.9.cloned.1.call-update) | async-done | bytes 1048592 | tf_op jit(solution)/shard_map/all_gather | solution.py:196
  178.8 1.2 broadcast.174
  180.0 1.2 broadcast.174.clone
  181.1 32.6 %while.5 = (s32[]{:T(128)}, f32[2,512,128]{2,1,0:T(8,128)}, bf16[2048,2,128]{2,0,1:T(8,128)(2,1)}, bf16[2048,2,128]{2,0,1:T(8,128)(2,1)}, s32[]{:T(128)}, /*inde...) while((s32[]{:T(128)}, f32[2,512,128]{2,1,0:T(8,128)}, ...), condition=%wide.region_4.5_spmd.clone, body=%wide.region_3.4_spmd.clone.sunk | while | flops 1353845248 | bytes 56657256 | solution.py:31
  181.1 1.3 constant_dynamic-slice_fusion.3
  182.6 2.7 fusion.108
  185.3 1.0 copy.234
  186.4 0.7 add_compare_fusion.2
  187.4 4.0 multiply_convert_fusion.7
  191.5 1.7 fusion.109
  193.2 1.5 fusion.110
  194.7 1.1 fusion.111
  195.8 1.0 copy-done.3
  196.8 1.3 constant_dynamic-slice_fusion.3
  198.3 2.7 fusion.108
  201.0 1.0 copy.234
  202.1 0.7 add_compare_fusion.2
  203.1 4.0 multiply_convert_fusion.7
  207.2 2.9 fusion.109
  210.1 1.5 fusion.110
  211.6 1.1 fusion.111
  212.7 1.0 copy-done.3
  215.0 47.0 %all-gather.11.cloned.1.call-done = bf16[2,1024,1,256]{3,0,2,1:T(2,128)(2,1)} async-done(((bf16[2,32,1,256]{3,0,2,1:T(2,128)(2,1)}), bf16[2,1024,1,256]{3,0,2,1:T(2,128)(2,1)}) %all-gather.11.cloned.1.call-update) | async-done | bytes 1048592 | tf_op jit(solution)/shard_map/all_gather | solution.py:209
  262.0 2.4 copy.148
  264.5 80.6 %all-gather.13.cloned.1.call-done = bf16[2,1024,1,256]{3,0,2,1:T(2,128)(2,1)} async-done(((bf16[2,32,1,256]{3,0,2,1:T(2,128)(2,1)}), bf16[2,1024,1,256]{3,0,2,1:T(2,128)(2,1)}) %all-gather.13.cloned.1.call-update) | async-done | bytes 1048592 | tf_op jit(solution)/shard_map/all_gather | solution.py:210
  345.1 2.4 copy.154
  347.6 2.6 fusion.38
  350.2 1.6 fusion.37
  351.8 1.3 copy-done.12
  353.1 1.7 fusion.51
  354.9 3.4 fusion.48
  358.3 1.9 fusion.68
  361.5 67.8 %psum.7 = f32[]{:T(128)} all-reduce(f32[]{:T(128)S(6)} %sub.88), channel_id=1, replica_groups=mesh['batch'=8,'pair'=2,'ctx'=32] {'ctx'}, use_global_device_ids=true, to_apply=%region_2.3 | all-reduce | flops 1 | bytes 8 | tf_op jit(solution)/shard_map/psum | solution.py:217
  430.1 2.5 fusion.57
  432.6 0.8 convert_element_type.194
  433.4 133.4 %reduce-scatter.7.cloned.1.call-done = bf16[64,2,128]{2,0,1:T(8,128)(2,1)} async-done(((bf16[2048,2,128]{2,0,1:T(8,128)(2,1)}), bf16[64,2,128]{2,0,1:T(8,128)(2,1)}) %reduce-scatter.7.cloned.1.call-update) | async-done | bytes 32784 | tf_op jit(solution)/shard_map/reduce_scatter | solution.py:223
  566.8 222.2 %reduce-scatter.5.cloned.1.call-done = bf16[64,2,128]{2,0,1:T(8,128)(2,1)} async-done(((bf16[2048,2,128]{2,0,1:T(8,128)(2,1)}), bf16[64,2,128]{2,0,1:T(8,128)(2,1)}) %reduce-scatter.5.cloned.1.call-update) | async-done | bytes 32784 | tf_op jit(solution)/shard_map/reduce_scatter | solution.py:220
  789.0 0.8 multiply_convert_fusion.4
  791.2 221.4 %reduce-scatter.9.cloned.1.call-done = bf16[32,2,2,128]{3,0,2,1:T(8,128)(2,1)} async-done(((bf16[1024,2,2,128]{3,0,2,1:T(8,128)(2,1)}), bf16[32,2,2,128]{3,0,2,1:T(8,128)(2,1)}) %reduce-scatter.9.cloned.1.call-update) | async-done | bytes 32784 | tf_op jit(solution)/shard_map/reduce_scatter | solution.py:226
  1012.6 223.5 %reduce-scatter.11.cloned.1.call-done = bf16[32,2,2,128]{3,0,2,1:T(8,128)(2,1)} async-done(((bf16[1024,2,2,128]{3,0,2,1:T(8,128)(2,1)}), bf16[32,2,2,128]{3,0,2,1:T(8,128)(2,1)}) %reduce-scatter.11.cloned.1.call-update) | async-done | bytes 32784 | tf_op jit(solution)/shard_map/reduce_scatter | solution.py:229
  1236.1 0.8 fusion.64
  (91 shorter events, 8.8 us)
Async XLA Ops:
  7.2 30.9 %copy-start.10 = (bf16[1,1,32,32]{3,2,1,0:T(8,128)(2,1)S(1)}, bf16[1,1,32,32]{3,2,1,0:T(8,128)(2,1)}, u32[]{:S(2)}) copy-start(bf16[1,1,32,32]{3,2,1,0:T(8,128)(2,1)} %param.19) | copy-start | bytes 6148
  7.2 89.0 %all-gather.7.cloned.1.call-start = ((), (), s32[]{:S(2)}) async-start(), calls=%async_computation.10 | async-start | bytes 1081344 | tf_op jit(solution)/shard_map/all_gather | solution.py:195
  7.9 170.9 %all-gather.9.cloned.1.call-start = ((), (), s32[]{:S(2)}) async-start(), calls=%async_computation.11 | async-start | bytes 1081344 | tf_op jit(solution)/shard_map/all_gather | solution.py:196
  8.7 253.4 %all-gather.11.cloned.1.call-start = ((), (), s32[]{:S(2)}) async-start(), calls=%async_computation.16 | async-start | bytes 1081344 | tf_op jit(solution)/shard_map/all_gather | solution.py:209
  15.3 5.2 all-to-all-start.5
  20.5 7.8 all-to-all-start
  24.0 321.1 %all-gather.13.cloned.1.call-start = ((), (), s32[]{:S(2)}) async-start(), calls=%async_computation.17 | async-start | bytes 1081344 | tf_op jit(solution)/shard_map/all_gather | solution.py:210
  28.3 6.1 all-to-all-start.1
  31.6 0.7 copy-start.4
  34.4 5.0 all-to-all-start.2
  39.4 4.8 all-to-all-start.3
  42.6 524.2 %reduce-scatter.7.cloned.1.call-start = ((), (), s32[]{:S(2)}) async-start(), calls=%async_computation.13 | async-start | bytes 1081344 | tf_op jit(solution)/shard_map/reduce_scatter | solution.py:223
  42.7 0.7 copy-start.6
  191.4 3.3 copy-start
  191.4 3.3 copy-start.2
  191.5 3.3 copy-start.8
  195.8 1.0 copy-start.3
  207.2 4.5 copy-start
  207.2 4.5 copy-start.2
  207.2 4.5 copy-start.8
  212.7 1.0 copy-start.3
  213.7 133.8 %copy-start.5 = (bf16[8,8,16,128]{3,2,1,0:T(8,128)(2,1)S(1)}, bf16[8,8,16,128]{3,2,1,0:T(8,128)(2,1)}, u32[]{:S(2)}) copy-start(bf16[8,8,16,128]{3,2,1,0:T(8,128)(2,1)} %copy-done.4) | copy-start | bytes 786436
  213.7 575.3 %reduce-scatter.5.cloned.1.call-start = ((), (), s32[]{:S(2)}) async-start(), calls=%async_computation.12 | async-start | bytes 1081344 | tf_op jit(solution)/shard_map/reduce_scatter | solution.py:220
  214.3 798.3 %reduce-scatter.9.cloned.1.call-start = ((), (), s32[]{:S(2)}) async-start(), calls=%async_computation.14 | async-start | bytes 1081344 | tf_op jit(solution)/shard_map/reduce_scatter | solution.py:226
  347.5 2.6 copy-start.7
  351.8 1.4 copy-start.12
  351.8 3.2 copy-start.9
  354.9 3.5 copy-start.11
  354.9 75.2 %copy-start.1 = (f32[2,512,128]{2,1,0:T(8,128)S(1)}, f32[2,512,128]{2,1,0:T(8,128)}, u32[]{:S(2)}) copy-start(f32[2,512,128]{2,1,0:T(8,128)} %get-tuple-element.246) | copy-start | bytes 1572868
  354.9 881.2 %reduce-scatter.11.cloned.1.call-start = ((), (), s32[]{:S(2)}) async-start(), calls=%async_computation.15 | async-start | bytes 1081344 | tf_op jit(solution)/shard_map/reduce_scatter | solution.py:229
Sparse Core Ops, SparseCore 0:
  11.2 84.9 all-gather.6
  99.3 79.4 all-gather.8
  182.5 79.4 all-gather.10
  265.6 79.4 all-gather.12
  349.3 217.4 reduce-scatter.6
  571.0 217.9 reduce-scatter.4
  793.4 219.1 reduce-scatter.8
  1017.0 219.0 reduce-scatter.10
where the time goes:
time: 1250 us
  waiting for transfers between devices  1060 us (85%)
  blocking collectives  71.5 us (6%)
  matrix products  35 us (3%)
  local copies, waits for them, and re-layouts  32.9 us (3%)
  between operations  17.6 us (1%)
  starting transfers between devices  17.1 us (1%)
    reduce_scatter x1, waiting for transfers between devices, per_device(): lax.psum_scatter(resp_carry[2].astype(jnp.bfloat16), 'ctx', scatter_dimen...  224 us
    reduce_scatter x1, waiting for transfers between devices, per_device(): lax.psum_scatter(prompt_carry[1].astype(jnp.bfloat16), 'ctx', scatter_dim...  222 us
    reduce_scatter x1, waiting for transfers between devices, per_device(): lax.psum_scatter(resp_carry[1].astype(jnp.bfloat16), 'ctx', scatter_dimen...  221 us
    reduce_scatter x1, waiting for transfers between devices, per_device(): lax.psum_scatter(prompt_carry[2].astype(jnp.bfloat16), 'ctx', scatter_dim...  133 us
    all_gather x1, waiting for transfers between devices, per_device(): lax.all_gather(prompt_values, 'ctx', axis=1, tiled=True)  82.6 us
    all_gather x1, waiting for transfers between devices, per_device(): lax.all_gather(resp_value_own, 'ctx', axis=1, tiled=True)  80.6 us
    psum x1, blocking collectives, per_device(): margin = lax.psum(chosen - rejected, 'ctx')  67.8 us
    all_gather x1, waiting for transfers between devices, per_device(): lax.all_gather(prompt_keys, 'ctx', axis=1, tiled=True)  51.7 us
  transfers between devices with their start and end apart: 13, of which 9 were waited for; matrix products, arithmetic and copies ran while one was open for 5% of the time, Pallas kernels for 0%

commit v1 on v0

v1 whole, which is shorter than its diff:
```python
import functools

import jax
import jax.numpy as jnp
from jax import lax
from jax.experimental import pallas as pl
from jax.experimental.pallas import tpu as pltpu
from jax.sharding import Mesh, PartitionSpec as P

beta_coef = 0.1
f32, bf16 = jnp.float32, jnp.bfloat16
LANES = 128
CTX = ("y", "x")
VMEM = pltpu.VMEM
SMEM = pltpu.SMEM

POS = 32
HEADS = 4
GROUP = 8
TILE = POS * GROUP
ROWS_Y = 8
CTX_N = 32
PROMPT_HALF = 32
RESP_HALF = 16
STAT_ROWS = 16
QUERY_ROWS = 2 * TILE + STAT_ROWS
DEAD = 1e30


def dot(a, b, dims):
    return lax.dot_general(a, b, (dims, ((), ())), preferred_element_type=f32)


def call(kernel, out_shape, n_in, smem=(), flops=0, scratch=(), size=0):
    specs = [pl.BlockSpec(memory_space=SMEM if i in smem else VMEM) for i in range(n_in)]
    many = isinstance(out_shape, tuple)
    return pl.pallas_call(
        kernel,
        out_shape=out_shape,
        in_specs=specs,
        out_specs=tuple(pl.BlockSpec(memory_space=VMEM) for _ in out_shape)
        if many
        else pl.BlockSpec(memory_space=VMEM),
        scratch_shapes=list(scratch),
        compiler_params=pltpu.CompilerParams(vmem_limit_bytes=40 * 2**20),
        cost_estimate=pl.CostEstimate(flops=flops, bytes_accessed=size, transcendentals=0),
    )


def pack_kernel(q_ref, g_ref, lse_ref, delta_ref, pk_ref, pv_ref, rk_ref, rv_ref, query_ref, pair_ref):
    sign = jnp.where(lax.axis_index("pair") == 0, -1.0, 1.0).astype(f32)
    for p in range(2):
        for h in range(2):
            columns = slice(h * LANES, (h + 1) * LANES)
            rows = slice(p * PROMPT_HALF, (p + 1) * PROMPT_HALF)
            pair_ref[p, h * 32 : h * 32 + 32, :] = pk_ref[rows, columns]
            pair_ref[p, 64 + h * 32 : 96 + h * 32, :] = pv_ref[rows, columns]
        for h in range(HEADS):
            columns = slice(h * LANES, (h + 1) * LANES)
            rows = slice(p * RESP_HALF, (p + 1) * RESP_HALF)
            pair_ref[p, 128 + h * 16 : 144 + h * 16, :] = rk_ref[rows, columns]
            pair_ref[p, 192 + h * 16 : 208 + h * 16, :] = rv_ref[rows, columns]
    for x in range(HEADS):
        for h in range(GROUP):
            columns = slice((x * GROUP + h) * LANES, (x * GROUP + h + 1) * LANES)
            query = q_ref[:, columns]
            grad = (g_ref[:, columns].astype(f32) * sign).astype(bf16)
            for p in range(2):
                query_ref[p * HEADS + x, h * POS : (h + 1) * POS, :] = query
                query_ref[p * HEADS + x, TILE + h * POS : TILE + (h + 1) * POS, :] = grad

    heads = HEADS * GROUP
    lane = lax.broadcasted_iota(jnp.int32, (POS, TILE), 1)
    spread = (lane % POS == lax.broadcasted_iota(jnp.int32, (POS, TILE), 0)).astype(bf16)
    lane = lax.broadcasted_iota(jnp.int32, (heads, TILE), 1)
    keep = lax.broadcasted_iota(jnp.int32, (heads, TILE), 0) % GROUP == lane // POS

    def rows_of(ref):
        spread_out = jnp.where(keep, dot(ref[...], spread, ((0,), (0,))), 0.0)
        return jnp.sum(spread_out.reshape(HEADS, GROUP, TILE), axis=1)

    lse, delta = rows_of(lse_ref), rows_of(delta_ref) * sign
    row = lax.broadcasted_iota(jnp.int32, (STAT_ROWS, LANES), 0)
    for x in range(HEADS):
        parts = [r[x : x + 1, i * LANES : (i + 1) * LANES] for r in (lse, delta) for i in range(2)]
        block = jnp.zeros((STAT_ROWS, LANES), f32)
        for i, part in enumerate(parts):
            block = jnp.where(row == i, part, block)
        for p in range(2):
            query_ref[p * HEADS + x, 2 * TILE :, :] = block.astype(bf16)


def spread_kernel(lengths_ref, logratio_ref, pair_ref, prompt_ref, resp_ref):
    core = lax.axis_index("pair")
    ctx = lax.axis_index("y") * HEADS + lax.axis_index("x")
    first = ctx * 2 * PROMPT_HALF + core * PROMPT_HALF
    key_live = first + lax.broadcasted_iota(jnp.int32, (PROMPT_HALF, LANES), 0) < lengths_ref[0, 0]
    position = ctx * POS + lax.broadcasted_iota(jnp.int32, (1, POS), 1)
    chosen = jnp.where(position < lengths_ref[0, 1], logratio_ref[0:1, :], 0.0)
    rejected = jnp.where(position < lengths_ref[0, 2], logratio_ref[1:2, :], 0.0)
    margin = jnp.sum(chosen - rejected, axis=1, keepdims=True)
    high = margin.astype(bf16).astype(f32)
    middle = (margin - high).astype(bf16).astype(f32)
    low = margin - high - middle
    lane = lax.broadcasted_iota(jnp.int32, (16, LANES), 1)
    row = lax.broadcasted_iota(jnp.int32, (16, LANES), 0)
    block = jnp.where(lane == 0, high, jnp.where(lane == 1, middle, jnp.where(lane == 2, low, 0.0)))
    block = jnp.where(row == 0, block, 0.0).astype(bf16)
    for x in range(HEADS):
        half, odd = x // 2, x % 2
        key = pair_ref[half, odd * 32 : odd * 32 + 32, :]
        key = jnp.where(key_live, key.astype(f32), 0.0).astype(bf16)
        value = pair_ref[half, 64 + odd * 32 : 96 + odd * 32, :]
        for y in range(ROWS_Y):
            to = y * HEADS + x
            prompt_ref[to, 0:32, :] = key
            prompt_ref[to, 32:64, :] = value
            for s in range(2):
                resp_ref[to, 32 * s : 32 * s + 16, :] = pair_ref[s, 128 + 16 * x : 144 + 16 * x, :]
                resp_ref[to, 32 * s + 16 : 32 * s + 32, :] = pair_ref[s, 192 + 16 * x : 208 + 16 * x, :]
            resp_ref[to, 64:80, :] = block


def row_stats(lengths_ref, query_ref, tile):
    block = query_ref[tile, 2 * TILE :, :].astype(f32)
    lse = jnp.concatenate([block[0:1], block[1:2]], axis=1) * 1.4426950408889634
    delta = jnp.concatenate([block[2:3], block[3:4]], axis=1)
    lane = lax.broadcasted_iota(jnp.int32, (1, TILE), 1)
    side = tile // HEADS
    first = (lax.axis_index("y") * HEADS + tile % HEADS) * POS
    position = first + lane % POS
    lse = jnp.where(position < lengths_ref[0, 1 + side], lse, DEAD)
    return lse, delta, position


def cell(key, value, query, grad, lse, delta, allowed=None):
    scale = LANES**-0.5
    scores = dot(key, query, ((1,), (1,)))
    weights = jnp.exp2(scores * (scale * 1.4426950408889634) - lse)
    if allowed is not None:
        weights = jnp.where(allowed, weights, 0.0)
    weight_grads = dot(value, grad, ((1,), (1,)))
    score_grads = (weights * (weight_grads - delta)).astype(bf16)
    return weights.astype(bf16), score_grads


def prompt_kernel(lengths_ref, query_ref, kv_ref, acc_ref, out_ref, key_acc, value_acc):
    scale = LANES**-0.5
    key_acc[...] = jnp.zeros_like(key_acc)
    value_acc[...] = jnp.zeros_like(value_acc)
    per = 8
    rows = per * PROMPT_HALF

    @pl.loop(0, 2 * HEADS)
    def _(tile):
        lse, delta, _ = row_stats(lengths_ref, query_ref, tile)
        query = query_ref[tile, 0:TILE, :]
        grad = query_ref[tile, TILE : 2 * TILE, :]
        total = None
        for c in range(CTX_N // per):
            key = kv_ref[c * per : (c + 1) * per, 0:PROMPT_HALF, :].reshape(rows, LANES)
            value = kv_ref[c * per : (c + 1) * per, PROMPT_HALF:, :].reshape(rows, LANES)
            weights, score_grads = cell(key, value, query, grad, lse, delta)
            at = slice(c * rows, (c + 1) * rows)
            value_acc[at, :] += dot(weights, grad, ((1,), (0,)))
            key_acc[at, :] += dot(score_grads, query, ((1,), (0,)))
            term = dot(score_grads, key, ((0,), (0,)))
            total = term if total is None else total + term
        acc_ref[tile] = total

    out_ref[:, 0:PROMPT_HALF, :] = (key_acc[...] * scale).astype(bf16).reshape(CTX_N, PROMPT_HALF, LANES)
    out_ref[:, PROMPT_HALF:, :] = value_acc[...].astype(bf16).reshape(CTX_N, PROMPT_HALF, LANES)


def resp_kernel(lengths_ref, query_ref, kv_ref, acc_ref, out_ref, dq_ref, gate_ref, key_acc, value_acc):
    scale = LANES**-0.5
    margin = jnp.sum(kv_ref[:, 64:80, :].astype(f32), axis=(0, 1), keepdims=True).reshape(1, LANES)
    margin = jnp.sum(margin, axis=1, keepdims=True)
    gate_ref[...] = jnp.broadcast_to(beta_coef * jax.nn.sigmoid(-beta_coef * margin), gate_ref.shape)
    key_acc[...] = jnp.zeros_like(key_acc)
    value_acc[...] = jnp.zeros_like(value_acc)
    core = lax.axis_index("pair")
    per = 16
    rows = per * RESP_HALF
    for s in range(2):

        @pl.loop(0, HEADS)
        def _(x):
            tile = s * HEADS + x
            lse, delta, position = row_stats(lengths_ref, query_ref, tile)
            query = query_ref[tile, 0:TILE, :]
            grad = query_ref[tile, TILE : 2 * TILE, :]
            total = acc_ref[tile]
            for c in range(CTX_N // per):
                k0 = 32 * s
                key = kv_ref[c * per : (c + 1) * per, k0 : k0 + 16, :].reshape(rows, LANES)
                value = kv_ref[c * per : (c + 1) * per, k0 + 16 : k0 + 32, :].reshape(rows, LANES)
                index = lax.broadcasted_iota(jnp.int32, (rows, 1), 0)
                key_position = (c * per + index // RESP_HALF) * POS + core * RESP_HALF + index % RESP_HALF
                weights, score_grads = cell(key, value, query, grad, lse, delta, key_position <= position)
                at = slice((s * (CTX_N // per) + c) * rows, (s * (CTX_N // per) + c + 1) * rows)
                value_acc[at, :] += dot(weights, grad, ((1,), (0,)))
                key_acc[at, :] += dot(score_grads, query, ((1,), (0,)))
                total += dot(score_grads, key, ((0,), (0,)))
            dq_ref[x, s * TILE : (s + 1) * TILE, :] = (total * scale).astype(bf16)

        at = slice(s * CTX_N * RESP_HALF, (s + 1) * CTX_N * RESP_HALF)
        shape = (CTX_N, RESP_HALF, LANES)
        out_ref[:, 32 * s : 32 * s + 16, :] = (key_acc[at, :] * scale).astype(bf16).reshape(shape)
        out_ref[:, 32 * s + 16 : 32 * s + 32, :] = value_acc[at, :].astype(bf16).reshape(shape)


def sum_kernel(prompt, lengths_ref, gate_ref, part_ref, pair_ref):
    gate = gate_ref[0:1, 0:1]
    if prompt:
        ctx = lax.axis_index("y") * HEADS + lax.axis_index("x")
        first = ctx * 2 * PROMPT_HALF + lax.axis_index("pair") * PROMPT_HALF
        row = lax.broadcasted_iota(jnp.int32, (64, LANES), 0) % PROMPT_HALF
        live = first + row < lengths_ref[0, 0]
    for x in range(HEADS):
        total = part_ref[x].astype(f32)
        for y in range(1, ROWS_Y):
            total += part_ref[y * HEADS + x].astype(f32)
        total = total * gate
        if prompt:
            total = jnp.where(live, total, 0.0)
        pair_ref[x // 2, (x % 2) * 64 : (x % 2) * 64 + 64, :] = total.astype(bf16)


def prompt_final_kernel(pair_ref, key_ref, value_ref):
    for p in range(2):
        for h in range(2):
            columns = slice(h * LANES, (h + 1) * LANES)
            key_ref[0, p * 32 : p * 32 + 32, columns] = pair_ref[p, h * 64 : h * 64 + 32, :]
            value_ref[0, p * 32 : p * 32 + 32, columns] = pair_ref[p, h * 64 + 32 : h * 64 + 64, :]


def resp_final_kernel(pair_ref, key_ref, value_ref):
    for p in range(2):
        for h in range(2):
            columns = slice(h * LANES, (h + 1) * LANES)
            for s in range(2):
                at = h * 64 + 32 * s
                key_ref[0, s, p * 16 : p * 16 + 16, columns] = pair_ref[p, at : at + 16, :]
                value_ref[0, s, p * 16 : p * 16 + 16, columns] = pair_ref[p, at + 16 : at + 32, :]


def query_final_kernel(gate_ref, pair_ref, out_ref):
    gate = gate_ref[0:1, 0:1]
    for h in range(2):
        for s in range(2):
            for g in range(GROUP):
                rows = slice(h * 2 * TILE + s * TILE + g * POS, h * 2 * TILE + s * TILE + (g + 1) * POS)
                total = pair_ref[0, rows, :].astype(f32) + pair_ref[1, rows, :].astype(f32)
                column = (h * GROUP + g) * LANES
                out_ref[0, s, :, column : column + LANES] = (gate * total).astype(bf16)


def swap(values, axes):
    return lax.all_to_all(values, axes, split_axis=0, concat_axis=0, tiled=True)


def per_device(
    prompt_keys,
    prompt_values,
    queries,
    resp_keys,
    resp_values,
    resp_grads,
    resp_lse,
    resp_delta,
    logratio,
    lengths,
):
    shape = jax.ShapeDtypeStruct
    query_send, pair_send = call(
        pack_kernel,
        (shape((8, QUERY_ROWS, LANES), bf16), shape((2, 256, LANES), bf16)),
        8,
        size=2 * 2**20,
    )(
        queries[0, 0],
        resp_grads[0, 0],
        resp_lse[0, 0],
        resp_delta[0, 0],
        prompt_keys[0],
        prompt_values[0],
        resp_keys[0, 0],
        resp_values[0, 0],
    )
    query_rows = swap(query_send, ("pair", "x"))
    pair_rows = swap(pair_send, "pair")
    prompt_send, resp_send = call(
        spread_kernel,
        (shape((CTX_N, 64, LANES), bf16), shape((CTX_N, 80, LANES), bf16)),
        3,
        smem=(0,),
        size=2 * 2**20,
    )(lengths, logratio[0], pair_rows)
    prompt_kv = swap(prompt_send, CTX)
    resp_kv = swap(resp_send, CTX)
    acc, prompt_part = call(
        prompt_kernel,
        (shape((8, TILE, LANES), f32), shape((CTX_N, 64, LANES), bf16)),
        3,
        smem=(0,),
        scratch=(pltpu.VMEM((1024, LANES), f32), pltpu.VMEM((1024, LANES), f32)),
        flops=5 * 2 * 2048 * 1024 * 128 * 2,
        size=3 * 2**20,
    )(lengths, query_rows, prompt_kv)
    prompt_back = swap(prompt_part, CTX)
    resp_part, query_part, gate = call(
        resp_kernel,
        (
            shape((CTX_N, 64, LANES), bf16),
            shape((HEADS, 2 * TILE, LANES), bf16),
            shape((8, LANES), f32),
        ),
        4,
        smem=(0,),
        scratch=(pltpu.VMEM((1024, LANES), f32), pltpu.VMEM((1024, LANES), f32)),
        flops=5 * 2 * 1024 * 1024 * 128 * 2,
        size=3 * 2**20,
    )(lengths, query_rows, resp_kv, acc)
    resp_back = swap(resp_part, CTX)
    query_back = swap(query_part, "x")

    pair_shape = shape((2, 128, LANES), bf16)
    prompt_pair = call(functools.partial(sum_kernel, True), pair_shape, 3, smem=(0,), size=2**19)(
        lengths, gate, prompt_back
    )
    prompt_pair = swap(prompt_pair, "pair")
    prompt_key_grad, prompt_value_grad = call(
        prompt_final_kernel, (shape((1, 64, 256), bf16),) * 2, 1, size=2**17
    )(prompt_pair)

    query_pair = swap(query_back.reshape(2, 4 * TILE, LANES), "pair")
    query_grad = call(query_final_kernel, shape((1, 2, POS, 2048), bf16), 2, size=2**20)(gate, query_pair)

    resp_pair = call(functools.partial(sum_kernel, False), pair_shape, 3, smem=(0,), size=2**19)(
        lengths, gate, resp_back
    )
    resp_pair = swap(resp_pair, "pair")
    key_grad, value_grad = call(resp_final_kernel, (shape((1, 2, POS, 256), bf16),) * 2, 1, size=2**17)(
        resp_pair
    )
    return prompt_key_grad, prompt_value_grad, query_grad, key_grad, value_grad, gate[0, 0:1]


def solution(mesh):
    batch, pair, ctx = mesh.devices.shape
    split = Mesh(mesh.devices.reshape(batch, pair, ctx // HEADS, HEADS), ("batch", "pair", "y", "x"))
    prompt_spec = P("batch", CTX, "pair")
    resp_spec = P("batch", "pair", CTX, None)
    out_spec = P("batch", None, CTX, "pair")
    return jax.shard_map(
        per_device,
        mesh=split,
        in_specs=(
            prompt_spec,
            prompt_spec,
            resp_spec,
            resp_spec,
            resp_spec,
            resp_spec,
            resp_spec,
            resp_spec,
            P("batch", None, CTX),
            P("batch", None),
        ),
        out_specs=(prompt_spec, prompt_spec, out_spec, out_spec, out_spec, P("batch")),
        check_vma=False,
    )
```

time: 1250 us -> 161 us (0.13)
  waiting for transfers between devices: 1060 us -> 35.1 us
  matrix products: 35 us -> 0 us
  Pallas kernels: 0 us -> 25.5 us
  local copies, waits for them, and re-layouts: 32.9 us -> 9.06 us
  between operations: 17.6 us -> 0.72 us
    reduce_scatter x4 -> x0, waiting for transfers between devices: 801 us -> none  [the longest x1 224 us: per_device(): lax.psum_scatter(resp_carry[2].astype(jnp.bfloat16), 'ctx', scatter_dimen...]
    all_gather x4 -> x0, waiting for transfers between devices: 262 us -> none  [the longest x1 82.6 us: per_device(): lax.all_gather(prompt_values, 'ctx', axis=1, tiled=True)]
    psum x1 -> x0, blocking collectives: 67.8 us -> none  [per_device(): margin = lax.psum(chosen - rejected, 'ctx')]
    all_to_all x1 -> x6, blocking collectives: 3.75 us -> 64 us  [swap(): return lax.all_to_all(values, axes, split_axis=0, concat_axis=0, tiled=True)]
    dot_general x15 -> x0, matrix products: 35 us -> none  [the longest x2 8.04 us: prompt_step(): jnp.einsum('kad,amd->kam', value_rows, grad_flat, preferred_element_type=...]
    all_to_all x5 -> x4, waiting for transfers between devices: 0.49 us -> 35.1 us  [swap(): return lax.all_to_all(values, axes, split_axis=0, concat_axis=0, tiled=True)]
    pallas_call x0 -> x9, Pallas kernels: none -> 25.5 us  [the longest x1 11.6 us: per_device(): call(prompt_kernel, (shape((8, TILE, LANES), f32), shape((CTX_N, 64, LANE...]
  transfers between devices with their start and end apart: 13 -> 4, of which waited for: 9 -> 4; matrix products, arithmetic and copies ran while one was open for 5% -> 0% of each run, Pallas kernels for 0% -> 10%
where the time goes in v1:
time: 161 us; the launch traced here: 158 us
  blocking collectives  64 us (40%)
  waiting for transfers between devices  35.1 us (22%)
  Pallas kernels  25.5 us (16%)
  starting transfers between devices  24.1 us (15%)
  local copies, waits for them, and re-layouts  9.06 us (6%)
    all_to_all x6, blocking collectives, swap(): return lax.all_to_all(values, axes, split_axis=0, concat_axis=0, tiled=True)  64 us
    all_to_all x4, waiting for transfers between devices, swap(): return lax.all_to_all(values, axes, split_axis=0, concat_axis=0, tiled=True)  35.1 us
    all_to_all x4, starting transfers between devices, swap(): return lax.all_to_all(values, axes, split_axis=0, concat_axis=0, tiled=True)  24.1 us
    pallas_call x1, Pallas kernels, per_device(): call(prompt_kernel, (shape((8, TILE, LANES), f32), shape((CTX_N, 64, LANE...  11.6 us
    unnamed x24, local copies, waits for them, and re-layouts  8.54 us
    pallas_call x1, Pallas kernels, per_device(): call(resp_kernel, (shape((CTX_N, 64, LANES), bf16), shape((HEADS, 2 * TIL...  7.87 us
  transfers between devices with their start and end apart: 4, of which 4 were waited for; matrix products, arithmetic and copies ran while one was open for 0% of the time, Pallas kernels for 10%

profile of v1, /device:TPU:6, one launch (start us, length us, event | category | flops | bytes accessed | tf_op | source)
XLA Modules:
  0.0 158.5 jit_solution(13218391540054085380)
XLA Ops:
  0.6 0.0 copy-start
  0.6 0.9 copy-done
  1.6 0.0 copy-start.1
  1.6 0.9 copy-done.1
  2.5 0.0 copy-start.2
  2.5 0.8 copy-done.2
  3.3 0.0 copy-start.3
  3.3 0.8 copy-done.3
  4.1 0.0 copy-start.4
  4.1 0.8 copy-done.4
  4.8 0.0 copy-start.5
  4.8 0.8 copy-done.5
  5.6 0.0 copy-start.6
  5.6 0.7 copy-done.6
  6.3 0.0 copy-start.7
  6.3 0.7 copy-done.7
  7.0 1.2 shard_map.145
  8.2 3.8 %all_to_all.50.pair_ref = bf16[2,256,128]{2,1,0:T(8,128)(2,1)S(1)} all-to-all(bf16[2,256,128]{2,1,0:T(8,128)(2,1)S(1)} %get-tuple-element.20), channel_id=1, replica_groups=mesh['batch'=8,'pair'=2,'y'=8,'x'=4] {'pair'}, dimensions={0} | all-to-all | bytes 262144 | tf_op jit(solution)/shard_map/all_to_all | solution.py:260
  12.0 0.0 copy-start.8
  12.0 0.0 copy-start.9
  12.0 9.5 %all-to-all-start = ((bf16[8,528,128]{2,1,0:T(8,128)(2,1)}), bf16[8,528,128]{2,1,0:T(8,128)(2,1)S(1)}, u32[]{:S(2)}, u32[]{:S(2)}) async-start(bf16[8,528,128]{2,1,0:T(8,128)(2,1)} %get-tuple-element.19), calls=%async_computation | async-start | bytes 2162688 | tf_op jit(solution)/shard_map/all_to_all | solution.py:260
  21.5 0.0 copy-done.8
  21.5 0.0 copy-done.9
  21.5 1.5 shard_map.146
  23.0 12.7 %all-to-all-done.query_ref = bf16[8,528,128]{2,1,0:T(8,128)(2,1)S(1)} async-done(((bf16[8,528,128]{2,1,0:T(8,128)(2,1)}), bf16[8,528,128]{2,1,0:T(8,128)(2,1)S(1)}, u32[]{:S(2)}, u32[]{:S(2)}) %all-to-all-start) | async-done | bytes 1081376 | tf_op jit(solution)/shard_map/all_to_all | solution.py:260
  35.7 21.8 %all_to_all.51.kv_ref = bf16[32,64,128]{2,1,0:T(8,128)(2,1)S(1)} all-to-all(bf16[32,64,128]{2,1,0:T(8,128)(2,1)S(1)} %get-tuple-element.22), channel_id=1, replica_groups=mesh['batch'=8,'pair'=2,'y'=8,'x'=4] {'y','x'}, dimensions={0} | all-to-all | bytes 1048576 | tf_op jit(solution)/shard_map/all_to_all | solution.py:260
  57.5 5.6 %all-to-all-start.2 = ((bf16[32,80,128]{2,1,0:T(8,128)(2,1)}), bf16[32,80,128]{2,1,0:T(8,128)(2,1)S(1)}, u32[]{:S(2)}, u32[]{:S(2)}) async-start(bf16[32,80,128]{2,1,0:T(8,128)(2,1)} %get-tuple-element.21), calls=%async_computation.2 | async-start | bytes 1310720 | tf_op jit(solution)/shard_map/all_to_all | solution.py:260
  63.1 11.6 %shard_map.147 = (f32[8,256,128]{2,1,0:T(8,128)S(1)}, bf16[32,64,128]{2,1,0:T(8,128)(2,1)S(1)}) custom-call(s32[1,3]{1,0:T(1,128)S(1)} %copy-done.8, bf16[8,528,128]{2,1,0:T(8,128)(2,1)S(1)} %all-to-all-done.query_ref, bf16[32,64,128]{2,1,0:T(8,128)(2,1)S(1)} %all_to_all.51.kv_ref), custom_call_target="tpu_custom_call" | custom-call | flops 5368709120 | bytes 3145728 | tf_op jit(solution)/shard_map/pallas_call | solution.py:302
  74.7 0.0 copy-start.10
  74.7 1.0 copy-done.10
  75.7 6.1 %all-to-all-done.2.kv_ref = bf16[32,80,128]{2,1,0:T(8,128)(2,1)S(1)} async-done(((bf16[32,80,128]{2,1,0:T(8,128)(2,1)}), bf16[32,80,128]{2,1,0:T(8,128)(2,1)S(1)}, u32[]{:S(2)}, u32[]{:S(2)}) %all-to-all-start.2) | async-done | bytes 655392 | tf_op jit(solution)/shard_map/all_to_all | solution.py:260
  81.8 0.0 copy-start.11
  81.8 1.2 copy-done.11
  83.0 7.9 %shard_map.148 = (bf16[32,64,128]{2,1,0:T(8,128)(2,1)}, bf16[4,512,128]{2,1,0:T(8,128)(2,1)S(1)}, f32[8,128]{1,0:T(8,128)S(1)}) custom-call(s32[1,3]{1,0:T(1,128)S(1)} %copy-done.8, bf16[8,528,128]{2,1,0:T(8,128)(2,1)S(1)} %all-to-all-done.query_ref, bf16[32,80,128]{2,1,0:T(8,128)(2,1)S(1)} %all-to-all-done.2.kv_ref, f32[8,256,128]{2,1,0:T(8,128)S(1)} %copy-done.11), custom_call_target="tpu_custom_call" | custom-call | flops 2684354560 | bytes 3145728 | tf_op jit(solution)/shard_map/pallas_call | solution.py:312
  90.9 10.7 %all_to_all.52 = bf16[4,512,128]{2,1,0:T(8,128)(2,1)} all-to-all(bf16[4,512,128]{2,1,0:T(8,128)(2,1)S(1)} %get-tuple-element.28), channel_id=1, replica_groups=mesh['batch'=8,'pair'=2,'y'=8,'x'=4] {'x'}, dimensions={0} | all-to-all | bytes 1048576 | tf_op jit(solution)/shard_map/all_to_all | solution.py:260
  101.6 20.1 %all_to_all.53.part_ref = bf16[32,64,128]{2,1,0:T(8,128)(2,1)S(1)} all-to-all(bf16[32,64,128]{2,1,0:T(8,128)(2,1)S(1)} %get-tuple-element.25), channel_id=1, replica_groups=mesh['batch'=8,'pair'=2,'y'=8,'x'=4] {'y','x'}, dimensions={0} | all-to-all | bytes 1048576 | tf_op jit(solution)/shard_map/all_to_all | solution.py:260
  121.7 3.5 %all-to-all-start.7 = ((bf16[2,1024,128]{2,1,0:T(8,128)(2,1)}), bf16[2,1024,128]{2,1,0:T(8,128)(2,1)S(1)}, u32[]{:S(2)}, u32[]{:S(2)}) async-start(bf16[2,1024,128]{2,1,0:T(8,128)(2,1)} %bitcast.9), calls=%async_computation.7 | async-start | bytes 1048576 | tf_op jit(solution)/shard_map/all_to_all | solution.py:260
  125.2 0.6 shard_map.149
  125.8 1.1 all-to-all-done.7.pair_ref
  126.9 3.8 %all_to_all.54.pair_ref = bf16[2,128,128]{2,1,0:T(8,128)(2,1)S(1)} all-to-all(bf16[2,128,128]{2,1,0:T(8,128)(2,1)S(1)} %shard_map.149), channel_id=1, replica_groups=mesh['batch'=8,'pair'=2,'y'=8,'x'=4] {'pair'}, dimensions={0} | all-to-all | bytes 131072 | tf_op jit(solution)/shard_map/all_to_all | solution.py:260
  130.7 5.6 %all-to-all-start.8 = ((bf16[32,64,128]{2,1,0:T(8,128)(2,1)}), bf16[32,64,128]{2,1,0:T(8,128)(2,1)S(1)}, u32[]{:S(2)}, u32[]{:S(2)}) async-start(bf16[32,64,128]{2,1,0:T(8,128)(2,1)} %get-tuple-element.29), calls=%async_computation.8 | async-start | bytes 1048576 | tf_op jit(solution)/shard_map/all_to_all | solution.py:260
  136.3 0.5 slice.3
  136.8 0.8 shard_map.151
  137.6 0.6 shard_map.150
  138.2 15.2 %all-to-all-done.8.part_ref = bf16[32,64,128]{2,1,0:T(8,128)(2,1)S(1)} async-done(((bf16[32,64,128]{2,1,0:T(8,128)(2,1)}), bf16[32,64,128]{2,1,0:T(8,128)(2,1)S(1)}, u32[]{:S(2)}, u32[]{:S(2)}) %all-to-all-start.8) | async-done | bytes 524320 | tf_op jit(solution)/shard_map/all_to_all | solution.py:260
  153.4 0.6 shard_map.152
  154.0 3.8 %all_to_all.55.pair_ref = bf16[2,128,128]{2,1,0:T(8,128)(2,1)S(1)} all-to-all(bf16[2,128,128]{2,1,0:T(8,128)(2,1)S(1)} %shard_map.152), channel_id=1, replica_groups=mesh['batch'=8,'pair'=2,'y'=8,'x'=4] {'pair'}, dimensions={0} | all-to-all | bytes 131072 | tf_op jit(solution)/shard_map/all_to_all | solution.py:260
  157.8 0.6 shard_map.153
Async XLA Ops:
  0.6 1.0 copy-start
  1.6 0.9 copy-start.1
  2.5 0.8 copy-start.2
  3.3 0.8 copy-start.3
  4.1 0.8 copy-start.4
  4.8 0.8 copy-start.5
  5.6 0.7 copy-start.6
  6.3 0.7 copy-start.7
  12.0 9.5 %copy-start.8 = (s32[1,3]{1,0:T(1,128)S(1)}, s32[1,3]{1,0:T(1,128)}, u32[]{:S(2)}) copy-start(s32[1,3]{1,0:T(1,128)} %lengths_ref.9) | copy-start | bytes 40
  12.0 9.5 %copy-start.9 = (f32[1,2,32]{2,1,0:T(2,128)S(1)}, f32[1,2,32]{2,1,0:T(2,128)}, u32[]{:S(2)}) copy-start(f32[1,2,32]{2,1,0:T(2,128)} %param.18) | copy-start | bytes 772
  12.0 23.7 %all-to-all-start = ((bf16[8,528,128]{2,1,0:T(8,128)(2,1)}), bf16[8,528,128]{2,1,0:T(8,128)(2,1)S(1)}, u32[]{:S(2)}, u32[]{:S(2)}) async-start(bf16[8,528,128]{2,1,0:T(8,128)(2,1)} %get-tuple-element.19), calls=%async_computation | async-start | bytes 2162688 | tf_op jit(solution)/shard_map/all_to_all | solution.py:260
  57.5 24.3 %all-to-all-start.2 = ((bf16[32,80,128]{2,1,0:T(8,128)(2,1)}), bf16[32,80,128]{2,1,0:T(8,128)(2,1)S(1)}, u32[]{:S(2)}, u32[]{:S(2)}) async-start(bf16[32,80,128]{2,1,0:T(8,128)(2,1)} %get-tuple-element.21), calls=%async_computation.2 | async-start | bytes 1310720 | tf_op jit(solution)/shard_map/all_to_all | solution.py:260
  74.7 1.0 copy-start.10
  81.8 1.2 copy-start.11
  121.7 5.2 %all-to-all-start.7 = ((bf16[2,1024,128]{2,1,0:T(8,128)(2,1)}), bf16[2,1024,128]{2,1,0:T(8,128)(2,1)S(1)}, u32[]{:S(2)}, u32[]{:S(2)}) async-start(bf16[2,1024,128]{2,1,0:T(8,128)(2,1)} %bitcast.9), calls=%async_computation.7 | async-start | bytes 1048576 | tf_op jit(solution)/shard_map/all_to_all | solution.py:260
  130.7 22.7 %all-to-all-start.8 = ((bf16[32,64,128]{2,1,0:T(8,128)(2,1)}), bf16[32,64,128]{2,1,0:T(8,128)(2,1)S(1)}, u32[]{:S(2)}, u32[]{:S(2)}) async-start(bf16[32,64,128]{2,1,0:T(8,128)(2,1)} %get-tuple-element.29), calls=%async_computation.8 | async-start | bytes 1048576 | tf_op jit(solution)/shard_map/all_to_all | solution.py:260

commit v2 on v1

v2 whole, which is shorter than its diff:
```python
import jax
import jax.numpy as jnp
from jax import lax
from jax.experimental import pallas as pl
from jax.experimental.pallas import tpu as pltpu
from jax.sharding import Mesh, PartitionSpec as P

beta_coef = 0.1
f32, bf16 = jnp.float32, jnp.bfloat16
LANES = 128
CTX = ("y", "x")

X = 4
ROWS_Y = 8
CTX_N = 32
POS = 32
GROUP = 8
TILE = POS * GROUP
PROMPT_HALF = 32
RESP_HALF = 16
STAT_ROWS = 16
QUERY_ROWS = 2 * TILE + STAT_ROWS
SIDE = 2 * RESP_HALF
KV_ROWS = 2 * PROMPT_HALF + 2 * SIDE
LOG2E = 1.4426950408889634
SCALE = LANES**-0.5
DEAD = 1e30


def dot(a, b, dims):
    return lax.dot_general(a, b, (dims, ((), ())), preferred_element_type=f32)


def call(kernel, out_shape, spaces, flops=0, scratch=(), size=0):
    space = {"v": pltpu.VMEM, "s": pltpu.SMEM, "a": pl.ANY}
    many = isinstance(out_shape, tuple)
    out_spec = pl.BlockSpec(memory_space=pltpu.VMEM)
    return pl.pallas_call(
        kernel,
        out_shape=out_shape,
        in_specs=[pl.BlockSpec(memory_space=space[s]) for s in spaces],
        out_specs=tuple(out_spec for _ in out_shape) if many else out_spec,
        scratch_shapes=list(scratch),
        compiler_params=pltpu.CompilerParams(vmem_limit_bytes=24 * 2**20),
        cost_estimate=pl.CostEstimate(flops=flops, bytes_accessed=size, transcendentals=0),
    )


def fetch(pairs, sems):
    copies = [pltpu.make_async_copy(a, b, sems.at[i]) for i, (a, b) in enumerate(pairs)]
    for copy in copies:
        copy.start()
    for copy in copies:
        copy.wait()


def kv_pack_kernel(
    lengths_hbm, logratio_hbm, pk_hbm, pv_hbm, rk_hbm, rv_hbm, kv_ref, lengths, logratio, pk, pv, rk, rv, sems
):
    pairs = (
        (lengths_hbm, lengths),
        (logratio_hbm.at[0], logratio),
        (pk_hbm.at[0], pk),
        (pv_hbm.at[0], pv),
        (rk_hbm.at[0, 0], rk),
        (rv_hbm.at[0, 0], rv),
    )
    fetch(pairs, sems)
    first_core = lax.axis_index("pair") == 0
    ctx = lax.axis_index("y") * X + lax.axis_index("x")
    position = ctx * POS + lax.broadcasted_iota(jnp.int32, (1, POS), 1)
    chosen = jnp.where(position < lengths[0, 1], logratio[0:1, :], 0.0)
    rejected = jnp.where(position < lengths[0, 2], logratio[1:2, :], 0.0)
    margin = jnp.sum(chosen - rejected, axis=1, keepdims=True)
    high = margin.astype(bf16).astype(f32)
    middle = (margin - high).astype(bf16).astype(f32)
    low = margin - high - middle
    lane = lax.broadcasted_iota(jnp.int32, (16, LANES), 1)
    row = lax.broadcasted_iota(jnp.int32, (16, LANES), 0)
    block = jnp.where(lane == 0, high, jnp.where(lane == 1, middle, jnp.where(lane == 2, low, 0.0)))
    block = jnp.where(row == 0, block, 0.0).astype(bf16)
    for x in range(X):
        odd, half = x % 2, x // 2
        columns = slice(odd * LANES, (odd + 1) * LANES)
        others = slice((2 + odd) * LANES, (3 + odd) * LANES)
        rows = slice(half * PROMPT_HALF, (half + 1) * PROMPT_HALF)
        index = ctx * 2 * PROMPT_HALF + half * PROMPT_HALF
        live = index + lax.broadcasted_iota(jnp.int32, (PROMPT_HALF, LANES), 0) < lengths[0, 0]
        parts = [jnp.where(live, pk[rows, columns].astype(f32), 0.0).astype(bf16), pv[rows, columns]]
        rows = slice(half * RESP_HALF, (half + 1) * RESP_HALF)
        low_head = [ref[rows, columns].astype(f32) for ref in (rk, rv)]
        high_head = [ref[rows, others].astype(f32) for ref in (rk, rv)]
        parts += [jnp.where(first_core, a, b).astype(bf16) for a, b in zip(low_head, high_head)]
        parts += [jnp.where(first_core, b, a).astype(bf16) for a, b in zip(low_head, high_head)]
        parts += [block]
        for y in range(ROWS_Y):
            at = 0
            for part in parts:
                kv_ref[y * X + x, at : at + part.shape[0], :] = part
                at += part.shape[0]


def query_pack_kernel(q_hbm, g_hbm, lse_hbm, delta_hbm, own_ref, other_ref, q, g, lse, delta, sems):
    core, parity = lax.axis_index("pair"), lax.axis_index("x") % 2
    pairs = [(lse_hbm.at[0, 0], lse), (delta_hbm.at[0, 0], delta)]
    heads = []
    for i in range(4):
        head = 2 * (core if i < 2 else 1 - core) + (parity + i) % 2
        heads.append(head)
        columns = pl.ds(pl.multiple_of(head * GROUP * LANES, GROUP * LANES), GROUP * LANES)
        pairs += [(q_hbm.at[0, 0, :, columns], q.at[i]), (g_hbm.at[0, 0, :, columns], g.at[i])]
    fetch(pairs, sems)
    sign = jnp.where(core == 0, -1.0, 1.0).astype(f32)

    count = X * GROUP
    lane = lax.broadcasted_iota(jnp.int32, (POS, TILE), 1)
    spread = (lane % POS == lax.broadcasted_iota(jnp.int32, (POS, TILE), 0)).astype(bf16)
    head_of = lax.broadcasted_iota(jnp.int32, (count, TILE), 0)
    lane = lax.broadcasted_iota(jnp.int32, (count, TILE), 1)
    lse_rows = dot(lse[...], spread, ((0,), (0,)))
    delta_rows = dot(delta[...], spread, ((0,), (0,))) * sign
    row = lax.broadcasted_iota(jnp.int32, (STAT_ROWS, LANES), 0)
    for i in range(4):
        ref, slot = (own_ref, other_ref)[i // 2], i % 2
        for h in range(GROUP):
            columns = slice(h * LANES, (h + 1) * LANES)
            ref[slot, h * POS : (h + 1) * POS, :] = q[i, :, columns]
            grad = (g[i, :, columns].astype(f32) * sign).astype(bf16)
            ref[slot, TILE + h * POS : TILE + (h + 1) * POS, :] = grad
        keep = head_of == heads[i] * GROUP + lane // POS
        block = jnp.zeros((STAT_ROWS, LANES), f32)
        for n, rows in enumerate((lse_rows, delta_rows)):
            line = jnp.sum(jnp.where(keep, rows, 0.0), axis=0, keepdims=True)
            block = jnp.where(row == 2 * n, line[:, :LANES], block)
            block = jnp.where(row == 2 * n + 1, line[:, LANES:], block)
        ref[slot, 2 * TILE :, :] = block.astype(bf16)


def join_kernel(own_ref, other_ref, same_ref, odd_ref):
    for i, ref in enumerate((same_ref, odd_ref)):
        ref[0] = own_ref[i]
        ref[1] = other_ref[i]


def row_stats(lengths_ref, block, k, j):
    block = block.astype(f32)
    lse = jnp.concatenate([block[0:1], block[1:2]], axis=1) * LOG2E
    delta = jnp.concatenate([block[2:3], block[3:4]], axis=1)
    core = lax.axis_index("pair")
    response = core + j - 2 * core * j
    x = (lax.axis_index("x") + X - k) % X
    position = (lax.axis_index("y") * X + x) * POS + lax.broadcasted_iota(jnp.int32, (1, TILE), 1) % POS
    return jnp.where(position < lengths_ref[0, 1 + response], lse, DEAD), delta, position


def cell(key, value, query, grad, lse, delta, allowed=None):
    scores = dot(key, query, ((1,), (1,)))
    weights = jnp.exp2(scores * (SCALE * LOG2E) - lse)
    if allowed is not None:
        weights = jnp.where(allowed, weights, 0.0)
    weight_grads = dot(value, grad, ((1,), (1,)))
    score_grads = (weights * (weight_grads - delta)).astype(bf16)
    return weights.astype(bf16), score_grads


def prompt_kernel(lengths_ref, q0, q1, q2, q3, kv_ref, acc_ref, out_ref, rows_ref, key_acc, value_acc):
    for k, ref in enumerate((q0, q1, q2, q3)):
        rows_ref[2 * k : 2 * k + 2] = ref[...]
    key_acc[...] = jnp.zeros_like(key_acc)
    value_acc[...] = jnp.zeros_like(value_acc)
    per = 8
    rows = per * PROMPT_HALF

    @pl.loop(0, 2 * X)
    def _(tile):
        lse, delta, _ = row_stats(lengths_ref, rows_ref[tile, 2 * TILE :, :], tile // 2, tile % 2)
        query = rows_ref[tile, 0:TILE, :]
        grad = rows_ref[tile, TILE : 2 * TILE, :]
        total = None
        for c in range(CTX_N // per):
            at = slice(c * per, (c + 1) * per)
            key = kv_ref[at, 0:PROMPT_HALF, :].reshape(rows, LANES)
            value = kv_ref[at, PROMPT_HALF : 2 * PROMPT_HALF, :].reshape(rows, LANES)
            weights, score_grads = cell(key, value, query, grad, lse, delta)
            at = slice(c * rows, (c + 1) * rows)
            value_acc[at, :] += dot(weights, grad, ((1,), (0,)))
            key_acc[at, :] += dot(score_grads, query, ((1,), (0,)))
            term = dot(score_grads, key, ((0,), (0,)))
            total = term if total is None else total + term
        acc_ref[tile] = total

    shape = (CTX_N, PROMPT_HALF, LANES)
    out_ref[:, 0:PROMPT_HALF, :] = (key_acc[...] * SCALE).astype(bf16).reshape(shape)
    out_ref[:, PROMPT_HALF:, :] = value_acc[...].astype(bf16).reshape(shape)


def resp_kernel(
    lengths_ref, q0, q1, q2, q3, kv_ref, side_ref, acc_ref, prompt_ref,
    out_ref, d0, d1, d2, d3, gate_ref, key_acc, value_acc,
):
    margin = jnp.sum(kv_ref[:, KV_ROWS:, :].astype(f32), axis=(0, 1), keepdims=True).reshape(1, LANES)
    margin = jnp.sum(margin, axis=1, keepdims=True)
    gate_ref[...] = jnp.broadcast_to(beta_coef * jax.nn.sigmoid(-beta_coef * margin), gate_ref.shape)
    out_ref[:, 0 : 2 * PROMPT_HALF, :] = prompt_ref[...]
    key_acc[...] = jnp.zeros_like(key_acc)
    value_acc[...] = jnp.zeros_like(value_acc)
    half = lax.axis_index("x") // 2
    per = 16
    rows = per * RESP_HALF
    for j, (source, first) in enumerate(((kv_ref, 2 * PROMPT_HALF), (side_ref, 0))):
        for k, (q_ref, d_ref) in enumerate(((q0, d0), (q1, d1), (q2, d2), (q3, d3))):
            lse, delta, position = row_stats(lengths_ref, q_ref[j, 2 * TILE :, :], k, j)
            query = q_ref[j, 0:TILE, :]
            grad = q_ref[j, TILE : 2 * TILE, :]
            total = acc_ref[2 * k + j]
            for c in range(CTX_N // per):
                at = slice(c * per, (c + 1) * per)
                key = source[at, first : first + RESP_HALF, :].reshape(rows, LANES)
                value = source[at, first + RESP_HALF : first + SIDE, :].reshape(rows, LANES)
                index = lax.broadcasted_iota(jnp.int32, (rows, 1), 0)
                key_position = (c * per + index // RESP_HALF) * POS + half * RESP_HALF + index % RESP_HALF
                weights, score_grads = cell(key, value, query, grad, lse, delta, key_position <= position)
                first_row = (j * (CTX_N // per) + c) * rows
                at = slice(first_row, first_row + rows)
                value_acc[at, :] += dot(weights, grad, ((1,), (0,)))
                key_acc[at, :] += dot(score_grads, query, ((1,), (0,)))
                total += dot(score_grads, key, ((0,), (0,)))
            d_ref[j] = (total * SCALE).astype(bf16)

        at = slice(j * CTX_N * RESP_HALF, (j + 1) * CTX_N * RESP_HALF)
        shape = (CTX_N, RESP_HALF, LANES)
        to = 2 * PROMPT_HALF + j * SIDE
        out_ref[:, to : to + RESP_HALF, :] = (key_acc[at, :] * SCALE).astype(bf16).reshape(shape)
        out_ref[:, to + RESP_HALF : to + SIDE, :] = value_acc[at, :].astype(bf16).reshape(shape)


def kv_final_kernel(lengths_ref, gate_ref, part_ref, pk_ref, pv_ref, rk_ref, rv_ref):
    gate = gate_ref[0:1, 0:1]
    core = lax.axis_index("pair")
    ctx = lax.axis_index("y") * X + lax.axis_index("x")
    for x in range(X):
        odd, half = x % 2, x // 2
        columns = slice(odd * LANES, (odd + 1) * LANES)
        total = part_ref[x].astype(f32)
        for y in range(1, ROWS_Y):
            total += part_ref[y * X + x].astype(f32)
        total = total * gate
        rows = slice(half * PROMPT_HALF, (half + 1) * PROMPT_HALF)
        index = ctx * 2 * PROMPT_HALF + half * PROMPT_HALF
        live = index + lax.broadcasted_iota(jnp.int32, (PROMPT_HALF, LANES), 0) < lengths_ref[0, 0]
        pk_ref[0, rows, columns] = jnp.where(live, total[0:PROMPT_HALF], 0.0).astype(bf16)
        pv_ref[0, rows, columns] = jnp.where(live, total[PROMPT_HALF : 2 * PROMPT_HALF], 0.0).astype(bf16)
        rows = slice(half * RESP_HALF, (half + 1) * RESP_HALF)
        for j in range(2):
            response = core + j - 2 * core * j
            at = 2 * PROMPT_HALF + j * SIDE
            rk_ref[0, response, rows, columns] = total[at : at + RESP_HALF].astype(bf16)
            rv_ref[0, response, rows, columns] = total[at + RESP_HALF : at + SIDE].astype(bf16)


def query_final_kernel(gate_ref, d0, d1, d2, d3, out_ref):
    gate = gate_ref[0:1, 0:1]
    core = lax.axis_index("pair")
    even = lax.axis_index("x") % 2 == 0
    for j in range(2):
        response = core + j - 2 * core * j
        for h in range(GROUP):
            rows = slice(h * POS, (h + 1) * POS)
            same = gate * (d0[j, rows, :].astype(f32) + d2[j, rows, :].astype(f32))
            odd = gate * (d1[j, rows, :].astype(f32) + d3[j, rows, :].astype(f32))
            first, second = jnp.where(even, same, odd), jnp.where(even, odd, same)
            out_ref[0, response, :, h * LANES : (h + 1) * LANES] = first.astype(bf16)
            out_ref[0, response, :, (GROUP + h) * LANES : (GROUP + h + 1) * LANES] = second.astype(bf16)


def swap(values):
    return lax.all_to_all(values, CTX, split_axis=0, concat_axis=0, tiled=True)


def cross(values):
    return lax.ppermute(values, "pair", [(0, 1), (1, 0)])


def shift(values, by):
    return lax.ppermute(values, "x", [(i, (i + by) % X) for i in range(X)])


def per_device(
    prompt_keys,
    prompt_values,
    queries,
    resp_keys,
    resp_values,
    resp_grads,
    resp_lse,
    resp_delta,
    logratio,
    lengths,
):
    shape = jax.ShapeDtypeStruct
    kv = call(
        kv_pack_kernel,
        shape((CTX_N, KV_ROWS + 16, LANES), bf16),
        "aaaaaa",
        size=2 * 2**20,
        scratch=(
            pltpu.SMEM((1, 3), jnp.int32),
            pltpu.VMEM((2, POS), f32),
            pltpu.VMEM((2 * PROMPT_HALF, 2 * LANES), bf16),
            pltpu.VMEM((2 * PROMPT_HALF, 2 * LANES), bf16),
            pltpu.VMEM((POS, X * LANES), bf16),
            pltpu.VMEM((POS, X * LANES), bf16),
            pltpu.SemaphoreType.DMA((6,)),
        ),
    )(lengths, logratio, prompt_keys, prompt_values, resp_keys, resp_values)
    kv = swap(kv)

    block = shape((2, QUERY_ROWS, LANES), bf16)
    own, other = call(
        query_pack_kernel,
        (block, block),
        "aaaa",
        size=2 * 2**20,
        scratch=(
            pltpu.VMEM((4, POS, GROUP * LANES), bf16),
            pltpu.VMEM((4, POS, GROUP * LANES), bf16),
            pltpu.VMEM((POS, X * GROUP), bf16),
            pltpu.VMEM((POS, X * GROUP), bf16),
            pltpu.SemaphoreType.DMA((10,)),
        ),
    )(queries, resp_grads, resp_lse, resp_delta)
    same, odd = call(join_kernel, (block, block), "vv", size=2**20)(own, cross(other))
    rows = (same, shift(odd, 1), shift(same, 2), shift(odd, 3))

    side = cross(kv[:, KV_ROWS - SIDE : KV_ROWS, :])
    acc, prompt_part = call(
        prompt_kernel,
        (shape((2 * X, TILE, LANES), f32), shape((CTX_N, 2 * PROMPT_HALF, LANES), bf16)),
        "svvvvv",
        scratch=(
            pltpu.VMEM((2 * X, QUERY_ROWS, LANES), bf16),
            pltpu.VMEM((1024, LANES), f32),
            pltpu.VMEM((1024, LANES), f32),
        ),
        flops=5 * 2 * 2048 * 1024 * 128 * 2,
        size=3 * 2**20,
    )(lengths, *rows, kv)
    part, *grads, gate = call(
        resp_kernel,
        (shape((CTX_N, KV_ROWS, LANES), bf16),)
        + (shape((2, TILE, LANES), bf16),) * X
        + (shape((8, LANES), f32),),
        "svvvvvvvv",
        scratch=(pltpu.VMEM((1024, LANES), f32), pltpu.VMEM((1024, LANES), f32)),
        flops=5 * 2 * 1024 * 1024 * 128 * 2,
        size=3 * 2**20,
    )(lengths, *rows, kv, side, acc, prompt_part)
    part = swap(part)
    back = [grads[0]] + [shift(grads[k], X - k) for k in range(1, X)]
    query_grad = call(query_final_kernel, shape((1, 2, POS, 2 * GROUP * LANES), bf16), "vvvvv", size=2**20)(
        gate, *back
    )
    outs = (shape((1, 2 * PROMPT_HALF, 2 * LANES), bf16),) * 2 + (shape((1, 2, POS, 2 * LANES), bf16),) * 2
    pk_grad, pv_grad, key_grad, value_grad = call(kv_final_kernel, outs, "svv", size=2**20)(lengths, gate, part)
    return pk_grad, pv_grad, query_grad, key_grad, value_grad, gate[0, 0:1]


def solution(mesh):
    batch, pair, ctx = mesh.devices.shape
    split = Mesh(mesh.devices.reshape(batch, pair, ctx // X, X), ("batch", "pair", "y", "x"))
    prompt_spec = P("batch", CTX, "pair")
    resp_spec = P("batch", "pair", CTX, None)
    out_spec = P("batch", None, CTX, "pair")
    return jax.shard_map(
        per_device,
        mesh=split,
        in_specs=(
            prompt_spec,
            prompt_spec,
            resp_spec,
            resp_spec,
            resp_spec,
            resp_spec,
            resp_spec,
            resp_spec,
            P("batch", None, CTX),
            P("batch", None),
        ),
        out_specs=(prompt_spec, prompt_spec, out_spec, out_spec, out_spec, P("batch")),
        check_vma=False,
    )
```

time: 161 us -> 105 us (0.65)
  blocking collectives: 64 us -> 0 us
  starting transfers between devices: 24.1 us -> 39.7 us
  local copies, waits for them, and re-layouts: 9.06 us -> 4.92 us
  Pallas kernels: 25.5 us -> 22.6 us
    all_to_all x6 -> x0, blocking collectives: 64 us -> none  [swap(): return lax.all_to_all(values, axes, split_axis=0, concat_axis=0, tiled=True)]
    ppermute x0 -> x8, starting transfers between devices: none -> 22.9 us  [the longest x6 19 us: shift(): return lax.ppermute(values, 'x', [(i, (i + by) % X) for i in range(X)])]
    ppermute x0 -> x8, waiting for transfers between devices: none -> 7.99 us  [the longest x6 6.48 us: shift(): return lax.ppermute(values, 'x', [(i, (i + by) % X) for i in range(X)])]
    all_to_all x4 -> x2, waiting for transfers between devices: 35.1 us -> 27.7 us  [swap(): return lax.all_to_all(values, CTX, split_axis=0, concat_axis=0, tiled=True)]
    all_to_all x4 -> x2, starting transfers between devices: 24.1 us -> 16.9 us  [swap(): return lax.all_to_all(values, CTX, split_axis=0, concat_axis=0, tiled=True)]
    unnamed x24 -> x22, local copies, waits for them, and re-layouts: 8.54 us -> 4.39 us
    pallas_call x9 -> x7, Pallas kernels: 25.5 us -> 22.6 us  [the longest x1 11.6 us: per_device(): call(prompt_kernel, (shape((2 * X, TILE, LANES), f32), shape((CTX_N, 2 *...]
  transfers between devices with their start and end apart: 4 -> 10, of which waited for: 4 -> 5; matrix products, arithmetic and copies ran while one was open for 0% -> 1% of each run, Pallas kernels for 10% -> 13%
where the time goes in v2:
time: 105 us; the launch traced here: 104 us
  starting transfers between devices  39.7 us (38%)
  waiting for transfers between devices  35.6 us (34%)
  Pallas kernels  22.6 us (22%)
  local copies, waits for them, and re-layouts  4.92 us (5%)
    all_to_all x2, waiting for transfers between devices, swap(): return lax.all_to_all(values, CTX, split_axis=0, concat_axis=0, tiled=True)  27.7 us
    ppermute x6, starting transfers between devices, shift(): return lax.ppermute(values, 'x', [(i, (i + by) % X) for i in range(X)])  19 us
    all_to_all x2, starting transfers between devices, swap(): return lax.all_to_all(values, CTX, split_axis=0, concat_axis=0, tiled=True)  16.9 us
    pallas_call x1, Pallas kernels, per_device(): call(prompt_kernel, (shape((2 * X, TILE, LANES), f32), shape((CTX_N, 2 *...  11.6 us
    pallas_call x1, Pallas kernels, per_device(): call(resp_kernel, (shape((CTX_N, KV_ROWS, LANES), bf16),) + (shape((2, TI...  6.5 us
    ppermute x6, waiting for transfers between devices, shift(): return lax.ppermute(values, 'x', [(i, (i + by) % X) for i in range(X)])  6.48 us
    unnamed x22, local copies, waits for them, and re-layouts  4.39 us
    ppermute x2, starting transfers between devices, cross(): return lax.ppermute(values, 'pair', [(0, 1), (1, 0)])  3.84 us
  transfers between devices with their start and end apart: 10, of which 5 were waited for; matrix products, arithmetic and copies ran while one was open for 1% of the time, Pallas kernels for 13%

profile of v2, /device:TPU:6, one launch (start us, length us, event | category | flops | bytes accessed | tf_op | source)
XLA Modules:
  0.0 103.8 jit_solution(9977095568926423916)
XLA Ops:
  0.6 0.0 copy-start.2
  0.6 0.7 copy-done.2
  1.4 0.0 copy-start.3
  1.4 0.8 copy-done.3
  2.2 0.0 copy-start.4
  2.2 0.8 copy-done.4
  2.9 0.0 copy-start.5
  2.9 0.8 copy-done.5
  3.7 0.0 copy-start.8
  3.7 0.7 copy-done.8
  4.3 0.0 copy-start.10
  4.3 0.7 copy-done.10
  5.0 1.8 %shard_map.147 = bf16[32,144,128]{2,1,0:T(8,128)(2,1)} custom-call(s32[1,3]{1,0:T(1,128)S(1)} %copy-done.8, f32[1,2,32]{2,1,0:T(2,128)S(1)} %copy-done.10, bf16[1,64,256]{2,1,0:T(8,128)(2,1)S(1)} %copy-done.2, bf16[1,64,256]{2,1,0:T(8,128)(2,1)S(1)} %copy-done.3, bf16[1,1,32,512]{3,2,1,0:T(8,128)(2,1)S(1)} %copy-done.4, bf16[1,1,32,512]{3,2,1,0:T(8,128)(2,1)S(1)} %copy-done.5), custom_call_target="tpu_custom_call" | custom-call | bytes 2097152 | tf_op jit(solution)/shard_map/pallas_call | solution.py:301
  6.8 0.0 copy-start
  6.8 0.0 copy-start.1
  6.8 0.0 copy-start.6
  6.8 0.0 copy-start.7
  6.8 10.3 %all-to-all-start = ((bf16[32,144,128]{2,1,0:T(8,128)(2,1)}), bf16[32,144,128]{2,1,0:T(8,128)(2,1)S(1)}, u32[]{:S(2)}, u32[]{:S(2)}) async-start(bf16[32,144,128]{2,1,0:T(8,128)(2,1)} %shard_map.147), calls=%async_computation | async-start | bytes 2359296 | tf_op jit(solution)/shard_map/all_to_all | solution.py:277
  17.2 0.0 copy-done
  17.2 0.0 copy-done.1
  17.2 0.0 copy-done.6
  17.2 0.0 copy-done.7
  17.2 0.0 copy-start.9
  17.2 0.6 shard_map.145
  17.8 1.9 %collective-permute-start = (bf16[2,528,128]{2,1,0:T(8,128)(2,1)S(1)}, bf16[2,528,128]{2,1,0:T(8,128)(2,1)S(1)}, u32[]{:S(2)}, u32[]{:S(2)}) collective-permute-start(bf16[2,528,128]{2,1,0:T(8,128)(2,1)S(1)} %get-tuple-element.23), channel_id=1, source_target_pairs={{0,32},{32,0},{1,33},{33,1},{2,34},{34,2},{3,35},{35,3},{4,36},{36... | collective-permute-start | bytes 811016 | tf_op jit(solution)/shard_map/ppermute | solution.py:281
  19.7 1.5 %collective-permute-done.other_ref = bf16[2,528,128]{2,1,0:T(8,128)(2,1)S(1)} collective-permute-done((bf16[2,528,128]{2,1,0:T(8,128)(2,1)S(1)}, bf16[2,528,128]{2,1,0:T(8,128)(2,1)S(1)}, u32[]{:S(2)}, u32[]{:S(2)}) %collective-permute-start) | collective-permute-done | bytes 270368 | tf_op jit(solution)/shard_map/ppermute | solution.py:281
  21.3 2.8 %collective-permute-start.3 = (bf16[2,528,128]{2,1,0:T(8,128)(2,1)S(1)}, bf16[2,528,128]{2,1,0:T(8,128)(2,1)S(1)}, u32[]{:S(2)}, u32[]{:S(2)}) collective-permute-start(bf16[2,528,128]{2,1,0:T(8,128)(2,1)S(1)} %get-tuple-element.25), channel_id=1, source_target_pairs={{0,3},{1,0},{2,1},{3,2},{4,7},{5,4},{6,5},{7,6},{8,11},{9,8},{10,9... | collective-permute-start | bytes 811016 | tf_op jit(solution)/shard_map/ppermute | solution.py:285
  24.1 4.3 %collective-permute-start.1 = (bf16[2,528,128]{2,1,0:T(8,128)(2,1)S(1)}, bf16[2,528,128]{2,1,0:T(8,128)(2,1)S(1)}, u32[]{:S(2)}, u32[]{:S(2)}) collective-permute-start(bf16[2,528,128]{2,1,0:T(8,128)(2,1)S(1)} %get-tuple-element.25), channel_id=1, source_target_pairs={{0,1},{1,2},{2,3},{3,0},{4,5},{5,6},{6,7},{7,4},{8,9},{9,10},{10,1... | collective-permute-start | bytes 811016 | tf_op jit(solution)/shard_map/ppermute | solution.py:285
  28.4 2.2 %collective-permute-start.2 = (bf16[2,528,128]{2,1,0:T(8,128)(2,1)S(1)}, bf16[2,528,128]{2,1,0:T(8,128)(2,1)S(1)}, u32[]{:S(2)}, u32[]{:S(2)}) collective-permute-start(bf16[2,528,128]{2,1,0:T(8,128)(2,1)S(1)} %get-tuple-element.24.q0), channel_id=1, source_target_pairs={{0,2},{1,3},{2,0},{3,1},{4,6},{5,7},{6,4},{7,5},{8,10},{9,11},{10,... | collective-permute-start | bytes 811016 | tf_op jit(solution)/shard_map/ppermute | solution.py:285
  30.5 17.5 %all-to-all-done.kv_ref = bf16[32,144,128]{2,1,0:T(8,128)(2,1)S(1)} async-done(((bf16[32,144,128]{2,1,0:T(8,128)(2,1)}), bf16[32,144,128]{2,1,0:T(8,128)(2,1)S(1)}, u32[]{:S(2)}, u32[]{:S(2)}) %all-to-all-start) | async-done | bytes 1179680 | tf_op jit(solution)/shard_map/all_to_all | solution.py:277
  48.1 1.9 %collective-permute-start.4 = (bf16[32,32,128]{2,1,0:T(8,128)(2,1)S(1)}, bf16[32,32,128]{2,1,0:T(8,128)(2,1)S(1)}, u32[]{:S(2)}, u32[]{:S(2)}) collective-permute-start(bf16[32,32,128]{2,1,0:T(8,128)(2,1)S(1)} %slice.8), channel_id=1, source_target_pairs={{0,32},{32,0},{1,33},{33,1},{2,34},{34,2},{3,35},{35,3},{4,36},{36... | collective-permute-start | bytes 786440 | tf_op jit(solution)/shard_map/ppermute | solution.py:281
  50.0 0.0 collective-permute-done.3.q3
  50.0 0.0 collective-permute-done.1.q1
  50.0 0.0 collective-permute-done.2.q2
  50.0 0.0 copy-done.9
  50.0 11.6 %shard_map.148 = (f32[8,256,128]{2,1,0:T(8,128)S(1)}, bf16[32,64,128]{2,1,0:T(8,128)(2,1)S(1)}) custom-call(s32[1,3]{1,0:T(1,128)S(1)} %copy-done.9, bf16[2,528,128]{2,1,0:T(8,128)(2,1)S(1)} %get-tuple-element.24.q0, bf16[2,528,128]{2,1,0:T(8,128)(2,1)S(1)} %collective-permute-done.1.q1, bf16[2,528,128]{2,1,0:T(8,128)(2,1)S(1)} %collective-permute-done.2.q2, ...), custom_call_target="tpu_custom_call" | custom-call | flops 5368709120 | bytes 3145728 | tf_op jit(solution)/shard_map/pallas_call | solution.py:336
  61.6 0.0 collective-permute-done.4.side_ref
  61.6 6.5 %shard_map.149 = (bf16[32,128,128]{2,1,0:T(8,128)(2,1)}, bf16[2,256,128]{2,1,0:T(8,128)(2,1)S(1)}, bf16[2,256,128]{2,1,0:T(8,128)(2,1)S(1)}, bf16[2,256,128]{2,1...) custom-call(s32[1,3]{1,0:T(1,128)S(1)} %copy-done.9, ...), custom_call_target="tpu_custom_call" | custom-call | flops 2684354560 | bytes 3145728 | tf_op jit(solution)/shard_map/pallas_call | solution.py:348
  68.1 6.5 %all-to-all-start.1 = ((bf16[32,128,128]{2,1,0:T(8,128)(2,1)}), bf16[32,128,128]{2,1,0:T(8,128)(2,1)S(1)}, u32[]{:S(2)}, u32[]{:S(2)}) async-start(bf16[32,128,128]{2,1,0:T(8,128)(2,1)} %get-tuple-element.29), calls=%async_computation.1 | async-start | bytes 2097152 | tf_op jit(solution)/shard_map/all_to_all | solution.py:277
  74.7 2.8 %collective-permute-start.5 = (bf16[2,256,128]{2,1,0:T(8,128)(2,1)S(1)}, bf16[2,256,128]{2,1,0:T(8,128)(2,1)S(1)}, u32[]{:S(2)}, u32[]{:S(2)}) collective-permute-start(bf16[2,256,128]{2,1,0:T(8,128)(2,1)S(1)} %get-tuple-element.33), channel_id=1, source_target_pairs={{0,3},{1,0},{2,1},{3,2},{4,7},{5,4},{6,5},{7,6},{8,11},{9,8},{10,9... | collective-permute-start | bytes 393224 | tf_op jit(solution)/shard_map/ppermute | solution.py:285
  77.4 2.7 %collective-permute-start.6 = (bf16[2,256,128]{2,1,0:T(8,128)(2,1)S(1)}, bf16[2,256,128]{2,1,0:T(8,128)(2,1)S(1)}, u32[]{:S(2)}, u32[]{:S(2)}) collective-permute-start(bf16[2,256,128]{2,1,0:T(8,128)(2,1)S(1)} %get-tuple-element.34), channel_id=1, source_target_pairs={{0,2},{1,3},{2,0},{3,1},{4,6},{5,7},{6,4},{7,5},{8,10},{9,11},{10,... | collective-permute-start | bytes 393224 | tf_op jit(solution)/shard_map/ppermute | solution.py:285
  80.2 4.3 %collective-permute-start.7 = (bf16[2,256,128]{2,1,0:T(8,128)(2,1)S(1)}, bf16[2,256,128]{2,1,0:T(8,128)(2,1)S(1)}, u32[]{:S(2)}, u32[]{:S(2)}) collective-permute-start(bf16[2,256,128]{2,1,0:T(8,128)(2,1)S(1)} %get-tuple-element.35), channel_id=1, source_target_pairs={{0,1},{1,2},{2,3},{3,0},{4,5},{5,6},{6,7},{7,4},{8,9},{9,10},{10,1... | collective-permute-start | bytes 393224 | tf_op jit(solution)/shard_map/ppermute | solution.py:285
  84.5 0.5 slice.7
  85.0 6.2 %collective-permute-done.5.d1 = bf16[2,256,128]{2,1,0:T(8,128)(2,1)S(1)} collective-permute-done((bf16[2,256,128]{2,1,0:T(8,128)(2,1)S(1)}, bf16[2,256,128]{2,1,0:T(8,128)(2,1)S(1)}, u32[]{:S(2)}, u32[]{:S(2)}) %collective-permute-start.5) | collective-permute-done | bytes 131104 | tf_op jit(solution)/shard_map/ppermute | solution.py:285
  91.2 0.0 collective-permute-done.6.d2
  91.2 0.3 collective-permute-done.7.d3
  91.5 0.8 shard_map.151
  92.3 10.1 %all-to-all-done.1.part_ref = bf16[32,128,128]{2,1,0:T(8,128)(2,1)S(1)} async-done(((bf16[32,128,128]{2,1,0:T(8,128)(2,1)}), bf16[32,128,128]{2,1,0:T(8,128)(2,1)S(1)}, u32[]{:S(2)}, u32[]{:S(2)}) %all-to-all-start.1) | async-done | bytes 1048608 | tf_op jit(solution)/shard_map/all_to_all | solution.py:277
  102.4 1.3 %shard_map.150 = (bf16[1,64,256]{2,1,0:T(8,128)(2,1)}, bf16[1,64,256]{2,1,0:T(8,128)(2,1)}, bf16[1,2,32,256]{3,2,1,0:T(8,128)(2,1)}, bf16[1,2,32,256]{3,2,1,0:T(8,128)(2,1)}) custom-call(s32[1,3]{1,0:T(1,128)S(1)} %copy-done.9, f32[8,128]{1,0:T(8,128)S(1)} %get-tuple-element.28.gate_ref, bf16[32,128,128]{2,1,0:T(8,128)(2,1)S(1)} %all-to-all-done.1.part_ref), custom_call_target="tpu_custom_call" | custom-call | bytes 1048576 | tf_op jit(solution)/shard_map/pallas_call | solution.py:364
  (2 shorter events, 0.1 us)
Async XLA Ops:
  0.6 0.8 copy-start.2
  1.4 0.8 copy-start.3
  2.2 0.8 copy-start.4
  2.9 0.8 copy-start.5
  3.7 0.7 copy-start.8
  4.3 0.7 copy-start.10
  6.8 10.4 %copy-start = (bf16[1,1,32,4096]{3,2,1,0:T(8,128)(2,1)S(1)}, bf16[1,1,32,4096]{3,2,1,0:T(8,128)(2,1)}, u32[]{:S(2)}) copy-start(bf16[1,1,32,4096]{3,2,1,0:T(8,128)(2,1)} %q_hbm.1) | copy-start | bytes 786436
  6.8 10.4 %copy-start.1 = (bf16[1,1,32,4096]{3,2,1,0:T(8,128)(2,1)S(1)}, bf16[1,1,32,4096]{3,2,1,0:T(8,128)(2,1)}, u32[]{:S(2)}) copy-start(bf16[1,1,32,4096]{3,2,1,0:T(8,128)(2,1)} %g_hbm.1) | copy-start | bytes 786436
  6.8 10.4 %copy-start.6 = (bf16[1,1,32,32]{3,2,1,0:T(8,128)(2,1)S(1)}, bf16[1,1,32,32]{3,2,1,0:T(8,128)(2,1)}, u32[]{:S(2)}) copy-start(bf16[1,1,32,32]{3,2,1,0:T(8,128)(2,1)} %lse_hbm.1) | copy-start | bytes 6148
  6.8 10.4 %copy-start.7 = (bf16[1,1,32,32]{3,2,1,0:T(8,128)(2,1)S(1)}, bf16[1,1,32,32]{3,2,1,0:T(8,128)(2,1)}, u32[]{:S(2)}) copy-start(bf16[1,1,32,32]{3,2,1,0:T(8,128)(2,1)} %delta_hbm.1) | copy-start | bytes 6148
  6.8 41.2 %all-to-all-start = ((bf16[32,144,128]{2,1,0:T(8,128)(2,1)}), bf16[32,144,128]{2,1,0:T(8,128)(2,1)S(1)}, u32[]{:S(2)}, u32[]{:S(2)}) async-start(bf16[32,144,128]{2,1,0:T(8,128)(2,1)} %shard_map.147), calls=%async_computation | async-start | bytes 2359296 | tf_op jit(solution)/shard_map/all_to_all | solution.py:277
  17.2 32.8 %copy-start.9 = (s32[1,3]{1,0:T(1,128)S(1)}, s32[1,3]{1,0:T(1,128)}, u32[]{:S(2)}) copy-start(s32[1,3]{1,0:T(1,128)} %lengths_ref.5) | copy-start | bytes 40
  17.8 3.4 %collective-permute-start = (bf16[2,528,128]{2,1,0:T(8,128)(2,1)S(1)}, bf16[2,528,128]{2,1,0:T(8,128)(2,1)S(1)}, u32[]{:S(2)}, u32[]{:S(2)}) collective-permute-start(bf16[2,528,128]{2,1,0:T(8,128)(2,1)S(1)} %get-tuple-element.23), channel_id=1, source_target_pairs={{0,32},{32,0},{1,33},{33,1},{2,34},{34,2},{3,35},{35,3},{4,36},{36... | collective-permute-start | bytes 811016 | tf_op jit(solution)/shard_map/ppermute | solution.py:281
  21.3 28.7 %collective-permute-start.3 = (bf16[2,528,128]{2,1,0:T(8,128)(2,1)S(1)}, bf16[2,528,128]{2,1,0:T(8,128)(2,1)S(1)}, u32[]{:S(2)}, u32[]{:S(2)}) collective-permute-start(bf16[2,528,128]{2,1,0:T(8,128)(2,1)S(1)} %get-tuple-element.25), channel_id=1, source_target_pairs={{0,3},{1,0},{2,1},{3,2},{4,7},{5,4},{6,5},{7,6},{8,11},{9,8},{10,9... | collective-permute-start | bytes 811016 | tf_op jit(solution)/shard_map/ppermute | solution.py:285
  24.1 26.0 %collective-permute-start.1 = (bf16[2,528,128]{2,1,0:T(8,128)(2,1)S(1)}, bf16[2,528,128]{2,1,0:T(8,128)(2,1)S(1)}, u32[]{:S(2)}, u32[]{:S(2)}) collective-permute-start(bf16[2,528,128]{2,1,0:T(8,128)(2,1)S(1)} %get-tuple-element.25), channel_id=1, source_target_pairs={{0,1},{1,2},{2,3},{3,0},{4,5},{5,6},{6,7},{7,4},{8,9},{9,10},{10,1... | collective-permute-start | bytes 811016 | tf_op jit(solution)/shard_map/ppermute | solution.py:285
  28.4 21.7 %collective-permute-start.2 = (bf16[2,528,128]{2,1,0:T(8,128)(2,1)S(1)}, bf16[2,528,128]{2,1,0:T(8,128)(2,1)S(1)}, u32[]{:S(2)}, u32[]{:S(2)}) collective-permute-start(bf16[2,528,128]{2,1,0:T(8,128)(2,1)S(1)} %get-tuple-element.24.q0), channel_id=1, source_target_pairs={{0,2},{1,3},{2,0},{3,1},{4,6},{5,7},{6,4},{7,5},{8,10},{9,11},{10,... | collective-permute-start | bytes 811016 | tf_op jit(solution)/shard_map/ppermute | solution.py:285
  48.1 13.5 %collective-permute-start.4 = (bf16[32,32,128]{2,1,0:T(8,128)(2,1)S(1)}, bf16[32,32,128]{2,1,0:T(8,128)(2,1)S(1)}, u32[]{:S(2)}, u32[]{:S(2)}) collective-permute-start(bf16[32,32,128]{2,1,0:T(8,128)(2,1)S(1)} %slice.8), channel_id=1, source_target_pairs={{0,32},{32,0},{1,33},{33,1},{2,34},{34,2},{3,35},{35,3},{4,36},{36... | collective-permute-start | bytes 786440 | tf_op jit(solution)/shard_map/ppermute | solution.py:281
  68.1 34.3 %all-to-all-start.1 = ((bf16[32,128,128]{2,1,0:T(8,128)(2,1)}), bf16[32,128,128]{2,1,0:T(8,128)(2,1)S(1)}, u32[]{:S(2)}, u32[]{:S(2)}) async-start(bf16[32,128,128]{2,1,0:T(8,128)(2,1)} %get-tuple-element.29), calls=%async_computation.1 | async-start | bytes 2097152 | tf_op jit(solution)/shard_map/all_to_all | solution.py:277
  74.7 16.5 %collective-permute-start.5 = (bf16[2,256,128]{2,1,0:T(8,128)(2,1)S(1)}, bf16[2,256,128]{2,1,0:T(8,128)(2,1)S(1)}, u32[]{:S(2)}, u32[]{:S(2)}) collective-permute-start(bf16[2,256,128]{2,1,0:T(8,128)(2,1)S(1)} %get-tuple-element.33), channel_id=1, source_target_pairs={{0,3},{1,0},{2,1},{3,2},{4,7},{5,4},{6,5},{7,6},{8,11},{9,8},{10,9... | collective-permute-start | bytes 393224 | tf_op jit(solution)/shard_map/ppermute | solution.py:285
  77.4 13.7 %collective-permute-start.6 = (bf16[2,256,128]{2,1,0:T(8,128)(2,1)S(1)}, bf16[2,256,128]{2,1,0:T(8,128)(2,1)S(1)}, u32[]{:S(2)}, u32[]{:S(2)}) collective-permute-start(bf16[2,256,128]{2,1,0:T(8,128)(2,1)S(1)} %get-tuple-element.34), channel_id=1, source_target_pairs={{0,2},{1,3},{2,0},{3,1},{4,6},{5,7},{6,4},{7,5},{8,10},{9,11},{10,... | collective-permute-start | bytes 393224 | tf_op jit(solution)/shard_map/ppermute | solution.py:285
  80.2 11.3 %collective-permute-start.7 = (bf16[2,256,128]{2,1,0:T(8,128)(2,1)S(1)}, bf16[2,256,128]{2,1,0:T(8,128)(2,1)S(1)}, u32[]{:S(2)}, u32[]{:S(2)}) collective-permute-start(bf16[2,256,128]{2,1,0:T(8,128)(2,1)S(1)} %get-tuple-element.35), channel_id=1, source_target_pairs={{0,1},{1,2},{2,3},{3,0},{4,5},{5,6},{6,7},{7,4},{8,9},{9,10},{10,1... | collective-permute-start | bytes 393224 | tf_op jit(solution)/shard_map/ppermute | solution.py:285

commit v3 on v2

--- a/solution.py
+++ b/solution.py
@@ -25,13 +25,15 @@
 LOG2E = 1.4426950408889634
 SCALE = LANES**-0.5
 DEAD = 1e30
+BLOCK = 256
+MARGIN_ROWS = 8
 
 
 def dot(a, b, dims):
     return lax.dot_general(a, b, (dims, ((), ())), preferred_element_type=f32)
 
 
-def call(kernel, out_shape, spaces, flops=0, scratch=(), size=0):
+def call(kernel, out_shape, spaces, flops=0, scratch=(), size=0, limit=24):
     space = {"v": pltpu.VMEM, "s": pltpu.SMEM, "a": pl.ANY}
     many = isinstance(out_shape, tuple)
     out_spec = pl.BlockSpec(memory_space=pltpu.VMEM)
@@ -41,7 +43,7 @@
         in_specs=[pl.BlockSpec(memory_space=space[s]) for s in spaces],
         out_specs=tuple(out_spec for _ in out_shape) if many else out_spec,
         scratch_shapes=list(scratch),
-        compiler_params=pltpu.CompilerParams(vmem_limit_bytes=24 * 2**20),
+        compiler_params=pltpu.CompilerParams(vmem_limit_bytes=limit * 2**20),
         cost_estimate=pl.CostEstimate(flops=flops, bytes_accessed=size, transcendentals=0),
     )
 
@@ -75,8 +77,8 @@
     high = margin.astype(bf16).astype(f32)
     middle = (margin - high).astype(bf16).astype(f32)
     low = margin - high - middle
-    lane = lax.broadcasted_iota(jnp.int32, (16, LANES), 1)
-    row = lax.broadcasted_iota(jnp.int32, (16, LANES), 0)
+    lane = lax.broadcasted_iota(jnp.int32, (MARGIN_ROWS, LANES), 1)
+    row = lax.broadcasted_iota(jnp.int32, (MARGIN_ROWS, LANES), 0)
     block = jnp.where(lane == 0, high, jnp.where(lane == 1, middle, jnp.where(lane == 2, low, 0.0)))
     block = jnp.where(row == 0, block, 0.0).astype(bf16)
     for x in range(X):
@@ -163,75 +165,112 @@
     return weights.astype(bf16), score_grads
 
 
-def prompt_kernel(lengths_ref, q0, q1, q2, q3, kv_ref, acc_ref, out_ref, rows_ref, key_acc, value_acc):
-    for k, ref in enumerate((q0, q1, q2, q3)):
-        rows_ref[2 * k : 2 * k + 2] = ref[...]
-    key_acc[...] = jnp.zeros_like(key_acc)
-    value_acc[...] = jnp.zeros_like(value_acc)
-    per = 8
-    rows = per * PROMPT_HALF
-
-    @pl.loop(0, 2 * X)
-    def _(tile):
-        lse, delta, _ = row_stats(lengths_ref, rows_ref[tile, 2 * TILE :, :], tile // 2, tile % 2)
-        query = rows_ref[tile, 0:TILE, :]
-        grad = rows_ref[tile, TILE : 2 * TILE, :]
-        total = None
-        for c in range(CTX_N // per):
-            at = slice(c * per, (c + 1) * per)
-            key = kv_ref[at, 0:PROMPT_HALF, :].reshape(rows, LANES)
-            value = kv_ref[at, PROMPT_HALF : 2 * PROMPT_HALF, :].reshape(rows, LANES)
-            weights, score_grads = cell(key, value, query, grad, lse, delta)
-            at = slice(c * rows, (c + 1) * rows)
-            value_acc[at, :] += dot(weights, grad, ((1,), (0,)))
-            key_acc[at, :] += dot(score_grads, query, ((1,), (0,)))
-            term = dot(score_grads, key, ((0,), (0,)))
-            total = term if total is None else total + term
-        acc_ref[tile] = total
-
-    shape = (CTX_N, PROMPT_HALF, LANES)
-    out_ref[:, 0:PROMPT_HALF, :] = (key_acc[...] * SCALE).astype(bf16).reshape(shape)
-    out_ref[:, PROMPT_HALF:, :] = value_acc[...].astype(bf16).reshape(shape)
+def staged(blocks, first, second):
+    for i, block in enumerate(blocks):
+        first(*block, i % 2)
+        if i:
+            second(*blocks[i - 1], (i - 1) % 2)
+    second(*blocks[-1], (len(blocks) - 1) % 2)
+
+
+def gather_rows(refs, query_rows, grad_rows):
+    for k, ref in enumerate(refs):
+        for j in range(2):
+            at = slice((j * X + k) * TILE, (j * X + k + 1) * TILE)
+            query_rows[at, :] = ref[j, 0:TILE, :]
+            grad_rows[at, :] = ref[j, TILE : 2 * TILE, :]
+
+
+def tile_rows(tile):
+    return slice(tile * TILE, (tile + 1) * TILE)
+
+
+def prompt_kernel(
+    lengths_ref, q0, q1, q2, q3, kv_ref, acc_ref, out_ref, query_rows, grad_rows, weights, score_grads
+):
+    refs = (q0, q1, q2, q3)
+    gather_rows(refs, query_rows, grad_rows)
+    stats = [row_stats(lengths_ref, refs[t % X][t // X, 2 * TILE :, :], t % X, t // X) for t in range(2 * X)]
+    per = BLOCK // PROMPT_HALF
+
+    def keys_of(c):
+        return kv_ref[c * per : (c + 1) * per, 0:PROMPT_HALF, :].reshape(BLOCK, LANES)
+
+    def first(c, slot):
+        key = keys_of(c)
+        value = kv_ref[c * per : (c + 1) * per, PROMPT_HALF : 2 * PROMPT_HALF, :].reshape(BLOCK, LANES)
+        for t in range(2 * X):
+            at = tile_rows(t)
+            lse, delta, _ = stats[t]
+            weights[slot, :, at], score_grads[slot, :, at] = cell(
+                key, value, query_rows[at, :], grad_rows[at, :], lse, delta
+            )
+
+    def second(c, slot):
+        value_grad = dot(weights[slot], grad_rows[...], ((1,), (0,)))
+        key_grad = dot(score_grads[slot], query_rows[...], ((1,), (0,))) * SCALE
+        shape = (per, PROMPT_HALF, LANES)
+        to = slice(c * per, (c + 1) * per)
+        out_ref[to, 0:PROMPT_HALF, :] = key_grad.astype(bf16).reshape(shape)
+        out_ref[to, PROMPT_HALF:, :] = value_grad.astype(bf16).reshape(shape)
+        key = keys_of(c)
+        for t in range(2 * X):
+            term = dot(score_grads[slot, :, tile_rows(t)], key, ((0,), (0,)))
+            acc_ref[t] = term if c == 0 else acc_ref[t] + term
+
+    staged([(c,) for c in range(CTX_N // per)], first, second)
 
 
 def resp_kernel(
     lengths_ref, q0, q1, q2, q3, kv_ref, side_ref, acc_ref, prompt_ref,
-    out_ref, d0, d1, d2, d3, gate_ref, key_acc, value_acc,
+    out_ref, d0, d1, d2, d3, gate_ref, query_rows, grad_rows, weights, score_grads, acc,
 ):
     margin = jnp.sum(kv_ref[:, KV_ROWS:, :].astype(f32), axis=(0, 1), keepdims=True).reshape(1, LANES)
     margin = jnp.sum(margin, axis=1, keepdims=True)
     gate_ref[...] = jnp.broadcast_to(beta_coef * jax.nn.sigmoid(-beta_coef * margin), gate_ref.shape)
     out_ref[:, 0 : 2 * PROMPT_HALF, :] = prompt_ref[...]
-    key_acc[...] = jnp.zeros_like(key_acc)
-    value_acc[...] = jnp.zeros_like(value_acc)
+    refs, grads = (q0, q1, q2, q3), (d0, d1, d2, d3)
+    gather_rows(refs, query_rows, grad_rows)
+    stats = [row_stats(lengths_ref, refs[t % X][t // X, 2 * TILE :, :], t % X, t // X) for t in range(2 * X)]
     half = lax.axis_index("x") // 2
-    per = 16
-    rows = per * RESP_HALF
-    for j, (source, first) in enumerate(((kv_ref, 2 * PROMPT_HALF), (side_ref, 0))):
-        for k, (q_ref, d_ref) in enumerate(((q0, d0), (q1, d1), (q2, d2), (q3, d3))):
-            lse, delta, position = row_stats(lengths_ref, q_ref[j, 2 * TILE :, :], k, j)
-            query = q_ref[j, 0:TILE, :]
-            grad = q_ref[j, TILE : 2 * TILE, :]
-            total = acc_ref[2 * k + j]
-            for c in range(CTX_N // per):
-                at = slice(c * per, (c + 1) * per)
-                key = source[at, first : first + RESP_HALF, :].reshape(rows, LANES)
-                value = source[at, first + RESP_HALF : first + SIDE, :].reshape(rows, LANES)
-                index = lax.broadcasted_iota(jnp.int32, (rows, 1), 0)
-                key_position = (c * per + index // RESP_HALF) * POS + half * RESP_HALF + index % RESP_HALF
-                weights, score_grads = cell(key, value, query, grad, lse, delta, key_position <= position)
-                first_row = (j * (CTX_N // per) + c) * rows
-                at = slice(first_row, first_row + rows)
-                value_acc[at, :] += dot(weights, grad, ((1,), (0,)))
-                key_acc[at, :] += dot(score_grads, query, ((1,), (0,)))
-                total += dot(score_grads, key, ((0,), (0,)))
-            d_ref[j] = (total * SCALE).astype(bf16)
-
-        at = slice(j * CTX_N * RESP_HALF, (j + 1) * CTX_N * RESP_HALF)
-        shape = (CTX_N, RESP_HALF, LANES)
-        to = 2 * PROMPT_HALF + j * SIDE
-        out_ref[:, to : to + RESP_HALF, :] = (key_acc[at, :] * SCALE).astype(bf16).reshape(shape)
-        out_ref[:, to + RESP_HALF : to + SIDE, :] = value_acc[at, :].astype(bf16).reshape(shape)
+    per = BLOCK // RESP_HALF
+    last = CTX_N // per - 1
+    sources = ((kv_ref, 2 * PROMPT_HALF), (side_ref, 0))
+
+    def rows_of(j, c, at):
+        ref, start = sources[j]
+        return ref[c * per : (c + 1) * per, start + at : start + at + RESP_HALF, :].reshape(BLOCK, LANES)
+
+    def first(j, c, slot):
+        key, value = rows_of(j, c, 0), rows_of(j, c, RESP_HALF)
+        index = lax.broadcasted_iota(jnp.int32, (BLOCK, 1), 0)
+        key_position = (c * per + index // RESP_HALF) * POS + half * RESP_HALF + index % RESP_HALF
+        for k in range(X):
+            at, to = tile_rows(j * X + k), tile_rows(k)
+            lse, delta, position = stats[j * X + k]
+            weights[slot, :, to], score_grads[slot, :, to] = cell(
+                key, value, query_rows[at, :], grad_rows[at, :], lse, delta, key_position <= position
+            )
+
+    def second(j, c, slot):
+        rows = slice(j * X * TILE, (j + 1) * X * TILE)
+        value_grad = dot(weights[slot], grad_rows[rows, :], ((1,), (0,)))
+        key_grad = dot(score_grads[slot], query_rows[rows, :], ((1,), (0,))) * SCALE
+        shape = (per, RESP_HALF, LANES)
+        to = slice(c * per, (c + 1) * per)
+        start = 2 * PROMPT_HALF + j * SIDE
+        out_ref[to, start : start + RESP_HALF, :] = key_grad.astype(bf16).reshape(shape)
+        out_ref[to, start + RESP_HALF : start + SIDE, :] = value_grad.astype(bf16).reshape(shape)
+        key = rows_of(j, c, 0)
+        for k in range(X):
+            total = dot(score_grads[slot, :, tile_rows(k)], key, ((0,), (0,)))
+            total += acc_ref[j * X + k] if c == 0 else acc[k]
+            if c == last:
+                grads[k][j] = (total * SCALE).astype(bf16)
+            else:
+                acc[k] = total
+
+    staged([(j, c) for j in range(2) for c in range(CTX_N // per)], first, second)
 
 
 def kv_final_kernel(lengths_ref, gate_ref, part_ref, pk_ref, pv_ref, rk_ref, rv_ref):
@@ -285,6 +324,43 @@
     return lax.ppermute(values, "x", [(i, (i + by) % X) for i in range(X)])
 
 
+def prompt_call(lengths, rows, kv):
+    shape = jax.ShapeDtypeStruct
+    return call(
+        prompt_kernel,
+        (shape((2 * X, TILE, LANES), f32), shape((CTX_N, 2 * PROMPT_HALF, LANES), bf16)),
+        "svvvvv",
+        scratch=(
+            pltpu.VMEM((2 * X * TILE, LANES), bf16),
+            pltpu.VMEM((2 * X * TILE, LANES), bf16),
+            pltpu.VMEM((2, BLOCK, 2 * X * TILE), bf16),
+            pltpu.VMEM((2, BLOCK, 2 * X * TILE), bf16),
+        ),
+        flops=5 * 2 * 2048 * 1024 * 128 * 2,
+        size=3 * 2**20,
+    )(lengths, *rows, kv)
+
+
+def resp_call(lengths, rows, kv, side, acc, prompt_part):
+    shape = jax.ShapeDtypeStruct
+    return call(
+        resp_kernel,
+        (shape((CTX_N, KV_ROWS, LANES), bf16),)
+        + (shape((2, TILE, LANES), bf16),) * X
+        + (shape((8, LANES), f32),),
+        "svvvvvvvv",
+        scratch=(
+            pltpu.VMEM((2 * X * TILE, LANES), bf16),
+            pltpu.VMEM((2 * X * TILE, LANES), bf16),
+            pltpu.VMEM((2, BLOCK, X * TILE), bf16),
+            pltpu.VMEM((2, BLOCK, X * TILE), bf16),
+            pltpu.VMEM((X, TILE, LANES), f32),
+        ),
+        flops=5 * 2 * 1024 * 1024 * 128 * 2,
+        size=3 * 2**20,
+    )(lengths, *rows, kv, side, acc, prompt_part)
+
+
 def per_device(
     prompt_keys,
     prompt_values,
@@ -300,9 +376,10 @@
     shape = jax.ShapeDtypeStruct
     kv = call(
         kv_pack_kernel,
-        shape((CTX_N, KV_ROWS + 16, LANES), bf16),
+        shape((CTX_N, KV_ROWS + MARGIN_ROWS, LANES), bf16),
         "aaaaaa",
         size=2 * 2**20,
+        limit=60,
         scratch=(
             pltpu.SMEM((1, 3), jnp.int32),
             pltpu.VMEM((2, POS), f32),
@@ -333,28 +410,8 @@
     rows = (same, shift(odd, 1), shift(same, 2), shift(odd, 3))
 
     side = cross(kv[:, KV_ROWS - SIDE : KV_ROWS, :])
-    acc, prompt_part = call(
-        prompt_kernel,
-        (shape((2 * X, TILE, LANES), f32), shape((CTX_N, 2 * PROMPT_HALF, LANES), bf16)),
-        "svvvvv",
-        scratch=(
-            pltpu.VMEM((2 * X, QUERY_ROWS, LANES), bf16),
-            pltpu.VMEM((1024, LANES), f32),
-            pltpu.VMEM((1024, LANES), f32),
-        ),
-        flops=5 * 2 * 2048 * 1024 * 128 * 2,
-        size=3 * 2**20,
-    )(lengths, *rows, kv)
-    part, *grads, gate = call(
-        resp_kernel,
-        (shape((CTX_N, KV_ROWS, LANES), bf16),)
-        + (shape((2, TILE, LANES), bf16),) * X
-        + (shape((8, LANES), f32),),
-        "svvvvvvvv",
-        scratch=(pltpu.VMEM((1024, LANES), f32), pltpu.VMEM((1024, LANES), f32)),
-        flops=5 * 2 * 1024 * 1024 * 128 * 2,
-        size=3 * 2**20,
-    )(lengths, *rows, kv, side, acc, prompt_part)
+    acc, prompt_part = prompt_call(lengths, rows, kv)
+    part, *grads, gate = resp_call(lengths, rows, kv, side, acc, prompt_part)
     part = swap(part)
     back = [grads[0]] + [shift(grads[k], X - k) for k in range(1, X)]
     query_grad = call(query_final_kernel, shape((1, 2, POS, 2 * GROUP * LANES), bf16), "vvvvv", size=2**20)(

time: 105 us -> 92.6 us (0.88)
  Pallas kernels: 22.6 us -> 15.8 us
  local copies, waits for them, and re-layouts: 4.92 us -> 0.56 us
  waiting for transfers between devices: 35.6 us -> 34.2 us
    pallas_call x3, Pallas kernels: 19.8 us -> 13 us  [the longest x1 6.26 us: prompt_call(): call(prompt_kernel, (shape((2 * X, TILE, LANES), f32), shape((CTX_N, 2 *...]
    unnamed x22 -> x10, local copies, waits for them, and re-layouts: 4.39 us -> 0.03 us
    all_to_all x2, waiting for transfers between devices: 27.7 us -> 26.3 us  [swap(): return lax.all_to_all(values, CTX, split_axis=0, concat_axis=0, tiled=True)]
  transfers between devices with their start and end apart: 10 -> 10, of which waited for: 5 -> 5; matrix products, arithmetic and copies ran while one was open for 1% -> 1% of each run, Pallas kernels for 13% -> 8%
where the time goes in v3:
time: 92.6 us; the launch traced here: 91.9 us
  starting transfers between devices  40.6 us (44%)
  waiting for transfers between devices  34.2 us (37%)
  Pallas kernels  15.8 us (17%)
    all_to_all x2, waiting for transfers between devices, swap(): return lax.all_to_all(values, CTX, split_axis=0, concat_axis=0, tiled=True)  26.3 us
    ppermute x6, starting transfers between devices, shift(): return lax.ppermute(values, 'x', [(i, (i + by) % X) for i in range(X)])  19 us
    all_to_all x2, starting transfers between devices, swap(): return lax.all_to_all(values, CTX, split_axis=0, concat_axis=0, tiled=True)  17.7 us
    ppermute x6, waiting for transfers between devices, shift(): return lax.ppermute(values, 'x', [(i, (i + by) % X) for i in range(X)])  6.34 us
    pallas_call x1, Pallas kernels, prompt_call(): call(prompt_kernel, (shape((2 * X, TILE, LANES), f32), shape((CTX_N, 2 *...  6.26 us
    pallas_call x1, Pallas kernels, resp_call(): call(resp_kernel, (shape((CTX_N, KV_ROWS, LANES), bf16),) + (shape((2, TI...  4.71 us
    ppermute x2, starting transfers between devices, cross(): return lax.ppermute(values, 'pair', [(0, 1), (1, 0)])  3.84 us
    pallas_call x1, Pallas kernels, per_device(): call(kv_pack_kernel, shape((CTX_N, KV_ROWS + MARGIN_ROWS, LANES), bf16),...  2.01 us
  transfers between devices with their start and end apart: 10, of which 5 were waited for; matrix products, arithmetic and copies ran while one was open for 1% of the time, Pallas kernels for 8%

profile of v3, /device:TPU:6, one launch (start us, length us, event | category | flops | bytes accessed | tf_op | source)
XLA Modules:
  0.0 91.9 jit_solution(3006939534286077506)
XLA Ops:
  0.6 2.0 %shard_map.147 = bf16[32,136,128]{2,1,0:T(8,128)(2,1)} custom-call(s32[1,3]{1,0:T(1,128)} %lengths_ref.5, f32[1,2,32]{2,1,0:T(2,128)} %logratio_hbm.1, bf16[1,64,256]{2,1,0:T(8,128)(2,1)} %pk_hbm.1, bf16[1,64,256]{2,1,0:T(8,128)(2,1)} %pv_hbm.1, bf16[1,1,32,512]{3,2,1,0:T(8,128)(2,1)} %rk_hbm.1, bf16[1,1,32,512]{3,2,1,0:T(8,128)(2,1)} %rv_hbm.1), custom_call_target="tpu_custom_call" | custom-call | bytes 2097152 | tf_op jit(solution)/shard_map/pallas_call | solution.py:377
  2.6 0.0 copy-start
  2.7 0.0 copy-start.1
  2.7 0.0 copy-start.2
  2.7 0.0 copy-start.3
  2.7 10.3 %all-to-all-start = ((bf16[32,136,128]{2,1,0:T(8,128)(2,1)}), bf16[32,136,128]{2,1,0:T(8,128)(2,1)S(1)}, u32[]{:S(2)}, u32[]{:S(2)}) async-start(bf16[32,136,128]{2,1,0:T(8,128)(2,1)} %shard_map.147), calls=%async_computation | async-start | bytes 2228224 | tf_op jit(solution)/shard_map/all_to_all | solution.py:316
  13.0 0.0 copy-done
  13.1 0.0 copy-done.1
  13.1 0.0 copy-done.2
  13.1 0.0 copy-done.3
  13.1 0.0 copy-start.4
  13.1 0.6 shard_map.145
  13.7 1.9 %collective-permute-start = (bf16[2,528,128]{2,1,0:T(8,128)(2,1)S(1)}, bf16[2,528,128]{2,1,0:T(8,128)(2,1)S(1)}, u32[]{:S(2)}, u32[]{:S(2)}) collective-permute-start(bf16[2,528,128]{2,1,0:T(8,128)(2,1)S(1)} %get-tuple-element.23), channel_id=1, source_target_pairs={{0,32},{32,0},{1,33},{33,1},{2,34},{34,2},{3,35},{35,3},{4,36},{36... | collective-permute-start | bytes 811016 | tf_op jit(solution)/shard_map/ppermute | solution.py:320
  15.6 1.5 %collective-permute-done.other_ref = bf16[2,528,128]{2,1,0:T(8,128)(2,1)S(1)} collective-permute-done((bf16[2,528,128]{2,1,0:T(8,128)(2,1)S(1)}, bf16[2,528,128]{2,1,0:T(8,128)(2,1)S(1)}, u32[]{:S(2)}, u32[]{:S(2)}) %collective-permute-start) | collective-permute-done | bytes 270368 | tf_op jit(solution)/shard_map/ppermute | solution.py:320
  17.2 2.8 %collective-permute-start.3 = (bf16[2,528,128]{2,1,0:T(8,128)(2,1)S(1)}, bf16[2,528,128]{2,1,0:T(8,128)(2,1)S(1)}, u32[]{:S(2)}, u32[]{:S(2)}) collective-permute-start(bf16[2,528,128]{2,1,0:T(8,128)(2,1)S(1)} %get-tuple-element.25), channel_id=1, source_target_pairs={{0,3},{1,0},{2,1},{3,2},{4,7},{5,4},{6,5},{7,6},{8,11},{9,8},{10,9... | collective-permute-start | bytes 811016 | tf_op jit(solution)/shard_map/ppermute | solution.py:324
  19.9 4.3 %collective-permute-start.1 = (bf16[2,528,128]{2,1,0:T(8,128)(2,1)S(1)}, bf16[2,528,128]{2,1,0:T(8,128)(2,1)S(1)}, u32[]{:S(2)}, u32[]{:S(2)}) collective-permute-start(bf16[2,528,128]{2,1,0:T(8,128)(2,1)S(1)} %get-tuple-element.25), channel_id=1, source_target_pairs={{0,1},{1,2},{2,3},{3,0},{4,5},{5,6},{6,7},{7,4},{8,9},{9,10},{10,1... | collective-permute-start | bytes 811016 | tf_op jit(solution)/shard_map/ppermute | solution.py:324
  24.2 2.2 %collective-permute-start.2 = (bf16[2,528,128]{2,1,0:T(8,128)(2,1)S(1)}, bf16[2,528,128]{2,1,0:T(8,128)(2,1)S(1)}, u32[]{:S(2)}, u32[]{:S(2)}) collective-permute-start(bf16[2,528,128]{2,1,0:T(8,128)(2,1)S(1)} %get-tuple-element.24.q0), channel_id=1, source_target_pairs={{0,2},{1,3},{2,0},{3,1},{4,6},{5,7},{6,4},{7,5},{8,10},{9,11},{10,... | collective-permute-start | bytes 811016 | tf_op jit(solution)/shard_map/ppermute | solution.py:324
  26.4 16.1 %all-to-all-done.kv_ref = bf16[32,136,128]{2,1,0:T(8,128)(2,1)S(1)} async-done(((bf16[32,136,128]{2,1,0:T(8,128)(2,1)}), bf16[32,136,128]{2,1,0:T(8,128)(2,1)S(1)}, u32[]{:S(2)}, u32[]{:S(2)}) %all-to-all-start) | async-done | bytes 1114144 | tf_op jit(solution)/shard_map/all_to_all | solution.py:316
  42.5 1.9 %collective-permute-start.4 = (bf16[32,32,128]{2,1,0:T(8,128)(2,1)S(1)}, bf16[32,32,128]{2,1,0:T(8,128)(2,1)S(1)}, u32[]{:S(2)}, u32[]{:S(2)}) collective-permute-start(bf16[32,32,128]{2,1,0:T(8,128)(2,1)S(1)} %slice.8), channel_id=1, source_target_pairs={{0,32},{32,0},{1,33},{33,1},{2,34},{34,2},{3,35},{35,3},{4,36},{36... | collective-permute-start | bytes 786440 | tf_op jit(solution)/shard_map/ppermute | solution.py:320
  44.5 0.0 collective-permute-done.3.q3
  44.5 0.0 collective-permute-done.1.q1
  44.5 0.0 collective-permute-done.2.q2
  44.5 0.0 copy-done.4
  44.5 6.3 %shard_map.148 = (f32[8,256,128]{2,1,0:T(8,128)S(1)}, bf16[32,64,128]{2,1,0:T(8,128)(2,1)S(1)}) custom-call(s32[1,3]{1,0:T(1,128)S(1)} %copy-done.4, bf16[2,528,128]{2,1,0:T(8,128)(2,1)S(1)} %get-tuple-element.24.q0, bf16[2,528,128]{2,1,0:T(8,128)(2,1)S(1)} %collective-permute-done.1.q1, bf16[2,528,128]{2,1,0:T(8,128)(2,1)S(1)} %collective-permute-done.2.q2, ...), custom_call_target="tpu_custom_call" | custom-call | flops 5368709120 | bytes 3145728 | tf_op jit(solution)/shard_map/pallas_call | solution.py:329
  50.8 0.0 collective-permute-done.4.side_ref
  50.8 4.7 %shard_map.149 = (bf16[32,128,128]{2,1,0:T(8,128)(2,1)}, bf16[2,256,128]{2,1,0:T(8,128)(2,1)S(1)}, bf16[2,256,128]{2,1,0:T(8,128)(2,1)S(1)}, bf16[2,256,128]{2,1...) custom-call(s32[1,3]{1,0:T(1,128)S(1)} %copy-done.4, ...), custom_call_target="tpu_custom_call" | custom-call | flops 2684354560 | bytes 3145728 | tf_op jit(solution)/shard_map/pallas_call | solution.py:346
  55.5 7.4 %all-to-all-start.1 = ((bf16[32,128,128]{2,1,0:T(8,128)(2,1)}), bf16[32,128,128]{2,1,0:T(8,128)(2,1)S(1)}, u32[]{:S(2)}, u32[]{:S(2)}) async-start(bf16[32,128,128]{2,1,0:T(8,128)(2,1)} %get-tuple-element.29), calls=%async_computation.1 | async-start | bytes 2097152 | tf_op jit(solution)/shard_map/all_to_all | solution.py:316
  62.9 2.8 %collective-permute-start.5 = (bf16[2,256,128]{2,1,0:T(8,128)(2,1)S(1)}, bf16[2,256,128]{2,1,0:T(8,128)(2,1)S(1)}, u32[]{:S(2)}, u32[]{:S(2)}) collective-permute-start(bf16[2,256,128]{2,1,0:T(8,128)(2,1)S(1)} %get-tuple-element.33), channel_id=1, source_target_pairs={{0,3},{1,0},{2,1},{3,2},{4,7},{5,4},{6,5},{7,6},{8,11},{9,8},{10,9... | collective-permute-start | bytes 393224 | tf_op jit(solution)/shard_map/ppermute | solution.py:324
  65.6 2.7 %collective-permute-start.6 = (bf16[2,256,128]{2,1,0:T(8,128)(2,1)S(1)}, bf16[2,256,128]{2,1,0:T(8,128)(2,1)S(1)}, u32[]{:S(2)}, u32[]{:S(2)}) collective-permute-start(bf16[2,256,128]{2,1,0:T(8,128)(2,1)S(1)} %get-tuple-element.34), channel_id=1, source_target_pairs={{0,2},{1,3},{2,0},{3,1},{4,6},{5,7},{6,4},{7,5},{8,10},{9,11},{10,... | collective-permute-start | bytes 393224 | tf_op jit(solution)/shard_map/ppermute | solution.py:324
  68.4 4.3 %collective-permute-start.7 = (bf16[2,256,128]{2,1,0:T(8,128)(2,1)S(1)}, bf16[2,256,128]{2,1,0:T(8,128)(2,1)S(1)}, u32[]{:S(2)}, u32[]{:S(2)}) collective-permute-start(bf16[2,256,128]{2,1,0:T(8,128)(2,1)S(1)} %get-tuple-element.35), channel_id=1, source_target_pairs={{0,1},{1,2},{2,3},{3,0},{4,5},{5,6},{6,7},{7,4},{8,9},{9,10},{10,1... | collective-permute-start | bytes 393224 | tf_op jit(solution)/shard_map/ppermute | solution.py:324
  72.7 0.5 slice.7
  73.2 0.0 collective-permute-done.5.d1
  73.2 5.8 %collective-permute-done.6.d2 = bf16[2,256,128]{2,1,0:T(8,128)(2,1)S(1)} collective-permute-done((bf16[2,256,128]{2,1,0:T(8,128)(2,1)S(1)}, bf16[2,256,128]{2,1,0:T(8,128)(2,1)S(1)}, u32[]{:S(2)}, u32[]{:S(2)}) %collective-permute-start.6) | collective-permute-done | bytes 131104 | tf_op jit(solution)/shard_map/ppermute | solution.py:324
  79.1 0.5 collective-permute-done.7.d3
  79.5 0.8 shard_map.151
  80.4 10.2 %all-to-all-done.1.part_ref = bf16[32,128,128]{2,1,0:T(8,128)(2,1)S(1)} async-done(((bf16[32,128,128]{2,1,0:T(8,128)(2,1)}), bf16[32,128,128]{2,1,0:T(8,128)(2,1)S(1)}, u32[]{:S(2)}, u32[]{:S(2)}) %all-to-all-start.1) | async-done | bytes 1048608 | tf_op jit(solution)/shard_map/all_to_all | solution.py:316
  90.6 1.3 %shard_map.150 = (bf16[1,64,256]{2,1,0:T(8,128)(2,1)}, bf16[1,64,256]{2,1,0:T(8,128)(2,1)}, bf16[1,2,32,256]{3,2,1,0:T(8,128)(2,1)}, bf16[1,2,32,256]{3,2,1,0:T(8,128)(2,1)}) custom-call(s32[1,3]{1,0:T(1,128)S(1)} %copy-done.4, f32[8,128]{1,0:T(8,128)S(1)} %get-tuple-element.28.gate_ref, bf16[32,128,128]{2,1,0:T(8,128)(2,1)S(1)} %all-to-all-done.1.part_ref), custom_call_target="tpu_custom_call" | custom-call | bytes 1048576 | tf_op jit(solution)/shard_map/pallas_call | solution.py:421
  (2 shorter events, 0.1 us)
Async XLA Ops:
  2.6 10.4 %copy-start = (bf16[1,1,32,4096]{3,2,1,0:T(8,128)(2,1)S(1)}, bf16[1,1,32,4096]{3,2,1,0:T(8,128)(2,1)}, u32[]{:S(2)}) copy-start(bf16[1,1,32,4096]{3,2,1,0:T(8,128)(2,1)} %q_hbm.1) | copy-start | bytes 786436
  2.7 10.4 %copy-start.1 = (bf16[1,1,32,4096]{3,2,1,0:T(8,128)(2,1)S(1)}, bf16[1,1,32,4096]{3,2,1,0:T(8,128)(2,1)}, u32[]{:S(2)}) copy-start(bf16[1,1,32,4096]{3,2,1,0:T(8,128)(2,1)} %g_hbm.1) | copy-start | bytes 786436
  2.7 10.4 %copy-start.2 = (bf16[1,1,32,32]{3,2,1,0:T(8,128)(2,1)S(1)}, bf16[1,1,32,32]{3,2,1,0:T(8,128)(2,1)}, u32[]{:S(2)}) copy-start(bf16[1,1,32,32]{3,2,1,0:T(8,128)(2,1)} %lse_hbm.1) | copy-start | bytes 6148
  2.7 10.4 %copy-start.3 = (bf16[1,1,32,32]{3,2,1,0:T(8,128)(2,1)S(1)}, bf16[1,1,32,32]{3,2,1,0:T(8,128)(2,1)}, u32[]{:S(2)}) copy-start(bf16[1,1,32,32]{3,2,1,0:T(8,128)(2,1)} %delta_hbm.1) | copy-start | bytes 6148
  2.7 39.8 %all-to-all-start = ((bf16[32,136,128]{2,1,0:T(8,128)(2,1)}), bf16[32,136,128]{2,1,0:T(8,128)(2,1)S(1)}, u32[]{:S(2)}, u32[]{:S(2)}) async-start(bf16[32,136,128]{2,1,0:T(8,128)(2,1)} %shard_map.147), calls=%async_computation | async-start | bytes 2228224 | tf_op jit(solution)/shard_map/all_to_all | solution.py:316
  13.1 31.4 %copy-start.4 = (s32[1,3]{1,0:T(1,128)S(1)}, s32[1,3]{1,0:T(1,128)}, u32[]{:S(2)}) copy-start(s32[1,3]{1,0:T(1,128)} %lengths_ref.5) | copy-start | bytes 40
  13.7 3.4 %collective-permute-start = (bf16[2,528,128]{2,1,0:T(8,128)(2,1)S(1)}, bf16[2,528,128]{2,1,0:T(8,128)(2,1)S(1)}, u32[]{:S(2)}, u32[]{:S(2)}) collective-permute-start(bf16[2,528,128]{2,1,0:T(8,128)(2,1)S(1)} %get-tuple-element.23), channel_id=1, source_target_pairs={{0,32},{32,0},{1,33},{33,1},{2,34},{34,2},{3,35},{35,3},{4,36},{36... | collective-permute-start | bytes 811016 | tf_op jit(solution)/shard_map/ppermute | solution.py:320
  17.2 27.3 %collective-permute-start.3 = (bf16[2,528,128]{2,1,0:T(8,128)(2,1)S(1)}, bf16[2,528,128]{2,1,0:T(8,128)(2,1)S(1)}, u32[]{:S(2)}, u32[]{:S(2)}) collective-permute-start(bf16[2,528,128]{2,1,0:T(8,128)(2,1)S(1)} %get-tuple-element.25), channel_id=1, source_target_pairs={{0,3},{1,0},{2,1},{3,2},{4,7},{5,4},{6,5},{7,6},{8,11},{9,8},{10,9... | collective-permute-start | bytes 811016 | tf_op jit(solution)/shard_map/ppermute | solution.py:324
  19.9 24.5 %collective-permute-start.1 = (bf16[2,528,128]{2,1,0:T(8,128)(2,1)S(1)}, bf16[2,528,128]{2,1,0:T(8,128)(2,1)S(1)}, u32[]{:S(2)}, u32[]{:S(2)}) collective-permute-start(bf16[2,528,128]{2,1,0:T(8,128)(2,1)S(1)} %get-tuple-element.25), channel_id=1, source_target_pairs={{0,1},{1,2},{2,3},{3,0},{4,5},{5,6},{6,7},{7,4},{8,9},{9,10},{10,1... | collective-permute-start | bytes 811016 | tf_op jit(solution)/shard_map/ppermute | solution.py:324
  24.2 20.3 %collective-permute-start.2 = (bf16[2,528,128]{2,1,0:T(8,128)(2,1)S(1)}, bf16[2,528,128]{2,1,0:T(8,128)(2,1)S(1)}, u32[]{:S(2)}, u32[]{:S(2)}) collective-permute-start(bf16[2,528,128]{2,1,0:T(8,128)(2,1)S(1)} %get-tuple-element.24.q0), channel_id=1, source_target_pairs={{0,2},{1,3},{2,0},{3,1},{4,6},{5,7},{6,4},{7,5},{8,10},{9,11},{10,... | collective-permute-start | bytes 811016 | tf_op jit(solution)/shard_map/ppermute | solution.py:324
  42.5 8.2 %collective-permute-start.4 = (bf16[32,32,128]{2,1,0:T(8,128)(2,1)S(1)}, bf16[32,32,128]{2,1,0:T(8,128)(2,1)S(1)}, u32[]{:S(2)}, u32[]{:S(2)}) collective-permute-start(bf16[32,32,128]{2,1,0:T(8,128)(2,1)S(1)} %slice.8), channel_id=1, source_target_pairs={{0,32},{32,0},{1,33},{33,1},{2,34},{34,2},{3,35},{35,3},{4,36},{36... | collective-permute-start | bytes 786440 | tf_op jit(solution)/shard_map/ppermute | solution.py:320
  55.5 35.1 %all-to-all-start.1 = ((bf16[32,128,128]{2,1,0:T(8,128)(2,1)}), bf16[32,128,128]{2,1,0:T(8,128)(2,1)S(1)}, u32[]{:S(2)}, u32[]{:S(2)}) async-start(bf16[32,128,128]{2,1,0:T(8,128)(2,1)} %get-tuple-element.29), calls=%async_computation.1 | async-start | bytes 2097152 | tf_op jit(solution)/shard_map/all_to_all | solution.py:316
  62.9 10.4 %collective-permute-start.5 = (bf16[2,256,128]{2,1,0:T(8,128)(2,1)S(1)}, bf16[2,256,128]{2,1,0:T(8,128)(2,1)S(1)}, u32[]{:S(2)}, u32[]{:S(2)}) collective-permute-start(bf16[2,256,128]{2,1,0:T(8,128)(2,1)S(1)} %get-tuple-element.33), channel_id=1, source_target_pairs={{0,3},{1,0},{2,1},{3,2},{4,7},{5,4},{6,5},{7,6},{8,11},{9,8},{10,9... | collective-permute-start | bytes 393224 | tf_op jit(solution)/shard_map/ppermute | solution.py:324
  65.6 13.4 %collective-permute-start.6 = (bf16[2,256,128]{2,1,0:T(8,128)(2,1)S(1)}, bf16[2,256,128]{2,1,0:T(8,128)(2,1)S(1)}, u32[]{:S(2)}, u32[]{:S(2)}) collective-permute-start(bf16[2,256,128]{2,1,0:T(8,128)(2,1)S(1)} %get-tuple-element.34), channel_id=1, source_target_pairs={{0,2},{1,3},{2,0},{3,1},{4,6},{5,7},{6,4},{7,5},{8,10},{9,11},{10,... | collective-permute-start | bytes 393224 | tf_op jit(solution)/shard_map/ppermute | solution.py:324
  68.4 11.2 %collective-permute-start.7 = (bf16[2,256,128]{2,1,0:T(8,128)(2,1)S(1)}, bf16[2,256,128]{2,1,0:T(8,128)(2,1)S(1)}, u32[]{:S(2)}, u32[]{:S(2)}) collective-permute-start(bf16[2,256,128]{2,1,0:T(8,128)(2,1)S(1)} %get-tuple-element.35), channel_id=1, source_target_pairs={{0,1},{1,2},{2,3},{3,0},{4,5},{5,6},{6,7},{7,4},{8,9},{9,10},{10,1... | collective-permute-start | bytes 393224 | tf_op jit(solution)/shard_map/ppermute | solution.py:324

commit v4 on v3

--- a/solution.py
+++ b/solution.py
@@ -25,7 +25,7 @@
 LOG2E = 1.4426950408889634
 SCALE = LANES**-0.5
 DEAD = 1e30
-BLOCK = 256
+BLOCK = 512
 MARGIN_ROWS = 8
 
 
@@ -33,15 +33,16 @@
     return lax.dot_general(a, b, (dims, ((), ())), preferred_element_type=f32)
 
 
-def call(kernel, out_shape, spaces, flops=0, scratch=(), size=0, limit=24):
+def call(kernel, out_shape, spaces, flops=0, scratch=(), size=0, limit=24, out_spaces=""):
     space = {"v": pltpu.VMEM, "s": pltpu.SMEM, "a": pl.ANY}
     many = isinstance(out_shape, tuple)
-    out_spec = pl.BlockSpec(memory_space=pltpu.VMEM)
+    out_spaces = out_spaces or "v" * (len(out_shape) if many else 1)
+    out_specs = tuple(pl.BlockSpec(memory_space=space[s]) for s in out_spaces)
     return pl.pallas_call(
         kernel,
         out_shape=out_shape,
         in_specs=[pl.BlockSpec(memory_space=space[s]) for s in spaces],
-        out_specs=tuple(out_spec for _ in out_shape) if many else out_spec,
+        out_specs=out_specs if many else out_specs[0],
         scratch_shapes=list(scratch),
         compiler_params=pltpu.CompilerParams(vmem_limit_bytes=limit * 2**20),
         cost_estimate=pl.CostEstimate(flops=flops, bytes_accessed=size, transcendentals=0),
@@ -144,15 +145,18 @@
         ref[1] = other_ref[i]
 
 
+def row_position(k):
+    x = (lax.axis_index("x") + X - k) % X
+    return (lax.axis_index("y") * X + x) * POS + lax.broadcasted_iota(jnp.int32, (1, TILE), 1) % POS
+
+
 def row_stats(lengths_ref, block, k, j):
     block = block.astype(f32)
     lse = jnp.concatenate([block[0:1], block[1:2]], axis=1) * LOG2E
     delta = jnp.concatenate([block[2:3], block[3:4]], axis=1)
     core = lax.axis_index("pair")
     response = core + j - 2 * core * j
-    x = (lax.axis_index("x") + X - k) % X
-    position = (lax.axis_index("y") * X + x) * POS + lax.broadcasted_iota(jnp.int32, (1, TILE), 1) % POS
-    return jnp.where(position < lengths_ref[0, 1 + response], lse, DEAD), delta, position
+    return jnp.where(row_position(k) < lengths_ref[0, 1 + response], lse, DEAD), delta
 
 
 def cell(key, value, query, grad, lse, delta, allowed=None):
@@ -173,104 +177,108 @@
     second(*blocks[-1], (len(blocks) - 1) % 2)
 
 
-def gather_rows(refs, query_rows, grad_rows):
-    for k, ref in enumerate(refs):
+def tile_rows(tile):
+    return slice(tile * TILE, (tile + 1) * TILE)
+
+
+def prompt_kernel(
+    lengths_ref, q0, q1, q2, q3, kv_ref, out_ref, score_grads, query_rows, grad_rows, lse_ref, delta_ref, weights
+):
+    for k, ref in enumerate((q0, q1, q2, q3)):
         for j in range(2):
-            at = slice((j * X + k) * TILE, (j * X + k + 1) * TILE)
+            t = j * X + k
+            at = tile_rows(t)
             query_rows[at, :] = ref[j, 0:TILE, :]
             grad_rows[at, :] = ref[j, TILE : 2 * TILE, :]
-
-
-def tile_rows(tile):
-    return slice(tile * TILE, (tile + 1) * TILE)
-
-
-def prompt_kernel(
-    lengths_ref, q0, q1, q2, q3, kv_ref, acc_ref, out_ref, query_rows, grad_rows, weights, score_grads
-):
-    refs = (q0, q1, q2, q3)
-    gather_rows(refs, query_rows, grad_rows)
-    stats = [row_stats(lengths_ref, refs[t % X][t // X, 2 * TILE :, :], t % X, t // X) for t in range(2 * X)]
+            lse, delta = row_stats(lengths_ref, ref[j, 2 * TILE :, :], k, j)
+            lse_ref[t : t + 1, :], delta_ref[t : t + 1, :] = lse, delta
     per = BLOCK // PROMPT_HALF
 
-    def keys_of(c):
-        return kv_ref[c * per : (c + 1) * per, 0:PROMPT_HALF, :].reshape(BLOCK, LANES)
-
     def first(c, slot):
-        key = keys_of(c)
-        value = kv_ref[c * per : (c + 1) * per, PROMPT_HALF : 2 * PROMPT_HALF, :].reshape(BLOCK, LANES)
+        rows = slice(c * per, (c + 1) * per)
+        key = kv_ref[rows, 0:PROMPT_HALF, :].reshape(BLOCK, LANES)
+        value = kv_ref[rows, PROMPT_HALF : 2 * PROMPT_HALF, :].reshape(BLOCK, LANES)
         for t in range(2 * X):
             at = tile_rows(t)
-            lse, delta, _ = stats[t]
-            weights[slot, :, at], score_grads[slot, :, at] = cell(
-                key, value, query_rows[at, :], grad_rows[at, :], lse, delta
+            weights[slot, :, at], score_grads[c * BLOCK : (c + 1) * BLOCK, at] = cell(
+                key, value, query_rows[at, :], grad_rows[at, :], lse_ref[t : t + 1, :], delta_ref[t : t + 1, :]
             )
 
     def second(c, slot):
         value_grad = dot(weights[slot], grad_rows[...], ((1,), (0,)))
-        key_grad = dot(score_grads[slot], query_rows[...], ((1,), (0,))) * SCALE
+        key_grad = dot(score_grads[c * BLOCK : (c + 1) * BLOCK, :], query_rows[...], ((1,), (0,))) * SCALE
         shape = (per, PROMPT_HALF, LANES)
         to = slice(c * per, (c + 1) * per)
         out_ref[to, 0:PROMPT_HALF, :] = key_grad.astype(bf16).reshape(shape)
         out_ref[to, PROMPT_HALF:, :] = value_grad.astype(bf16).reshape(shape)
-        key = keys_of(c)
-        for t in range(2 * X):
-            term = dot(score_grads[slot, :, tile_rows(t)], key, ((0,), (0,)))
-            acc_ref[t] = term if c == 0 else acc_ref[t] + term
 
     staged([(c,) for c in range(CTX_N // per)], first, second)
 
 
 def resp_kernel(
-    lengths_ref, q0, q1, q2, q3, kv_ref, side_ref, acc_ref, prompt_ref,
-    out_ref, d0, d1, d2, d3, gate_ref, query_rows, grad_rows, weights, score_grads, acc,
+    kv_ref, side_ref, prompt_ref, query_rows, grad_rows, lse_ref, delta_ref,
+    out_hbm, score_grads, gate_ref, weights, parts, sems,
 ):
+    copies = [pltpu.make_async_copy(prompt_ref, out_hbm.at[:, 0 : 2 * PROMPT_HALF, :], sems.at[0])]
+    copies[0].start()
     margin = jnp.sum(kv_ref[:, KV_ROWS:, :].astype(f32), axis=(0, 1), keepdims=True).reshape(1, LANES)
     margin = jnp.sum(margin, axis=1, keepdims=True)
     gate_ref[...] = jnp.broadcast_to(beta_coef * jax.nn.sigmoid(-beta_coef * margin), gate_ref.shape)
-    out_ref[:, 0 : 2 * PROMPT_HALF, :] = prompt_ref[...]
-    refs, grads = (q0, q1, q2, q3), (d0, d1, d2, d3)
-    gather_rows(refs, query_rows, grad_rows)
-    stats = [row_stats(lengths_ref, refs[t % X][t // X, 2 * TILE :, :], t % X, t // X) for t in range(2 * X)]
     half = lax.axis_index("x") // 2
     per = BLOCK // RESP_HALF
-    last = CTX_N // per - 1
+    blocks = CTX_N // per
     sources = ((kv_ref, 2 * PROMPT_HALF), (side_ref, 0))
 
-    def rows_of(j, c, at):
+    def first(j, c, slot):
         ref, start = sources[j]
-        return ref[c * per : (c + 1) * per, start + at : start + at + RESP_HALF, :].reshape(BLOCK, LANES)
-
-    def first(j, c, slot):
-        key, value = rows_of(j, c, 0), rows_of(j, c, RESP_HALF)
+        rows = slice(c * per, (c + 1) * per)
+        key = ref[rows, start : start + RESP_HALF, :].reshape(BLOCK, LANES)
+        value = ref[rows, start + RESP_HALF : start + SIDE, :].reshape(BLOCK, LANES)
         index = lax.broadcasted_iota(jnp.int32, (BLOCK, 1), 0)
         key_position = (c * per + index // RESP_HALF) * POS + half * RESP_HALF + index % RESP_HALF
         for k in range(X):
-            at, to = tile_rows(j * X + k), tile_rows(k)
-            lse, delta, position = stats[j * X + k]
-            weights[slot, :, to], score_grads[slot, :, to] = cell(
-                key, value, query_rows[at, :], grad_rows[at, :], lse, delta, key_position <= position
+            t = j * X + k
+            at, to = tile_rows(t), tile_rows(k)
+            position = row_position(k)
+            weights[slot, :, to], score_grads[j, c * BLOCK : (c + 1) * BLOCK, to] = cell(
+                key,
+                value,
+                query_rows[at, :],
+                grad_rows[at, :],
+                lse_ref[t : t + 1, :],
+                delta_ref[t : t + 1, :],
+                key_position <= position,
             )
 
     def second(j, c, slot):
         rows = slice(j * X * TILE, (j + 1) * X * TILE)
         value_grad = dot(weights[slot], grad_rows[rows, :], ((1,), (0,)))
-        key_grad = dot(score_grads[slot], query_rows[rows, :], ((1,), (0,))) * SCALE
+        key_grad = dot(score_grads[j, c * BLOCK : (c + 1) * BLOCK, :], query_rows[rows, :], ((1,), (0,))) * SCALE
         shape = (per, RESP_HALF, LANES)
-        to = slice(c * per, (c + 1) * per)
+        n = j * blocks + c
+        parts[n, :, 0:RESP_HALF, :] = key_grad.astype(bf16).reshape(shape)
+        parts[n, :, RESP_HALF:, :] = value_grad.astype(bf16).reshape(shape)
         start = 2 * PROMPT_HALF + j * SIDE
-        out_ref[to, start : start + RESP_HALF, :] = key_grad.astype(bf16).reshape(shape)
-        out_ref[to, start + RESP_HALF : start + SIDE, :] = value_grad.astype(bf16).reshape(shape)
-        key = rows_of(j, c, 0)
-        for k in range(X):
-            total = dot(score_grads[slot, :, tile_rows(k)], key, ((0,), (0,)))
-            total += acc_ref[j * X + k] if c == 0 else acc[k]
-            if c == last:
-                grads[k][j] = (total * SCALE).astype(bf16)
-            else:
-                acc[k] = total
-
-    staged([(j, c) for j in range(2) for c in range(CTX_N // per)], first, second)
+        to = out_hbm.at[c * per : (c + 1) * per, start : start + SIDE, :]
+        copies.append(pltpu.make_async_copy(parts.at[n], to, sems.at[1 + n]))
+        copies[-1].start()
+
+    staged([(j, c) for j in range(2) for c in range(blocks)], first, second)
+    for copy in copies:
+        copy.wait()
+
+
+def query_kernel(kv_ref, side_ref, prompt_grads, resp_grads, d0, d1, d2, d3):
+    def keys(ref, start, count):
+        return ref[:, start : start + count, :].reshape(CTX_N * count, LANES)
+
+    prompt = keys(kv_ref, 0, PROMPT_HALF)
+    resp = (keys(kv_ref, 2 * PROMPT_HALF, RESP_HALF), keys(side_ref, 0, RESP_HALF))
+    for k, ref in enumerate((d0, d1, d2, d3)):
+        for j in range(2):
+            total = dot(prompt_grads[:, tile_rows(j * X + k)], prompt, ((0,), (0,)))
+            total += dot(resp_grads[j, :, tile_rows(k)], resp[j], ((0,), (0,)))
+            ref[j] = (total * SCALE).astype(bf16)
 
 
 def kv_final_kernel(lengths_ref, gate_ref, part_ref, pk_ref, pv_ref, rk_ref, rv_ref):
@@ -326,39 +334,54 @@
 
 def prompt_call(lengths, rows, kv):
     shape = jax.ShapeDtypeStruct
+    count = 2 * X * TILE
     return call(
         prompt_kernel,
-        (shape((2 * X, TILE, LANES), f32), shape((CTX_N, 2 * PROMPT_HALF, LANES), bf16)),
+        (
+            shape((CTX_N, 2 * PROMPT_HALF, LANES), bf16),
+            shape((CTX_N * PROMPT_HALF, count), bf16),
+            shape((count, LANES), bf16),
+            shape((count, LANES), bf16),
+            shape((2 * X, TILE), f32),
+            shape((2 * X, TILE), f32),
+        ),
         "svvvvv",
-        scratch=(
-            pltpu.VMEM((2 * X * TILE, LANES), bf16),
-            pltpu.VMEM((2 * X * TILE, LANES), bf16),
-            pltpu.VMEM((2, BLOCK, 2 * X * TILE), bf16),
-            pltpu.VMEM((2, BLOCK, 2 * X * TILE), bf16),
-        ),
-        flops=5 * 2 * 2048 * 1024 * 128 * 2,
+        scratch=(pltpu.VMEM((2, BLOCK, count), bf16),),
+        flops=4 * 2 * 2048 * 1024 * 128 * 2,
         size=3 * 2**20,
     )(lengths, *rows, kv)
 
 
-def resp_call(lengths, rows, kv, side, acc, prompt_part):
+def resp_call(kv, side, prompt_part, *rows):
     shape = jax.ShapeDtypeStruct
+    blocks = 2 * CTX_N * RESP_HALF // BLOCK
     return call(
         resp_kernel,
-        (shape((CTX_N, KV_ROWS, LANES), bf16),)
-        + (shape((2, TILE, LANES), bf16),) * X
-        + (shape((8, LANES), f32),),
-        "svvvvvvvv",
+        (
+            shape((CTX_N, KV_ROWS, LANES), bf16),
+            shape((2, CTX_N * RESP_HALF, X * TILE), bf16),
+            shape((8, LANES), f32),
+        ),
+        "vvvvvvv",
+        out_spaces="avv",
         scratch=(
-            pltpu.VMEM((2 * X * TILE, LANES), bf16),
-            pltpu.VMEM((2 * X * TILE, LANES), bf16),
             pltpu.VMEM((2, BLOCK, X * TILE), bf16),
-            pltpu.VMEM((2, BLOCK, X * TILE), bf16),
-            pltpu.VMEM((X, TILE, LANES), f32),
-        ),
-        flops=5 * 2 * 1024 * 1024 * 128 * 2,
+            pltpu.VMEM((blocks, BLOCK // RESP_HALF, SIDE, LANES), bf16),
+            pltpu.SemaphoreType.DMA((blocks + 1,)),
+        ),
+        flops=4 * 2 * 1024 * 1024 * 128 * 2,
         size=3 * 2**20,
-    )(lengths, *rows, kv, side, acc, prompt_part)
+    )(kv, side, prompt_part, *rows)
+
+
+def query_call(kv, side, prompt_grads, resp_grads):
+    return call(
+        query_kernel,
+        (jax.ShapeDtypeStruct((2, TILE, LANES), bf16),) * X,
+        "vvvv",
+        flops=2 * 2048 * 1536 * 128 * 2,
+        size=8 * 2**20,
+    )(kv, side, prompt_grads, resp_grads)
 
 
 def per_device(
@@ -410,8 +433,9 @@
     rows = (same, shift(odd, 1), shift(same, 2), shift(odd, 3))
 
     side = cross(kv[:, KV_ROWS - SIDE : KV_ROWS, :])
-    acc, prompt_part = prompt_call(lengths, rows, kv)
-    part, *grads, gate = resp_call(lengths, rows, kv, side, acc, prompt_part)
+    prompt_part, prompt_grads, *rows = prompt_call(lengths, rows, kv)
+    part, resp_grads, gate = resp_call(kv, side, prompt_part, *rows)
+    grads = query_call(kv, side, prompt_grads, resp_grads)
     part = swap(part)
     back = [grads[0]] + [shift(grads[k], X - k) for k in range(1, X)]
     query_grad = call(query_final_kernel, shape((1, 2, POS, 2 * GROUP * LANES), bf16), "vvvvv", size=2**20)(

time: 92.6 us -> 92.4 us (level)
  local copies, waits for them, and re-layouts: 0.56 us -> 7.61 us
  waiting for transfers between devices: 34.2 us -> 27.8 us
    all_to_all x2, waiting for transfers between devices: 26.3 us -> 17.8 us  [swap(): return lax.all_to_all(values, CTX, split_axis=0, concat_axis=0, tiled=True)]
    unnamed x10 -> x18, local copies, waits for them, and re-layouts: 0.03 us -> 7.08 us
    ppermute x6, waiting for transfers between devices: 6.34 us -> 8.5 us  [shift(): return lax.ppermute(values, 'x', [(i, (i + by) % X) for i in range(X)])]
    all_to_all x2, starting transfers between devices: 17.7 us -> 16.1 us  [swap(): return lax.all_to_all(values, CTX, split_axis=0, concat_axis=0, tiled=True)]
    ppermute x6, starting transfers between devices: 19 us -> 20.2 us  [shift(): return lax.ppermute(values, 'x', [(i, (i + by) % X) for i in range(X)])]
    pallas_call x2 -> x3, Pallas kernels: 11 us -> 10.4 us  [the longest x1 5.17 us: prompt_call(): call(prompt_kernel, (shape((CTX_N, 2 * PROMPT_HALF, LANES), bf16), shape(...]
  transfers between devices with their start and end apart: 10 -> 10, of which waited for: 5 -> 5; matrix products, arithmetic and copies ran while one was open for 1% -> 1% of each run, Pallas kernels for 8% -> 10%
where the time goes in v4:
time: 92.4 us; the launch traced here: 91.7 us
  starting transfers between devices  40.1 us (43%)
  waiting for transfers between devices  27.8 us (30%)
  Pallas kernels  15.3 us (17%)
  local copies, waits for them, and re-layouts  7.61 us (8%)
    ppermute x6, starting transfers between devices, shift(): return lax.ppermute(values, 'x', [(i, (i + by) % X) for i in range(X)])  20.2 us
    all_to_all x2, waiting for transfers between devices, swap(): return lax.all_to_all(values, CTX, split_axis=0, concat_axis=0, tiled=True)  17.8 us
    all_to_all x2, starting transfers between devices, swap(): return lax.all_to_all(values, CTX, split_axis=0, concat_axis=0, tiled=True)  16.1 us
    ppermute x6, waiting for transfers between devices, shift(): return lax.ppermute(values, 'x', [(i, (i + by) % X) for i in range(X)])  8.5 us
    unnamed x18, local copies, waits for them, and re-layouts  7.08 us
    pallas_call x1, Pallas kernels, prompt_call(): call(prompt_kernel, (shape((CTX_N, 2 * PROMPT_HALF, LANES), bf16), shape(...  5.17 us
    ppermute x2, starting transfers between devices, cross(): return lax.ppermute(values, 'pair', [(0, 1), (1, 0)])  3.84 us
    pallas_call x1, Pallas kernels, resp_call(): call(resp_kernel, (shape((CTX_N, KV_ROWS, LANES), bf16), shape((2, CTX_N...  3.14 us
  transfers between devices with their start and end apart: 10, of which 5 were waited for; matrix products, arithmetic and copies ran while one was open for 1% of the time, Pallas kernels for 10%

profile of v4, /device:TPU:6, one launch (start us, length us, event | category | flops | bytes accessed | tf_op | source)
XLA Modules:
  0.0 91.7 jit_solution(3903804741719028416)
XLA Ops:
  0.6 0.0 copy-start.7
  0.6 0.0 copy-start.6
  0.7 0.0 copy-start.5
  0.7 0.0 copy-start.4
  0.7 2.1 %shard_map.145 = bf16[32,136,128]{2,1,0:T(8,128)(2,1)} custom-call(s32[1,3]{1,0:T(1,128)} %lengths_ref.3, f32[1,2,32]{2,1,0:T(2,128)} %logratio_hbm.1, bf16[1,64,256]{2,1,0:T(8,128)(2,1)} %pk_hbm.1, bf16[1,64,256]{2,1,0:T(8,128)(2,1)} %pv_hbm.1, bf16[1,1,32,512]{3,2,1,0:T(8,128)(2,1)} %rk_hbm.1, bf16[1,1,32,512]{3,2,1,0:T(8,128)(2,1)} %rv_hbm.1), custom_call_target="tpu_custom_call" | custom-call | bytes 2097152 | tf_op jit(solution)/shard_map/pallas_call | solution.py:400
  2.7 0.0 copy-start.8
  2.8 10.2 %all-to-all-start = ((bf16[32,136,128]{2,1,0:T(8,128)(2,1)}), bf16[32,136,128]{2,1,0:T(8,128)(2,1)S(1)}, u32[]{:S(2)}, u32[]{:S(2)}) async-start(bf16[32,136,128]{2,1,0:T(8,128)(2,1)} %shard_map.145), calls=%async_computation | async-start | bytes 2228224 | tf_op jit(solution)/shard_map/all_to_all | solution.py:324
  13.0 0.0 copy-done.7
  13.0 0.0 copy-done.6
  13.0 0.0 copy-done.5
  13.0 0.0 copy-done.4
  13.0 0.6 shard_map.146
  13.6 1.9 %collective-permute-start.1 = (bf16[2,528,128]{2,1,0:T(8,128)(2,1)S(1)}, bf16[2,528,128]{2,1,0:T(8,128)(2,1)S(1)}, u32[]{:S(2)}, u32[]{:S(2)}) collective-permute-start(bf16[2,528,128]{2,1,0:T(8,128)(2,1)S(1)} %get-tuple-element.28), channel_id=1, source_target_pairs={{0,32},{32,0},{1,33},{33,1},{2,34},{34,2},{3,35},{35,3},{4,36},{36... | collective-permute-start | bytes 811016 | tf_op jit(solution)/shard_map/ppermute | solution.py:328
  15.5 1.5 %collective-permute-done.1.other_ref = bf16[2,528,128]{2,1,0:T(8,128)(2,1)S(1)} collective-permute-done((bf16[2,528,128]{2,1,0:T(8,128)(2,1)S(1)}, bf16[2,528,128]{2,1,0:T(8,128)(2,1)S(1)}, u32[]{:S(2)}, u32[]{:S(2)}) %collective-permute-start.1) | collective-permute-done | bytes 270368 | tf_op jit(solution)/shard_map/ppermute | solution.py:328
  17.1 3.4 %collective-permute-start.3 = (bf16[2,528,128]{2,1,0:T(8,128)(2,1)S(1)}, bf16[2,528,128]{2,1,0:T(8,128)(2,1)S(1)}, u32[]{:S(2)}, u32[]{:S(2)}) collective-permute-start(bf16[2,528,128]{2,1,0:T(8,128)(2,1)S(1)} %get-tuple-element.29.q0), channel_id=1, source_target_pairs={{0,2},{1,3},{2,0},{3,1},{4,6},{5,7},{6,4},{7,5},{8,10},{9,11},{10,... | collective-permute-start | bytes 811016 | tf_op jit(solution)/shard_map/ppermute | solution.py:332
  20.4 1.9 %collective-permute-start.4 = (bf16[2,528,128]{2,1,0:T(8,128)(2,1)S(1)}, bf16[2,528,128]{2,1,0:T(8,128)(2,1)S(1)}, u32[]{:S(2)}, u32[]{:S(2)}) collective-permute-start(bf16[2,528,128]{2,1,0:T(8,128)(2,1)S(1)} %get-tuple-element.30), channel_id=1, source_target_pairs={{0,3},{1,0},{2,1},{3,2},{4,7},{5,4},{6,5},{7,6},{8,11},{9,8},{10,9... | collective-permute-start | bytes 811016 | tf_op jit(solution)/shard_map/ppermute | solution.py:332
  22.4 5.1 %collective-permute-start.2 = (bf16[2,528,128]{2,1,0:T(8,128)(2,1)S(1)}, bf16[2,528,128]{2,1,0:T(8,128)(2,1)S(1)}, u32[]{:S(2)}, u32[]{:S(2)}) collective-permute-start(bf16[2,528,128]{2,1,0:T(8,128)(2,1)S(1)} %get-tuple-element.30), channel_id=1, source_target_pairs={{0,1},{1,2},{2,3},{3,0},{4,5},{5,6},{6,7},{7,4},{8,9},{9,10},{10,1... | collective-permute-start | bytes 811016 | tf_op jit(solution)/shard_map/ppermute | solution.py:332
  27.5 14.9 %all-to-all-done.kv_ref = bf16[32,136,128]{2,1,0:T(8,128)(2,1)S(1)} async-done(((bf16[32,136,128]{2,1,0:T(8,128)(2,1)}), bf16[32,136,128]{2,1,0:T(8,128)(2,1)S(1)}, u32[]{:S(2)}, u32[]{:S(2)}) %all-to-all-start) | async-done | bytes 1114144 | tf_op jit(solution)/shard_map/all_to_all | solution.py:324
  42.5 1.9 %collective-permute-start = (bf16[32,32,128]{2,1,0:T(8,128)(2,1)S(1)}, bf16[32,32,128]{2,1,0:T(8,128)(2,1)S(1)}, u32[]{:S(2)}, u32[]{:S(2)}) collective-permute-start(bf16[32,32,128]{2,1,0:T(8,128)(2,1)S(1)} %slice.8), channel_id=1, source_target_pairs={{0,32},{32,0},{1,33},{33,1},{2,34},{34,2},{3,35},{35,3},{4,36},{36... | collective-permute-start | bytes 786440 | tf_op jit(solution)/shard_map/ppermute | solution.py:328
  44.4 0.0 collective-permute-done.3.q2
  44.4 0.0 collective-permute-done.4.q3
  44.4 0.0 collective-permute-done.2.q1
  44.4 0.0 copy-done.8
  44.4 5.2 %shard_map.148 = (bf16[32,64,128]{2,1,0:T(8,128)(2,1)S(1)}, bf16[1024,2048]{1,0:T(8,128)(2,1)S(1)}, bf16[2048,128]{1,0:T(8,128)(2,1)S(1)}, bf16[2048,128]{1,0:T(...) custom-call(s32[1,3]{1,0:T(1,128)S(1)} %copy-done.8, bf16[2,528,128]{2,1,0:T(8,128)(2,1)S(1)} %get-tuple-element.29.q0, ...), custom_call_target="tpu_custom_call" | custom-call | flops 4294967296 | bytes 3145728 | tf_op jit(solution)/shard_map/pallas_call | solution.py:338
  49.6 0.0 copy-start
  49.6 1.9 %copy-done = bf16[1024,2048]{1,0:T(8,128)(2,1)} copy-done((bf16[1024,2048]{1,0:T(8,128)(2,1)}, bf16[1024,2048]{1,0:T(8,128)(2,1)S(1)}, u32[]{:S(2)}) %copy-start) | copy-done | bytes 4194328
  51.5 0.0 collective-permute-done.side_ref
  51.5 3.1 %shard_map.149 = (bf16[32,128,128]{2,1,0:T(8,128)(2,1)}, bf16[2,512,1024]{2,1,0:T(8,128)(2,1)S(1)}, f32[8,128]{1,0:T(8,128)S(1)}) custom-call(bf16[32,136,128]{2,1,0:T(8,128)(2,1)S(1)} %all-to-all-done.kv_ref, bf16[32,32,128]{2,1,0:T(8,128)(2,1)S(1)} %collective-permute-done.side_ref, bf16[32,64,128]{2,1,0:T(8,128)(2,1)S(1)} %get-tuple-element.31.prompt_ref, ...), custom_call_target="tpu_custom_call" | custom-call | flops 2147483648 | bytes 3145728 | tf_op jit(solution)/shard_map/pallas_call | solution.py:358
  54.7 0.0 copy-start.2
  54.7 1.4 %copy-done.2 = bf16[2,512,1024]{2,1,0:T(8,128)(2,1)} copy-done((bf16[2,512,1024]{2,1,0:T(8,128)(2,1)}, bf16[2,512,1024]{2,1,0:T(8,128)(2,1)S(1)}, u32[]{:S(2)}) %copy-start.2) | copy-done | bytes 2097176
  56.1 5.9 %all-to-all-start.1 = ((bf16[32,128,128]{2,1,0:T(8,128)(2,1)}), bf16[32,128,128]{2,1,0:T(8,128)(2,1)S(1)}, u32[]{:S(2)}, u32[]{:S(2)}) async-start(bf16[32,128,128]{2,1,0:T(8,128)(2,1)} %get-tuple-element.37), calls=%async_computation.1 | async-start | bytes 2097152 | tf_op jit(solution)/shard_map/all_to_all | solution.py:324
  61.9 0.0 copy-start.1
  61.9 2.2 %copy-done.1 = bf16[1024,2048]{1,0:T(8,128)(2,1)S(1)} copy-done((bf16[1024,2048]{1,0:T(8,128)(2,1)S(1)}, bf16[1024,2048]{1,0:T(8,128)(2,1)}, u32[]{:S(2)}) %copy-start.1) | copy-done | bytes 4194328
  64.1 0.0 copy-start.3
  64.1 1.6 %copy-done.3 = bf16[2,512,1024]{2,1,0:T(8,128)(2,1)S(1)} copy-done((bf16[2,512,1024]{2,1,0:T(8,128)(2,1)S(1)}, bf16[2,512,1024]{2,1,0:T(8,128)(2,1)}, u32[]{:S(2)}) %copy-start.3) | copy-done | bytes 2097176
  65.7 2.1 %shard_map.151 = (bf16[2,256,128]{2,1,0:T(8,128)(2,1)S(1)}, bf16[2,256,128]{2,1,0:T(8,128)(2,1)S(1)}, bf16[2,256,128]{2,1,0:T(8,128)(2,1)S(1)}, bf16[2,256,128]{2,1,0:T(8,128)(2,1)S(1)}) custom-call(bf16[32,136,128]{2,1,0:T(8,128)(2,1)S(1)} %all-to-all-done.kv_ref, bf16[32,32,128]{2,1,0:T(8,128)(2,1)S(1)} %collective-permute-done.side_ref, ...), custom_call_target="tpu_custom_call" | custom-call | flops 1610612736 | bytes 8388608 | tf_op jit(solution)/shard_map/pallas_call | solution.py:378
  67.8 2.8 %collective-permute-start.5 = (bf16[2,256,128]{2,1,0:T(8,128)(2,1)S(1)}, bf16[2,256,128]{2,1,0:T(8,128)(2,1)S(1)}, u32[]{:S(2)}, u32[]{:S(2)}) collective-permute-start(bf16[2,256,128]{2,1,0:T(8,128)(2,1)S(1)} %get-tuple-element.43), channel_id=1, source_target_pairs={{0,3},{1,0},{2,1},{3,2},{4,7},{5,4},{6,5},{7,6},{8,11},{9,8},{10,9... | collective-permute-start | bytes 393224 | tf_op jit(solution)/shard_map/ppermute | solution.py:332
  70.6 2.7 %collective-permute-start.6 = (bf16[2,256,128]{2,1,0:T(8,128)(2,1)S(1)}, bf16[2,256,128]{2,1,0:T(8,128)(2,1)S(1)}, u32[]{:S(2)}, u32[]{:S(2)}) collective-permute-start(bf16[2,256,128]{2,1,0:T(8,128)(2,1)S(1)} %get-tuple-element.44), channel_id=1, source_target_pairs={{0,2},{1,3},{2,0},{3,1},{4,6},{5,7},{6,4},{7,5},{8,10},{9,11},{10,... | collective-permute-start | bytes 393224 | tf_op jit(solution)/shard_map/ppermute | solution.py:332
  73.4 4.3 %collective-permute-start.7 = (bf16[2,256,128]{2,1,0:T(8,128)(2,1)S(1)}, bf16[2,256,128]{2,1,0:T(8,128)(2,1)S(1)}, u32[]{:S(2)}, u32[]{:S(2)}) collective-permute-start(bf16[2,256,128]{2,1,0:T(8,128)(2,1)S(1)} %get-tuple-element.45), channel_id=1, source_target_pairs={{0,1},{1,2},{2,3},{3,0},{4,5},{5,6},{6,7},{7,4},{8,9},{9,10},{10,1... | collective-permute-start | bytes 393224 | tf_op jit(solution)/shard_map/ppermute | solution.py:332
  77.7 0.5 slice.7
  78.2 4.6 %collective-permute-done.5.d1 = bf16[2,256,128]{2,1,0:T(8,128)(2,1)S(1)} collective-permute-done((bf16[2,256,128]{2,1,0:T(8,128)(2,1)S(1)}, bf16[2,256,128]{2,1,0:T(8,128)(2,1)S(1)}, u32[]{:S(2)}, u32[]{:S(2)}) %collective-permute-start.5) | collective-permute-done | bytes 131104 | tf_op jit(solution)/shard_map/ppermute | solution.py:332
  82.8 0.0 collective-permute-done.6.d2
  82.8 3.9 %collective-permute-done.7.d3 = bf16[2,256,128]{2,1,0:T(8,128)(2,1)S(1)} collective-permute-done((bf16[2,256,128]{2,1,0:T(8,128)(2,1)S(1)}, bf16[2,256,128]{2,1,0:T(8,128)(2,1)S(1)}, u32[]{:S(2)}, u32[]{:S(2)}) %collective-permute-start.7) | collective-permute-done | bytes 131104 | tf_op jit(solution)/shard_map/ppermute | solution.py:332
  86.7 0.8 shard_map.152
  87.5 2.9 %all-to-all-done.1.part_ref = bf16[32,128,128]{2,1,0:T(8,128)(2,1)S(1)} async-done(((bf16[32,128,128]{2,1,0:T(8,128)(2,1)}), bf16[32,128,128]{2,1,0:T(8,128)(2,1)S(1)}, u32[]{:S(2)}, u32[]{:S(2)}) %all-to-all-start.1) | async-done | bytes 1048608 | tf_op jit(solution)/shard_map/all_to_all | solution.py:324
  90.4 1.3 %shard_map.150 = (bf16[1,64,256]{2,1,0:T(8,128)(2,1)}, bf16[1,64,256]{2,1,0:T(8,128)(2,1)}, bf16[1,2,32,256]{3,2,1,0:T(8,128)(2,1)}, bf16[1,2,32,256]{3,2,1,0:T(8,128)(2,1)}) custom-call(s32[1,3]{1,0:T(1,128)S(1)} %copy-done.8, f32[8,128]{1,0:T(8,128)S(1)} %get-tuple-element.36.gate_ref, bf16[32,128,128]{2,1,0:T(8,128)(2,1)S(1)} %all-to-all-done.1.part_ref), custom_call_target="tpu_custom_call" | custom-call | bytes 1048576 | tf_op jit(solution)/shard_map/pallas_call | solution.py:445
  (2 shorter events, 0.1 us)
Async XLA Ops:
  0.6 12.3 %copy-start.7 = (bf16[1,1,32,32]{3,2,1,0:T(8,128)(2,1)S(1)}, bf16[1,1,32,32]{3,2,1,0:T(8,128)(2,1)}, u32[]{:S(2)}) copy-start(bf16[1,1,32,32]{3,2,1,0:T(8,128)(2,1)} %delta_hbm.1) | copy-start | bytes 6148
  0.6 12.3 %copy-start.6 = (bf16[1,1,32,32]{3,2,1,0:T(8,128)(2,1)S(1)}, bf16[1,1,32,32]{3,2,1,0:T(8,128)(2,1)}, u32[]{:S(2)}) copy-start(bf16[1,1,32,32]{3,2,1,0:T(8,128)(2,1)} %lse_hbm.1) | copy-start | bytes 6148
  0.7 12.3 %copy-start.5 = (bf16[1,1,32,4096]{3,2,1,0:T(8,128)(2,1)S(1)}, bf16[1,1,32,4096]{3,2,1,0:T(8,128)(2,1)}, u32[]{:S(2)}) copy-start(bf16[1,1,32,4096]{3,2,1,0:T(8,128)(2,1)} %g_hbm.1) | copy-start | bytes 786436
  0.7 12.3 %copy-start.4 = (bf16[1,1,32,4096]{3,2,1,0:T(8,128)(2,1)S(1)}, bf16[1,1,32,4096]{3,2,1,0:T(8,128)(2,1)}, u32[]{:S(2)}) copy-start(bf16[1,1,32,4096]{3,2,1,0:T(8,128)(2,1)} %q_hbm.1) | copy-start | bytes 786436
  2.7 41.7 %copy-start.8 = (s32[1,3]{1,0:T(1,128)S(1)}, s32[1,3]{1,0:T(1,128)}, u32[]{:S(2)}) copy-start(s32[1,3]{1,0:T(1,128)} %lengths_ref.3) | copy-start | bytes 40
  2.8 39.7 %all-to-all-start = ((bf16[32,136,128]{2,1,0:T(8,128)(2,1)}), bf16[32,136,128]{2,1,0:T(8,128)(2,1)S(1)}, u32[]{:S(2)}, u32[]{:S(2)}) async-start(bf16[32,136,128]{2,1,0:T(8,128)(2,1)} %shard_map.145), calls=%async_computation | async-start | bytes 2228224 | tf_op jit(solution)/shard_map/all_to_all | solution.py:324
  13.6 3.4 %collective-permute-start.1 = (bf16[2,528,128]{2,1,0:T(8,128)(2,1)S(1)}, bf16[2,528,128]{2,1,0:T(8,128)(2,1)S(1)}, u32[]{:S(2)}, u32[]{:S(2)}) collective-permute-start(bf16[2,528,128]{2,1,0:T(8,128)(2,1)S(1)} %get-tuple-element.28), channel_id=1, source_target_pairs={{0,32},{32,0},{1,33},{33,1},{2,34},{34,2},{3,35},{35,3},{4,36},{36... | collective-permute-start | bytes 811016 | tf_op jit(solution)/shard_map/ppermute | solution.py:328
  17.1 27.3 %collective-permute-start.3 = (bf16[2,528,128]{2,1,0:T(8,128)(2,1)S(1)}, bf16[2,528,128]{2,1,0:T(8,128)(2,1)S(1)}, u32[]{:S(2)}, u32[]{:S(2)}) collective-permute-start(bf16[2,528,128]{2,1,0:T(8,128)(2,1)S(1)} %get-tuple-element.29.q0), channel_id=1, source_target_pairs={{0,2},{1,3},{2,0},{3,1},{4,6},{5,7},{6,4},{7,5},{8,10},{9,11},{10,... | collective-permute-start | bytes 811016 | tf_op jit(solution)/shard_map/ppermute | solution.py:332
  20.4 24.0 %collective-permute-start.4 = (bf16[2,528,128]{2,1,0:T(8,128)(2,1)S(1)}, bf16[2,528,128]{2,1,0:T(8,128)(2,1)S(1)}, u32[]{:S(2)}, u32[]{:S(2)}) collective-permute-start(bf16[2,528,128]{2,1,0:T(8,128)(2,1)S(1)} %get-tuple-element.30), channel_id=1, source_target_pairs={{0,3},{1,0},{2,1},{3,2},{4,7},{5,4},{6,5},{7,6},{8,11},{9,8},{10,9... | collective-permute-start | bytes 811016 | tf_op jit(solution)/shard_map/ppermute | solution.py:332
  22.4 22.0 %collective-permute-start.2 = (bf16[2,528,128]{2,1,0:T(8,128)(2,1)S(1)}, bf16[2,528,128]{2,1,0:T(8,128)(2,1)S(1)}, u32[]{:S(2)}, u32[]{:S(2)}) collective-permute-start(bf16[2,528,128]{2,1,0:T(8,128)(2,1)S(1)} %get-tuple-element.30), channel_id=1, source_target_pairs={{0,1},{1,2},{2,3},{3,0},{4,5},{5,6},{6,7},{7,4},{8,9},{9,10},{10,1... | collective-permute-start | bytes 811016 | tf_op jit(solution)/shard_map/ppermute | solution.py:332
  42.5 9.1 %collective-permute-start = (bf16[32,32,128]{2,1,0:T(8,128)(2,1)S(1)}, bf16[32,32,128]{2,1,0:T(8,128)(2,1)S(1)}, u32[]{:S(2)}, u32[]{:S(2)}) collective-permute-start(bf16[32,32,128]{2,1,0:T(8,128)(2,1)S(1)} %slice.8), channel_id=1, source_target_pairs={{0,32},{32,0},{1,33},{33,1},{2,34},{34,2},{3,35},{35,3},{4,36},{36... | collective-permute-start | bytes 786440 | tf_op jit(solution)/shard_map/ppermute | solution.py:328
  49.6 1.9 %copy-start = (bf16[1024,2048]{1,0:T(8,128)(2,1)}, bf16[1024,2048]{1,0:T(8,128)(2,1)S(1)}, u32[]{:S(2)}) copy-start(bf16[1024,2048]{1,0:T(8,128)(2,1)S(1)} %get-tuple-element.40.prompt_grads) | copy-start | bytes 12582916
  54.7 1.4 %copy-start.2 = (bf16[2,512,1024]{2,1,0:T(8,128)(2,1)}, bf16[2,512,1024]{2,1,0:T(8,128)(2,1)S(1)}, u32[]{:S(2)}) copy-start(bf16[2,512,1024]{2,1,0:T(8,128)(2,1)S(1)} %get-tuple-element.41.resp_grads) | copy-start | bytes 6291460
  56.1 34.3 %all-to-all-start.1 = ((bf16[32,128,128]{2,1,0:T(8,128)(2,1)}), bf16[32,128,128]{2,1,0:T(8,128)(2,1)S(1)}, u32[]{:S(2)}, u32[]{:S(2)}) async-start(bf16[32,128,128]{2,1,0:T(8,128)(2,1)} %get-tuple-element.37), calls=%async_computation.1 | async-start | bytes 2097152 | tf_op jit(solution)/shard_map/all_to_all | solution.py:324
  61.9 2.2 %copy-start.1 = (bf16[1024,2048]{1,0:T(8,128)(2,1)S(1)}, bf16[1024,2048]{1,0:T(8,128)(2,1)}, u32[]{:S(2)}) copy-start(bf16[1024,2048]{1,0:T(8,128)(2,1)} %copy-done) | copy-start | bytes 12582916
  64.1 1.6 %copy-start.3 = (bf16[2,512,1024]{2,1,0:T(8,128)(2,1)S(1)}, bf16[2,512,1024]{2,1,0:T(8,128)(2,1)}, u32[]{:S(2)}) copy-start(bf16[2,512,1024]{2,1,0:T(8,128)(2,1)} %copy-done.2) | copy-start | bytes 6291460
  67.8 14.9 %collective-permute-start.5 = (bf16[2,256,128]{2,1,0:T(8,128)(2,1)S(1)}, bf16[2,256,128]{2,1,0:T(8,128)(2,1)S(1)}, u32[]{:S(2)}, u32[]{:S(2)}) collective-permute-start(bf16[2,256,128]{2,1,0:T(8,128)(2,1)S(1)} %get-tuple-element.43), channel_id=1, source_target_pairs={{0,3},{1,0},{2,1},{3,2},{4,7},{5,4},{6,5},{7,6},{8,11},{9,8},{10,9... | collective-permute-start | bytes 393224 | tf_op jit(solution)/shard_map/ppermute | solution.py:332
  70.6 12.2 %collective-permute-start.6 = (bf16[2,256,128]{2,1,0:T(8,128)(2,1)S(1)}, bf16[2,256,128]{2,1,0:T(8,128)(2,1)S(1)}, u32[]{:S(2)}, u32[]{:S(2)}) collective-permute-start(bf16[2,256,128]{2,1,0:T(8,128)(2,1)S(1)} %get-tuple-element.44), channel_id=1, source_target_pairs={{0,2},{1,3},{2,0},{3,1},{4,6},{5,7},{6,4},{7,5},{8,10},{9,11},{10,... | collective-permute-start | bytes 393224 | tf_op jit(solution)/shard_map/ppermute | solution.py:332
  73.4 13.3 %collective-permute-start.7 = (bf16[2,256,128]{2,1,0:T(8,128)(2,1)S(1)}, bf16[2,256,128]{2,1,0:T(8,128)(2,1)S(1)}, u32[]{:S(2)}, u32[]{:S(2)}) collective-permute-start(bf16[2,256,128]{2,1,0:T(8,128)(2,1)S(1)} %get-tuple-element.45), channel_id=1, source_target_pairs={{0,1},{1,2},{2,3},{3,0},{4,5},{5,6},{6,7},{7,4},{8,9},{9,10},{10,1... | collective-permute-start | bytes 393224 | tf_op jit(solution)/shard_map/ppermute | solution.py:332

commit v5 on v4

--- a/solution.py
+++ b/solution.py
@@ -1,3 +1,5 @@
+import functools
+
 import jax
 import jax.numpy as jnp
 from jax import lax
@@ -150,6 +152,12 @@
     return (lax.axis_index("y") * X + x) * POS + lax.broadcasted_iota(jnp.int32, (1, TILE), 1) % POS
 
 
+def key_positions(block, count):
+    index = lax.broadcasted_iota(jnp.int32, (count, 1), 0)
+    source = block * (count // RESP_HALF) + index // RESP_HALF
+    return source * POS + lax.axis_index("x") // 2 * RESP_HALF + index % RESP_HALF
+
+
 def row_stats(lengths_ref, block, k, j):
     block = block.astype(f32)
     lse = jnp.concatenate([block[0:1], block[1:2]], axis=1) * LOG2E
@@ -182,7 +190,7 @@
 
 
 def prompt_kernel(
-    lengths_ref, q0, q1, q2, q3, kv_ref, out_ref, score_grads, query_rows, grad_rows, lse_ref, delta_ref, weights
+    lengths_ref, q0, q1, q2, q3, kv_ref, out_ref, query_rows, grad_rows, lse_ref, delta_ref, weights, score_grads
 ):
     for k, ref in enumerate((q0, q1, q2, q3)):
         for j in range(2):
@@ -200,13 +208,13 @@
         value = kv_ref[rows, PROMPT_HALF : 2 * PROMPT_HALF, :].reshape(BLOCK, LANES)
         for t in range(2 * X):
             at = tile_rows(t)
-            weights[slot, :, at], score_grads[c * BLOCK : (c + 1) * BLOCK, at] = cell(
+            weights[slot, :, at], score_grads[slot, :, at] = cell(
                 key, value, query_rows[at, :], grad_rows[at, :], lse_ref[t : t + 1, :], delta_ref[t : t + 1, :]
             )
 
     def second(c, slot):
         value_grad = dot(weights[slot], grad_rows[...], ((1,), (0,)))
-        key_grad = dot(score_grads[c * BLOCK : (c + 1) * BLOCK, :], query_rows[...], ((1,), (0,))) * SCALE
+        key_grad = dot(score_grads[slot], query_rows[...], ((1,), (0,))) * SCALE
         shape = (per, PROMPT_HALF, LANES)
         to = slice(c * per, (c + 1) * per)
         out_ref[to, 0:PROMPT_HALF, :] = key_grad.astype(bf16).reshape(shape)
@@ -217,14 +225,13 @@
 
 def resp_kernel(
     kv_ref, side_ref, prompt_ref, query_rows, grad_rows, lse_ref, delta_ref,
-    out_hbm, score_grads, gate_ref, weights, parts, sems,
+    out_hbm, gate_ref, weights, score_grads, parts, sems,
 ):
     copies = [pltpu.make_async_copy(prompt_ref, out_hbm.at[:, 0 : 2 * PROMPT_HALF, :], sems.at[0])]
     copies[0].start()
     margin = jnp.sum(kv_ref[:, KV_ROWS:, :].astype(f32), axis=(0, 1), keepdims=True).reshape(1, LANES)
     margin = jnp.sum(margin, axis=1, keepdims=True)
     gate_ref[...] = jnp.broadcast_to(beta_coef * jax.nn.sigmoid(-beta_coef * margin), gate_ref.shape)
-    half = lax.axis_index("x") // 2
     per = BLOCK // RESP_HALF
     blocks = CTX_N // per
     sources = ((kv_ref, 2 * PROMPT_HALF), (side_ref, 0))
@@ -234,26 +241,24 @@
         rows = slice(c * per, (c + 1) * per)
         key = ref[rows, start : start + RESP_HALF, :].reshape(BLOCK, LANES)
         value = ref[rows, start + RESP_HALF : start + SIDE, :].reshape(BLOCK, LANES)
-        index = lax.broadcasted_iota(jnp.int32, (BLOCK, 1), 0)
-        key_position = (c * per + index // RESP_HALF) * POS + half * RESP_HALF + index % RESP_HALF
+        positions = key_positions(c, BLOCK)
         for k in range(X):
             t = j * X + k
             at, to = tile_rows(t), tile_rows(k)
-            position = row_position(k)
-            weights[slot, :, to], score_grads[j, c * BLOCK : (c + 1) * BLOCK, to] = cell(
+            weights[slot, :, to], score_grads[slot, :, to] = cell(
                 key,
                 value,
                 query_rows[at, :],
                 grad_rows[at, :],
                 lse_ref[t : t + 1, :],
                 delta_ref[t : t + 1, :],
-                key_position <= position,
+                positions <= row_position(k),
             )
 
     def second(j, c, slot):
         rows = slice(j * X * TILE, (j + 1) * X * TILE)
         value_grad = dot(weights[slot], grad_rows[rows, :], ((1,), (0,)))
-        key_grad = dot(score_grads[j, c * BLOCK : (c + 1) * BLOCK, :], query_rows[rows, :], ((1,), (0,))) * SCALE
+        key_grad = dot(score_grads[slot], query_rows[rows, :], ((1,), (0,))) * SCALE
         shape = (per, RESP_HALF, LANES)
         n = j * blocks + c
         parts[n, :, 0:RESP_HALF, :] = key_grad.astype(bf16).reshape(shape)
@@ -268,17 +273,25 @@
         copy.wait()
 
 
-def query_kernel(kv_ref, side_ref, prompt_grads, resp_grads, d0, d1, d2, d3):
-    def keys(ref, start, count):
-        return ref[:, start : start + count, :].reshape(CTX_N * count, LANES)
-
-    prompt = keys(kv_ref, 0, PROMPT_HALF)
-    resp = (keys(kv_ref, 2 * PROMPT_HALF, RESP_HALF), keys(side_ref, 0, RESP_HALF))
-    for k, ref in enumerate((d0, d1, d2, d3)):
-        for j in range(2):
-            total = dot(prompt_grads[:, tile_rows(j * X + k)], prompt, ((0,), (0,)))
-            total += dot(resp_grads[j, :, tile_rows(k)], resp[j], ((0,), (0,)))
-            ref[j] = (total * SCALE).astype(bf16)
+def query_kernel(k, kv_ref, side_ref, query_rows, grad_rows, lse_ref, delta_ref, out_ref):
+    for j in range(2):
+        t = j * X + k
+        query, grad = query_rows[tile_rows(t), :], grad_rows[tile_rows(t), :]
+        lse, delta = lse_ref[t : t + 1, :], delta_ref[t : t + 1, :]
+        total = None
+        resp, start = ((kv_ref, 2 * PROMPT_HALF), (side_ref, 0))[j]
+        parts = [(kv_ref, c, PROMPT_HALF, 0, None) for c in range(CTX_N * PROMPT_HALF // BLOCK)]
+        for c in range(CTX_N * RESP_HALF // BLOCK):
+            parts.append((resp, c, RESP_HALF, start, key_positions(c, BLOCK) <= row_position(k)))
+        for ref, c, count, start, allowed in parts:
+            per = BLOCK // count
+            rows = slice(c * per, (c + 1) * per)
+            key = ref[rows, start : start + count, :].reshape(BLOCK, LANES)
+            value = ref[rows, start + count : start + 2 * count, :].reshape(BLOCK, LANES)
+            _, score_grads = cell(key, value, query, grad, lse, delta, allowed)
+            term = dot(score_grads, key, ((0,), (0,)))
+            total = term if total is None else total + term
+        out_ref[j] = (total * SCALE).astype(bf16)
 
 
 def kv_final_kernel(lengths_ref, gate_ref, part_ref, pk_ref, pv_ref, rk_ref, rv_ref):
@@ -339,14 +352,13 @@
         prompt_kernel,
         (
             shape((CTX_N, 2 * PROMPT_HALF, LANES), bf16),
-            shape((CTX_N * PROMPT_HALF, count), bf16),
             shape((count, LANES), bf16),
             shape((count, LANES), bf16),
             shape((2 * X, TILE), f32),
             shape((2 * X, TILE), f32),
         ),
         "svvvvv",
-        scratch=(pltpu.VMEM((2, BLOCK, count), bf16),),
+        scratch=(pltpu.VMEM((2, BLOCK, count), bf16), pltpu.VMEM((2, BLOCK, count), bf16)),
         flops=4 * 2 * 2048 * 1024 * 128 * 2,
         size=3 * 2**20,
     )(lengths, *rows, kv)
@@ -359,12 +371,12 @@
         resp_kernel,
         (
             shape((CTX_N, KV_ROWS, LANES), bf16),
-            shape((2, CTX_N * RESP_HALF, X * TILE), bf16),
             shape((8, LANES), f32),
         ),
         "vvvvvvv",
-        out_spaces="avv",
+        out_spaces="av",
         scratch=(
+            pltpu.VMEM((2, BLOCK, X * TILE), bf16),
             pltpu.VMEM((2, BLOCK, X * TILE), bf16),
             pltpu.VMEM((blocks, BLOCK // RESP_HALF, SIDE, LANES), bf16),
             pltpu.SemaphoreType.DMA((blocks + 1,)),
@@ -374,14 +386,14 @@
     )(kv, side, prompt_part, *rows)
 
 
-def query_call(kv, side, prompt_grads, resp_grads):
+def query_call(k, kv, side, *rows):
     return call(
-        query_kernel,
-        (jax.ShapeDtypeStruct((2, TILE, LANES), bf16),) * X,
-        "vvvv",
-        flops=2 * 2048 * 1536 * 128 * 2,
-        size=8 * 2**20,
-    )(kv, side, prompt_grads, resp_grads)
+        functools.partial(query_kernel, k),
+        jax.ShapeDtypeStruct((2, TILE, LANES), bf16),
+        "vvvvvv",
+        flops=3 * 2 * 512 * 1536 * 128 * 2,
+        size=3 * 2**20,
+    )(kv, side, *rows)
 
 
 def per_device(
@@ -433,9 +445,9 @@
     rows = (same, shift(odd, 1), shift(same, 2), shift(odd, 3))
 
     side = cross(kv[:, KV_ROWS - SIDE : KV_ROWS, :])
-    prompt_part, prompt_grads, *rows = prompt_call(lengths, rows, kv)
-    part, resp_grads, gate = resp_call(kv, side, prompt_part, *rows)
-    grads = query_call(kv, side, prompt_grads, resp_grads)
+    prompt_part, *rows = prompt_call(lengths, rows, kv)
+    part, gate = resp_call(kv, side, prompt_part, *rows)
+    grads = [query_call(k, kv, side, *rows) for k in range(X)]
     part = swap(part)
     back = [grads[0]] + [shift(grads[k], X - k) for k in range(1, X)]
     query_grad = call(query_final_kernel, shape((1, 2, POS, 2 * GROUP * LANES), bf16), "vvvvv", size=2**20)(

time: 92.4 us -> 89.3 us (0.966)
  local copies, waits for them, and re-layouts: 7.61 us -> 0.57 us
  Pallas kernels: 15.3 us -> 21.4 us
  waiting for transfers between devices: 27.8 us -> 25.1 us
    unnamed x18 -> x14, local copies, waits for them, and re-layouts: 7.08 us -> 0.04 us
    pallas_call x2 -> x5, Pallas kernels: 5.27 us -> 11.5 us  [the longest x4 8.38 us: query_call(): call(functools.partial(query_kernel, k), jax.ShapeDtypeStruct((2, TILE, L...]
    ppermute x6, waiting for transfers between devices: 8.5 us -> 4.51 us  [shift(): return lax.ppermute(values, 'x', [(i, (i + by) % X) for i in range(X)])]
    all_to_all x2, waiting for transfers between devices: 17.8 us -> 19.1 us  [swap(): return lax.all_to_all(values, CTX, split_axis=0, concat_axis=0, tiled=True)]
  transfers between devices with their start and end apart: 10 -> 10, of which waited for: 5 -> 4; matrix products, arithmetic and copies ran while one was open for 1% -> 1% of each run, Pallas kernels for 10% -> 17%
where the time goes in v5:
time: 89.3 us; the launch traced here: 88.6 us
  starting transfers between devices  40.6 us (45%)
  waiting for transfers between devices  25.1 us (28%)
  Pallas kernels  21.4 us (24%)
  between operations  0.93 us (1%)
    ppermute x6, starting transfers between devices, shift(): return lax.ppermute(values, 'x', [(i, (i + by) % X) for i in range(X)])  20.4 us
    all_to_all x2, waiting for transfers between devices, swap(): return lax.all_to_all(values, CTX, split_axis=0, concat_axis=0, tiled=True)  19.1 us
    all_to_all x2, starting transfers between devices, swap(): return lax.all_to_all(values, CTX, split_axis=0, concat_axis=0, tiled=True)  16.3 us
    pallas_call x4, Pallas kernels, query_call(): call(functools.partial(query_kernel, k), jax.ShapeDtypeStruct((2, TILE, L...  8.38 us
    pallas_call x1, Pallas kernels, prompt_call(): call(prompt_kernel, (shape((CTX_N, 2 * PROMPT_HALF, LANES), bf16), shape(...  5.14 us
    ppermute x6, waiting for transfers between devices, shift(): return lax.ppermute(values, 'x', [(i, (i + by) % X) for i in range(X)])  4.51 us
    ppermute x2, starting transfers between devices, cross(): return lax.ppermute(values, 'pair', [(0, 1), (1, 0)])  3.84 us
    pallas_call x1, Pallas kernels, resp_call(): call(resp_kernel, (shape((CTX_N, KV_ROWS, LANES), bf16), shape((8, LANES)...  3.13 us
  transfers between devices with their start and end apart: 10, of which 4 were waited for; matrix products, arithmetic and copies ran while one was open for 1% of the time, Pallas kernels for 17%

profile of v5, /device:TPU:6, one launch (start us, length us, event | category | flops | bytes accessed | tf_op | source)
XLA Modules:
  0.0 88.6 jit_solution(752499596149748214)
XLA Ops:
  0.6 2.0 %shard_map.145 = bf16[32,136,128]{2,1,0:T(8,128)(2,1)} custom-call(s32[1,3]{1,0:T(1,128)} %lengths_ref.3, f32[1,2,32]{2,1,0:T(2,128)} %logratio_hbm.1, bf16[1,64,256]{2,1,0:T(8,128)(2,1)} %pk_hbm.1, bf16[1,64,256]{2,1,0:T(8,128)(2,1)} %pv_hbm.1, bf16[1,1,32,512]{3,2,1,0:T(8,128)(2,1)} %rk_hbm.1, bf16[1,1,32,512]{3,2,1,0:T(8,128)(2,1)} %rv_hbm.1), custom_call_target="tpu_custom_call" | custom-call | bytes 2097152 | tf_op jit(solution)/shard_map/pallas_call | solution.py:412
  2.7 0.0 copy-start
  2.7 0.0 copy-start.1
  2.7 0.0 copy-start.2
  2.7 0.0 copy-start.3
  2.7 10.3 %all-to-all-start = ((bf16[32,136,128]{2,1,0:T(8,128)(2,1)}), bf16[32,136,128]{2,1,0:T(8,128)(2,1)S(1)}, u32[]{:S(2)}, u32[]{:S(2)}) async-start(bf16[32,136,128]{2,1,0:T(8,128)(2,1)} %shard_map.145), calls=%async_computation | async-start | bytes 2228224 | tf_op jit(solution)/shard_map/all_to_all | solution.py:337
  13.1 0.0 copy-done
  13.1 0.0 copy-done.1
  13.1 0.0 copy-done.2
  13.1 0.0 copy-done.3
  13.1 0.0 copy-start.4
  13.1 0.6 shard_map.146
  13.7 1.9 %collective-permute-start.1 = (bf16[2,528,128]{2,1,0:T(8,128)(2,1)S(1)}, bf16[2,528,128]{2,1,0:T(8,128)(2,1)S(1)}, u32[]{:S(2)}, u32[]{:S(2)}) collective-permute-start(bf16[2,528,128]{2,1,0:T(8,128)(2,1)S(1)} %get-tuple-element.22), channel_id=1, source_target_pairs={{0,32},{32,0},{1,33},{33,1},{2,34},{34,2},{3,35},{35,3},{4,36},{36... | collective-permute-start | bytes 811016 | tf_op jit(solution)/shard_map/ppermute | solution.py:341
  15.6 1.5 %collective-permute-done.1.other_ref = bf16[2,528,128]{2,1,0:T(8,128)(2,1)S(1)} collective-permute-done((bf16[2,528,128]{2,1,0:T(8,128)(2,1)S(1)}, bf16[2,528,128]{2,1,0:T(8,128)(2,1)S(1)}, u32[]{:S(2)}, u32[]{:S(2)}) %collective-permute-start.1) | collective-permute-done | bytes 270368 | tf_op jit(solution)/shard_map/ppermute | solution.py:341
  17.2 3.4 %collective-permute-start.3 = (bf16[2,528,128]{2,1,0:T(8,128)(2,1)S(1)}, bf16[2,528,128]{2,1,0:T(8,128)(2,1)S(1)}, u32[]{:S(2)}, u32[]{:S(2)}) collective-permute-start(bf16[2,528,128]{2,1,0:T(8,128)(2,1)S(1)} %get-tuple-element.23.q0), channel_id=1, source_target_pairs={{0,2},{1,3},{2,0},{3,1},{4,6},{5,7},{6,4},{7,5},{8,10},{9,11},{10,... | collective-permute-start | bytes 811016 | tf_op jit(solution)/shard_map/ppermute | solution.py:345
  20.5 1.9 %collective-permute-start.4 = (bf16[2,528,128]{2,1,0:T(8,128)(2,1)S(1)}, bf16[2,528,128]{2,1,0:T(8,128)(2,1)S(1)}, u32[]{:S(2)}, u32[]{:S(2)}) collective-permute-start(bf16[2,528,128]{2,1,0:T(8,128)(2,1)S(1)} %get-tuple-element.24), channel_id=1, source_target_pairs={{0,3},{1,0},{2,1},{3,2},{4,7},{5,4},{6,5},{7,6},{8,11},{9,8},{10,9... | collective-permute-start | bytes 811016 | tf_op jit(solution)/shard_map/ppermute | solution.py:345
  22.5 5.1 %collective-permute-start.2 = (bf16[2,528,128]{2,1,0:T(8,128)(2,1)S(1)}, bf16[2,528,128]{2,1,0:T(8,128)(2,1)S(1)}, u32[]{:S(2)}, u32[]{:S(2)}) collective-permute-start(bf16[2,528,128]{2,1,0:T(8,128)(2,1)S(1)} %get-tuple-element.24), channel_id=1, source_target_pairs={{0,1},{1,2},{2,3},{3,0},{4,5},{5,6},{6,7},{7,4},{8,9},{9,10},{10,1... | collective-permute-start | bytes 811016 | tf_op jit(solution)/shard_map/ppermute | solution.py:345
  27.6 14.9 %all-to-all-done.kv_ref = bf16[32,136,128]{2,1,0:T(8,128)(2,1)S(1)} async-done(((bf16[32,136,128]{2,1,0:T(8,128)(2,1)}), bf16[32,136,128]{2,1,0:T(8,128)(2,1)S(1)}, u32[]{:S(2)}, u32[]{:S(2)}) %all-to-all-start) | async-done | bytes 1114144 | tf_op jit(solution)/shard_map/all_to_all | solution.py:337
  42.5 1.9 %collective-permute-start = (bf16[32,32,128]{2,1,0:T(8,128)(2,1)S(1)}, bf16[32,32,128]{2,1,0:T(8,128)(2,1)S(1)}, u32[]{:S(2)}, u32[]{:S(2)}) collective-permute-start(bf16[32,32,128]{2,1,0:T(8,128)(2,1)S(1)} %slice.8), channel_id=1, source_target_pairs={{0,32},{32,0},{1,33},{33,1},{2,34},{34,2},{3,35},{35,3},{4,36},{36... | collective-permute-start | bytes 786440 | tf_op jit(solution)/shard_map/ppermute | solution.py:341
  44.5 0.0 collective-permute-done.3.q2
  44.5 0.0 collective-permute-done.4.q3
  44.5 0.0 collective-permute-done.2.q1
  44.5 0.0 copy-done.4
  44.5 5.1 %shard_map.148 = (bf16[32,64,128]{2,1,0:T(8,128)(2,1)S(1)}, bf16[2048,128]{1,0:T(8,128)(2,1)S(1)}, bf16[2048,128]{1,0:T(8,128)(2,1)S(1)}, f32[8,256]{1,0:T(8,128)S(1)}, f32[8,256]{1,0:T(8,128)S(1)}) custom-call(s32[1,3]{1,0:T(1,128)S(1)} %copy-done.4, bf16[2,528,128]{2,1,0:T(8,128)(2,1)S(1)} %get-tuple-element.23.q0, ...), custom_call_target="tpu_custom_call" | custom-call | flops 4294967296 | bytes 3145728 | tf_op jit(solution)/shard_map/pallas_call | solution.py:351
  49.7 0.0 copy-start.5
  49.7 0.0 collective-permute-done.side_ref
  49.7 3.1 %shard_map.149 = (bf16[32,128,128]{2,1,0:T(8,128)(2,1)}, f32[8,128]{1,0:T(8,128)S(1)}) custom-call(bf16[32,136,128]{2,1,0:T(8,128)(2,1)S(1)} %all-to-all-done.kv_ref, bf16[32,32,128]{2,1,0:T(8,128)(2,1)S(1)} %collective-permute-done.side_ref, bf16[32,64,128]{2,1,0:T(8,128)(2,1)S(1)} %get-tuple-element.25.prompt_ref, ...), custom_call_target="tpu_custom_call" | custom-call | flops 2147483648 | bytes 3145728 | tf_op jit(solution)/shard_map/pallas_call | solution.py:370
  52.8 0.0 copy-done.5
  52.8 0.0 copy-start.6
  52.8 6.0 %all-to-all-start.1 = ((bf16[32,128,128]{2,1,0:T(8,128)(2,1)}), bf16[32,128,128]{2,1,0:T(8,128)(2,1)S(1)}, u32[]{:S(2)}, u32[]{:S(2)}) async-start(bf16[32,128,128]{2,1,0:T(8,128)(2,1)} %get-tuple-element.31), calls=%async_computation.1 | async-start | bytes 2097152 | tf_op jit(solution)/shard_map/all_to_all | solution.py:337
  58.9 0.0 copy-done.6
  58.9 2.1 %shard_map.152 = bf16[2,256,128]{2,1,0:T(8,128)(2,1)S(1)} custom-call(bf16[32,136,128]{2,1,0:T(8,128)(2,1)S(1)} %all-to-all-done.kv_ref, bf16[32,32,128]{2,1,0:T(8,128)(2,1)S(1)} %collective-permute-done.side_ref, bf16[2048,128]{1,0:T(8,128)(2,1)S(1)} %get-tuple-element.26.query_rows, bf16[2048,128]{1,0:T(8,128)(2,1)S(1)} %copy-done.6, ...), custom_call_target="tpu_custom_call" | custom-call | flops 1207959552 | bytes 3145728 | tf_op jit(solution)/shard_map/pallas_call | solution.py:390
  61.0 2.9 %collective-permute-start.5 = (bf16[2,256,128]{2,1,0:T(8,128)(2,1)S(1)}, bf16[2,256,128]{2,1,0:T(8,128)(2,1)S(1)}, u32[]{:S(2)}, u32[]{:S(2)}) collective-permute-start(bf16[2,256,128]{2,1,0:T(8,128)(2,1)S(1)} %shard_map.152), channel_id=1, source_target_pairs={{0,3},{1,0},{2,1},{3,2},{4,7},{5,4},{6,5},{7,6},{8,11},{9,8},{10,9... | collective-permute-start | bytes 393224 | tf_op jit(solution)/shard_map/ppermute | solution.py:345
  63.9 2.1 %shard_map.153 = bf16[2,256,128]{2,1,0:T(8,128)(2,1)S(1)} custom-call(bf16[32,136,128]{2,1,0:T(8,128)(2,1)S(1)} %all-to-all-done.kv_ref, bf16[32,32,128]{2,1,0:T(8,128)(2,1)S(1)} %collective-permute-done.side_ref, bf16[2048,128]{1,0:T(8,128)(2,1)S(1)} %get-tuple-element.26.query_rows, bf16[2048,128]{1,0:T(8,128)(2,1)S(1)} %copy-done.6, ...), custom_call_target="tpu_custom_call" | custom-call | flops 1207959552 | bytes 3145728 | tf_op jit(solution)/shard_map/pallas_call | solution.py:390
  66.0 2.7 %collective-permute-start.6 = (bf16[2,256,128]{2,1,0:T(8,128)(2,1)S(1)}, bf16[2,256,128]{2,1,0:T(8,128)(2,1)S(1)}, u32[]{:S(2)}, u32[]{:S(2)}) collective-permute-start(bf16[2,256,128]{2,1,0:T(8,128)(2,1)S(1)} %shard_map.153), channel_id=1, source_target_pairs={{0,2},{1,3},{2,0},{3,1},{4,6},{5,7},{6,4},{7,5},{8,10},{9,11},{10,... | collective-permute-start | bytes 393224 | tf_op jit(solution)/shard_map/ppermute | solution.py:345
  68.8 2.1 %shard_map.154 = bf16[2,256,128]{2,1,0:T(8,128)(2,1)S(1)} custom-call(bf16[32,136,128]{2,1,0:T(8,128)(2,1)S(1)} %all-to-all-done.kv_ref, bf16[32,32,128]{2,1,0:T(8,128)(2,1)S(1)} %collective-permute-done.side_ref, bf16[2048,128]{1,0:T(8,128)(2,1)S(1)} %get-tuple-element.26.query_rows, bf16[2048,128]{1,0:T(8,128)(2,1)S(1)} %copy-done.6, ...), custom_call_target="tpu_custom_call" | custom-call | flops 1207959552 | bytes 3145728 | tf_op jit(solution)/shard_map/pallas_call | solution.py:390
  70.9 4.3 %collective-permute-start.7 = (bf16[2,256,128]{2,1,0:T(8,128)(2,1)S(1)}, bf16[2,256,128]{2,1,0:T(8,128)(2,1)S(1)}, u32[]{:S(2)}, u32[]{:S(2)}) collective-permute-start(bf16[2,256,128]{2,1,0:T(8,128)(2,1)S(1)} %shard_map.154), channel_id=1, source_target_pairs={{0,1},{1,2},{2,3},{3,0},{4,5},{5,6},{6,7},{7,4},{8,9},{9,10},{10,1... | collective-permute-start | bytes 393224 | tf_op jit(solution)/shard_map/ppermute | solution.py:345
  75.2 0.5 slice.7
  75.7 2.1 %shard_map.151.d0 = bf16[2,256,128]{2,1,0:T(8,128)(2,1)S(1)} custom-call(bf16[32,136,128]{2,1,0:T(8,128)(2,1)S(1)} %all-to-all-done.kv_ref, bf16[32,32,128]{2,1,0:T(8,128)(2,1)S(1)} %collective-permute-done.side_ref, bf16[2048,128]{1,0:T(8,128)(2,1)S(1)} %get-tuple-element.26.query_rows, bf16[2048,128]{1,0:T(8,128)(2,1)S(1)} %copy-done.6, ...), custom_call_target="tpu_custom_call" | custom-call | flops 1207959552 | bytes 3145728 | tf_op jit(solution)/shard_map/pallas_call | solution.py:390
  77.8 0.0 collective-permute-done.5.d1
  77.8 0.0 collective-permute-done.6.d2
  77.8 4.5 %collective-permute-done.7.d3 = bf16[2,256,128]{2,1,0:T(8,128)(2,1)S(1)} collective-permute-done((bf16[2,256,128]{2,1,0:T(8,128)(2,1)S(1)}, bf16[2,256,128]{2,1,0:T(8,128)(2,1)S(1)}, u32[]{:S(2)}, u32[]{:S(2)}) %collective-permute-start.7) | collective-permute-done | bytes 131104 | tf_op jit(solution)/shard_map/ppermute | solution.py:345
  82.3 0.8 shard_map.155
  83.1 4.1 %all-to-all-done.1.part_ref = bf16[32,128,128]{2,1,0:T(8,128)(2,1)S(1)} async-done(((bf16[32,128,128]{2,1,0:T(8,128)(2,1)}), bf16[32,128,128]{2,1,0:T(8,128)(2,1)S(1)}, u32[]{:S(2)}, u32[]{:S(2)}) %all-to-all-start.1) | async-done | bytes 1048608 | tf_op jit(solution)/shard_map/all_to_all | solution.py:337
  87.3 1.3 %shard_map.150 = (bf16[1,64,256]{2,1,0:T(8,128)(2,1)}, bf16[1,64,256]{2,1,0:T(8,128)(2,1)}, bf16[1,2,32,256]{3,2,1,0:T(8,128)(2,1)}, bf16[1,2,32,256]{3,2,1,0:T(8,128)(2,1)}) custom-call(s32[1,3]{1,0:T(1,128)S(1)} %copy-done.4, f32[8,128]{1,0:T(8,128)S(1)} %get-tuple-element.30.gate_ref, bf16[32,128,128]{2,1,0:T(8,128)(2,1)S(1)} %all-to-all-done.1.part_ref), custom_call_target="tpu_custom_call" | custom-call | bytes 1048576 | tf_op jit(solution)/shard_map/pallas_call | solution.py:457
  (2 shorter events, 0.1 us)
Async XLA Ops:
  2.7 10.4 %copy-start = (bf16[1,1,32,4096]{3,2,1,0:T(8,128)(2,1)S(1)}, bf16[1,1,32,4096]{3,2,1,0:T(8,128)(2,1)}, u32[]{:S(2)}) copy-start(bf16[1,1,32,4096]{3,2,1,0:T(8,128)(2,1)} %q_hbm.1) | copy-start | bytes 786436
  2.7 10.4 %copy-start.1 = (bf16[1,1,32,4096]{3,2,1,0:T(8,128)(2,1)S(1)}, bf16[1,1,32,4096]{3,2,1,0:T(8,128)(2,1)}, u32[]{:S(2)}) copy-start(bf16[1,1,32,4096]{3,2,1,0:T(8,128)(2,1)} %g_hbm.1) | copy-start | bytes 786436
  2.7 10.4 %copy-start.2 = (bf16[1,1,32,32]{3,2,1,0:T(8,128)(2,1)S(1)}, bf16[1,1,32,32]{3,2,1,0:T(8,128)(2,1)}, u32[]{:S(2)}) copy-start(bf16[1,1,32,32]{3,2,1,0:T(8,128)(2,1)} %lse_hbm.1) | copy-start | bytes 6148
  2.7 10.4 %copy-start.3 = (bf16[1,1,32,32]{3,2,1,0:T(8,128)(2,1)S(1)}, bf16[1,1,32,32]{3,2,1,0:T(8,128)(2,1)}, u32[]{:S(2)}) copy-start(bf16[1,1,32,32]{3,2,1,0:T(8,128)(2,1)} %delta_hbm.1) | copy-start | bytes 6148
  2.7 39.8 %all-to-all-start = ((bf16[32,136,128]{2,1,0:T(8,128)(2,1)}), bf16[32,136,128]{2,1,0:T(8,128)(2,1)S(1)}, u32[]{:S(2)}, u32[]{:S(2)}) async-start(bf16[32,136,128]{2,1,0:T(8,128)(2,1)} %shard_map.145), calls=%async_computation | async-start | bytes 2228224 | tf_op jit(solution)/shard_map/all_to_all | solution.py:337
  13.1 31.4 %copy-start.4 = (s32[1,3]{1,0:T(1,128)S(1)}, s32[1,3]{1,0:T(1,128)}, u32[]{:S(2)}) copy-start(s32[1,3]{1,0:T(1,128)} %lengths_ref.3) | copy-start | bytes 40
  13.7 3.4 %collective-permute-start.1 = (bf16[2,528,128]{2,1,0:T(8,128)(2,1)S(1)}, bf16[2,528,128]{2,1,0:T(8,128)(2,1)S(1)}, u32[]{:S(2)}, u32[]{:S(2)}) collective-permute-start(bf16[2,528,128]{2,1,0:T(8,128)(2,1)S(1)} %get-tuple-element.22), channel_id=1, source_target_pairs={{0,32},{32,0},{1,33},{33,1},{2,34},{34,2},{3,35},{35,3},{4,36},{36... | collective-permute-start | bytes 811016 | tf_op jit(solution)/shard_map/ppermute | solution.py:341
  17.2 27.3 %collective-permute-start.3 = (bf16[2,528,128]{2,1,0:T(8,128)(2,1)S(1)}, bf16[2,528,128]{2,1,0:T(8,128)(2,1)S(1)}, u32[]{:S(2)}, u32[]{:S(2)}) collective-permute-start(bf16[2,528,128]{2,1,0:T(8,128)(2,1)S(1)} %get-tuple-element.23.q0), channel_id=1, source_target_pairs={{0,2},{1,3},{2,0},{3,1},{4,6},{5,7},{6,4},{7,5},{8,10},{9,11},{10,... | collective-permute-start | bytes 811016 | tf_op jit(solution)/shard_map/ppermute | solution.py:345
  20.5 23.9 %collective-permute-start.4 = (bf16[2,528,128]{2,1,0:T(8,128)(2,1)S(1)}, bf16[2,528,128]{2,1,0:T(8,128)(2,1)S(1)}, u32[]{:S(2)}, u32[]{:S(2)}) collective-permute-start(bf16[2,528,128]{2,1,0:T(8,128)(2,1)S(1)} %get-tuple-element.24), channel_id=1, source_target_pairs={{0,3},{1,0},{2,1},{3,2},{4,7},{5,4},{6,5},{7,6},{8,11},{9,8},{10,9... | collective-permute-start | bytes 811016 | tf_op jit(solution)/shard_map/ppermute | solution.py:345
  22.5 22.0 %collective-permute-start.2 = (bf16[2,528,128]{2,1,0:T(8,128)(2,1)S(1)}, bf16[2,528,128]{2,1,0:T(8,128)(2,1)S(1)}, u32[]{:S(2)}, u32[]{:S(2)}) collective-permute-start(bf16[2,528,128]{2,1,0:T(8,128)(2,1)S(1)} %get-tuple-element.24), channel_id=1, source_target_pairs={{0,1},{1,2},{2,3},{3,0},{4,5},{5,6},{6,7},{7,4},{8,9},{9,10},{10,1... | collective-permute-start | bytes 811016 | tf_op jit(solution)/shard_map/ppermute | solution.py:345
  42.5 7.1 %collective-permute-start = (bf16[32,32,128]{2,1,0:T(8,128)(2,1)S(1)}, bf16[32,32,128]{2,1,0:T(8,128)(2,1)S(1)}, u32[]{:S(2)}, u32[]{:S(2)}) collective-permute-start(bf16[32,32,128]{2,1,0:T(8,128)(2,1)S(1)} %slice.8), channel_id=1, source_target_pairs={{0,32},{32,0},{1,33},{33,1},{2,34},{34,2},{3,35},{35,3},{4,36},{36... | collective-permute-start | bytes 786440 | tf_op jit(solution)/shard_map/ppermute | solution.py:341
  49.7 3.2 %copy-start.5 = (bf16[2048,128]{1,0:T(8,128)(2,1)}, bf16[2048,128]{1,0:T(8,128)(2,1)S(1)}, u32[]{:S(2)}) copy-start(bf16[2048,128]{1,0:T(8,128)(2,1)S(1)} %get-tuple-element.27.grad_rows) | copy-start | bytes 1572868
  52.8 6.0 %copy-start.6 = (bf16[2048,128]{1,0:T(8,128)(2,1)S(1)}, bf16[2048,128]{1,0:T(8,128)(2,1)}, u32[]{:S(2)}) copy-start(bf16[2048,128]{1,0:T(8,128)(2,1)} %copy-done.5) | copy-start | bytes 1572868
  52.8 34.4 %all-to-all-start.1 = ((bf16[32,128,128]{2,1,0:T(8,128)(2,1)}), bf16[32,128,128]{2,1,0:T(8,128)(2,1)S(1)}, u32[]{:S(2)}, u32[]{:S(2)}) async-start(bf16[32,128,128]{2,1,0:T(8,128)(2,1)} %get-tuple-element.31), calls=%async_computation.1 | async-start | bytes 2097152 | tf_op jit(solution)/shard_map/all_to_all | solution.py:337
  61.0 16.8 %collective-permute-start.5 = (bf16[2,256,128]{2,1,0:T(8,128)(2,1)S(1)}, bf16[2,256,128]{2,1,0:T(8,128)(2,1)S(1)}, u32[]{:S(2)}, u32[]{:S(2)}) collective-permute-start(bf16[2,256,128]{2,1,0:T(8,128)(2,1)S(1)} %shard_map.152), channel_id=1, source_target_pairs={{0,3},{1,0},{2,1},{3,2},{4,7},{5,4},{6,5},{7,6},{8,11},{9,8},{10,9... | collective-permute-start | bytes 393224 | tf_op jit(solution)/shard_map/ppermute | solution.py:345
  66.0 11.8 %collective-permute-start.6 = (bf16[2,256,128]{2,1,0:T(8,128)(2,1)S(1)}, bf16[2,256,128]{2,1,0:T(8,128)(2,1)S(1)}, u32[]{:S(2)}, u32[]{:S(2)}) collective-permute-start(bf16[2,256,128]{2,1,0:T(8,128)(2,1)S(1)} %shard_map.153), channel_id=1, source_target_pairs={{0,2},{1,3},{2,0},{3,1},{4,6},{5,7},{6,4},{7,5},{8,10},{9,11},{10,... | collective-permute-start | bytes 393224 | tf_op jit(solution)/shard_map/ppermute | solution.py:345
  70.9 11.4 %collective-permute-start.7 = (bf16[2,256,128]{2,1,0:T(8,128)(2,1)S(1)}, bf16[2,256,128]{2,1,0:T(8,128)(2,1)S(1)}, u32[]{:S(2)}, u32[]{:S(2)}) collective-permute-start(bf16[2,256,128]{2,1,0:T(8,128)(2,1)S(1)} %shard_map.154), channel_id=1, source_target_pairs={{0,1},{1,2},{2,3},{3,0},{4,5},{5,6},{6,7},{7,4},{8,9},{9,10},{10,1... | collective-permute-start | bytes 393224 | tf_op jit(solution)/shard_map/ppermute | solution.py:345

commit v6 on v5

--- a/solution.py
+++ b/solution.py
@@ -10,20 +10,21 @@
 beta_coef = 0.1
 f32, bf16 = jnp.float32, jnp.bfloat16
 LANES = 128
-CTX = ("y", "x")
+CTX = ("y", "xh", "xl")
+ROW = ("xh", "xl")
+PEERS = ("y", "xl")
 
 X = 4
 ROWS_Y = 8
-CTX_N = 32
+PEERS_N = 16
 POS = 32
+PROMPT = 64
 GROUP = 8
 TILE = POS * GROUP
-PROMPT_HALF = 32
-RESP_HALF = 16
 STAT_ROWS = 16
 QUERY_ROWS = 2 * TILE + STAT_ROWS
-SIDE = 2 * RESP_HALF
-KV_ROWS = 2 * PROMPT_HALF + 2 * SIDE
+SIDE = 2 * POS
+KV_ROWS = 2 * PROMPT + 2 * SIDE
 LOG2E = 1.4426950408889634
 SCALE = LANES**-0.5
 DEAD = 1e30
@@ -59,6 +60,22 @@
         copy.wait()
 
 
+def split_margin(margin, rows):
+    high = margin.astype(bf16).astype(f32)
+    middle = (margin - high).astype(bf16).astype(f32)
+    low = margin - high - middle
+    lane = lax.broadcasted_iota(jnp.int32, (rows, LANES), 1)
+    row = lax.broadcasted_iota(jnp.int32, (rows, LANES), 0)
+    block = jnp.where(lane == 0, high, jnp.where(lane == 1, middle, jnp.where(lane == 2, low, 0.0)))
+    return jnp.where(row == 0, block, 0.0).astype(bf16)
+
+
+def gate_of(margin, block):
+    other = jnp.sum(block.astype(f32), axis=0, keepdims=True)
+    margin = margin + jnp.sum(other, axis=1, keepdims=True)
+    return beta_coef * jax.nn.sigmoid(-beta_coef * margin)
+
+
 def kv_pack_kernel(
     lengths_hbm, logratio_hbm, pk_hbm, pv_hbm, rk_hbm, rv_hbm, kv_ref, lengths, logratio, pk, pv, rk, rv, sems
 ):
@@ -72,41 +89,31 @@
     )
     fetch(pairs, sems)
     first_core = lax.axis_index("pair") == 0
-    ctx = lax.axis_index("y") * X + lax.axis_index("x")
+    ctx = lax.axis_index(CTX)
     position = ctx * POS + lax.broadcasted_iota(jnp.int32, (1, POS), 1)
     chosen = jnp.where(position < lengths[0, 1], logratio[0:1, :], 0.0)
     rejected = jnp.where(position < lengths[0, 2], logratio[1:2, :], 0.0)
     margin = jnp.sum(chosen - rejected, axis=1, keepdims=True)
-    high = margin.astype(bf16).astype(f32)
-    middle = (margin - high).astype(bf16).astype(f32)
-    low = margin - high - middle
-    lane = lax.broadcasted_iota(jnp.int32, (MARGIN_ROWS, LANES), 1)
-    row = lax.broadcasted_iota(jnp.int32, (MARGIN_ROWS, LANES), 0)
-    block = jnp.where(lane == 0, high, jnp.where(lane == 1, middle, jnp.where(lane == 2, low, 0.0)))
-    block = jnp.where(row == 0, block, 0.0).astype(bf16)
-    for x in range(X):
-        odd, half = x % 2, x // 2
-        columns = slice(odd * LANES, (odd + 1) * LANES)
-        others = slice((2 + odd) * LANES, (3 + odd) * LANES)
-        rows = slice(half * PROMPT_HALF, (half + 1) * PROMPT_HALF)
-        index = ctx * 2 * PROMPT_HALF + half * PROMPT_HALF
-        live = index + lax.broadcasted_iota(jnp.int32, (PROMPT_HALF, LANES), 0) < lengths[0, 0]
-        parts = [jnp.where(live, pk[rows, columns].astype(f32), 0.0).astype(bf16), pv[rows, columns]]
-        rows = slice(half * RESP_HALF, (half + 1) * RESP_HALF)
-        low_head = [ref[rows, columns].astype(f32) for ref in (rk, rv)]
-        high_head = [ref[rows, others].astype(f32) for ref in (rk, rv)]
+    block = split_margin(margin, MARGIN_ROWS)
+    live = ctx * PROMPT + lax.broadcasted_iota(jnp.int32, (PROMPT, LANES), 0) < lengths[0, 0]
+    for xl in range(2):
+        columns = slice(xl * LANES, (xl + 1) * LANES)
+        others = slice((2 + xl) * LANES, (3 + xl) * LANES)
+        parts = [jnp.where(live, pk[:, columns].astype(f32), 0.0).astype(bf16), pv[:, columns]]
+        low_head = [ref[:, columns].astype(f32) for ref in (rk, rv)]
+        high_head = [ref[:, others].astype(f32) for ref in (rk, rv)]
         parts += [jnp.where(first_core, a, b).astype(bf16) for a, b in zip(low_head, high_head)]
         parts += [jnp.where(first_core, b, a).astype(bf16) for a, b in zip(low_head, high_head)]
         parts += [block]
         for y in range(ROWS_Y):
             at = 0
             for part in parts:
-                kv_ref[y * X + x, at : at + part.shape[0], :] = part
+                kv_ref[y * 2 + xl, at : at + part.shape[0], :] = part
                 at += part.shape[0]
 
 
 def query_pack_kernel(q_hbm, g_hbm, lse_hbm, delta_hbm, own_ref, other_ref, q, g, lse, delta, sems):
-    core, parity = lax.axis_index("pair"), lax.axis_index("x") % 2
+    core, parity = lax.axis_index("pair"), lax.axis_index("xl")
     pairs = [(lse_hbm.at[0, 0], lse), (delta_hbm.at[0, 0], delta)]
     heads = []
     for i in range(4):
@@ -148,14 +155,15 @@
 
 
 def row_position(k):
-    x = (lax.axis_index("x") + X - k) % X
+    x = (lax.axis_index(ROW) + X - k) % X
     return (lax.axis_index("y") * X + x) * POS + lax.broadcasted_iota(jnp.int32, (1, TILE), 1) % POS
 
 
 def key_positions(block, count):
     index = lax.broadcasted_iota(jnp.int32, (count, 1), 0)
-    source = block * (count // RESP_HALF) + index // RESP_HALF
-    return source * POS + lax.axis_index("x") // 2 * RESP_HALF + index % RESP_HALF
+    source = block * (count // POS) + index // POS
+    ctx = source // 2 * X + 2 * lax.axis_index("xh") + source % 2
+    return ctx * POS + index % POS
 
 
 def row_stats(lengths_ref, block, k, j):
@@ -200,12 +208,12 @@
             grad_rows[at, :] = ref[j, TILE : 2 * TILE, :]
             lse, delta = row_stats(lengths_ref, ref[j, 2 * TILE :, :], k, j)
             lse_ref[t : t + 1, :], delta_ref[t : t + 1, :] = lse, delta
-    per = BLOCK // PROMPT_HALF
+    per = BLOCK // PROMPT
 
     def first(c, slot):
         rows = slice(c * per, (c + 1) * per)
-        key = kv_ref[rows, 0:PROMPT_HALF, :].reshape(BLOCK, LANES)
-        value = kv_ref[rows, PROMPT_HALF : 2 * PROMPT_HALF, :].reshape(BLOCK, LANES)
+        key = kv_ref[rows, 0:PROMPT, :].reshape(BLOCK, LANES)
+        value = kv_ref[rows, PROMPT : 2 * PROMPT, :].reshape(BLOCK, LANES)
         for t in range(2 * X):
             at = tile_rows(t)
             weights[slot, :, at], score_grads[slot, :, at] = cell(
@@ -215,32 +223,32 @@
     def second(c, slot):
         value_grad = dot(weights[slot], grad_rows[...], ((1,), (0,)))
         key_grad = dot(score_grads[slot], query_rows[...], ((1,), (0,))) * SCALE
-        shape = (per, PROMPT_HALF, LANES)
+        shape = (per, PROMPT, LANES)
         to = slice(c * per, (c + 1) * per)
-        out_ref[to, 0:PROMPT_HALF, :] = key_grad.astype(bf16).reshape(shape)
-        out_ref[to, PROMPT_HALF:, :] = value_grad.astype(bf16).reshape(shape)
-
-    staged([(c,) for c in range(CTX_N // per)], first, second)
+        out_ref[to, 0:PROMPT, :] = key_grad.astype(bf16).reshape(shape)
+        out_ref[to, PROMPT:, :] = value_grad.astype(bf16).reshape(shape)
+
+    staged([(c,) for c in range(PEERS_N // per)], first, second)
 
 
 def resp_kernel(
     kv_ref, side_ref, prompt_ref, query_rows, grad_rows, lse_ref, delta_ref,
-    out_hbm, gate_ref, weights, score_grads, parts, sems,
+    out_hbm, margin_ref, weights, score_grads, parts, sems,
 ):
-    copies = [pltpu.make_async_copy(prompt_ref, out_hbm.at[:, 0 : 2 * PROMPT_HALF, :], sems.at[0])]
+    copies = [pltpu.make_async_copy(prompt_ref, out_hbm.at[:, 0 : 2 * PROMPT, :], sems.at[0])]
     copies[0].start()
     margin = jnp.sum(kv_ref[:, KV_ROWS:, :].astype(f32), axis=(0, 1), keepdims=True).reshape(1, LANES)
     margin = jnp.sum(margin, axis=1, keepdims=True)
-    gate_ref[...] = jnp.broadcast_to(beta_coef * jax.nn.sigmoid(-beta_coef * margin), gate_ref.shape)
-    per = BLOCK // RESP_HALF
-    blocks = CTX_N // per
-    sources = ((kv_ref, 2 * PROMPT_HALF), (side_ref, 0))
+    margin_ref[...] = jnp.broadcast_to(margin, margin_ref.shape)
+    per = BLOCK // POS
+    blocks = PEERS_N // per
+    sources = ((kv_ref, 2 * PROMPT), (side_ref, 0))
 
     def first(j, c, slot):
         ref, start = sources[j]
         rows = slice(c * per, (c + 1) * per)
-        key = ref[rows, start : start + RESP_HALF, :].reshape(BLOCK, LANES)
-        value = ref[rows, start + RESP_HALF : start + SIDE, :].reshape(BLOCK, LANES)
+        key = ref[rows, start : start + POS, :].reshape(BLOCK, LANES)
+        value = ref[rows, start + POS : start + SIDE, :].reshape(BLOCK, LANES)
         positions = key_positions(c, BLOCK)
         for k in range(X):
             t = j * X + k
@@ -259,11 +267,11 @@
         rows = slice(j * X * TILE, (j + 1) * X * TILE)
         value_grad = dot(weights[slot], grad_rows[rows, :], ((1,), (0,)))
         key_grad = dot(score_grads[slot], query_rows[rows, :], ((1,), (0,))) * SCALE
-        shape = (per, RESP_HALF, LANES)
+        shape = (per, POS, LANES)
         n = j * blocks + c
-        parts[n, :, 0:RESP_HALF, :] = key_grad.astype(bf16).reshape(shape)
-        parts[n, :, RESP_HALF:, :] = value_grad.astype(bf16).reshape(shape)
-        start = 2 * PROMPT_HALF + j * SIDE
+        parts[n, :, 0:POS, :] = key_grad.astype(bf16).reshape(shape)
+        parts[n, :, POS:, :] = value_grad.astype(bf16).reshape(shape)
+        start = 2 * PROMPT + j * SIDE
         to = out_hbm.at[c * per : (c + 1) * per, start : start + SIDE, :]
         copies.append(pltpu.make_async_copy(parts.at[n], to, sems.at[1 + n]))
         copies[-1].start()
@@ -273,16 +281,16 @@
         copy.wait()
 
 
-def query_kernel(k, kv_ref, side_ref, query_rows, grad_rows, lse_ref, delta_ref, out_ref):
+def query_kernel(k, margin_ref, kv_ref, side_ref, query_rows, grad_rows, lse_ref, delta_ref, out_ref):
     for j in range(2):
         t = j * X + k
         query, grad = query_rows[tile_rows(t), :], grad_rows[tile_rows(t), :]
         lse, delta = lse_ref[t : t + 1, :], delta_ref[t : t + 1, :]
         total = None
-        resp, start = ((kv_ref, 2 * PROMPT_HALF), (side_ref, 0))[j]
-        parts = [(kv_ref, c, PROMPT_HALF, 0, None) for c in range(CTX_N * PROMPT_HALF // BLOCK)]
-        for c in range(CTX_N * RESP_HALF // BLOCK):
-            parts.append((resp, c, RESP_HALF, start, key_positions(c, BLOCK) <= row_position(k)))
+        resp, start = ((kv_ref, 2 * PROMPT), (side_ref, 0))[j]
+        parts = [(kv_ref, c, PROMPT, 0, None) for c in range(PEERS_N * PROMPT // BLOCK)]
+        for c in range(PEERS_N * POS // BLOCK):
+            parts.append((resp, c, POS, start, key_positions(c, BLOCK) <= row_position(k)))
         for ref, c, count, start, allowed in parts:
             per = BLOCK // count
             rows = slice(c * per, (c + 1) * per)
@@ -291,50 +299,48 @@
             _, score_grads = cell(key, value, query, grad, lse, delta, allowed)
             term = dot(score_grads, key, ((0,), (0,)))
             total = term if total is None else total + term
-        out_ref[j] = (total * SCALE).astype(bf16)
-
-
-def kv_final_kernel(lengths_ref, gate_ref, part_ref, pk_ref, pv_ref, rk_ref, rv_ref):
-    gate = gate_ref[0:1, 0:1]
+        out_ref[tile_rows(j), :] = (total * SCALE).astype(bf16)
+    if k == 2:
+        out_ref[2 * TILE :, :] = split_margin(margin_ref[0:1, 0:1], STAT_ROWS)
+
+
+def kv_final_kernel(lengths_ref, margin_ref, d2, part_ref, pk_ref, pv_ref, rk_ref, rv_ref):
+    gate = gate_of(margin_ref[0:1, 0:1], d2[2 * TILE :, :])
     core = lax.axis_index("pair")
-    ctx = lax.axis_index("y") * X + lax.axis_index("x")
-    for x in range(X):
-        odd, half = x % 2, x // 2
-        columns = slice(odd * LANES, (odd + 1) * LANES)
-        total = part_ref[x].astype(f32)
+    live = lax.axis_index(CTX) * PROMPT + lax.broadcasted_iota(jnp.int32, (PROMPT, LANES), 0) < lengths_ref[0, 0]
+    for xl in range(2):
+        columns = slice(xl * LANES, (xl + 1) * LANES)
+        total = part_ref[xl].astype(f32)
         for y in range(1, ROWS_Y):
-            total += part_ref[y * X + x].astype(f32)
+            total += part_ref[y * 2 + xl].astype(f32)
         total = total * gate
-        rows = slice(half * PROMPT_HALF, (half + 1) * PROMPT_HALF)
-        index = ctx * 2 * PROMPT_HALF + half * PROMPT_HALF
-        live = index + lax.broadcasted_iota(jnp.int32, (PROMPT_HALF, LANES), 0) < lengths_ref[0, 0]
-        pk_ref[0, rows, columns] = jnp.where(live, total[0:PROMPT_HALF], 0.0).astype(bf16)
-        pv_ref[0, rows, columns] = jnp.where(live, total[PROMPT_HALF : 2 * PROMPT_HALF], 0.0).astype(bf16)
-        rows = slice(half * RESP_HALF, (half + 1) * RESP_HALF)
+        pk_ref[0, :, columns] = jnp.where(live, total[0:PROMPT], 0.0).astype(bf16)
+        pv_ref[0, :, columns] = jnp.where(live, total[PROMPT : 2 * PROMPT], 0.0).astype(bf16)
         for j in range(2):
             response = core + j - 2 * core * j
-            at = 2 * PROMPT_HALF + j * SIDE
-            rk_ref[0, response, rows, columns] = total[at : at + RESP_HALF].astype(bf16)
-            rv_ref[0, response, rows, columns] = total[at + RESP_HALF : at + SIDE].astype(bf16)
-
-
-def query_final_kernel(gate_ref, d0, d1, d2, d3, out_ref):
-    gate = gate_ref[0:1, 0:1]
+            at = 2 * PROMPT + j * SIDE
+            rk_ref[0, response, :, columns] = total[at : at + POS].astype(bf16)
+            rv_ref[0, response, :, columns] = total[at + POS : at + SIDE].astype(bf16)
+
+
+def query_final_kernel(margin_ref, d0, d1, d2, d3, out_ref, gate_ref):
+    gate = gate_of(margin_ref[0:1, 0:1], d2[2 * TILE :, :])
+    gate_ref[...] = jnp.broadcast_to(gate, gate_ref.shape)
     core = lax.axis_index("pair")
-    even = lax.axis_index("x") % 2 == 0
+    even = lax.axis_index("xl") == 0
     for j in range(2):
         response = core + j - 2 * core * j
         for h in range(GROUP):
-            rows = slice(h * POS, (h + 1) * POS)
-            same = gate * (d0[j, rows, :].astype(f32) + d2[j, rows, :].astype(f32))
-            odd = gate * (d1[j, rows, :].astype(f32) + d3[j, rows, :].astype(f32))
+            rows = slice(j * TILE + h * POS, j * TILE + (h + 1) * POS)
+            same = gate * (d0[rows, :].astype(f32) + d2[rows, :].astype(f32))
+            odd = gate * (d1[rows, :].astype(f32) + d3[rows, :].astype(f32))
             first, second = jnp.where(even, same, odd), jnp.where(even, odd, same)
             out_ref[0, response, :, h * LANES : (h + 1) * LANES] = first.astype(bf16)
             out_ref[0, response, :, (GROUP + h) * LANES : (GROUP + h + 1) * LANES] = second.astype(bf16)
 
 
 def swap(values):
-    return lax.all_to_all(values, CTX, split_axis=0, concat_axis=0, tiled=True)
+    return lax.all_to_all(values, PEERS, split_axis=0, concat_axis=0, tiled=True)
 
 
 def cross(values):
@@ -342,7 +348,7 @@
 
 
 def shift(values, by):
-    return lax.ppermute(values, "x", [(i, (i + by) % X) for i in range(X)])
+    return lax.ppermute(values, ROW, [(i, (i + by) % X) for i in range(X)])
 
 
 def prompt_call(lengths, rows, kv):
@@ -351,7 +357,7 @@
     return call(
         prompt_kernel,
         (
-            shape((CTX_N, 2 * PROMPT_HALF, LANES), bf16),
+            shape((PEERS_N, 2 * PROMPT, LANES), bf16),
             shape((count, LANES), bf16),
             shape((count, LANES), bf16),
             shape((2 * X, TILE), f32),
@@ -366,11 +372,11 @@
 
 def resp_call(kv, side, prompt_part, *rows):
     shape = jax.ShapeDtypeStruct
-    blocks = 2 * CTX_N * RESP_HALF // BLOCK
+    blocks = 2 * PEERS_N * POS // BLOCK
     return call(
         resp_kernel,
         (
-            shape((CTX_N, KV_ROWS, LANES), bf16),
+            shape((PEERS_N, KV_ROWS, LANES), bf16),
             shape((8, LANES), f32),
         ),
         "vvvvvvv",
@@ -378,7 +384,7 @@
         scratch=(
             pltpu.VMEM((2, BLOCK, X * TILE), bf16),
             pltpu.VMEM((2, BLOCK, X * TILE), bf16),
-            pltpu.VMEM((blocks, BLOCK // RESP_HALF, SIDE, LANES), bf16),
+            pltpu.VMEM((blocks, BLOCK // POS, SIDE, LANES), bf16),
             pltpu.SemaphoreType.DMA((blocks + 1,)),
         ),
         flops=4 * 2 * 1024 * 1024 * 128 * 2,
@@ -386,14 +392,15 @@
     )(kv, side, prompt_part, *rows)
 
 
-def query_call(k, kv, side, *rows):
+def query_call(k, margin, kv, side, *rows):
+    extra = STAT_ROWS if k == 2 else 0
     return call(
         functools.partial(query_kernel, k),
-        jax.ShapeDtypeStruct((2, TILE, LANES), bf16),
-        "vvvvvv",
+        jax.ShapeDtypeStruct((2 * TILE + extra, LANES), bf16),
+        "vvvvvvv",
         flops=3 * 2 * 512 * 1536 * 128 * 2,
         size=3 * 2**20,
-    )(kv, side, *rows)
+    )(margin, kv, side, *rows)
 
 
 def per_device(
@@ -411,15 +418,15 @@
     shape = jax.ShapeDtypeStruct
     kv = call(
         kv_pack_kernel,
-        shape((CTX_N, KV_ROWS + MARGIN_ROWS, LANES), bf16),
+        shape((PEERS_N, KV_ROWS + MARGIN_ROWS, LANES), bf16),
         "aaaaaa",
         size=2 * 2**20,
         limit=60,
         scratch=(
             pltpu.SMEM((1, 3), jnp.int32),
             pltpu.VMEM((2, POS), f32),
-            pltpu.VMEM((2 * PROMPT_HALF, 2 * LANES), bf16),
-            pltpu.VMEM((2 * PROMPT_HALF, 2 * LANES), bf16),
+            pltpu.VMEM((PROMPT, 2 * LANES), bf16),
+            pltpu.VMEM((PROMPT, 2 * LANES), bf16),
             pltpu.VMEM((POS, X * LANES), bf16),
             pltpu.VMEM((POS, X * LANES), bf16),
             pltpu.SemaphoreType.DMA((6,)),
@@ -446,21 +453,26 @@
 
     side = cross(kv[:, KV_ROWS - SIDE : KV_ROWS, :])
     prompt_part, *rows = prompt_call(lengths, rows, kv)
-    part, gate = resp_call(kv, side, prompt_part, *rows)
-    grads = [query_call(k, kv, side, *rows) for k in range(X)]
+    part, margin = resp_call(kv, side, prompt_part, *rows)
+    grads = [query_call(k, margin, kv, side, *rows) for k in range(X)]
     part = swap(part)
     back = [grads[0]] + [shift(grads[k], X - k) for k in range(1, X)]
-    query_grad = call(query_final_kernel, shape((1, 2, POS, 2 * GROUP * LANES), bf16), "vvvvv", size=2**20)(
-        gate, *back
+    query_grad, gate = call(
+        query_final_kernel,
+        (shape((1, 2, POS, 2 * GROUP * LANES), bf16), shape((8, LANES), f32)),
+        "vvvvv",
+        size=2**20,
+    )(margin, *back)
+    outs = (shape((1, PROMPT, 2 * LANES), bf16),) * 2 + (shape((1, 2, POS, 2 * LANES), bf16),) * 2
+    pk_grad, pv_grad, key_grad, value_grad = call(kv_final_kernel, outs, "svvv", size=2**20)(
+        lengths, margin, back[2], part
     )
-    outs = (shape((1, 2 * PROMPT_HALF, 2 * LANES), bf16),) * 2 + (shape((1, 2, POS, 2 * LANES), bf16),) * 2
-    pk_grad, pv_grad, key_grad, value_grad = call(kv_final_kernel, outs, "svv", size=2**20)(lengths, gate, part)
     return pk_grad, pv_grad, query_grad, key_grad, value_grad, gate[0, 0:1]
 
 
 def solution(mesh):
     batch, pair, ctx = mesh.devices.shape
-    split = Mesh(mesh.devices.reshape(batch, pair, ctx // X, X), ("batch", "pair", "y", "x"))
+    split = Mesh(mesh.devices.reshape(batch, pair, ctx // X, 2, 2), ("batch", "pair", "y", "xh", "xl"))
     prompt_spec = P("batch", CTX, "pair")
     resp_spec = P("batch", "pair", CTX, None)
     out_spec = P("batch", None, CTX, "pair")

time: 89.3 us -> 91.4 us (1.024)
  the two profiles are of different devices: /device:TPU:6 before, /device:TPU:1 now
where the time goes in v6:
time: 91.4 us; the launch traced here: 90.8 us
  starting transfers between devices  46.3 us (51%)
  Pallas kernels  21.6 us (24%)
  waiting for transfers between devices  20.3 us (22%)
  local copies, waits for them, and re-layouts  1.62 us (2%)
  between operations  0.95 us (1%)
    ppermute x6, starting transfers between devices, shift(): return lax.ppermute(values, ROW, [(i, (i + by) % X) for i in range(X)])  20 us
    all_to_all x2, starting transfers between devices, swap(): lax.all_to_all(values, PEERS, split_axis=0, concat_axis=0, tiled=True)  15.7 us
    ppermute x2, starting transfers between devices, cross(): return lax.ppermute(values, 'pair', [(0, 1), (1, 0)])  10.6 us
    all_to_all x2, waiting for transfers between devices, swap(): lax.all_to_all(values, PEERS, split_axis=0, concat_axis=0, tiled=True)  9.83 us
    ppermute x6, waiting for transfers between devices, shift(): return lax.ppermute(values, ROW, [(i, (i + by) % X) for i in range(X)])  9.33 us
    pallas_call x4, Pallas kernels, query_call(): call(functools.partial(query_kernel, k), jax.ShapeDtypeStruct((2 * TILE +...  8.46 us
    pallas_call x1, Pallas kernels, prompt_call(): call(prompt_kernel, (shape((PEERS_N, 2 * PROMPT, LANES), bf16), shape((co...  5.15 us
    pallas_call x1, Pallas kernels, resp_call(): call(resp_kernel, (shape((PEERS_N, KV_ROWS, LANES), bf16), shape((8, LANE...  3.15 us
  transfers between devices with their start and end apart: 10, of which 5 were waited for; matrix products, arithmetic and copies ran while one was open for 1% of the time, Pallas kernels for 17%

profile of v6, /device:TPU:1, one launch (start us, length us, event | category | flops | bytes accessed | tf_op | source)
XLA Modules:
  0.0 90.8 jit_solution(810651291767079294)
XLA Ops:
  0.6 2.0 %shard_map.145 = bf16[16,264,128]{2,1,0:T(8,128)(2,1)} custom-call(s32[1,3]{1,0:T(1,128)} %lengths_ref.3, f32[1,2,32]{2,1,0:T(2,128)} %logratio_hbm.1, bf16[1,64,256]{2,1,0:T(8,128)(2,1)} %pk_hbm.1, bf16[1,64,256]{2,1,0:T(8,128)(2,1)} %pv_hbm.1, bf16[1,1,32,512]{3,2,1,0:T(8,128)(2,1)} %rk_hbm.1, bf16[1,1,32,512]{3,2,1,0:T(8,128)(2,1)} %rv_hbm.1), custom_call_target="tpu_custom_call" | custom-call | bytes 2097152 | tf_op jit(solution)/shard_map/pallas_call | solution.py:419
  2.6 0.0 copy-start
  2.6 0.0 copy-start.1
  2.7 0.0 copy-start.2
  2.7 0.0 copy-start.3
  2.7 8.8 %all-to-all-start = ((bf16[16,264,128]{2,1,0:T(8,128)(2,1)}), bf16[16,264,128]{2,1,0:T(8,128)(2,1)S(1)}, u32[]{:S(2)}, u32[]{:S(2)}) async-start(bf16[16,264,128]{2,1,0:T(8,128)(2,1)} %shard_map.145), calls=%async_computation | async-start | bytes 2162688 | tf_op jit(solution)/shard_map/all_to_all | solution.py:343
  11.5 0.0 copy-done
  11.5 0.0 copy-done.1
  11.5 0.0 copy-done.2
  11.5 0.0 copy-done.3
  11.6 0.0 copy-start.4
  11.6 0.6 shard_map.146
  12.1 3.8 %collective-permute-start.1 = (bf16[2,528,128]{2,1,0:T(8,128)(2,1)S(1)}, bf16[2,528,128]{2,1,0:T(8,128)(2,1)S(1)}, u32[]{:S(2)}, u32[]{:S(2)}) collective-permute-start(bf16[2,528,128]{2,1,0:T(8,128)(2,1)S(1)} %get-tuple-element.24), channel_id=1, source_target_pairs={{0,32},{32,0},{1,33},{33,1},{2,34},{34,2},{3,35},{35,3},{4,36},{36... | collective-permute-start | bytes 811016 | tf_op jit(solution)/shard_map/ppermute | solution.py:347
  16.0 1.2 %collective-permute-done.1.other_ref = bf16[2,528,128]{2,1,0:T(8,128)(2,1)S(1)} collective-permute-done((bf16[2,528,128]{2,1,0:T(8,128)(2,1)S(1)}, bf16[2,528,128]{2,1,0:T(8,128)(2,1)S(1)}, u32[]{:S(2)}, u32[]{:S(2)}) %collective-permute-start.1) | collective-permute-done | bytes 270368 | tf_op jit(solution)/shard_map/ppermute | solution.py:347
  17.1 3.4 %collective-permute-start.2 = (bf16[2,528,128]{2,1,0:T(8,128)(2,1)S(1)}, bf16[2,528,128]{2,1,0:T(8,128)(2,1)S(1)}, u32[]{:S(2)}, u32[]{:S(2)}) collective-permute-start(bf16[2,528,128]{2,1,0:T(8,128)(2,1)S(1)} %get-tuple-element.26), channel_id=1, source_target_pairs={{0,1},{1,2},{2,3},{3,0},{4,5},{5,6},{6,7},{7,4},{8,9},{9,10},{10,1... | collective-permute-start | bytes 811016 | tf_op jit(solution)/shard_map/ppermute | solution.py:351
  20.6 3.5 %collective-permute-start.3 = (bf16[2,528,128]{2,1,0:T(8,128)(2,1)S(1)}, bf16[2,528,128]{2,1,0:T(8,128)(2,1)S(1)}, u32[]{:S(2)}, u32[]{:S(2)}) collective-permute-start(bf16[2,528,128]{2,1,0:T(8,128)(2,1)S(1)} %get-tuple-element.25.q0), channel_id=1, source_target_pairs={{0,2},{1,3},{2,0},{3,1},{4,6},{5,7},{6,4},{7,5},{8,10},{9,11},{10,... | collective-permute-start | bytes 811016 | tf_op jit(solution)/shard_map/ppermute | solution.py:351
  24.1 2.7 %collective-permute-start.4 = (bf16[2,528,128]{2,1,0:T(8,128)(2,1)S(1)}, bf16[2,528,128]{2,1,0:T(8,128)(2,1)S(1)}, u32[]{:S(2)}, u32[]{:S(2)}) collective-permute-start(bf16[2,528,128]{2,1,0:T(8,128)(2,1)S(1)} %get-tuple-element.26), channel_id=1, source_target_pairs={{0,3},{1,0},{2,1},{3,2},{4,7},{5,4},{6,5},{7,6},{8,11},{9,8},{10,9... | collective-permute-start | bytes 811016 | tf_op jit(solution)/shard_map/ppermute | solution.py:351
  26.8 9.8 %all-to-all-done.kv_ref = bf16[16,264,128]{2,1,0:T(8,128)(2,1)S(1)} async-done(((bf16[16,264,128]{2,1,0:T(8,128)(2,1)}), bf16[16,264,128]{2,1,0:T(8,128)(2,1)S(1)}, u32[]{:S(2)}, u32[]{:S(2)}) %all-to-all-start) | async-done | bytes 1081376 | tf_op jit(solution)/shard_map/all_to_all | solution.py:343
  36.7 6.8 %collective-permute-start = (bf16[16,64,128]{2,1,0:T(8,128)(2,1)S(1)}, bf16[16,64,128]{2,1,0:T(8,128)(2,1)S(1)}, u32[]{:S(2)}, u32[]{:S(2)}) collective-permute-start(bf16[16,64,128]{2,1,0:T(8,128)(2,1)S(1)} %slice.8), channel_id=1, source_target_pairs={{0,32},{32,0},{1,33},{33,1},{2,34},{34,2},{3,35},{35,3},{4,36},{36... | collective-permute-start | bytes 786440 | tf_op jit(solution)/shard_map/ppermute | solution.py:347
  43.4 0.0 collective-permute-done.2.q1
  43.4 0.8 collective-permute-done.3.q2
  44.2 1.2 %collective-permute-done.4.q3 = bf16[2,528,128]{2,1,0:T(8,128)(2,1)S(1)} collective-permute-done((bf16[2,528,128]{2,1,0:T(8,128)(2,1)S(1)}, bf16[2,528,128]{2,1,0:T(8,128)(2,1)S(1)}, u32[]{:S(2)}, u32[]{:S(2)}) %collective-permute-start.4) | collective-permute-done | bytes 270368 | tf_op jit(solution)/shard_map/ppermute | solution.py:351
  45.4 0.0 copy-done.4
  45.4 5.1 %shard_map.148 = (bf16[16,128,128]{2,1,0:T(8,128)(2,1)S(1)}, bf16[2048,128]{1,0:T(8,128)(2,1)S(1)}, bf16[2048,128]{1,0:T(8,128)(2,1)S(1)}, f32[8,256]{1,0:T(8,128)S(1)}, f32[8,256]{1,0:T(8,128)S(1)}) custom-call(s32[1,3]{1,0:T(1,128)S(1)} %copy-done.4, bf16[2,528,128]{2,1,0:T(8,128)(2,1)S(1)} %get-tuple-element.25.q0, ...), custom_call_target="tpu_custom_call" | custom-call | flops 4294967296 | bytes 3145728 | tf_op jit(solution)/shard_map/pallas_call | solution.py:357
  50.6 0.0 copy-start.5
  50.6 0.0 copy-start.8
  50.6 0.0 collective-permute-done.side_ref
  50.6 3.1 %shard_map.149 = (bf16[16,256,128]{2,1,0:T(8,128)(2,1)}, f32[8,128]{1,0:T(8,128)S(1)}) custom-call(bf16[16,264,128]{2,1,0:T(8,128)(2,1)S(1)} %all-to-all-done.kv_ref, bf16[16,64,128]{2,1,0:T(8,128)(2,1)S(1)} %collective-permute-done.side_ref, bf16[16,128,128]{2,1,0:T(8,128)(2,1)S(1)} %get-tuple-element.27.prompt_ref, ...), custom_call_target="tpu_custom_call" | custom-call | flops 2147483648 | bytes 3145728 | tf_op jit(solution)/shard_map/pallas_call | solution.py:376
  53.8 0.0 copy-done.5
  53.8 0.0 copy-done.8
  53.8 0.0 copy-start.6
  53.8 6.9 %all-to-all-start.1 = ((bf16[16,256,128]{2,1,0:T(8,128)(2,1)}), bf16[16,256,128]{2,1,0:T(8,128)(2,1)S(1)}, u32[]{:S(2)}, u32[]{:S(2)}) async-start(bf16[16,256,128]{2,1,0:T(8,128)(2,1)} %get-tuple-element.33), calls=%async_computation.1 | async-start | bytes 2097152 | tf_op jit(solution)/shard_map/all_to_all | solution.py:343
  60.7 0.0 copy-done.6
  60.7 0.0 copy-start.9
  60.7 1.0 %copy-done.9 = bf16[2048,128]{1,0:T(8,128)(2,1)S(1)} copy-done((bf16[2048,128]{1,0:T(8,128)(2,1)S(1)}, bf16[2048,128]{1,0:T(8,128)(2,1)}, u32[]{:S(2)}) %copy-start.9) | copy-done | bytes 524312
  61.7 0.0 copy-start.10
  61.7 2.1 %shard_map.154 = bf16[512,128]{1,0:T(8,128)(2,1)S(1)} custom-call(f32[8,128]{1,0:T(8,128)S(1)} %get-tuple-element.32.margin_ref, bf16[16,264,128]{2,1,0:T(8,128)(2,1)S(1)} %all-to-all-done.kv_ref, bf16[16,64,128]{2,1,0:T(8,128)(2,1)S(1)} %collective-permute-done.side_ref, bf16[2048,128]{1,0:T(8,128)(2,1)S(1)} %copy-done.6, bf16[2048,128]{1,0:T(8,128)(2,1)S(1)} %copy-done.9, ...), custom_call_target="tpu_custom_call" | custom-call | flops 1207959552 | bytes 3145728 | tf_op jit(solution)/shard_map/pallas_call | solution.py:397
  63.8 0.0 copy-start.7
  63.9 3.4 %collective-permute-start.7 = (bf16[512,128]{1,0:T(8,128)(2,1)S(1)}, bf16[512,128]{1,0:T(8,128)(2,1)S(1)}, u32[]{:S(2)}, u32[]{:S(2)}) collective-permute-start(bf16[512,128]{1,0:T(8,128)(2,1)S(1)} %shard_map.154), channel_id=1, source_target_pairs={{0,1},{1,2},{2,3},{3,0},{4,5},{5,6},{6,7},{7,4},{8,9},{9,10},{10,1... | collective-permute-start | bytes 393224 | tf_op jit(solution)/shard_map/ppermute | solution.py:351
  67.3 0.0 copy-done.10
  67.3 2.1 %shard_map.150 = bf16[528,128]{1,0:T(8,128)(2,1)S(1)} custom-call(f32[8,128]{1,0:T(8,128)S(1)} %get-tuple-element.32.margin_ref, bf16[16,264,128]{2,1,0:T(8,128)(2,1)S(1)} %all-to-all-done.kv_ref, bf16[16,64,128]{2,1,0:T(8,128)(2,1)S(1)} %collective-permute-done.side_ref, bf16[2048,128]{1,0:T(8,128)(2,1)S(1)} %copy-done.6, bf16[2048,128]{1,0:T(8,128)(2,1)S(1)} %copy-done.10, ...), custom_call_target="tpu_custom_call" | custom-call | flops 1207959552 | bytes 3145728 | tf_op jit(solution)/shard_map/pallas_call | solution.py:397
  69.4 4.4 %collective-permute-start.5 = (bf16[528,128]{1,0:T(8,128)(2,1)S(1)}, bf16[528,128]{1,0:T(8,128)(2,1)S(1)}, u32[]{:S(2)}, u32[]{:S(2)}) collective-permute-start(bf16[528,128]{1,0:T(8,128)(2,1)S(1)} %shard_map.150), channel_id=1, source_target_pairs={{0,2},{1,3},{2,0},{3,1},{4,6},{5,7},{6,4},{7,5},{8,10},{9,11},{10,... | collective-permute-start | bytes 405512 | tf_op jit(solution)/shard_map/ppermute | solution.py:351
  73.8 0.0 copy-done.7
  73.8 2.1 %shard_map.153 = bf16[512,128]{1,0:T(8,128)(2,1)S(1)} custom-call(f32[8,128]{1,0:T(8,128)S(1)} %get-tuple-element.32.margin_ref, bf16[16,264,128]{2,1,0:T(8,128)(2,1)S(1)} %all-to-all-done.kv_ref, bf16[16,64,128]{2,1,0:T(8,128)(2,1)S(1)} %collective-permute-done.side_ref, bf16[2048,128]{1,0:T(8,128)(2,1)S(1)} %copy-done.7, bf16[2048,128]{1,0:T(8,128)(2,1)S(1)} %copy-done.10, ...), custom_call_target="tpu_custom_call" | custom-call | flops 1207959552 | bytes 3145728 | tf_op jit(solution)/shard_map/pallas_call | solution.py:397
  75.9 2.6 %collective-permute-start.6 = (bf16[512,128]{1,0:T(8,128)(2,1)S(1)}, bf16[512,128]{1,0:T(8,128)(2,1)S(1)}, u32[]{:S(2)}, u32[]{:S(2)}) collective-permute-start(bf16[512,128]{1,0:T(8,128)(2,1)S(1)} %shard_map.153), channel_id=1, source_target_pairs={{0,3},{1,0},{2,1},{3,2},{4,7},{5,4},{6,5},{7,6},{8,11},{9,8},{10,9... | collective-permute-start | bytes 393224 | tf_op jit(solution)/shard_map/ppermute | solution.py:351
  78.5 2.1 %shard_map.152.d0 = bf16[512,128]{1,0:T(8,128)(2,1)S(1)} custom-call(f32[8,128]{1,0:T(8,128)S(1)} %get-tuple-element.32.margin_ref, bf16[16,264,128]{2,1,0:T(8,128)(2,1)S(1)} %all-to-all-done.kv_ref, bf16[16,64,128]{2,1,0:T(8,128)(2,1)S(1)} %collective-permute-done.side_ref, bf16[2048,128]{1,0:T(8,128)(2,1)S(1)} %copy-done.7, ...), custom_call_target="tpu_custom_call" | custom-call | flops 1207959552 | bytes 3145728 | tf_op jit(solution)/shard_map/pallas_call | solution.py:397
  80.7 0.0 collective-permute-done.7.d3
  80.7 7.4 %collective-permute-done.6.d1 = bf16[512,128]{1,0:T(8,128)(2,1)S(1)} collective-permute-done((bf16[512,128]{1,0:T(8,128)(2,1)S(1)}, bf16[512,128]{1,0:T(8,128)(2,1)S(1)}, u32[]{:S(2)}, u32[]{:S(2)}) %collective-permute-start.6) | collective-permute-done | bytes 131104 | tf_op jit(solution)/shard_map/ppermute | solution.py:351
  88.0 0.0 collective-permute-done.5.d2
  88.0 0.9 shard_map.155
  88.9 0.5 slice.7
  89.4 0.0 all-to-all-done.1.part_ref
  89.4 1.4 %shard_map.151 = (bf16[1,64,256]{2,1,0:T(8,128)(2,1)}, bf16[1,64,256]{2,1,0:T(8,128)(2,1)}, bf16[1,2,32,256]{3,2,1,0:T(8,128)(2,1)}, bf16[1,2,32,256]{3,2,1,0:T(8,128)(2,1)}) custom-call(s32[1,3]{1,0:T(1,128)S(1)} %copy-done.4, f32[8,128]{1,0:T(8,128)S(1)} %get-tuple-element.32.margin_ref, bf16[528,128]{1,0:T(8,128)(2,1)S(1)} %collective-permute-done.5.d2, ...), custom_call_target="tpu_custom_call" | custom-call | bytes 1048576 | tf_op jit(solution)/shard_map/pallas_call | solution.py:467
  (2 shorter events, 0.1 us)
Async XLA Ops:
  2.6 8.9 %copy-start = (bf16[1,1,32,4096]{3,2,1,0:T(8,128)(2,1)S(1)}, bf16[1,1,32,4096]{3,2,1,0:T(8,128)(2,1)}, u32[]{:S(2)}) copy-start(bf16[1,1,32,4096]{3,2,1,0:T(8,128)(2,1)} %q_hbm.1) | copy-start | bytes 786436
  2.6 8.9 %copy-start.1 = (bf16[1,1,32,4096]{3,2,1,0:T(8,128)(2,1)S(1)}, bf16[1,1,32,4096]{3,2,1,0:T(8,128)(2,1)}, u32[]{:S(2)}) copy-start(bf16[1,1,32,4096]{3,2,1,0:T(8,128)(2,1)} %g_hbm.1) | copy-start | bytes 786436
  2.7 8.9 %copy-start.2 = (bf16[1,1,32,32]{3,2,1,0:T(8,128)(2,1)S(1)}, bf16[1,1,32,32]{3,2,1,0:T(8,128)(2,1)}, u32[]{:S(2)}) copy-start(bf16[1,1,32,32]{3,2,1,0:T(8,128)(2,1)} %lse_hbm.1) | copy-start | bytes 6148
  2.7 8.9 %copy-start.3 = (bf16[1,1,32,32]{3,2,1,0:T(8,128)(2,1)S(1)}, bf16[1,1,32,32]{3,2,1,0:T(8,128)(2,1)}, u32[]{:S(2)}) copy-start(bf16[1,1,32,32]{3,2,1,0:T(8,128)(2,1)} %delta_hbm.1) | copy-start | bytes 6148
  2.7 34.0 %all-to-all-start = ((bf16[16,264,128]{2,1,0:T(8,128)(2,1)}), bf16[16,264,128]{2,1,0:T(8,128)(2,1)S(1)}, u32[]{:S(2)}, u32[]{:S(2)}) async-start(bf16[16,264,128]{2,1,0:T(8,128)(2,1)} %shard_map.145), calls=%async_computation | async-start | bytes 2162688 | tf_op jit(solution)/shard_map/all_to_all | solution.py:343
  11.6 33.9 %copy-start.4 = (s32[1,3]{1,0:T(1,128)S(1)}, s32[1,3]{1,0:T(1,128)}, u32[]{:S(2)}) copy-start(s32[1,3]{1,0:T(1,128)} %lengths_ref.3) | copy-start | bytes 40
  12.1 5.0 %collective-permute-start.1 = (bf16[2,528,128]{2,1,0:T(8,128)(2,1)S(1)}, bf16[2,528,128]{2,1,0:T(8,128)(2,1)S(1)}, u32[]{:S(2)}, u32[]{:S(2)}) collective-permute-start(bf16[2,528,128]{2,1,0:T(8,128)(2,1)S(1)} %get-tuple-element.24), channel_id=1, source_target_pairs={{0,32},{32,0},{1,33},{33,1},{2,34},{34,2},{3,35},{35,3},{4,36},{36... | collective-permute-start | bytes 811016 | tf_op jit(solution)/shard_map/ppermute | solution.py:347
  17.1 26.3 %collective-permute-start.2 = (bf16[2,528,128]{2,1,0:T(8,128)(2,1)S(1)}, bf16[2,528,128]{2,1,0:T(8,128)(2,1)S(1)}, u32[]{:S(2)}, u32[]{:S(2)}) collective-permute-start(bf16[2,528,128]{2,1,0:T(8,128)(2,1)S(1)} %get-tuple-element.26), channel_id=1, source_target_pairs={{0,1},{1,2},{2,3},{3,0},{4,5},{5,6},{6,7},{7,4},{8,9},{9,10},{10,1... | collective-permute-start | bytes 811016 | tf_op jit(solution)/shard_map/ppermute | solution.py:351
  20.6 23.6 %collective-permute-start.3 = (bf16[2,528,128]{2,1,0:T(8,128)(2,1)S(1)}, bf16[2,528,128]{2,1,0:T(8,128)(2,1)S(1)}, u32[]{:S(2)}, u32[]{:S(2)}) collective-permute-start(bf16[2,528,128]{2,1,0:T(8,128)(2,1)S(1)} %get-tuple-element.25.q0), channel_id=1, source_target_pairs={{0,2},{1,3},{2,0},{3,1},{4,6},{5,7},{6,4},{7,5},{8,10},{9,11},{10,... | collective-permute-start | bytes 811016 | tf_op jit(solution)/shard_map/ppermute | solution.py:351
  24.1 21.3 %collective-permute-start.4 = (bf16[2,528,128]{2,1,0:T(8,128)(2,1)S(1)}, bf16[2,528,128]{2,1,0:T(8,128)(2,1)S(1)}, u32[]{:S(2)}, u32[]{:S(2)}) collective-permute-start(bf16[2,528,128]{2,1,0:T(8,128)(2,1)S(1)} %get-tuple-element.26), channel_id=1, source_target_pairs={{0,3},{1,0},{2,1},{3,2},{4,7},{5,4},{6,5},{7,6},{8,11},{9,8},{10,9... | collective-permute-start | bytes 811016 | tf_op jit(solution)/shard_map/ppermute | solution.py:351
  36.7 13.9 %collective-permute-start = (bf16[16,64,128]{2,1,0:T(8,128)(2,1)S(1)}, bf16[16,64,128]{2,1,0:T(8,128)(2,1)S(1)}, u32[]{:S(2)}, u32[]{:S(2)}) collective-permute-start(bf16[16,64,128]{2,1,0:T(8,128)(2,1)S(1)} %slice.8), channel_id=1, source_target_pairs={{0,32},{32,0},{1,33},{33,1},{2,34},{34,2},{3,35},{35,3},{4,36},{36... | collective-permute-start | bytes 786440 | tf_op jit(solution)/shard_map/ppermute | solution.py:347
  50.6 3.2 %copy-start.5 = (bf16[2048,128]{1,0:T(8,128)(2,1)}, bf16[2048,128]{1,0:T(8,128)(2,1)S(1)}, u32[]{:S(2)}) copy-start(bf16[2048,128]{1,0:T(8,128)(2,1)S(1)} %get-tuple-element.28.query_rows) | copy-start | bytes 1572868
  50.6 3.2 %copy-start.8 = (bf16[2048,128]{1,0:T(8,128)(2,1)}, bf16[2048,128]{1,0:T(8,128)(2,1)S(1)}, u32[]{:S(2)}) copy-start(bf16[2048,128]{1,0:T(8,128)(2,1)S(1)} %get-tuple-element.29.grad_rows) | copy-start | bytes 1572868
  53.8 6.9 %copy-start.6 = (bf16[2048,128]{1,0:T(8,128)(2,1)S(1)}, bf16[2048,128]{1,0:T(8,128)(2,1)}, u32[]{:S(2)}) copy-start(bf16[2048,128]{1,0:T(8,128)(2,1)} %copy-done.5) | copy-start | bytes 1572868
  53.8 35.6 %all-to-all-start.1 = ((bf16[16,256,128]{2,1,0:T(8,128)(2,1)}), bf16[16,256,128]{2,1,0:T(8,128)(2,1)S(1)}, u32[]{:S(2)}, u32[]{:S(2)}) async-start(bf16[16,256,128]{2,1,0:T(8,128)(2,1)} %get-tuple-element.33), calls=%async_computation.1 | async-start | bytes 2097152 | tf_op jit(solution)/shard_map/all_to_all | solution.py:343
  60.7 1.0 %copy-start.9 = (bf16[2048,128]{1,0:T(8,128)(2,1)S(1)}, bf16[2048,128]{1,0:T(8,128)(2,1)}, u32[]{:S(2)}) copy-start(bf16[2048,128]{1,0:T(8,128)(2,1)} %copy-done.8) | copy-start | bytes 1572868
  61.7 5.5 %copy-start.10 = (bf16[2048,128]{1,0:T(8,128)(2,1)S(1)}, bf16[2048,128]{1,0:T(8,128)(2,1)}, u32[]{:S(2)}) copy-start(bf16[2048,128]{1,0:T(8,128)(2,1)} %copy-done.8) | copy-start | bytes 1572868
  63.8 9.9 %copy-start.7 = (bf16[2048,128]{1,0:T(8,128)(2,1)S(1)}, bf16[2048,128]{1,0:T(8,128)(2,1)}, u32[]{:S(2)}) copy-start(bf16[2048,128]{1,0:T(8,128)(2,1)} %copy-done.5) | copy-start | bytes 1572868
  63.9 16.8 %collective-permute-start.7 = (bf16[512,128]{1,0:T(8,128)(2,1)S(1)}, bf16[512,128]{1,0:T(8,128)(2,1)S(1)}, u32[]{:S(2)}, u32[]{:S(2)}) collective-permute-start(bf16[512,128]{1,0:T(8,128)(2,1)S(1)} %shard_map.154), channel_id=1, source_target_pairs={{0,1},{1,2},{2,3},{3,0},{4,5},{5,6},{6,7},{7,4},{8,9},{9,10},{10,1... | collective-permute-start | bytes 393224 | tf_op jit(solution)/shard_map/ppermute | solution.py:351
  69.4 18.6 %collective-permute-start.5 = (bf16[528,128]{1,0:T(8,128)(2,1)S(1)}, bf16[528,128]{1,0:T(8,128)(2,1)S(1)}, u32[]{:S(2)}, u32[]{:S(2)}) collective-permute-start(bf16[528,128]{1,0:T(8,128)(2,1)S(1)} %shard_map.150), channel_id=1, source_target_pairs={{0,2},{1,3},{2,0},{3,1},{4,6},{5,7},{6,4},{7,5},{8,10},{9,11},{10,... | collective-permute-start | bytes 405512 | tf_op jit(solution)/shard_map/ppermute | solution.py:351
  75.9 12.1 %collective-permute-start.6 = (bf16[512,128]{1,0:T(8,128)(2,1)S(1)}, bf16[512,128]{1,0:T(8,128)(2,1)S(1)}, u32[]{:S(2)}, u32[]{:S(2)}) collective-permute-start(bf16[512,128]{1,0:T(8,128)(2,1)S(1)} %shard_map.153), channel_id=1, source_target_pairs={{0,3},{1,0},{2,1},{3,2},{4,7},{5,4},{6,5},{7,6},{8,11},{9,8},{10,9... | collective-permute-start | bytes 393224 | tf_op jit(solution)/shard_map/ppermute | solution.py:351

commit v7 on v6

--- a/solution.py
+++ b/solution.py
@@ -29,6 +29,7 @@
 SCALE = LANES**-0.5
 DEAD = 1e30
 BLOCK = 512
+PROMPT_BLOCK = 256
 MARGIN_ROWS = 8
 
 
@@ -197,24 +198,28 @@
     return slice(tile * TILE, (tile + 1) * TILE)
 
 
-def prompt_kernel(
-    lengths_ref, q0, q1, q2, q3, kv_ref, out_ref, query_rows, grad_rows, lse_ref, delta_ref, weights, score_grads
-):
-    for k, ref in enumerate((q0, q1, q2, q3)):
+def prompt_kernel(first_half, lengths_ref, qa, qb, kv_ref, *refs):
+    if first_half:
+        key_sum, value_sum = refs[:2]
+    else:
+        key_sum, value_sum, out_ref = refs[:3]
+    query_rows, grad_rows, lse_ref, delta_ref, weights, score_grads = refs[-6:]
+    for n, ref in enumerate((qa, qb)):
         for j in range(2):
-            t = j * X + k
+            t = j * 2 + n
             at = tile_rows(t)
             query_rows[at, :] = ref[j, 0:TILE, :]
             grad_rows[at, :] = ref[j, TILE : 2 * TILE, :]
+            k = n if first_half else 2 + n
             lse, delta = row_stats(lengths_ref, ref[j, 2 * TILE :, :], k, j)
             lse_ref[t : t + 1, :], delta_ref[t : t + 1, :] = lse, delta
-    per = BLOCK // PROMPT
+    per = PROMPT_BLOCK // PROMPT
 
     def first(c, slot):
         rows = slice(c * per, (c + 1) * per)
-        key = kv_ref[rows, 0:PROMPT, :].reshape(BLOCK, LANES)
-        value = kv_ref[rows, PROMPT : 2 * PROMPT, :].reshape(BLOCK, LANES)
-        for t in range(2 * X):
+        key = kv_ref[rows, 0:PROMPT, :].reshape(PROMPT_BLOCK, LANES)
+        value = kv_ref[rows, PROMPT : 2 * PROMPT, :].reshape(PROMPT_BLOCK, LANES)
+        for t in range(X):
             at = tile_rows(t)
             weights[slot, :, at], score_grads[slot, :, at] = cell(
                 key, value, query_rows[at, :], grad_rows[at, :], lse_ref[t : t + 1, :], delta_ref[t : t + 1, :]
@@ -222,19 +227,24 @@
 
     def second(c, slot):
         value_grad = dot(weights[slot], grad_rows[...], ((1,), (0,)))
-        key_grad = dot(score_grads[slot], query_rows[...], ((1,), (0,))) * SCALE
-        shape = (per, PROMPT, LANES)
-        to = slice(c * per, (c + 1) * per)
-        out_ref[to, 0:PROMPT, :] = key_grad.astype(bf16).reshape(shape)
-        out_ref[to, PROMPT:, :] = value_grad.astype(bf16).reshape(shape)
+        key_grad = dot(score_grads[slot], query_rows[...], ((1,), (0,)))
+        at = slice(c * PROMPT_BLOCK, (c + 1) * PROMPT_BLOCK)
+        if first_half:
+            key_sum[at, :], value_sum[at, :] = key_grad, value_grad
+        else:
+            shape = (per, PROMPT, LANES)
+            to = slice(c * per, (c + 1) * per)
+            out_ref[to, 0:PROMPT, :] = ((key_sum[at, :] + key_grad) * SCALE).astype(bf16).reshape(shape)
+            out_ref[to, PROMPT:, :] = (value_sum[at, :] + value_grad).astype(bf16).reshape(shape)
 
     staged([(c,) for c in range(PEERS_N // per)], first, second)
 
 
 def resp_kernel(
-    kv_ref, side_ref, prompt_ref, query_rows, grad_rows, lse_ref, delta_ref,
+    kv_ref, side_ref, prompt_ref, query_a, grad_a, lse_a, delta_a, query_b, grad_b, lse_b, delta_b,
     out_hbm, margin_ref, weights, score_grads, parts, sems,
 ):
+    halves = ((query_a, grad_a, lse_a, delta_a), (query_b, grad_b, lse_b, delta_b))
     copies = [pltpu.make_async_copy(prompt_ref, out_hbm.at[:, 0 : 2 * PROMPT, :], sems.at[0])]
     copies[0].start()
     margin = jnp.sum(kv_ref[:, KV_ROWS:, :].astype(f32), axis=(0, 1), keepdims=True).reshape(1, LANES)
@@ -251,7 +261,8 @@
         value = ref[rows, start + POS : start + SIDE, :].reshape(BLOCK, LANES)
         positions = key_positions(c, BLOCK)
         for k in range(X):
-            t = j * X + k
+            query_rows, grad_rows, lse_ref, delta_ref = halves[k // 2]
+            t = j * 2 + k % 2
             at, to = tile_rows(t), tile_rows(k)
             weights[slot, :, to], score_grads[slot, :, to] = cell(
                 key,
@@ -264,9 +275,15 @@
             )
 
     def second(j, c, slot):
-        rows = slice(j * X * TILE, (j + 1) * X * TILE)
-        value_grad = dot(weights[slot], grad_rows[rows, :], ((1,), (0,)))
-        key_grad = dot(score_grads[slot], query_rows[rows, :], ((1,), (0,))) * SCALE
+        rows = slice(j * 2 * TILE, (j + 1) * 2 * TILE)
+        value_grad, key_grad = None, None
+        for n, (query_rows, grad_rows, _, _) in enumerate(halves):
+            columns = slice(n * 2 * TILE, (n + 1) * 2 * TILE)
+            value_term = dot(weights[slot, :, columns], grad_rows[rows, :], ((1,), (0,)))
+            key_term = dot(score_grads[slot, :, columns], query_rows[rows, :], ((1,), (0,)))
+            value_grad = value_term if n == 0 else value_grad + value_term
+            key_grad = key_term if n == 0 else key_grad + key_term
+        key_grad *= SCALE
         shape = (per, POS, LANES)
         n = j * blocks + c
         parts[n, :, 0:POS, :] = key_grad.astype(bf16).reshape(shape)
@@ -281,25 +298,32 @@
         copy.wait()
 
 
-def query_kernel(k, margin_ref, kv_ref, side_ref, query_rows, grad_rows, lse_ref, delta_ref, out_ref):
+def query_kernel(k, lengths_ref, margin_ref, q_ref, kv_ref, side_ref, out_ref):
+    items = []
     for j in range(2):
-        t = j * X + k
-        query, grad = query_rows[tile_rows(t), :], grad_rows[tile_rows(t), :]
-        lse, delta = lse_ref[t : t + 1, :], delta_ref[t : t + 1, :]
-        total = None
         resp, start = ((kv_ref, 2 * PROMPT), (side_ref, 0))[j]
-        parts = [(kv_ref, c, PROMPT, 0, None) for c in range(PEERS_N * PROMPT // BLOCK)]
-        for c in range(PEERS_N * POS // BLOCK):
-            parts.append((resp, c, POS, start, key_positions(c, BLOCK) <= row_position(k)))
-        for ref, c, count, start, allowed in parts:
+        items += [(j, kv_ref, c, PROMPT, 0) for c in range(PEERS_N * PROMPT // BLOCK)]
+        items += [(j, resp, c, POS, start) for c in range(PEERS_N * POS // BLOCK)]
+    totals, waiting = [None, None], None
+    for item in items + [None]:
+        if item:
+            j, ref, c, count, start = item
             per = BLOCK // count
             rows = slice(c * per, (c + 1) * per)
             key = ref[rows, start : start + count, :].reshape(BLOCK, LANES)
             value = ref[rows, start + count : start + 2 * count, :].reshape(BLOCK, LANES)
-            _, score_grads = cell(key, value, query, grad, lse, delta, allowed)
-            term = dot(score_grads, key, ((0,), (0,)))
-            total = term if total is None else total + term
-        out_ref[tile_rows(j), :] = (total * SCALE).astype(bf16)
+            allowed = key_positions(c, BLOCK) <= row_position(k) if count == POS else None
+            lse, delta = row_stats(lengths_ref, q_ref[j, 2 * TILE :, :], k, j)
+            _, score_grads = cell(
+                key, value, q_ref[j, 0:TILE, :], q_ref[j, TILE : 2 * TILE, :], lse, delta, allowed
+            )
+        if waiting:
+            n, grads, keys = waiting
+            term = dot(grads, keys, ((0,), (0,)))
+            totals[n] = term if totals[n] is None else totals[n] + term
+        waiting = (j, score_grads, key)
+    for j in range(2):
+        out_ref[tile_rows(j), :] = (totals[j] * SCALE).astype(bf16)
     if k == 2:
         out_ref[2 * TILE :, :] = split_margin(margin_ref[0:1, 0:1], STAT_ROWS)
 
@@ -353,21 +377,26 @@
 
 def prompt_call(lengths, rows, kv):
     shape = jax.ShapeDtypeStruct
-    count = 2 * X * TILE
-    return call(
-        prompt_kernel,
-        (
-            shape((PEERS_N, 2 * PROMPT, LANES), bf16),
-            shape((count, LANES), bf16),
-            shape((count, LANES), bf16),
-            shape((2 * X, TILE), f32),
-            shape((2 * X, TILE), f32),
-        ),
+    count = X * TILE
+    tables = (
+        shape((count, LANES), bf16),
+        shape((count, LANES), bf16),
+        shape((X, TILE), f32),
+        shape((X, TILE), f32),
+    )
+    sums = (shape((PEERS_N * PROMPT, LANES), f32),) * 2
+    scratch = (pltpu.VMEM((2, PROMPT_BLOCK, count), bf16), pltpu.VMEM((2, PROMPT_BLOCK, count), bf16))
+    cost = dict(flops=2 * 2 * 2048 * 1024 * 128 * 2, size=2 * 2**20, scratch=scratch)
+    key_sum, value_sum, *first = call(functools.partial(prompt_kernel, True), sums + tables, "svvv", **cost)(
+        lengths, rows[0], rows[1], kv
+    )
+    part, *second = call(
+        functools.partial(prompt_kernel, False),
+        (shape((PEERS_N, 2 * PROMPT, LANES), bf16),) + tables,
         "svvvvv",
-        scratch=(pltpu.VMEM((2, BLOCK, count), bf16), pltpu.VMEM((2, BLOCK, count), bf16)),
-        flops=4 * 2 * 2048 * 1024 * 128 * 2,
-        size=3 * 2**20,
-    )(lengths, *rows, kv)
+        **cost,
+    )(lengths, rows[2], rows[3], kv, key_sum, value_sum)
+    return part, *first, *second
 
 
 def resp_call(kv, side, prompt_part, *rows):
@@ -379,7 +408,7 @@
             shape((PEERS_N, KV_ROWS, LANES), bf16),
             shape((8, LANES), f32),
         ),
-        "vvvvvvv",
+        "v" * 11,
         out_spaces="av",
         scratch=(
             pltpu.VMEM((2, BLOCK, X * TILE), bf16),
@@ -392,15 +421,15 @@
     )(kv, side, prompt_part, *rows)
 
 
-def query_call(k, margin, kv, side, *rows):
+def query_call(k, lengths, margin, rows, kv, side):
     extra = STAT_ROWS if k == 2 else 0
     return call(
         functools.partial(query_kernel, k),
         jax.ShapeDtypeStruct((2 * TILE + extra, LANES), bf16),
-        "vvvvvvv",
+        "svvvv",
         flops=3 * 2 * 512 * 1536 * 128 * 2,
         size=3 * 2**20,
-    )(margin, kv, side, *rows)
+    )(lengths, margin, rows, kv, side)
 
 
 def per_device(
@@ -452,9 +481,9 @@
     rows = (same, shift(odd, 1), shift(same, 2), shift(odd, 3))
 
     side = cross(kv[:, KV_ROWS - SIDE : KV_ROWS, :])
-    prompt_part, *rows = prompt_call(lengths, rows, kv)
-    part, margin = resp_call(kv, side, prompt_part, *rows)
-    grads = [query_call(k, margin, kv, side, *rows) for k in range(X)]
+    prompt_part, *tables = prompt_call(lengths, rows, kv)
+    part, margin = resp_call(kv, side, prompt_part, *tables)
+    grads = [query_call(k, lengths, margin, rows[k], kv, side) for k in range(X)]
     part = swap(part)
     back = [grads[0]] + [shift(grads[k], X - k) for k in range(1, X)]
     query_grad, gate = call(

time: 91.4 us -> 89.5 us (0.979)
  the two profiles are of different devices: /device:TPU:1 before, /device:TPU:6 now
where the time goes in v7:
time: 89.5 us; the launch traced here: 88.9 us
  starting transfers between devices  40.7 us (45%)
  waiting for transfers between devices  23.7 us (26%)
  Pallas kernels  22.1 us (25%)
  local copies, waits for them, and re-layouts  1.51 us (2%)
    ppermute x6, starting transfers between devices, shift(): return lax.ppermute(values, ROW, [(i, (i + by) % X) for i in range(X)])  20.1 us
    all_to_all x2, starting transfers between devices, swap(): lax.all_to_all(values, PEERS, split_axis=0, concat_axis=0, tiled=True)  16.7 us
    all_to_all x2, waiting for transfers between devices, swap(): lax.all_to_all(values, PEERS, split_axis=0, concat_axis=0, tiled=True)  13.9 us
    ppermute x6, waiting for transfers between devices, shift(): return lax.ppermute(values, ROW, [(i, (i + by) % X) for i in range(X)])  8.3 us
    pallas_call x4, Pallas kernels, query_call(): call(functools.partial(query_kernel, k), jax.ShapeDtypeStruct((2 * TILE +...  8.14 us
    ppermute x2, starting transfers between devices, cross(): return lax.ppermute(values, 'pair', [(0, 1), (1, 0)])  3.84 us
    pallas_call x1, Pallas kernels, resp_call(): call(resp_kernel, (shape((PEERS_N, KV_ROWS, LANES), bf16), shape((8, LANE...  3.12 us
    pallas_call x1, Pallas kernels, prompt_call(): call(functools.partial(prompt_kernel, False), (shape((PEERS_N, 2 * PROMPT...  2.99 us
  transfers between devices with their start and end apart: 10, of which 4 were waited for; matrix products, arithmetic and copies ran while one was open for 1% of the time, Pallas kernels for 18%

profile of v7, /device:TPU:6, one launch (start us, length us, event | category | flops | bytes accessed | tf_op | source)
XLA Modules:
  0.0 88.9 jit_solution(16816173785153638202)
XLA Ops:
  0.6 2.0 %shard_map.145 = bf16[16,264,128]{2,1,0:T(8,128)(2,1)} custom-call(s32[1,3]{1,0:T(1,128)} %lengths_ref.13, f32[1,2,32]{2,1,0:T(2,128)} %logratio_hbm.1, bf16[1,64,256]{2,1,0:T(8,128)(2,1)} %pk_hbm.1, bf16[1,64,256]{2,1,0:T(8,128)(2,1)} %pv_hbm.1, bf16[1,1,32,512]{3,2,1,0:T(8,128)(2,1)} %rk_hbm.1, bf16[1,1,32,512]{3,2,1,0:T(8,128)(2,1)} %rv_hbm.1), custom_call_target="tpu_custom_call" | custom-call | bytes 2097152 | tf_op jit(solution)/shard_map/pallas_call | solution.py:448
  2.6 0.0 copy-start
  2.7 0.0 copy-start.1
  2.7 0.0 copy-start.2
  2.7 0.0 copy-start.3
  2.7 8.7 %all-to-all-start = ((bf16[16,264,128]{2,1,0:T(8,128)(2,1)}), bf16[16,264,128]{2,1,0:T(8,128)(2,1)S(1)}, u32[]{:S(2)}, u32[]{:S(2)}) async-start(bf16[16,264,128]{2,1,0:T(8,128)(2,1)} %shard_map.145), calls=%async_computation | async-start | bytes 2162688 | tf_op jit(solution)/shard_map/all_to_all | solution.py:367
  11.4 0.0 copy-done
  11.4 0.0 copy-done.1
  11.4 0.0 copy-done.2
  11.4 0.0 copy-done.3
  11.4 0.0 copy-start.4
  11.5 0.6 shard_map.146
  12.0 1.9 %collective-permute-start.1 = (bf16[2,528,128]{2,1,0:T(8,128)(2,1)S(1)}, bf16[2,528,128]{2,1,0:T(8,128)(2,1)S(1)}, u32[]{:S(2)}, u32[]{:S(2)}) collective-permute-start(bf16[2,528,128]{2,1,0:T(8,128)(2,1)S(1)} %get-tuple-element.30), channel_id=1, source_target_pairs={{0,32},{32,0},{1,33},{33,1},{2,34},{34,2},{3,35},{35,3},{4,36},{36... | collective-permute-start | bytes 811016 | tf_op jit(solution)/shard_map/ppermute | solution.py:371
  14.0 1.5 %collective-permute-done.1.other_ref = bf16[2,528,128]{2,1,0:T(8,128)(2,1)S(1)} collective-permute-done((bf16[2,528,128]{2,1,0:T(8,128)(2,1)S(1)}, bf16[2,528,128]{2,1,0:T(8,128)(2,1)S(1)}, u32[]{:S(2)}, u32[]{:S(2)}) %collective-permute-start.1) | collective-permute-done | bytes 270368 | tf_op jit(solution)/shard_map/ppermute | solution.py:371
  15.5 2.9 %collective-permute-start.4 = (bf16[2,528,128]{2,1,0:T(8,128)(2,1)S(1)}, bf16[2,528,128]{2,1,0:T(8,128)(2,1)S(1)}, u32[]{:S(2)}, u32[]{:S(2)}) collective-permute-start(bf16[2,528,128]{2,1,0:T(8,128)(2,1)S(1)} %get-tuple-element.32), channel_id=1, source_target_pairs={{0,1},{1,2},{2,3},{3,0},{4,5},{5,6},{6,7},{7,4},{8,9},{9,10},{10,1... | collective-permute-start | bytes 811016 | tf_op jit(solution)/shard_map/ppermute | solution.py:375
  18.4 2.9 %collective-permute-start.3 = (bf16[2,528,128]{2,1,0:T(8,128)(2,1)S(1)}, bf16[2,528,128]{2,1,0:T(8,128)(2,1)S(1)}, u32[]{:S(2)}, u32[]{:S(2)}) collective-permute-start(bf16[2,528,128]{2,1,0:T(8,128)(2,1)S(1)} %get-tuple-element.32), channel_id=1, source_target_pairs={{0,3},{1,0},{2,1},{3,2},{4,7},{5,4},{6,5},{7,6},{8,11},{9,8},{10,9... | collective-permute-start | bytes 811016 | tf_op jit(solution)/shard_map/ppermute | solution.py:375
  21.4 4.1 %collective-permute-start.2 = (bf16[2,528,128]{2,1,0:T(8,128)(2,1)S(1)}, bf16[2,528,128]{2,1,0:T(8,128)(2,1)S(1)}, u32[]{:S(2)}, u32[]{:S(2)}) collective-permute-start(bf16[2,528,128]{2,1,0:T(8,128)(2,1)S(1)} %get-tuple-element.31.qa.q_ref), channel_id=1, source_target_pairs={{0,2},{1,3},{2,0},{3,1},{4,6},{5,7},{6,4},{7,5},{8,10},{9,11},{10,... | collective-permute-start | bytes 811016 | tf_op jit(solution)/shard_map/ppermute | solution.py:375
  25.5 13.9 %all-to-all-done.kv_ref = bf16[16,264,128]{2,1,0:T(8,128)(2,1)S(1)} async-done(((bf16[16,264,128]{2,1,0:T(8,128)(2,1)}), bf16[16,264,128]{2,1,0:T(8,128)(2,1)S(1)}, u32[]{:S(2)}, u32[]{:S(2)}) %all-to-all-start) | async-done | bytes 1081376 | tf_op jit(solution)/shard_map/all_to_all | solution.py:367
  39.4 1.9 %collective-permute-start = (bf16[16,64,128]{2,1,0:T(8,128)(2,1)S(1)}, bf16[16,64,128]{2,1,0:T(8,128)(2,1)S(1)}, u32[]{:S(2)}, u32[]{:S(2)}) collective-permute-start(bf16[16,64,128]{2,1,0:T(8,128)(2,1)S(1)} %slice.8), channel_id=1, source_target_pairs={{0,32},{32,0},{1,33},{33,1},{2,34},{34,2},{3,35},{35,3},{4,36},{36... | collective-permute-start | bytes 786440 | tf_op jit(solution)/shard_map/ppermute | solution.py:371
  41.3 0.0 collective-permute-done.4.qb.q_ref
  41.4 0.0 copy-done.4
  41.4 3.0 %shard_map.148 = (f32[1024,128]{1,0:T(8,128)S(1)}, f32[1024,128]{1,0:T(8,128)S(1)}, bf16[1024,128]{1,0:T(8,128)(2,1)S(1)}, bf16[1024,128]{1,0:T(8,128)(2,1)S(1)}...) custom-call(s32[1,3]{1,0:T(1,128)S(1)} %copy-done.4, bf16[2,528,128]{2,1,0:T(8,128)(2,1)S(1)} %get-tuple-element.31.qa.q_ref, ...), custom_call_target="tpu_custom_call" | custom-call | flops 2147483648 | bytes 2097152 | tf_op jit(solution)/shard_map/pallas_call | solution.py:390
  44.3 0.0 collective-permute-done.3.qb.q_ref
  44.3 0.6 collective-permute-done.2.qa.q_ref
  44.9 3.0 %shard_map.149 = (bf16[16,128,128]{2,1,0:T(8,128)(2,1)S(1)}, bf16[1024,128]{1,0:T(8,128)(2,1)S(1)}, bf16[1024,128]{1,0:T(8,128)(2,1)S(1)}, f32[4,256]{1,0:T(4,128)S(1)}, f32[4,256]{1,0:T(4,128)S(1)}) custom-call(s32[1,3]{1,0:T(1,128)S(1)} %copy-done.4, bf16[2,528,128]{2,1,0:T(8,128)(2,1)S(1)} %collective-permute-done.2.qa.q_ref, ...), custom_call_target="tpu_custom_call" | custom-call | flops 2147483648 | bytes 2097152 | tf_op jit(solution)/shard_map/pallas_call | solution.py:393
  47.9 0.0 collective-permute-done.side_ref
  47.9 0.0 copy-start.5
  47.9 3.1 %shard_map.150 = (bf16[16,256,128]{2,1,0:T(8,128)(2,1)}, f32[8,128]{1,0:T(8,128)S(1)}) custom-call(bf16[16,264,128]{2,1,0:T(8,128)(2,1)S(1)} %all-to-all-done.kv_ref, bf16[16,64,128]{2,1,0:T(8,128)(2,1)S(1)} %collective-permute-done.side_ref, bf16[16,128,128]{2,1,0:T(8,128)(2,1)S(1)} %get-tuple-element.35.prompt_ref, ...), custom_call_target="tpu_custom_call" | custom-call | flops 2147483648 | bytes 3145728 | tf_op jit(solution)/shard_map/pallas_call | solution.py:405
  51.1 0.0 copy-done.5
  51.1 8.0 %all-to-all-start.1 = ((bf16[16,256,128]{2,1,0:T(8,128)(2,1)}), bf16[16,256,128]{2,1,0:T(8,128)(2,1)S(1)}, u32[]{:S(2)}, u32[]{:S(2)}) async-start(bf16[16,256,128]{2,1,0:T(8,128)(2,1)} %get-tuple-element.45), calls=%async_computation.1 | async-start | bytes 2097152 | tf_op jit(solution)/shard_map/all_to_all | solution.py:367
  59.1 0.0 copy-start.6
  59.1 0.9 %copy-done.6 = bf16[16,64,128]{2,1,0:T(8,128)(2,1)S(1)} copy-done((bf16[16,64,128]{2,1,0:T(8,128)(2,1)S(1)}, bf16[16,64,128]{2,1,0:T(8,128)(2,1)}, u32[]{:S(2)}) %copy-start.6) | copy-done | bytes 262168
  60.1 2.0 %shard_map.154 = bf16[512,128]{1,0:T(8,128)(2,1)S(1)} custom-call(s32[1,3]{1,0:T(1,128)S(1)} %copy-done.4, f32[8,128]{1,0:T(8,128)S(1)} %get-tuple-element.44.margin_ref, bf16[2,528,128]{2,1,0:T(8,128)(2,1)S(1)} %collective-permute-done.4.qb.q_ref, bf16[16,264,128]{2,1,0:T(8,128)(2,1)S(1)} %all-to-all-done.kv_ref, bf16[16,64,128]{2,1,0:T(8,128)(2,1)S(1)} %copy-done.6), custom_call_target="tpu_custom_call" | custom-call | flops 1207959552 | bytes 3145728 | tf_op jit(solution)/shard_map/pallas_call | solution.py:426
  62.1 2.0 %collective-permute-start.6 = (bf16[512,128]{1,0:T(8,128)(2,1)S(1)}, bf16[512,128]{1,0:T(8,128)(2,1)S(1)}, u32[]{:S(2)}, u32[]{:S(2)}) collective-permute-start(bf16[512,128]{1,0:T(8,128)(2,1)S(1)} %shard_map.154), channel_id=1, source_target_pairs={{0,3},{1,0},{2,1},{3,2},{4,7},{5,4},{6,5},{7,6},{8,11},{9,8},{10,9... | collective-permute-start | bytes 393224 | tf_op jit(solution)/shard_map/ppermute | solution.py:375
  64.1 2.0 %shard_map.151 = bf16[528,128]{1,0:T(8,128)(2,1)S(1)} custom-call(s32[1,3]{1,0:T(1,128)S(1)} %copy-done.4, f32[8,128]{1,0:T(8,128)S(1)} %get-tuple-element.44.margin_ref, bf16[2,528,128]{2,1,0:T(8,128)(2,1)S(1)} %collective-permute-done.2.qa.q_ref, bf16[16,264,128]{2,1,0:T(8,128)(2,1)S(1)} %all-to-all-done.kv_ref, bf16[16,64,128]{2,1,0:T(8,128)(2,1)S(1)} %copy-done.6), custom_call_target="tpu_custom_call" | custom-call | flops 1207959552 | bytes 3145728 | tf_op jit(solution)/shard_map/pallas_call | solution.py:426
  66.2 3.7 %collective-permute-start.5 = (bf16[528,128]{1,0:T(8,128)(2,1)S(1)}, bf16[528,128]{1,0:T(8,128)(2,1)S(1)}, u32[]{:S(2)}, u32[]{:S(2)}) collective-permute-start(bf16[528,128]{1,0:T(8,128)(2,1)S(1)} %shard_map.151), channel_id=1, source_target_pairs={{0,2},{1,3},{2,0},{3,1},{4,6},{5,7},{6,4},{7,5},{8,10},{9,11},{10,... | collective-permute-start | bytes 405512 | tf_op jit(solution)/shard_map/ppermute | solution.py:375
  69.9 2.0 %shard_map.155 = bf16[512,128]{1,0:T(8,128)(2,1)S(1)} custom-call(s32[1,3]{1,0:T(1,128)S(1)} %copy-done.4, f32[8,128]{1,0:T(8,128)S(1)} %get-tuple-element.44.margin_ref, bf16[2,528,128]{2,1,0:T(8,128)(2,1)S(1)} %collective-permute-done.3.qb.q_ref, bf16[16,264,128]{2,1,0:T(8,128)(2,1)S(1)} %all-to-all-done.kv_ref, bf16[16,64,128]{2,1,0:T(8,128)(2,1)S(1)} %copy-done.6), custom_call_target="tpu_custom_call" | custom-call | flops 1207959552 | bytes 3145728 | tf_op jit(solution)/shard_map/pallas_call | solution.py:426
  71.9 4.4 %collective-permute-start.7 = (bf16[512,128]{1,0:T(8,128)(2,1)S(1)}, bf16[512,128]{1,0:T(8,128)(2,1)S(1)}, u32[]{:S(2)}, u32[]{:S(2)}) collective-permute-start(bf16[512,128]{1,0:T(8,128)(2,1)S(1)} %shard_map.155), channel_id=1, source_target_pairs={{0,1},{1,2},{2,3},{3,0},{4,5},{5,6},{6,7},{7,4},{8,9},{9,10},{10,1... | collective-permute-start | bytes 393224 | tf_op jit(solution)/shard_map/ppermute | solution.py:375
  76.4 2.0 %shard_map.153.d0 = bf16[512,128]{1,0:T(8,128)(2,1)S(1)} custom-call(s32[1,3]{1,0:T(1,128)S(1)} %copy-done.4, f32[8,128]{1,0:T(8,128)S(1)} %get-tuple-element.44.margin_ref, bf16[2,528,128]{2,1,0:T(8,128)(2,1)S(1)} %get-tuple-element.31.qa.q_ref, bf16[16,264,128]{2,1,0:T(8,128)(2,1)S(1)} %all-to-all-done.kv_ref, bf16[16,64,128]{2,1,0:T(8,128)(2,1)S(1)} %copy-done.6), custom_call_target="tpu_custom_call" | custom-call | flops 1207959552 | bytes 3145728 | tf_op jit(solution)/shard_map/pallas_call | solution.py:426
  78.4 0.0 collective-permute-done.6.d1
  78.4 7.7 %collective-permute-done.7.d3 = bf16[512,128]{1,0:T(8,128)(2,1)S(1)} collective-permute-done((bf16[512,128]{1,0:T(8,128)(2,1)S(1)}, bf16[512,128]{1,0:T(8,128)(2,1)S(1)}, u32[]{:S(2)}, u32[]{:S(2)}) %collective-permute-start.7) | collective-permute-done | bytes 131104 | tf_op jit(solution)/shard_map/ppermute | solution.py:375
  86.1 0.0 collective-permute-done.5.d2
  86.1 0.9 %shard_map.156 = (bf16[1,2,32,2048]{3,2,1,0:T(8,128)(2,1)}, f32[8,128]{1,0:T(8,128)S(1)}) custom-call(f32[8,128]{1,0:T(8,128)S(1)} %get-tuple-element.44.margin_ref, bf16[512,128]{1,0:T(8,128)(2,1)S(1)} %shard_map.153.d0, bf16[512,128]{1,0:T(8,128)(2,1)S(1)} %collective-permute-done.6.d1, bf16[528,128]{1,0:T(8,128)(2,1)S(1)} %collective-permute-done.5.d2, ...), custom_call_target="tpu_custom_call" | custom-call | bytes 1048576 | tf_op jit(solution)/shard_map/pallas_call | solution.py:489
  87.0 0.5 slice.7
  87.5 0.0 all-to-all-done.1.part_ref
  87.5 1.4 %shard_map.152 = (bf16[1,64,256]{2,1,0:T(8,128)(2,1)}, bf16[1,64,256]{2,1,0:T(8,128)(2,1)}, bf16[1,2,32,256]{3,2,1,0:T(8,128)(2,1)}, bf16[1,2,32,256]{3,2,1,0:T(8,128)(2,1)}) custom-call(s32[1,3]{1,0:T(1,128)S(1)} %copy-done.4, f32[8,128]{1,0:T(8,128)S(1)} %get-tuple-element.44.margin_ref, bf16[528,128]{1,0:T(8,128)(2,1)S(1)} %collective-permute-done.5.d2, ...), custom_call_target="tpu_custom_call" | custom-call | bytes 1048576 | tf_op jit(solution)/shard_map/pallas_call | solution.py:496
  (2 shorter events, 0.1 us)
Async XLA Ops:
  2.6 8.8 %copy-start = (bf16[1,1,32,4096]{3,2,1,0:T(8,128)(2,1)S(1)}, bf16[1,1,32,4096]{3,2,1,0:T(8,128)(2,1)}, u32[]{:S(2)}) copy-start(bf16[1,1,32,4096]{3,2,1,0:T(8,128)(2,1)} %q_hbm.1) | copy-start | bytes 786436
  2.7 8.8 %copy-start.1 = (bf16[1,1,32,4096]{3,2,1,0:T(8,128)(2,1)S(1)}, bf16[1,1,32,4096]{3,2,1,0:T(8,128)(2,1)}, u32[]{:S(2)}) copy-start(bf16[1,1,32,4096]{3,2,1,0:T(8,128)(2,1)} %g_hbm.1) | copy-start | bytes 786436
  2.7 8.8 %copy-start.2 = (bf16[1,1,32,32]{3,2,1,0:T(8,128)(2,1)S(1)}, bf16[1,1,32,32]{3,2,1,0:T(8,128)(2,1)}, u32[]{:S(2)}) copy-start(bf16[1,1,32,32]{3,2,1,0:T(8,128)(2,1)} %lse_hbm.1) | copy-start | bytes 6148
  2.7 8.8 %copy-start.3 = (bf16[1,1,32,32]{3,2,1,0:T(8,128)(2,1)S(1)}, bf16[1,1,32,32]{3,2,1,0:T(8,128)(2,1)}, u32[]{:S(2)}) copy-start(bf16[1,1,32,32]{3,2,1,0:T(8,128)(2,1)} %delta_hbm.1) | copy-start | bytes 6148
  2.7 36.7 %all-to-all-start = ((bf16[16,264,128]{2,1,0:T(8,128)(2,1)}), bf16[16,264,128]{2,1,0:T(8,128)(2,1)S(1)}, u32[]{:S(2)}, u32[]{:S(2)}) async-start(bf16[16,264,128]{2,1,0:T(8,128)(2,1)} %shard_map.145), calls=%async_computation | async-start | bytes 2162688 | tf_op jit(solution)/shard_map/all_to_all | solution.py:367
  11.4 29.9 %copy-start.4 = (s32[1,3]{1,0:T(1,128)S(1)}, s32[1,3]{1,0:T(1,128)}, u32[]{:S(2)}) copy-start(s32[1,3]{1,0:T(1,128)} %lengths_ref.13) | copy-start | bytes 40
  12.0 3.4 %collective-permute-start.1 = (bf16[2,528,128]{2,1,0:T(8,128)(2,1)S(1)}, bf16[2,528,128]{2,1,0:T(8,128)(2,1)S(1)}, u32[]{:S(2)}, u32[]{:S(2)}) collective-permute-start(bf16[2,528,128]{2,1,0:T(8,128)(2,1)S(1)} %get-tuple-element.30), channel_id=1, source_target_pairs={{0,32},{32,0},{1,33},{33,1},{2,34},{34,2},{3,35},{35,3},{4,36},{36... | collective-permute-start | bytes 811016 | tf_op jit(solution)/shard_map/ppermute | solution.py:371
  15.5 25.8 %collective-permute-start.4 = (bf16[2,528,128]{2,1,0:T(8,128)(2,1)S(1)}, bf16[2,528,128]{2,1,0:T(8,128)(2,1)S(1)}, u32[]{:S(2)}, u32[]{:S(2)}) collective-permute-start(bf16[2,528,128]{2,1,0:T(8,128)(2,1)S(1)} %get-tuple-element.32), channel_id=1, source_target_pairs={{0,1},{1,2},{2,3},{3,0},{4,5},{5,6},{6,7},{7,4},{8,9},{9,10},{10,1... | collective-permute-start | bytes 811016 | tf_op jit(solution)/shard_map/ppermute | solution.py:375
  18.4 25.9 %collective-permute-start.3 = (bf16[2,528,128]{2,1,0:T(8,128)(2,1)S(1)}, bf16[2,528,128]{2,1,0:T(8,128)(2,1)S(1)}, u32[]{:S(2)}, u32[]{:S(2)}) collective-permute-start(bf16[2,528,128]{2,1,0:T(8,128)(2,1)S(1)} %get-tuple-element.32), channel_id=1, source_target_pairs={{0,3},{1,0},{2,1},{3,2},{4,7},{5,4},{6,5},{7,6},{8,11},{9,8},{10,9... | collective-permute-start | bytes 811016 | tf_op jit(solution)/shard_map/ppermute | solution.py:375
  21.4 23.5 %collective-permute-start.2 = (bf16[2,528,128]{2,1,0:T(8,128)(2,1)S(1)}, bf16[2,528,128]{2,1,0:T(8,128)(2,1)S(1)}, u32[]{:S(2)}, u32[]{:S(2)}) collective-permute-start(bf16[2,528,128]{2,1,0:T(8,128)(2,1)S(1)} %get-tuple-element.31.qa.q_ref), channel_id=1, source_target_pairs={{0,2},{1,3},{2,0},{3,1},{4,6},{5,7},{6,4},{7,5},{8,10},{9,11},{10,... | collective-permute-start | bytes 811016 | tf_op jit(solution)/shard_map/ppermute | solution.py:375
  39.4 8.5 %collective-permute-start = (bf16[16,64,128]{2,1,0:T(8,128)(2,1)S(1)}, bf16[16,64,128]{2,1,0:T(8,128)(2,1)S(1)}, u32[]{:S(2)}, u32[]{:S(2)}) collective-permute-start(bf16[16,64,128]{2,1,0:T(8,128)(2,1)S(1)} %slice.8), channel_id=1, source_target_pairs={{0,32},{32,0},{1,33},{33,1},{2,34},{34,2},{3,35},{35,3},{4,36},{36... | collective-permute-start | bytes 786440 | tf_op jit(solution)/shard_map/ppermute | solution.py:371
  47.9 3.1 %copy-start.5 = (bf16[16,64,128]{2,1,0:T(8,128)(2,1)}, bf16[16,64,128]{2,1,0:T(8,128)(2,1)S(1)}, u32[]{:S(2)}) copy-start(bf16[16,64,128]{2,1,0:T(8,128)(2,1)S(1)} %collective-permute-done.side_ref) | copy-start | bytes 786436
  51.1 36.4 %all-to-all-start.1 = ((bf16[16,256,128]{2,1,0:T(8,128)(2,1)}), bf16[16,256,128]{2,1,0:T(8,128)(2,1)S(1)}, u32[]{:S(2)}, u32[]{:S(2)}) async-start(bf16[16,256,128]{2,1,0:T(8,128)(2,1)} %get-tuple-element.45), calls=%async_computation.1 | async-start | bytes 2097152 | tf_op jit(solution)/shard_map/all_to_all | solution.py:367
  59.1 0.9 %copy-start.6 = (bf16[16,64,128]{2,1,0:T(8,128)(2,1)S(1)}, bf16[16,64,128]{2,1,0:T(8,128)(2,1)}, u32[]{:S(2)}) copy-start(bf16[16,64,128]{2,1,0:T(8,128)(2,1)} %copy-done.5) | copy-start | bytes 786436
  62.1 16.3 %collective-permute-start.6 = (bf16[512,128]{1,0:T(8,128)(2,1)S(1)}, bf16[512,128]{1,0:T(8,128)(2,1)S(1)}, u32[]{:S(2)}, u32[]{:S(2)}) collective-permute-start(bf16[512,128]{1,0:T(8,128)(2,1)S(1)} %shard_map.154), channel_id=1, source_target_pairs={{0,3},{1,0},{2,1},{3,2},{4,7},{5,4},{6,5},{7,6},{8,11},{9,8},{10,9... | collective-permute-start | bytes 393224 | tf_op jit(solution)/shard_map/ppermute | solution.py:375
  66.2 20.0 %collective-permute-start.5 = (bf16[528,128]{1,0:T(8,128)(2,1)S(1)}, bf16[528,128]{1,0:T(8,128)(2,1)S(1)}, u32[]{:S(2)}, u32[]{:S(2)}) collective-permute-start(bf16[528,128]{1,0:T(8,128)(2,1)S(1)} %shard_map.151), channel_id=1, source_target_pairs={{0,2},{1,3},{2,0},{3,1},{4,6},{5,7},{6,4},{7,5},{8,10},{9,11},{10,... | collective-permute-start | bytes 405512 | tf_op jit(solution)/shard_map/ppermute | solution.py:375
  71.9 14.2 %collective-permute-start.7 = (bf16[512,128]{1,0:T(8,128)(2,1)S(1)}, bf16[512,128]{1,0:T(8,128)(2,1)S(1)}, u32[]{:S(2)}, u32[]{:S(2)}) collective-permute-start(bf16[512,128]{1,0:T(8,128)(2,1)S(1)} %shard_map.155), channel_id=1, source_target_pairs={{0,1},{1,2},{2,3},{3,0},{4,5},{5,6},{6,7},{7,4},{8,9},{9,10},{10,1... | collective-permute-start | bytes 393224 | tf_op jit(solution)/shard_map/ppermute | solution.py:375

commit v8 on v7

--- a/solution.py
+++ b/solution.py
@@ -319,18 +319,35 @@
             )
         if waiting:
             n, grads, keys = waiting
-            term = dot(grads, keys, ((0,), (0,)))
+            term = dot(keys, grads, ((0,), (0,)))
             totals[n] = term if totals[n] is None else totals[n] + term
         waiting = (j, score_grads, key)
     for j in range(2):
-        out_ref[tile_rows(j), :] = (totals[j] * SCALE).astype(bf16)
+        out_ref[tile_rows(j), :] = jnp.transpose(totals[j] * SCALE).astype(bf16)
     if k == 2:
         out_ref[2 * TILE :, :] = split_margin(margin_ref[0:1, 0:1], STAT_ROWS)
 
 
-def kv_final_kernel(lengths_ref, margin_ref, d2, part_ref, pk_ref, pv_ref, rk_ref, rv_ref):
+def final_kernel(
+    lengths_ref, margin_ref, d0, d1, d2, d3, part_ref, pk_hbm, pv_hbm, q_hbm, rk_hbm, rv_hbm, gate_ref,
+    pk, pv, q, rk, rv, sems,
+):
     gate = gate_of(margin_ref[0:1, 0:1], d2[2 * TILE :, :])
+    gate_ref[0] = gate[0, 0]
     core = lax.axis_index("pair")
+    even = lax.axis_index("xl") == 0
+    outs = ((q, q_hbm), (pk, pk_hbm), (pv, pv_hbm), (rk, rk_hbm), (rv, rv_hbm))
+    copies = [pltpu.make_async_copy(ref, hbm.at[0], sems.at[i]) for i, (ref, hbm) in enumerate(outs)]
+    for j in range(2):
+        response = core + j - 2 * core * j
+        for h in range(GROUP):
+            rows = slice(j * TILE + h * POS, j * TILE + (h + 1) * POS)
+            same = gate * (d0[rows, :].astype(f32) + d2[rows, :].astype(f32))
+            odd = gate * (d1[rows, :].astype(f32) + d3[rows, :].astype(f32))
+            first, second = jnp.where(even, same, odd), jnp.where(even, odd, same)
+            q[response, :, h * LANES : (h + 1) * LANES] = first.astype(bf16)
+            q[response, :, (GROUP + h) * LANES : (GROUP + h + 1) * LANES] = second.astype(bf16)
+    copies[0].start()
     live = lax.axis_index(CTX) * PROMPT + lax.broadcasted_iota(jnp.int32, (PROMPT, LANES), 0) < lengths_ref[0, 0]
     for xl in range(2):
         columns = slice(xl * LANES, (xl + 1) * LANES)
@@ -338,29 +355,17 @@
         for y in range(1, ROWS_Y):
             total += part_ref[y * 2 + xl].astype(f32)
         total = total * gate
-        pk_ref[0, :, columns] = jnp.where(live, total[0:PROMPT], 0.0).astype(bf16)
-        pv_ref[0, :, columns] = jnp.where(live, total[PROMPT : 2 * PROMPT], 0.0).astype(bf16)
+        pk[:, columns] = jnp.where(live, total[0:PROMPT], 0.0).astype(bf16)
+        pv[:, columns] = jnp.where(live, total[PROMPT : 2 * PROMPT], 0.0).astype(bf16)
         for j in range(2):
             response = core + j - 2 * core * j
             at = 2 * PROMPT + j * SIDE
-            rk_ref[0, response, :, columns] = total[at : at + POS].astype(bf16)
-            rv_ref[0, response, :, columns] = total[at + POS : at + SIDE].astype(bf16)
-
-
-def query_final_kernel(margin_ref, d0, d1, d2, d3, out_ref, gate_ref):
-    gate = gate_of(margin_ref[0:1, 0:1], d2[2 * TILE :, :])
-    gate_ref[...] = jnp.broadcast_to(gate, gate_ref.shape)
-    core = lax.axis_index("pair")
-    even = lax.axis_index("xl") == 0
-    for j in range(2):
-        response = core + j - 2 * core * j
-        for h in range(GROUP):
-            rows = slice(j * TILE + h * POS, j * TILE + (h + 1) * POS)
-            same = gate * (d0[rows, :].astype(f32) + d2[rows, :].astype(f32))
-            odd = gate * (d1[rows, :].astype(f32) + d3[rows, :].astype(f32))
-            first, second = jnp.where(even, same, odd), jnp.where(even, odd, same)
-            out_ref[0, response, :, h * LANES : (h + 1) * LANES] = first.astype(bf16)
-            out_ref[0, response, :, (GROUP + h) * LANES : (GROUP + h + 1) * LANES] = second.astype(bf16)
+            rk[response, :, columns] = total[at : at + POS].astype(bf16)
+            rv[response, :, columns] = total[at + POS : at + SIDE].astype(bf16)
+    for copy in copies[1:]:
+        copy.start()
+    for copy in copies:
+        copy.wait()
 
 
 def swap(values):
@@ -486,17 +491,18 @@
     grads = [query_call(k, lengths, margin, rows[k], kv, side) for k in range(X)]
     part = swap(part)
     back = [grads[0]] + [shift(grads[k], X - k) for k in range(1, X)]
-    query_grad, gate = call(
-        query_final_kernel,
-        (shape((1, 2, POS, 2 * GROUP * LANES), bf16), shape((8, LANES), f32)),
-        "vvvvv",
-        size=2**20,
-    )(margin, *back)
-    outs = (shape((1, PROMPT, 2 * LANES), bf16),) * 2 + (shape((1, 2, POS, 2 * LANES), bf16),) * 2
-    pk_grad, pv_grad, key_grad, value_grad = call(kv_final_kernel, outs, "svvv", size=2**20)(
-        lengths, margin, back[2], part
-    )
-    return pk_grad, pv_grad, query_grad, key_grad, value_grad, gate[0, 0:1]
+    prompt_out, resp_out = shape((1, PROMPT, 2 * LANES), bf16), shape((1, 2, POS, 2 * LANES), bf16)
+    query_out = shape((1, 2, POS, 2 * GROUP * LANES), bf16)
+    outs = (prompt_out, prompt_out, query_out, resp_out, resp_out)
+    return call(
+        final_kernel,
+        outs + (shape((1,), f32),),
+        "svvvvvv",
+        out_spaces="aaaaas",
+        scratch=[pltpu.VMEM(out.shape[1:], bf16) for out in outs]
+        + [pltpu.SemaphoreType.DMA((5,))],
+        size=2 * 2**20,
+    )(lengths, margin, *back, part)
 
 
 def solution(mesh):

time: 89.5 us -> 89.7 us (level)
    pallas_call x2 -> x1, Pallas kernels: 2.26 us -> 2.1 us  [per_device(): call(final_kernel, outs + (shape((1,), f32),), 'svvvvvv', out_spaces='aaa...]
  transfers between devices with their start and end apart: 10 -> 10, of which waited for: 4 -> 4; matrix products, arithmetic and copies ran while one was open for 1% -> 0% of each run, Pallas kernels for 18% -> 16%
where the time goes in v8:
time: 89.7 us; the launch traced here: 88.4 us
  starting transfers between devices  40.7 us (45%)
  waiting for transfers between devices  23.8 us (27%)
  Pallas kernels  21.8 us (24%)
  between operations  1.05 us (1%)
  local copies, waits for them, and re-layouts  1 us (1%)
    ppermute x6, starting transfers between devices, shift(): return lax.ppermute(values, ROW, [(i, (i + by) % X) for i in range(X)])  20.1 us
    all_to_all x2, starting transfers between devices, swap(): lax.all_to_all(values, PEERS, split_axis=0, concat_axis=0, tiled=True)  16.8 us
    all_to_all x2, waiting for transfers between devices, swap(): lax.all_to_all(values, PEERS, split_axis=0, concat_axis=0, tiled=True)  13.9 us
    ppermute x6, waiting for transfers between devices, shift(): return lax.ppermute(values, ROW, [(i, (i + by) % X) for i in range(X)])  8.41 us
    pallas_call x4, Pallas kernels, query_call(): call(functools.partial(query_kernel, k), jax.ShapeDtypeStruct((2 * TILE +...  7.99 us
    ppermute x2, starting transfers between devices, cross(): return lax.ppermute(values, 'pair', [(0, 1), (1, 0)])  3.84 us
    pallas_call x1, Pallas kernels, resp_call(): call(resp_kernel, (shape((PEERS_N, KV_ROWS, LANES), bf16), shape((8, LANE...  3.15 us
    pallas_call x1, Pallas kernels, prompt_call(): call(functools.partial(prompt_kernel, False), (shape((PEERS_N, 2 * PROMPT...  3 us
  transfers between devices with their start and end apart: 10, of which 4 were waited for; matrix products, arithmetic and copies ran while one was open for 0% of the time, Pallas kernels for 16%

profile of v8, /device:TPU:6, one launch (start us, length us, event | category | flops | bytes accessed | tf_op | source)
XLA Modules:
  0.0 88.4 jit_solution(3602476790443841816)
XLA Ops:
  0.6 2.0 %shard_map.145 = bf16[16,264,128]{2,1,0:T(8,128)(2,1)} custom-call(s32[1,3]{1,0:T(1,128)} %lengths_ref.13, f32[1,2,32]{2,1,0:T(2,128)} %logratio_hbm.1, bf16[1,64,256]{2,1,0:T(8,128)(2,1)} %pk_hbm.1, bf16[1,64,256]{2,1,0:T(8,128)(2,1)} %pv_hbm.1, bf16[1,1,32,512]{3,2,1,0:T(8,128)(2,1)} %rk_hbm.1, bf16[1,1,32,512]{3,2,1,0:T(8,128)(2,1)} %rv_hbm.1), custom_call_target="tpu_custom_call" | custom-call | bytes 2097152 | tf_op jit(solution)/shard_map/pallas_call | solution.py:453
  2.6 0.0 copy-start
  2.6 0.0 copy-start.1
  2.7 0.0 copy-start.2
  2.7 0.0 copy-start.3
  2.7 8.7 %all-to-all-start = ((bf16[16,264,128]{2,1,0:T(8,128)(2,1)}), bf16[16,264,128]{2,1,0:T(8,128)(2,1)S(1)}, u32[]{:S(2)}, u32[]{:S(2)}) async-start(bf16[16,264,128]{2,1,0:T(8,128)(2,1)} %shard_map.145), calls=%async_computation | async-start | bytes 2162688 | tf_op jit(solution)/shard_map/all_to_all | solution.py:372
  11.4 0.0 copy-done
  11.4 0.0 copy-done.1
  11.4 0.0 copy-done.2
  11.4 0.0 copy-done.3
  11.4 0.0 copy-start.4
  11.5 0.6 shard_map.146
  12.0 1.9 %collective-permute-start.1 = (bf16[2,528,128]{2,1,0:T(8,128)(2,1)S(1)}, bf16[2,528,128]{2,1,0:T(8,128)(2,1)S(1)}, u32[]{:S(2)}, u32[]{:S(2)}) collective-permute-start(bf16[2,528,128]{2,1,0:T(8,128)(2,1)S(1)} %get-tuple-element.24), channel_id=1, source_target_pairs={{0,32},{32,0},{1,33},{33,1},{2,34},{34,2},{3,35},{35,3},{4,36},{36... | collective-permute-start | bytes 811016 | tf_op jit(solution)/shard_map/ppermute | solution.py:376
  14.0 1.5 %collective-permute-done.1.other_ref = bf16[2,528,128]{2,1,0:T(8,128)(2,1)S(1)} collective-permute-done((bf16[2,528,128]{2,1,0:T(8,128)(2,1)S(1)}, bf16[2,528,128]{2,1,0:T(8,128)(2,1)S(1)}, u32[]{:S(2)}, u32[]{:S(2)}) %collective-permute-start.1) | collective-permute-done | bytes 270368 | tf_op jit(solution)/shard_map/ppermute | solution.py:376
  15.5 2.9 %collective-permute-start.4 = (bf16[2,528,128]{2,1,0:T(8,128)(2,1)S(1)}, bf16[2,528,128]{2,1,0:T(8,128)(2,1)S(1)}, u32[]{:S(2)}, u32[]{:S(2)}) collective-permute-start(bf16[2,528,128]{2,1,0:T(8,128)(2,1)S(1)} %get-tuple-element.26), channel_id=1, source_target_pairs={{0,1},{1,2},{2,3},{3,0},{4,5},{5,6},{6,7},{7,4},{8,9},{9,10},{10,1... | collective-permute-start | bytes 811016 | tf_op jit(solution)/shard_map/ppermute | solution.py:380
  18.4 2.9 %collective-permute-start.3 = (bf16[2,528,128]{2,1,0:T(8,128)(2,1)S(1)}, bf16[2,528,128]{2,1,0:T(8,128)(2,1)S(1)}, u32[]{:S(2)}, u32[]{:S(2)}) collective-permute-start(bf16[2,528,128]{2,1,0:T(8,128)(2,1)S(1)} %get-tuple-element.26), channel_id=1, source_target_pairs={{0,3},{1,0},{2,1},{3,2},{4,7},{5,4},{6,5},{7,6},{8,11},{9,8},{10,9... | collective-permute-start | bytes 811016 | tf_op jit(solution)/shard_map/ppermute | solution.py:380
  21.4 4.1 %collective-permute-start.2 = (bf16[2,528,128]{2,1,0:T(8,128)(2,1)S(1)}, bf16[2,528,128]{2,1,0:T(8,128)(2,1)S(1)}, u32[]{:S(2)}, u32[]{:S(2)}) collective-permute-start(bf16[2,528,128]{2,1,0:T(8,128)(2,1)S(1)} %get-tuple-element.25.qa.q_ref), channel_id=1, source_target_pairs={{0,2},{1,3},{2,0},{3,1},{4,6},{5,7},{6,4},{7,5},{8,10},{9,11},{10,... | collective-permute-start | bytes 811016 | tf_op jit(solution)/shard_map/ppermute | solution.py:380
  25.5 13.9 %all-to-all-done.kv_ref = bf16[16,264,128]{2,1,0:T(8,128)(2,1)S(1)} async-done(((bf16[16,264,128]{2,1,0:T(8,128)(2,1)}), bf16[16,264,128]{2,1,0:T(8,128)(2,1)S(1)}, u32[]{:S(2)}, u32[]{:S(2)}) %all-to-all-start) | async-done | bytes 1081376 | tf_op jit(solution)/shard_map/all_to_all | solution.py:372
  39.4 1.9 %collective-permute-start = (bf16[16,64,128]{2,1,0:T(8,128)(2,1)S(1)}, bf16[16,64,128]{2,1,0:T(8,128)(2,1)S(1)}, u32[]{:S(2)}, u32[]{:S(2)}) collective-permute-start(bf16[16,64,128]{2,1,0:T(8,128)(2,1)S(1)} %slice.4), channel_id=1, source_target_pairs={{0,32},{32,0},{1,33},{33,1},{2,34},{34,2},{3,35},{35,3},{4,36},{36... | collective-permute-start | bytes 786440 | tf_op jit(solution)/shard_map/ppermute | solution.py:376
  41.3 0.0 collective-permute-done.4.qb.q_ref
  41.3 0.0 copy-done.4
  41.4 3.0 %shard_map.148 = (f32[1024,128]{1,0:T(8,128)S(1)}, f32[1024,128]{1,0:T(8,128)S(1)}, bf16[1024,128]{1,0:T(8,128)(2,1)S(1)}, bf16[1024,128]{1,0:T(8,128)(2,1)S(1)}...) custom-call(s32[1,3]{1,0:T(1,128)S(1)} %copy-done.4, bf16[2,528,128]{2,1,0:T(8,128)(2,1)S(1)} %get-tuple-element.25.qa.q_ref, ...), custom_call_target="tpu_custom_call" | custom-call | flops 2147483648 | bytes 2097152 | tf_op jit(solution)/shard_map/pallas_call | solution.py:395
  44.3 0.0 collective-permute-done.3.qb.q_ref
  44.3 0.6 collective-permute-done.2.qa.q_ref
  44.9 3.0 %shard_map.149 = (bf16[16,128,128]{2,1,0:T(8,128)(2,1)S(1)}, bf16[1024,128]{1,0:T(8,128)(2,1)S(1)}, bf16[1024,128]{1,0:T(8,128)(2,1)S(1)}, f32[4,256]{1,0:T(4,128)S(1)}, f32[4,256]{1,0:T(4,128)S(1)}) custom-call(s32[1,3]{1,0:T(1,128)S(1)} %copy-done.4, bf16[2,528,128]{2,1,0:T(8,128)(2,1)S(1)} %collective-permute-done.2.qa.q_ref, ...), custom_call_target="tpu_custom_call" | custom-call | flops 2147483648 | bytes 2097152 | tf_op jit(solution)/shard_map/pallas_call | solution.py:398
  47.9 0.0 collective-permute-done.side_ref
  47.9 0.0 copy-start.5
  48.0 3.1 %shard_map.150 = (bf16[16,256,128]{2,1,0:T(8,128)(2,1)}, f32[8,128]{1,0:T(8,128)S(1)}) custom-call(bf16[16,264,128]{2,1,0:T(8,128)(2,1)S(1)} %all-to-all-done.kv_ref, bf16[16,64,128]{2,1,0:T(8,128)(2,1)S(1)} %collective-permute-done.side_ref, bf16[16,128,128]{2,1,0:T(8,128)(2,1)S(1)} %get-tuple-element.29.prompt_ref, ...), custom_call_target="tpu_custom_call" | custom-call | flops 2147483648 | bytes 3145728 | tf_op jit(solution)/shard_map/pallas_call | solution.py:410
  51.1 0.0 copy-done.5
  51.1 8.0 %all-to-all-start.1 = ((bf16[16,256,128]{2,1,0:T(8,128)(2,1)}), bf16[16,256,128]{2,1,0:T(8,128)(2,1)S(1)}, u32[]{:S(2)}, u32[]{:S(2)}) async-start(bf16[16,256,128]{2,1,0:T(8,128)(2,1)} %get-tuple-element.39), calls=%async_computation.1 | async-start | bytes 2097152 | tf_op jit(solution)/shard_map/all_to_all | solution.py:372
  59.1 0.0 copy-start.6
  59.2 0.9 %copy-done.6 = bf16[16,64,128]{2,1,0:T(8,128)(2,1)S(1)} copy-done((bf16[16,64,128]{2,1,0:T(8,128)(2,1)S(1)}, bf16[16,64,128]{2,1,0:T(8,128)(2,1)}, u32[]{:S(2)}) %copy-start.6) | copy-done | bytes 262168
  60.1 2.0 %shard_map.152 = bf16[512,128]{1,0:T(8,128)(2,1)S(1)} custom-call(s32[1,3]{1,0:T(1,128)S(1)} %copy-done.4, f32[8,128]{1,0:T(8,128)S(1)} %get-tuple-element.38.margin_ref, bf16[2,528,128]{2,1,0:T(8,128)(2,1)S(1)} %collective-permute-done.4.qb.q_ref, bf16[16,264,128]{2,1,0:T(8,128)(2,1)S(1)} %all-to-all-done.kv_ref, bf16[16,64,128]{2,1,0:T(8,128)(2,1)S(1)} %copy-done.6), custom_call_target="tpu_custom_call" | custom-call | flops 1207959552 | bytes 3145728 | tf_op jit(solution)/shard_map/pallas_call | solution.py:431
  62.1 2.0 %collective-permute-start.5 = (bf16[512,128]{1,0:T(8,128)(2,1)S(1)}, bf16[512,128]{1,0:T(8,128)(2,1)S(1)}, u32[]{:S(2)}, u32[]{:S(2)}) collective-permute-start(bf16[512,128]{1,0:T(8,128)(2,1)S(1)} %shard_map.152), channel_id=1, source_target_pairs={{0,3},{1,0},{2,1},{3,2},{4,7},{5,4},{6,5},{7,6},{8,11},{9,8},{10,9... | collective-permute-start | bytes 393224 | tf_op jit(solution)/shard_map/ppermute | solution.py:380
  64.1 2.0 %shard_map.153 = bf16[528,128]{1,0:T(8,128)(2,1)S(1)} custom-call(s32[1,3]{1,0:T(1,128)S(1)} %copy-done.4, f32[8,128]{1,0:T(8,128)S(1)} %get-tuple-element.38.margin_ref, bf16[2,528,128]{2,1,0:T(8,128)(2,1)S(1)} %collective-permute-done.2.qa.q_ref, bf16[16,264,128]{2,1,0:T(8,128)(2,1)S(1)} %all-to-all-done.kv_ref, bf16[16,64,128]{2,1,0:T(8,128)(2,1)S(1)} %copy-done.6), custom_call_target="tpu_custom_call" | custom-call | flops 1207959552 | bytes 3145728 | tf_op jit(solution)/shard_map/pallas_call | solution.py:431
  66.1 3.7 %collective-permute-start.6 = (bf16[528,128]{1,0:T(8,128)(2,1)S(1)}, bf16[528,128]{1,0:T(8,128)(2,1)S(1)}, u32[]{:S(2)}, u32[]{:S(2)}) collective-permute-start(bf16[528,128]{1,0:T(8,128)(2,1)S(1)} %shard_map.153), channel_id=1, source_target_pairs={{0,2},{1,3},{2,0},{3,1},{4,6},{5,7},{6,4},{7,5},{8,10},{9,11},{10,... | collective-permute-start | bytes 405512 | tf_op jit(solution)/shard_map/ppermute | solution.py:380
  69.8 2.0 %shard_map.154 = bf16[512,128]{1,0:T(8,128)(2,1)S(1)} custom-call(s32[1,3]{1,0:T(1,128)S(1)} %copy-done.4, f32[8,128]{1,0:T(8,128)S(1)} %get-tuple-element.38.margin_ref, bf16[2,528,128]{2,1,0:T(8,128)(2,1)S(1)} %collective-permute-done.3.qb.q_ref, bf16[16,264,128]{2,1,0:T(8,128)(2,1)S(1)} %all-to-all-done.kv_ref, bf16[16,64,128]{2,1,0:T(8,128)(2,1)S(1)} %copy-done.6), custom_call_target="tpu_custom_call" | custom-call | flops 1207959552 | bytes 3145728 | tf_op jit(solution)/shard_map/pallas_call | solution.py:431
  71.9 4.4 %collective-permute-start.7 = (bf16[512,128]{1,0:T(8,128)(2,1)S(1)}, bf16[512,128]{1,0:T(8,128)(2,1)S(1)}, u32[]{:S(2)}, u32[]{:S(2)}) collective-permute-start(bf16[512,128]{1,0:T(8,128)(2,1)S(1)} %shard_map.154), channel_id=1, source_target_pairs={{0,1},{1,2},{2,3},{3,0},{4,5},{5,6},{6,7},{7,4},{8,9},{9,10},{10,1... | collective-permute-start | bytes 393224 | tf_op jit(solution)/shard_map/ppermute | solution.py:380
  76.3 2.0 %shard_map.151.d0 = bf16[512,128]{1,0:T(8,128)(2,1)S(1)} custom-call(s32[1,3]{1,0:T(1,128)S(1)} %copy-done.4, f32[8,128]{1,0:T(8,128)S(1)} %get-tuple-element.38.margin_ref, bf16[2,528,128]{2,1,0:T(8,128)(2,1)S(1)} %get-tuple-element.25.qa.q_ref, bf16[16,264,128]{2,1,0:T(8,128)(2,1)S(1)} %all-to-all-done.kv_ref, bf16[16,64,128]{2,1,0:T(8,128)(2,1)S(1)} %copy-done.6), custom_call_target="tpu_custom_call" | custom-call | flops 1207959552 | bytes 3145728 | tf_op jit(solution)/shard_map/pallas_call | solution.py:431
  78.3 0.0 collective-permute-done.5.d1
  78.3 7.8 %collective-permute-done.7.d3 = bf16[512,128]{1,0:T(8,128)(2,1)S(1)} collective-permute-done((bf16[512,128]{1,0:T(8,128)(2,1)S(1)}, bf16[512,128]{1,0:T(8,128)(2,1)S(1)}, u32[]{:S(2)}, u32[]{:S(2)}) %collective-permute-start.7) | collective-permute-done | bytes 131104 | tf_op jit(solution)/shard_map/ppermute | solution.py:380
  86.1 0.0 collective-permute-done.6.d2
  86.1 0.0 all-to-all-done.1.part_ref
  86.1 2.1 %shard_map.155 = (bf16[1,64,256]{2,1,0:T(8,128)(2,1)}, bf16[1,64,256]{2,1,0:T(8,128)(2,1)}, bf16[1,2,32,2048]{3,2,1,0:T(8,128)(2,1)}, bf16[1,2,32,256]{3,2,1,0:T...) custom-call(s32[1,3]{1,0:T(1,128)S(1)} %copy-done.4, f32[8,128]{1,0:T(8,128)S(1)} %get-tuple-element.38.margin_ref, ...), custom_call_target="tpu_custom_call" | custom-call | bytes 2097152 | tf_op jit(solution)/shard_map/pallas_call | solution.py:497
  (2 shorter events, 0.1 us)
Async XLA Ops:
  2.6 8.8 %copy-start = (bf16[1,1,32,4096]{3,2,1,0:T(8,128)(2,1)S(1)}, bf16[1,1,32,4096]{3,2,1,0:T(8,128)(2,1)}, u32[]{:S(2)}) copy-start(bf16[1,1,32,4096]{3,2,1,0:T(8,128)(2,1)} %q_hbm.1) | copy-start | bytes 786436
  2.6 8.8 %copy-start.1 = (bf16[1,1,32,4096]{3,2,1,0:T(8,128)(2,1)S(1)}, bf16[1,1,32,4096]{3,2,1,0:T(8,128)(2,1)}, u32[]{:S(2)}) copy-start(bf16[1,1,32,4096]{3,2,1,0:T(8,128)(2,1)} %g_hbm.1) | copy-start | bytes 786436
  2.7 8.8 %copy-start.2 = (bf16[1,1,32,32]{3,2,1,0:T(8,128)(2,1)S(1)}, bf16[1,1,32,32]{3,2,1,0:T(8,128)(2,1)}, u32[]{:S(2)}) copy-start(bf16[1,1,32,32]{3,2,1,0:T(8,128)(2,1)} %lse_hbm.1) | copy-start | bytes 6148
  2.7 8.8 %copy-start.3 = (bf16[1,1,32,32]{3,2,1,0:T(8,128)(2,1)S(1)}, bf16[1,1,32,32]{3,2,1,0:T(8,128)(2,1)}, u32[]{:S(2)}) copy-start(bf16[1,1,32,32]{3,2,1,0:T(8,128)(2,1)} %delta_hbm.1) | copy-start | bytes 6148
  2.7 36.7 %all-to-all-start = ((bf16[16,264,128]{2,1,0:T(8,128)(2,1)}), bf16[16,264,128]{2,1,0:T(8,128)(2,1)S(1)}, u32[]{:S(2)}, u32[]{:S(2)}) async-start(bf16[16,264,128]{2,1,0:T(8,128)(2,1)} %shard_map.145), calls=%async_computation | async-start | bytes 2162688 | tf_op jit(solution)/shard_map/all_to_all | solution.py:372
  11.4 29.9 %copy-start.4 = (s32[1,3]{1,0:T(1,128)S(1)}, s32[1,3]{1,0:T(1,128)}, u32[]{:S(2)}) copy-start(s32[1,3]{1,0:T(1,128)} %lengths_ref.13) | copy-start | bytes 40
  12.0 3.4 %collective-permute-start.1 = (bf16[2,528,128]{2,1,0:T(8,128)(2,1)S(1)}, bf16[2,528,128]{2,1,0:T(8,128)(2,1)S(1)}, u32[]{:S(2)}, u32[]{:S(2)}) collective-permute-start(bf16[2,528,128]{2,1,0:T(8,128)(2,1)S(1)} %get-tuple-element.24), channel_id=1, source_target_pairs={{0,32},{32,0},{1,33},{33,1},{2,34},{34,2},{3,35},{35,3},{4,36},{36... | collective-permute-start | bytes 811016 | tf_op jit(solution)/shard_map/ppermute | solution.py:376
  15.5 25.8 %collective-permute-start.4 = (bf16[2,528,128]{2,1,0:T(8,128)(2,1)S(1)}, bf16[2,528,128]{2,1,0:T(8,128)(2,1)S(1)}, u32[]{:S(2)}, u32[]{:S(2)}) collective-permute-start(bf16[2,528,128]{2,1,0:T(8,128)(2,1)S(1)} %get-tuple-element.26), channel_id=1, source_target_pairs={{0,1},{1,2},{2,3},{3,0},{4,5},{5,6},{6,7},{7,4},{8,9},{9,10},{10,1... | collective-permute-start | bytes 811016 | tf_op jit(solution)/shard_map/ppermute | solution.py:380
  18.4 25.9 %collective-permute-start.3 = (bf16[2,528,128]{2,1,0:T(8,128)(2,1)S(1)}, bf16[2,528,128]{2,1,0:T(8,128)(2,1)S(1)}, u32[]{:S(2)}, u32[]{:S(2)}) collective-permute-start(bf16[2,528,128]{2,1,0:T(8,128)(2,1)S(1)} %get-tuple-element.26), channel_id=1, source_target_pairs={{0,3},{1,0},{2,1},{3,2},{4,7},{5,4},{6,5},{7,6},{8,11},{9,8},{10,9... | collective-permute-start | bytes 811016 | tf_op jit(solution)/shard_map/ppermute | solution.py:380
  21.4 23.5 %collective-permute-start.2 = (bf16[2,528,128]{2,1,0:T(8,128)(2,1)S(1)}, bf16[2,528,128]{2,1,0:T(8,128)(2,1)S(1)}, u32[]{:S(2)}, u32[]{:S(2)}) collective-permute-start(bf16[2,528,128]{2,1,0:T(8,128)(2,1)S(1)} %get-tuple-element.25.qa.q_ref), channel_id=1, source_target_pairs={{0,2},{1,3},{2,0},{3,1},{4,6},{5,7},{6,4},{7,5},{8,10},{9,11},{10,... | collective-permute-start | bytes 811016 | tf_op jit(solution)/shard_map/ppermute | solution.py:380
  39.4 8.5 %collective-permute-start = (bf16[16,64,128]{2,1,0:T(8,128)(2,1)S(1)}, bf16[16,64,128]{2,1,0:T(8,128)(2,1)S(1)}, u32[]{:S(2)}, u32[]{:S(2)}) collective-permute-start(bf16[16,64,128]{2,1,0:T(8,128)(2,1)S(1)} %slice.4), channel_id=1, source_target_pairs={{0,32},{32,0},{1,33},{33,1},{2,34},{34,2},{3,35},{35,3},{4,36},{36... | collective-permute-start | bytes 786440 | tf_op jit(solution)/shard_map/ppermute | solution.py:376
  47.9 3.2 %copy-start.5 = (bf16[16,64,128]{2,1,0:T(8,128)(2,1)}, bf16[16,64,128]{2,1,0:T(8,128)(2,1)S(1)}, u32[]{:S(2)}) copy-start(bf16[16,64,128]{2,1,0:T(8,128)(2,1)S(1)} %collective-permute-done.side_ref) | copy-start | bytes 786436
  51.1 35.0 %all-to-all-start.1 = ((bf16[16,256,128]{2,1,0:T(8,128)(2,1)}), bf16[16,256,128]{2,1,0:T(8,128)(2,1)S(1)}, u32[]{:S(2)}, u32[]{:S(2)}) async-start(bf16[16,256,128]{2,1,0:T(8,128)(2,1)} %get-tuple-element.39), calls=%async_computation.1 | async-start | bytes 2097152 | tf_op jit(solution)/shard_map/all_to_all | solution.py:372
  59.1 0.9 %copy-start.6 = (bf16[16,64,128]{2,1,0:T(8,128)(2,1)S(1)}, bf16[16,64,128]{2,1,0:T(8,128)(2,1)}, u32[]{:S(2)}) copy-start(bf16[16,64,128]{2,1,0:T(8,128)(2,1)} %copy-done.5) | copy-start | bytes 786436
  62.1 16.2 %collective-permute-start.5 = (bf16[512,128]{1,0:T(8,128)(2,1)S(1)}, bf16[512,128]{1,0:T(8,128)(2,1)S(1)}, u32[]{:S(2)}, u32[]{:S(2)}) collective-permute-start(bf16[512,128]{1,0:T(8,128)(2,1)S(1)} %shard_map.152), channel_id=1, source_target_pairs={{0,3},{1,0},{2,1},{3,2},{4,7},{5,4},{6,5},{7,6},{8,11},{9,8},{10,9... | collective-permute-start | bytes 393224 | tf_op jit(solution)/shard_map/ppermute | solution.py:380
  66.1 20.0 %collective-permute-start.6 = (bf16[528,128]{1,0:T(8,128)(2,1)S(1)}, bf16[528,128]{1,0:T(8,128)(2,1)S(1)}, u32[]{:S(2)}, u32[]{:S(2)}) collective-permute-start(bf16[528,128]{1,0:T(8,128)(2,1)S(1)} %shard_map.153), channel_id=1, source_target_pairs={{0,2},{1,3},{2,0},{3,1},{4,6},{5,7},{6,4},{7,5},{8,10},{9,11},{10,... | collective-permute-start | bytes 405512 | tf_op jit(solution)/shard_map/ppermute | solution.py:380
  71.9 14.3 %collective-permute-start.7 = (bf16[512,128]{1,0:T(8,128)(2,1)S(1)}, bf16[512,128]{1,0:T(8,128)(2,1)S(1)}, u32[]{:S(2)}, u32[]{:S(2)}) collective-permute-start(bf16[512,128]{1,0:T(8,128)(2,1)S(1)} %shard_map.154), channel_id=1, source_target_pairs={{0,1},{1,2},{2,3},{3,0},{4,5},{5,6},{6,7},{7,4},{8,9},{9,10},{10,1... | collective-permute-start | bytes 393224 | tf_op jit(solution)/shard_map/ppermute | solution.py:380

commit v9 on v7

--- a/solution.py
+++ b/solution.py
@@ -78,7 +78,7 @@
 
 
 def kv_pack_kernel(
-    lengths_hbm, logratio_hbm, pk_hbm, pv_hbm, rk_hbm, rv_hbm, kv_ref, lengths, logratio, pk, pv, rk, rv, sems
+    lengths_hbm, logratio_hbm, pk_hbm, pv_hbm, rk_hbm, rv_hbm, kv_hbm, lengths, logratio, pk, pv, rk, rv, kv_ref, sems
 ):
     pairs = (
         (lengths_hbm, lengths),
@@ -106,11 +106,17 @@
         parts += [jnp.where(first_core, a, b).astype(bf16) for a, b in zip(low_head, high_head)]
         parts += [jnp.where(first_core, b, a).astype(bf16) for a, b in zip(low_head, high_head)]
         parts += [block]
-        for y in range(ROWS_Y):
-            at = 0
-            for part in parts:
-                kv_ref[y * 2 + xl, at : at + part.shape[0], :] = part
-                at += part.shape[0]
+        at = 0
+        for part in parts:
+            kv_ref[xl, at : at + part.shape[0], :] = part
+            at += part.shape[0]
+    copies = [
+        pltpu.make_async_copy(kv_ref, kv_hbm.at[2 * y : 2 * y + 2], sems.at[6 + y]) for y in range(ROWS_Y)
+    ]
+    for copy in copies:
+        copy.start()
+    for copy in copies:
+        copy.wait()
 
 
 def query_pack_kernel(q_hbm, g_hbm, lse_hbm, delta_hbm, own_ref, other_ref, q, g, lse, delta, sems):
@@ -319,11 +325,11 @@
             )
         if waiting:
             n, grads, keys = waiting
-            term = dot(grads, keys, ((0,), (0,)))
+            term = dot(keys, grads, ((0,), (0,)))
             totals[n] = term if totals[n] is None else totals[n] + term
         waiting = (j, score_grads, key)
     for j in range(2):
-        out_ref[tile_rows(j), :] = (totals[j] * SCALE).astype(bf16)
+        out_ref[tile_rows(j), :] = jnp.transpose(totals[j] * SCALE).astype(bf16)
     if k == 2:
         out_ref[2 * TILE :, :] = split_margin(margin_ref[0:1, 0:1], STAT_ROWS)
 
@@ -349,7 +355,7 @@
 
 def query_final_kernel(margin_ref, d0, d1, d2, d3, out_ref, gate_ref):
     gate = gate_of(margin_ref[0:1, 0:1], d2[2 * TILE :, :])
-    gate_ref[...] = jnp.broadcast_to(gate, gate_ref.shape)
+    gate_ref[0] = gate[0, 0]
     core = lax.axis_index("pair")
     even = lax.axis_index("xl") == 0
     for j in range(2):
@@ -449,6 +455,7 @@
         kv_pack_kernel,
         shape((PEERS_N, KV_ROWS + MARGIN_ROWS, LANES), bf16),
         "aaaaaa",
+        out_spaces="a",
         size=2 * 2**20,
         limit=60,
         scratch=(
@@ -458,7 +465,8 @@
             pltpu.VMEM((PROMPT, 2 * LANES), bf16),
             pltpu.VMEM((POS, X * LANES), bf16),
             pltpu.VMEM((POS, X * LANES), bf16),
-            pltpu.SemaphoreType.DMA((6,)),
+            pltpu.VMEM((2, KV_ROWS + MARGIN_ROWS, LANES), bf16),
+            pltpu.SemaphoreType.DMA((6 + ROWS_Y,)),
         ),
     )(lengths, logratio, prompt_keys, prompt_values, resp_keys, resp_values)
     kv = swap(kv)
@@ -488,15 +496,16 @@
     back = [grads[0]] + [shift(grads[k], X - k) for k in range(1, X)]
     query_grad, gate = call(
         query_final_kernel,
-        (shape((1, 2, POS, 2 * GROUP * LANES), bf16), shape((8, LANES), f32)),
+        (shape((1, 2, POS, 2 * GROUP * LANES), bf16), shape((1,), f32)),
         "vvvvv",
+        out_spaces="vs",
         size=2**20,
     )(margin, *back)
     outs = (shape((1, PROMPT, 2 * LANES), bf16),) * 2 + (shape((1, 2, POS, 2 * LANES), bf16),) * 2
     pk_grad, pv_grad, key_grad, value_grad = call(kv_final_kernel, outs, "svvv", size=2**20)(
         lengths, margin, back[2], part
     )
-    return pk_grad, pv_grad, query_grad, key_grad, value_grad, gate[0, 0:1]
+    return pk_grad, pv_grad, query_grad, key_grad, value_grad, gate
 
 
 def solution(mesh):

time: 89.5 us -> 89.1 us (level)
  transfers between devices with their start and end apart: 10 -> 10, of which waited for: 4 -> 4; matrix products, arithmetic and copies ran while one was open for 1% -> 0% of each run, Pallas kernels for 18% -> 17%
where the time goes in v9:
time: 89.1 us; the launch traced here: 88.5 us
  starting transfers between devices  40.7 us (46%)
  waiting for transfers between devices  23.8 us (27%)
  Pallas kernels  22 us (25%)
  local copies, waits for them, and re-layouts  1 us (1%)
  between operations  0.9 us (1%)
    ppermute x6, starting transfers between devices, shift(): return lax.ppermute(values, ROW, [(i, (i + by) % X) for i in range(X)])  20.2 us
    all_to_all x2, starting transfers between devices, swap(): lax.all_to_all(values, PEERS, split_axis=0, concat_axis=0, tiled=True)  16.7 us
    all_to_all x2, waiting for transfers between devices, swap(): lax.all_to_all(values, PEERS, split_axis=0, concat_axis=0, tiled=True)  13.9 us
    ppermute x6, waiting for transfers between devices, shift(): return lax.ppermute(values, ROW, [(i, (i + by) % X) for i in range(X)])  8.4 us
    pallas_call x4, Pallas kernels, query_call(): call(functools.partial(query_kernel, k), jax.ShapeDtypeStruct((2 * TILE +...  7.98 us
    ppermute x2, starting transfers between devices, cross(): return lax.ppermute(values, 'pair', [(0, 1), (1, 0)])  3.84 us
    pallas_call x1, Pallas kernels, resp_call(): call(resp_kernel, (shape((PEERS_N, KV_ROWS, LANES), bf16), shape((8, LANE...  3.13 us
    pallas_call x1, Pallas kernels, prompt_call(): call(functools.partial(prompt_kernel, False), (shape((PEERS_N, 2 * PROMPT...  3 us
  transfers between devices with their start and end apart: 10, of which 4 were waited for; matrix products, arithmetic and copies ran while one was open for 0% of the time, Pallas kernels for 17%

profile of v9, /device:TPU:6, one launch (start us, length us, event | category | flops | bytes accessed | tf_op | source)
XLA Modules:
  0.0 88.5 jit_solution(5855784702106662675)
XLA Ops:
  0.6 2.1 %shard_map.145 = bf16[16,264,128]{2,1,0:T(8,128)(2,1)} custom-call(s32[1,3]{1,0:T(1,128)} %lengths_ref.13, f32[1,2,32]{2,1,0:T(2,128)} %logratio_hbm.1, bf16[1,64,256]{2,1,0:T(8,128)(2,1)} %pk_hbm.1, bf16[1,64,256]{2,1,0:T(8,128)(2,1)} %pv_hbm.1, bf16[1,1,32,512]{3,2,1,0:T(8,128)(2,1)} %rk_hbm.1, bf16[1,1,32,512]{3,2,1,0:T(8,128)(2,1)} %rv_hbm.1), custom_call_target="tpu_custom_call" | custom-call | bytes 2097152 | tf_op jit(solution)/shard_map/pallas_call | solution.py:454
  2.7 0.0 copy-start
  2.7 0.0 copy-start.1
  2.7 0.0 copy-start.2
  2.7 0.0 copy-start.3
  2.8 8.7 %all-to-all-start = ((bf16[16,264,128]{2,1,0:T(8,128)(2,1)}), bf16[16,264,128]{2,1,0:T(8,128)(2,1)S(1)}, u32[]{:S(2)}, u32[]{:S(2)}) async-start(bf16[16,264,128]{2,1,0:T(8,128)(2,1)} %shard_map.145), calls=%async_computation | async-start | bytes 2162688 | tf_op jit(solution)/shard_map/all_to_all | solution.py:373
  11.5 0.0 copy-done
  11.5 0.0 copy-done.1
  11.5 0.0 copy-done.2
  11.5 0.0 copy-done.3
  11.5 0.0 copy-start.4
  11.5 0.6 shard_map.146
  12.1 1.9 %collective-permute-start.1 = (bf16[2,528,128]{2,1,0:T(8,128)(2,1)S(1)}, bf16[2,528,128]{2,1,0:T(8,128)(2,1)S(1)}, u32[]{:S(2)}, u32[]{:S(2)}) collective-permute-start(bf16[2,528,128]{2,1,0:T(8,128)(2,1)S(1)} %get-tuple-element.30), channel_id=1, source_target_pairs={{0,32},{32,0},{1,33},{33,1},{2,34},{34,2},{3,35},{35,3},{4,36},{36... | collective-permute-start | bytes 811016 | tf_op jit(solution)/shard_map/ppermute | solution.py:377
  14.0 1.5 %collective-permute-done.1.other_ref = bf16[2,528,128]{2,1,0:T(8,128)(2,1)S(1)} collective-permute-done((bf16[2,528,128]{2,1,0:T(8,128)(2,1)S(1)}, bf16[2,528,128]{2,1,0:T(8,128)(2,1)S(1)}, u32[]{:S(2)}, u32[]{:S(2)}) %collective-permute-start.1) | collective-permute-done | bytes 270368 | tf_op jit(solution)/shard_map/ppermute | solution.py:377
  15.6 2.9 %collective-permute-start.4 = (bf16[2,528,128]{2,1,0:T(8,128)(2,1)S(1)}, bf16[2,528,128]{2,1,0:T(8,128)(2,1)S(1)}, u32[]{:S(2)}, u32[]{:S(2)}) collective-permute-start(bf16[2,528,128]{2,1,0:T(8,128)(2,1)S(1)} %get-tuple-element.32), channel_id=1, source_target_pairs={{0,1},{1,2},{2,3},{3,0},{4,5},{5,6},{6,7},{7,4},{8,9},{9,10},{10,1... | collective-permute-start | bytes 811016 | tf_op jit(solution)/shard_map/ppermute | solution.py:381
  18.5 2.9 %collective-permute-start.3 = (bf16[2,528,128]{2,1,0:T(8,128)(2,1)S(1)}, bf16[2,528,128]{2,1,0:T(8,128)(2,1)S(1)}, u32[]{:S(2)}, u32[]{:S(2)}) collective-permute-start(bf16[2,528,128]{2,1,0:T(8,128)(2,1)S(1)} %get-tuple-element.32), channel_id=1, source_target_pairs={{0,3},{1,0},{2,1},{3,2},{4,7},{5,4},{6,5},{7,6},{8,11},{9,8},{10,9... | collective-permute-start | bytes 811016 | tf_op jit(solution)/shard_map/ppermute | solution.py:381
  21.4 4.1 %collective-permute-start.2 = (bf16[2,528,128]{2,1,0:T(8,128)(2,1)S(1)}, bf16[2,528,128]{2,1,0:T(8,128)(2,1)S(1)}, u32[]{:S(2)}, u32[]{:S(2)}) collective-permute-start(bf16[2,528,128]{2,1,0:T(8,128)(2,1)S(1)} %get-tuple-element.31.qa.q_ref), channel_id=1, source_target_pairs={{0,2},{1,3},{2,0},{3,1},{4,6},{5,7},{6,4},{7,5},{8,10},{9,11},{10,... | collective-permute-start | bytes 811016 | tf_op jit(solution)/shard_map/ppermute | solution.py:381
  25.6 13.9 %all-to-all-done.kv_ref = bf16[16,264,128]{2,1,0:T(8,128)(2,1)S(1)} async-done(((bf16[16,264,128]{2,1,0:T(8,128)(2,1)}), bf16[16,264,128]{2,1,0:T(8,128)(2,1)S(1)}, u32[]{:S(2)}, u32[]{:S(2)}) %all-to-all-start) | async-done | bytes 1081376 | tf_op jit(solution)/shard_map/all_to_all | solution.py:373
  39.5 1.9 %collective-permute-start = (bf16[16,64,128]{2,1,0:T(8,128)(2,1)S(1)}, bf16[16,64,128]{2,1,0:T(8,128)(2,1)S(1)}, u32[]{:S(2)}, u32[]{:S(2)}) collective-permute-start(bf16[16,64,128]{2,1,0:T(8,128)(2,1)S(1)} %slice.4), channel_id=1, source_target_pairs={{0,32},{32,0},{1,33},{33,1},{2,34},{34,2},{3,35},{35,3},{4,36},{36... | collective-permute-start | bytes 786440 | tf_op jit(solution)/shard_map/ppermute | solution.py:377
  41.4 0.0 collective-permute-done.4.qb.q_ref
  41.4 0.0 copy-done.4
  41.4 3.0 %shard_map.148 = (f32[1024,128]{1,0:T(8,128)S(1)}, f32[1024,128]{1,0:T(8,128)S(1)}, bf16[1024,128]{1,0:T(8,128)(2,1)S(1)}, bf16[1024,128]{1,0:T(8,128)(2,1)S(1)}...) custom-call(s32[1,3]{1,0:T(1,128)S(1)} %copy-done.4, bf16[2,528,128]{2,1,0:T(8,128)(2,1)S(1)} %get-tuple-element.31.qa.q_ref, ...), custom_call_target="tpu_custom_call" | custom-call | flops 2147483648 | bytes 2097152 | tf_op jit(solution)/shard_map/pallas_call | solution.py:396
  44.4 0.0 collective-permute-done.3.qb.q_ref
  44.4 0.6 collective-permute-done.2.qa.q_ref
  45.0 3.0 %shard_map.149 = (bf16[16,128,128]{2,1,0:T(8,128)(2,1)S(1)}, bf16[1024,128]{1,0:T(8,128)(2,1)S(1)}, bf16[1024,128]{1,0:T(8,128)(2,1)S(1)}, f32[4,256]{1,0:T(4,128)S(1)}, f32[4,256]{1,0:T(4,128)S(1)}) custom-call(s32[1,3]{1,0:T(1,128)S(1)} %copy-done.4, bf16[2,528,128]{2,1,0:T(8,128)(2,1)S(1)} %collective-permute-done.2.qa.q_ref, ...), custom_call_target="tpu_custom_call" | custom-call | flops 2147483648 | bytes 2097152 | tf_op jit(solution)/shard_map/pallas_call | solution.py:399
  48.0 0.0 collective-permute-done.side_ref
  48.0 0.0 copy-start.5
  48.0 3.1 %shard_map.150 = (bf16[16,256,128]{2,1,0:T(8,128)(2,1)}, f32[8,128]{1,0:T(8,128)S(1)}) custom-call(bf16[16,264,128]{2,1,0:T(8,128)(2,1)S(1)} %all-to-all-done.kv_ref, bf16[16,64,128]{2,1,0:T(8,128)(2,1)S(1)} %collective-permute-done.side_ref, bf16[16,128,128]{2,1,0:T(8,128)(2,1)S(1)} %get-tuple-element.35.prompt_ref, ...), custom_call_target="tpu_custom_call" | custom-call | flops 2147483648 | bytes 3145728 | tf_op jit(solution)/shard_map/pallas_call | solution.py:411
  51.2 0.0 copy-done.5
  51.2 8.0 %all-to-all-start.1 = ((bf16[16,256,128]{2,1,0:T(8,128)(2,1)}), bf16[16,256,128]{2,1,0:T(8,128)(2,1)S(1)}, u32[]{:S(2)}, u32[]{:S(2)}) async-start(bf16[16,256,128]{2,1,0:T(8,128)(2,1)} %get-tuple-element.45), calls=%async_computation.1 | async-start | bytes 2097152 | tf_op jit(solution)/shard_map/all_to_all | solution.py:373
  59.2 0.0 copy-start.6
  59.2 0.9 %copy-done.6 = bf16[16,64,128]{2,1,0:T(8,128)(2,1)S(1)} copy-done((bf16[16,64,128]{2,1,0:T(8,128)(2,1)S(1)}, bf16[16,64,128]{2,1,0:T(8,128)(2,1)}, u32[]{:S(2)}) %copy-start.6) | copy-done | bytes 262168
  60.1 2.0 %shard_map.154 = bf16[512,128]{1,0:T(8,128)(2,1)S(1)} custom-call(s32[1,3]{1,0:T(1,128)S(1)} %copy-done.4, f32[8,128]{1,0:T(8,128)S(1)} %get-tuple-element.44.margin_ref, bf16[2,528,128]{2,1,0:T(8,128)(2,1)S(1)} %collective-permute-done.4.qb.q_ref, bf16[16,264,128]{2,1,0:T(8,128)(2,1)S(1)} %all-to-all-done.kv_ref, bf16[16,64,128]{2,1,0:T(8,128)(2,1)S(1)} %copy-done.6), custom_call_target="tpu_custom_call" | custom-call | flops 1207959552 | bytes 3145728 | tf_op jit(solution)/shard_map/pallas_call | solution.py:432
  62.1 2.0 %collective-permute-start.6 = (bf16[512,128]{1,0:T(8,128)(2,1)S(1)}, bf16[512,128]{1,0:T(8,128)(2,1)S(1)}, u32[]{:S(2)}, u32[]{:S(2)}) collective-permute-start(bf16[512,128]{1,0:T(8,128)(2,1)S(1)} %shard_map.154), channel_id=1, source_target_pairs={{0,3},{1,0},{2,1},{3,2},{4,7},{5,4},{6,5},{7,6},{8,11},{9,8},{10,9... | collective-permute-start | bytes 393224 | tf_op jit(solution)/shard_map/ppermute | solution.py:381
  64.2 2.0 %shard_map.151 = bf16[528,128]{1,0:T(8,128)(2,1)S(1)} custom-call(s32[1,3]{1,0:T(1,128)S(1)} %copy-done.4, f32[8,128]{1,0:T(8,128)S(1)} %get-tuple-element.44.margin_ref, bf16[2,528,128]{2,1,0:T(8,128)(2,1)S(1)} %collective-permute-done.2.qa.q_ref, bf16[16,264,128]{2,1,0:T(8,128)(2,1)S(1)} %all-to-all-done.kv_ref, bf16[16,64,128]{2,1,0:T(8,128)(2,1)S(1)} %copy-done.6), custom_call_target="tpu_custom_call" | custom-call | flops 1207959552 | bytes 3145728 | tf_op jit(solution)/shard_map/pallas_call | solution.py:432
  66.2 3.7 %collective-permute-start.5 = (bf16[528,128]{1,0:T(8,128)(2,1)S(1)}, bf16[528,128]{1,0:T(8,128)(2,1)S(1)}, u32[]{:S(2)}, u32[]{:S(2)}) collective-permute-start(bf16[528,128]{1,0:T(8,128)(2,1)S(1)} %shard_map.151), channel_id=1, source_target_pairs={{0,2},{1,3},{2,0},{3,1},{4,6},{5,7},{6,4},{7,5},{8,10},{9,11},{10,... | collective-permute-start | bytes 405512 | tf_op jit(solution)/shard_map/ppermute | solution.py:381
  69.9 2.0 %shard_map.155 = bf16[512,128]{1,0:T(8,128)(2,1)S(1)} custom-call(s32[1,3]{1,0:T(1,128)S(1)} %copy-done.4, f32[8,128]{1,0:T(8,128)S(1)} %get-tuple-element.44.margin_ref, bf16[2,528,128]{2,1,0:T(8,128)(2,1)S(1)} %collective-permute-done.3.qb.q_ref, bf16[16,264,128]{2,1,0:T(8,128)(2,1)S(1)} %all-to-all-done.kv_ref, bf16[16,64,128]{2,1,0:T(8,128)(2,1)S(1)} %copy-done.6), custom_call_target="tpu_custom_call" | custom-call | flops 1207959552 | bytes 3145728 | tf_op jit(solution)/shard_map/pallas_call | solution.py:432
  71.9 4.4 %collective-permute-start.7 = (bf16[512,128]{1,0:T(8,128)(2,1)S(1)}, bf16[512,128]{1,0:T(8,128)(2,1)S(1)}, u32[]{:S(2)}, u32[]{:S(2)}) collective-permute-start(bf16[512,128]{1,0:T(8,128)(2,1)S(1)} %shard_map.155), channel_id=1, source_target_pairs={{0,1},{1,2},{2,3},{3,0},{4,5},{5,6},{6,7},{7,4},{8,9},{9,10},{10,1... | collective-permute-start | bytes 393224 | tf_op jit(solution)/shard_map/ppermute | solution.py:381
  76.4 2.0 %shard_map.153.d0 = bf16[512,128]{1,0:T(8,128)(2,1)S(1)} custom-call(s32[1,3]{1,0:T(1,128)S(1)} %copy-done.4, f32[8,128]{1,0:T(8,128)S(1)} %get-tuple-element.44.margin_ref, bf16[2,528,128]{2,1,0:T(8,128)(2,1)S(1)} %get-tuple-element.31.qa.q_ref, bf16[16,264,128]{2,1,0:T(8,128)(2,1)S(1)} %all-to-all-done.kv_ref, bf16[16,64,128]{2,1,0:T(8,128)(2,1)S(1)} %copy-done.6), custom_call_target="tpu_custom_call" | custom-call | flops 1207959552 | bytes 3145728 | tf_op jit(solution)/shard_map/pallas_call | solution.py:432
  78.3 0.0 collective-permute-done.6.d1
  78.4 7.8 %collective-permute-done.7.d3 = bf16[512,128]{1,0:T(8,128)(2,1)S(1)} collective-permute-done((bf16[512,128]{1,0:T(8,128)(2,1)S(1)}, bf16[512,128]{1,0:T(8,128)(2,1)S(1)}, u32[]{:S(2)}, u32[]{:S(2)}) %collective-permute-start.7) | collective-permute-done | bytes 131104 | tf_op jit(solution)/shard_map/ppermute | solution.py:381
  86.2 0.0 collective-permute-done.5.d2
  86.2 0.9 %shard_map.156 = (bf16[1,2,32,2048]{3,2,1,0:T(8,128)(2,1)}, f32[1]{0:T(128)}) custom-call(f32[8,128]{1,0:T(8,128)S(1)} %get-tuple-element.44.margin_ref, bf16[512,128]{1,0:T(8,128)(2,1)S(1)} %shard_map.153.d0, bf16[512,128]{1,0:T(8,128)(2,1)S(1)} %collective-permute-done.6.d1, bf16[528,128]{1,0:T(8,128)(2,1)S(1)} %collective-permute-done.5.d2, ...), custom_call_target="tpu_custom_call" | custom-call | bytes 1048576 | tf_op jit(solution)/shard_map/pallas_call | solution.py:497
  87.1 0.0 all-to-all-done.1.part_ref
  87.1 1.4 %shard_map.152 = (bf16[1,64,256]{2,1,0:T(8,128)(2,1)}, bf16[1,64,256]{2,1,0:T(8,128)(2,1)}, bf16[1,2,32,256]{3,2,1,0:T(8,128)(2,1)}, bf16[1,2,32,256]{3,2,1,0:T(8,128)(2,1)}) custom-call(s32[1,3]{1,0:T(1,128)S(1)} %copy-done.4, f32[8,128]{1,0:T(8,128)S(1)} %get-tuple-element.44.margin_ref, bf16[528,128]{1,0:T(8,128)(2,1)S(1)} %collective-permute-done.5.d2, ...), custom_call_target="tpu_custom_call" | custom-call | bytes 1048576 | tf_op jit(solution)/shard_map/pallas_call | solution.py:505
  (2 shorter events, 0.1 us)
Async XLA Ops:
  2.7 8.8 %copy-start = (bf16[1,1,32,4096]{3,2,1,0:T(8,128)(2,1)S(1)}, bf16[1,1,32,4096]{3,2,1,0:T(8,128)(2,1)}, u32[]{:S(2)}) copy-start(bf16[1,1,32,4096]{3,2,1,0:T(8,128)(2,1)} %q_hbm.1) | copy-start | bytes 786436
  2.7 8.8 %copy-start.1 = (bf16[1,1,32,4096]{3,2,1,0:T(8,128)(2,1)S(1)}, bf16[1,1,32,4096]{3,2,1,0:T(8,128)(2,1)}, u32[]{:S(2)}) copy-start(bf16[1,1,32,4096]{3,2,1,0:T(8,128)(2,1)} %g_hbm.1) | copy-start | bytes 786436
  2.7 8.8 %copy-start.2 = (bf16[1,1,32,32]{3,2,1,0:T(8,128)(2,1)S(1)}, bf16[1,1,32,32]{3,2,1,0:T(8,128)(2,1)}, u32[]{:S(2)}) copy-start(bf16[1,1,32,32]{3,2,1,0:T(8,128)(2,1)} %lse_hbm.1) | copy-start | bytes 6148
  2.7 8.8 %copy-start.3 = (bf16[1,1,32,32]{3,2,1,0:T(8,128)(2,1)S(1)}, bf16[1,1,32,32]{3,2,1,0:T(8,128)(2,1)}, u32[]{:S(2)}) copy-start(bf16[1,1,32,32]{3,2,1,0:T(8,128)(2,1)} %delta_hbm.1) | copy-start | bytes 6148
  2.8 36.7 %all-to-all-start = ((bf16[16,264,128]{2,1,0:T(8,128)(2,1)}), bf16[16,264,128]{2,1,0:T(8,128)(2,1)S(1)}, u32[]{:S(2)}, u32[]{:S(2)}) async-start(bf16[16,264,128]{2,1,0:T(8,128)(2,1)} %shard_map.145), calls=%async_computation | async-start | bytes 2162688 | tf_op jit(solution)/shard_map/all_to_all | solution.py:373
  11.5 29.9 %copy-start.4 = (s32[1,3]{1,0:T(1,128)S(1)}, s32[1,3]{1,0:T(1,128)}, u32[]{:S(2)}) copy-start(s32[1,3]{1,0:T(1,128)} %lengths_ref.13) | copy-start | bytes 40
  12.1 3.4 %collective-permute-start.1 = (bf16[2,528,128]{2,1,0:T(8,128)(2,1)S(1)}, bf16[2,528,128]{2,1,0:T(8,128)(2,1)S(1)}, u32[]{:S(2)}, u32[]{:S(2)}) collective-permute-start(bf16[2,528,128]{2,1,0:T(8,128)(2,1)S(1)} %get-tuple-element.30), channel_id=1, source_target_pairs={{0,32},{32,0},{1,33},{33,1},{2,34},{34,2},{3,35},{35,3},{4,36},{36... | collective-permute-start | bytes 811016 | tf_op jit(solution)/shard_map/ppermute | solution.py:377
  15.6 25.8 %collective-permute-start.4 = (bf16[2,528,128]{2,1,0:T(8,128)(2,1)S(1)}, bf16[2,528,128]{2,1,0:T(8,128)(2,1)S(1)}, u32[]{:S(2)}, u32[]{:S(2)}) collective-permute-start(bf16[2,528,128]{2,1,0:T(8,128)(2,1)S(1)} %get-tuple-element.32), channel_id=1, source_target_pairs={{0,1},{1,2},{2,3},{3,0},{4,5},{5,6},{6,7},{7,4},{8,9},{9,10},{10,1... | collective-permute-start | bytes 811016 | tf_op jit(solution)/shard_map/ppermute | solution.py:381
  18.5 25.9 %collective-permute-start.3 = (bf16[2,528,128]{2,1,0:T(8,128)(2,1)S(1)}, bf16[2,528,128]{2,1,0:T(8,128)(2,1)S(1)}, u32[]{:S(2)}, u32[]{:S(2)}) collective-permute-start(bf16[2,528,128]{2,1,0:T(8,128)(2,1)S(1)} %get-tuple-element.32), channel_id=1, source_target_pairs={{0,3},{1,0},{2,1},{3,2},{4,7},{5,4},{6,5},{7,6},{8,11},{9,8},{10,9... | collective-permute-start | bytes 811016 | tf_op jit(solution)/shard_map/ppermute | solution.py:381
  21.4 23.5 %collective-permute-start.2 = (bf16[2,528,128]{2,1,0:T(8,128)(2,1)S(1)}, bf16[2,528,128]{2,1,0:T(8,128)(2,1)S(1)}, u32[]{:S(2)}, u32[]{:S(2)}) collective-permute-start(bf16[2,528,128]{2,1,0:T(8,128)(2,1)S(1)} %get-tuple-element.31.qa.q_ref), channel_id=1, source_target_pairs={{0,2},{1,3},{2,0},{3,1},{4,6},{5,7},{6,4},{7,5},{8,10},{9,11},{10,... | collective-permute-start | bytes 811016 | tf_op jit(solution)/shard_map/ppermute | solution.py:381
  39.5 8.5 %collective-permute-start = (bf16[16,64,128]{2,1,0:T(8,128)(2,1)S(1)}, bf16[16,64,128]{2,1,0:T(8,128)(2,1)S(1)}, u32[]{:S(2)}, u32[]{:S(2)}) collective-permute-start(bf16[16,64,128]{2,1,0:T(8,128)(2,1)S(1)} %slice.4), channel_id=1, source_target_pairs={{0,32},{32,0},{1,33},{33,1},{2,34},{34,2},{3,35},{35,3},{4,36},{36... | collective-permute-start | bytes 786440 | tf_op jit(solution)/shard_map/ppermute | solution.py:377
  48.0 3.2 %copy-start.5 = (bf16[16,64,128]{2,1,0:T(8,128)(2,1)}, bf16[16,64,128]{2,1,0:T(8,128)(2,1)S(1)}, u32[]{:S(2)}) copy-start(bf16[16,64,128]{2,1,0:T(8,128)(2,1)S(1)} %collective-permute-done.side_ref) | copy-start | bytes 786436
  51.2 35.9 %all-to-all-start.1 = ((bf16[16,256,128]{2,1,0:T(8,128)(2,1)}), bf16[16,256,128]{2,1,0:T(8,128)(2,1)S(1)}, u32[]{:S(2)}, u32[]{:S(2)}) async-start(bf16[16,256,128]{2,1,0:T(8,128)(2,1)} %get-tuple-element.45), calls=%async_computation.1 | async-start | bytes 2097152 | tf_op jit(solution)/shard_map/all_to_all | solution.py:373
  59.2 0.9 %copy-start.6 = (bf16[16,64,128]{2,1,0:T(8,128)(2,1)S(1)}, bf16[16,64,128]{2,1,0:T(8,128)(2,1)}, u32[]{:S(2)}) copy-start(bf16[16,64,128]{2,1,0:T(8,128)(2,1)} %copy-done.5) | copy-start | bytes 786436
  62.1 16.2 %collective-permute-start.6 = (bf16[512,128]{1,0:T(8,128)(2,1)S(1)}, bf16[512,128]{1,0:T(8,128)(2,1)S(1)}, u32[]{:S(2)}, u32[]{:S(2)}) collective-permute-start(bf16[512,128]{1,0:T(8,128)(2,1)S(1)} %shard_map.154), channel_id=1, source_target_pairs={{0,3},{1,0},{2,1},{3,2},{4,7},{5,4},{6,5},{7,6},{8,11},{9,8},{10,9... | collective-permute-start | bytes 393224 | tf_op jit(solution)/shard_map/ppermute | solution.py:381
  66.2 20.0 %collective-permute-start.5 = (bf16[528,128]{1,0:T(8,128)(2,1)S(1)}, bf16[528,128]{1,0:T(8,128)(2,1)S(1)}, u32[]{:S(2)}, u32[]{:S(2)}) collective-permute-start(bf16[528,128]{1,0:T(8,128)(2,1)S(1)} %shard_map.151), channel_id=1, source_target_pairs={{0,2},{1,3},{2,0},{3,1},{4,6},{5,7},{6,4},{7,5},{8,10},{9,11},{10,... | collective-permute-start | bytes 405512 | tf_op jit(solution)/shard_map/ppermute | solution.py:381
  71.9 14.3 %collective-permute-start.7 = (bf16[512,128]{1,0:T(8,128)(2,1)S(1)}, bf16[512,128]{1,0:T(8,128)(2,1)S(1)}, u32[]{:S(2)}, u32[]{:S(2)}) collective-permute-start(bf16[512,128]{1,0:T(8,128)(2,1)S(1)} %shard_map.155), channel_id=1, source_target_pairs={{0,1},{1,2},{2,3},{3,0},{4,5},{5,6},{6,7},{7,4},{8,9},{9,10},{10,1... | collective-permute-start | bytes 393224 | tf_op jit(solution)/shard_map/ppermute | solution.py:381

commit v10 on v9

--- a/solution.py
+++ b/solution.py
@@ -216,7 +216,7 @@
             at = tile_rows(t)
             query_rows[at, :] = ref[j, 0:TILE, :]
             grad_rows[at, :] = ref[j, TILE : 2 * TILE, :]
-            k = n if first_half else 2 + n
+            k = 2 * n if first_half else 2 * n + 1
             lse, delta = row_stats(lengths_ref, ref[j, 2 * TILE :, :], k, j)
             lse_ref[t : t + 1, :], delta_ref[t : t + 1, :] = lse, delta
     per = PROMPT_BLOCK // PROMPT
@@ -267,9 +267,9 @@
         value = ref[rows, start + POS : start + SIDE, :].reshape(BLOCK, LANES)
         positions = key_positions(c, BLOCK)
         for k in range(X):
-            query_rows, grad_rows, lse_ref, delta_ref = halves[k // 2]
-            t = j * 2 + k % 2
-            at, to = tile_rows(t), tile_rows(k)
+            query_rows, grad_rows, lse_ref, delta_ref = halves[k % 2]
+            t = j * 2 + k // 2
+            at, to = tile_rows(t), tile_rows(k % 2 * 2 + k // 2)
             weights[slot, :, to], score_grads[slot, :, to] = cell(
                 key,
                 value,
@@ -394,15 +394,17 @@
     scratch = (pltpu.VMEM((2, PROMPT_BLOCK, count), bf16), pltpu.VMEM((2, PROMPT_BLOCK, count), bf16))
     cost = dict(flops=2 * 2 * 2048 * 1024 * 128 * 2, size=2 * 2**20, scratch=scratch)
     key_sum, value_sum, *first = call(functools.partial(prompt_kernel, True), sums + tables, "svvv", **cost)(
-        lengths, rows[0], rows[1], kv
+        lengths, rows[0], rows[2], kv
     )
+    key_sum, source = lax.optimization_barrier((key_sum, kv))
+    side = cross(source[:, KV_ROWS - SIDE : KV_ROWS, :])
     part, *second = call(
         functools.partial(prompt_kernel, False),
         (shape((PEERS_N, 2 * PROMPT, LANES), bf16),) + tables,
         "svvvvv",
         **cost,
-    )(lengths, rows[2], rows[3], kv, key_sum, value_sum)
-    return part, *first, *second
+    )(lengths, rows[1], rows[3], kv, key_sum, value_sum)
+    return side, part, *first, *second
 
 
 def resp_call(kv, side, prompt_part, *rows):
@@ -488,8 +490,7 @@
     same, odd = call(join_kernel, (block, block), "vv", size=2**20)(own, cross(other))
     rows = (same, shift(odd, 1), shift(same, 2), shift(odd, 3))
 
-    side = cross(kv[:, KV_ROWS - SIDE : KV_ROWS, :])
-    prompt_part, *tables = prompt_call(lengths, rows, kv)
+    side, prompt_part, *tables = prompt_call(lengths, rows, kv)
     part, margin = resp_call(kv, side, prompt_part, *tables)
     grads = [query_call(k, lengths, margin, rows[k], kv, side) for k in range(X)]
     part = swap(part)

time: 89.1 us -> 88.6 us (level); the launches traced: 88.5 us -> 86.9 us
  waiting for transfers between devices: 23.8 us -> 21.8 us
    all_to_all x2, waiting for transfers between devices: 13.9 us -> 7.1 us  [swap(): lax.all_to_all(values, PEERS, split_axis=0, concat_axis=0, tiled=True)]
    ppermute x6, waiting for transfers between devices: 8.4 us -> 13.2 us  [shift(): return lax.ppermute(values, ROW, [(i, (i + by) % X) for i in range(X)])]
    ppermute x6, starting transfers between devices: 20.2 us -> 22.2 us  [shift(): return lax.ppermute(values, ROW, [(i, (i + by) % X) for i in range(X)])]
    all_to_all x2, starting transfers between devices: 16.7 us -> 15.2 us  [swap(): lax.all_to_all(values, PEERS, split_axis=0, concat_axis=0, tiled=True)]
  transfers between devices with their start and end apart: 10 -> 10, of which waited for: 4 -> 4; matrix products, arithmetic and copies ran while one was open for 0% -> 0% of each run, Pallas kernels for 17% -> 18%
where the time goes in v10:
time: 88.6 us; the launch traced here: 86.9 us
  starting transfers between devices  41.2 us (47%)
  Pallas kernels  22 us (25%)
  waiting for transfers between devices  21.8 us (25%)
  local copies, waits for them, and re-layouts  1 us (1%)
  between operations  0.89 us (1%)
    ppermute x6, starting transfers between devices, shift(): return lax.ppermute(values, ROW, [(i, (i + by) % X) for i in range(X)])  22.2 us
    all_to_all x2, starting transfers between devices, swap(): lax.all_to_all(values, PEERS, split_axis=0, concat_axis=0, tiled=True)  15.2 us
    ppermute x6, waiting for transfers between devices, shift(): return lax.ppermute(values, ROW, [(i, (i + by) % X) for i in range(X)])  13.2 us
    pallas_call x4, Pallas kernels, query_call(): call(functools.partial(query_kernel, k), jax.ShapeDtypeStruct((2 * TILE +...  7.98 us
    all_to_all x2, waiting for transfers between devices, swap(): lax.all_to_all(values, PEERS, split_axis=0, concat_axis=0, tiled=True)  7.1 us
    ppermute x2, starting transfers between devices, cross(): return lax.ppermute(values, 'pair', [(0, 1), (1, 0)])  3.84 us
    pallas_call x1, Pallas kernels, resp_call(): call(resp_kernel, (shape((PEERS_N, KV_ROWS, LANES), bf16), shape((8, LANE...  3.15 us
    pallas_call x1, Pallas kernels, prompt_call(): call(functools.partial(prompt_kernel, False), (shape((PEERS_N, 2 * PROMPT...  3 us
  transfers between devices with their start and end apart: 10, of which 4 were waited for; matrix products, arithmetic and copies ran while one was open for 0% of the time, Pallas kernels for 18%

profile of v10, /device:TPU:6, one launch (start us, length us, event | category | flops | bytes accessed | tf_op | source)
XLA Modules:
  0.0 86.9 jit_solution(15407380518571708366)
XLA Ops:
  0.6 2.1 %shard_map.145 = bf16[16,264,128]{2,1,0:T(8,128)(2,1)} custom-call(s32[1,3]{1,0:T(1,128)} %lengths_ref.13, f32[1,2,32]{2,1,0:T(2,128)} %logratio_hbm.1, bf16[1,64,256]{2,1,0:T(8,128)(2,1)} %pk_hbm.1, bf16[1,64,256]{2,1,0:T(8,128)(2,1)} %pv_hbm.1, bf16[1,1,32,512]{3,2,1,0:T(8,128)(2,1)} %rk_hbm.1, bf16[1,1,32,512]{3,2,1,0:T(8,128)(2,1)} %rv_hbm.1), custom_call_target="tpu_custom_call" | custom-call | bytes 2097152 | tf_op jit(solution)/shard_map/pallas_call | solution.py:456
  2.7 0.0 copy-start
  2.7 0.0 copy-start.1
  2.7 0.0 copy-start.2
  2.7 0.0 copy-start.3
  2.8 8.7 %all-to-all-start = ((bf16[16,264,128]{2,1,0:T(8,128)(2,1)}), bf16[16,264,128]{2,1,0:T(8,128)(2,1)S(1)}, u32[]{:S(2)}, u32[]{:S(2)}) async-start(bf16[16,264,128]{2,1,0:T(8,128)(2,1)} %shard_map.145), calls=%async_computation | async-start | bytes 2162688 | tf_op jit(solution)/shard_map/all_to_all | solution.py:373
  11.5 0.0 copy-done
  11.5 0.0 copy-done.1
  11.5 0.0 copy-done.2
  11.5 0.0 copy-done.3
  11.5 0.0 copy-start.4
  11.5 0.6 shard_map.146
  12.1 1.9 %collective-permute-start = (bf16[2,528,128]{2,1,0:T(8,128)(2,1)S(1)}, bf16[2,528,128]{2,1,0:T(8,128)(2,1)S(1)}, u32[]{:S(2)}, u32[]{:S(2)}) collective-permute-start(bf16[2,528,128]{2,1,0:T(8,128)(2,1)S(1)} %get-tuple-element.32), channel_id=1, source_target_pairs={{0,32},{32,0},{1,33},{33,1},{2,34},{34,2},{3,35},{35,3},{4,36},{36... | collective-permute-start | bytes 811016 | tf_op jit(solution)/shard_map/ppermute | solution.py:377
  14.0 1.5 %collective-permute-done.other_ref = bf16[2,528,128]{2,1,0:T(8,128)(2,1)S(1)} collective-permute-done((bf16[2,528,128]{2,1,0:T(8,128)(2,1)S(1)}, bf16[2,528,128]{2,1,0:T(8,128)(2,1)S(1)}, u32[]{:S(2)}, u32[]{:S(2)}) %collective-permute-start) | collective-permute-done | bytes 270368 | tf_op jit(solution)/shard_map/ppermute | solution.py:377
  15.6 4.1 %collective-permute-start.1 = (bf16[2,528,128]{2,1,0:T(8,128)(2,1)S(1)}, bf16[2,528,128]{2,1,0:T(8,128)(2,1)S(1)}, u32[]{:S(2)}, u32[]{:S(2)}) collective-permute-start(bf16[2,528,128]{2,1,0:T(8,128)(2,1)S(1)} %get-tuple-element.33.qa.q_ref), channel_id=1, source_target_pairs={{0,2},{1,3},{2,0},{3,1},{4,6},{5,7},{6,4},{7,5},{8,10},{9,11},{10,... | collective-permute-start | bytes 811016 | tf_op jit(solution)/shard_map/ppermute | solution.py:381
  19.7 1.9 %collective-permute-start.4 = (bf16[2,528,128]{2,1,0:T(8,128)(2,1)S(1)}, bf16[2,528,128]{2,1,0:T(8,128)(2,1)S(1)}, u32[]{:S(2)}, u32[]{:S(2)}) collective-permute-start(bf16[2,528,128]{2,1,0:T(8,128)(2,1)S(1)} %get-tuple-element.36), channel_id=1, source_target_pairs={{0,3},{1,0},{2,1},{3,2},{4,7},{5,4},{6,5},{7,6},{8,11},{9,8},{10,9... | collective-permute-start | bytes 811016 | tf_op jit(solution)/shard_map/ppermute | solution.py:381
  21.6 5.1 %collective-permute-start.3 = (bf16[2,528,128]{2,1,0:T(8,128)(2,1)S(1)}, bf16[2,528,128]{2,1,0:T(8,128)(2,1)S(1)}, u32[]{:S(2)}, u32[]{:S(2)}) collective-permute-start(bf16[2,528,128]{2,1,0:T(8,128)(2,1)S(1)} %get-tuple-element.36), channel_id=1, source_target_pairs={{0,1},{1,2},{2,3},{3,0},{4,5},{5,6},{6,7},{7,4},{8,9},{9,10},{10,1... | collective-permute-start | bytes 811016 | tf_op jit(solution)/shard_map/ppermute | solution.py:381
  26.8 5.6 %collective-permute-done.1.qb.q_ref = bf16[2,528,128]{2,1,0:T(8,128)(2,1)S(1)} collective-permute-done((bf16[2,528,128]{2,1,0:T(8,128)(2,1)S(1)}, bf16[2,528,128]{2,1,0:T(8,128)(2,1)S(1)}, u32[]{:S(2)}, u32[]{:S(2)}) %collective-permute-start.1) | collective-permute-done | bytes 270368 | tf_op jit(solution)/shard_map/ppermute | solution.py:381
  32.4 7.1 %all-to-all-done.kv_ref = bf16[16,264,128]{2,1,0:T(8,128)(2,1)S(1)} async-done(((bf16[16,264,128]{2,1,0:T(8,128)(2,1)}), bf16[16,264,128]{2,1,0:T(8,128)(2,1)S(1)}, u32[]{:S(2)}, u32[]{:S(2)}) %all-to-all-start) | async-done | bytes 1081376 | tf_op jit(solution)/shard_map/all_to_all | solution.py:373
  39.5 0.0 copy-done.4
  39.5 3.0 %shard_map.148 = (f32[1024,128]{1,0:T(8,128)S(1)}, f32[1024,128]{1,0:T(8,128)S(1)}, bf16[1024,128]{1,0:T(8,128)(2,1)S(1)}, bf16[1024,128]{1,0:T(8,128)(2,1)S(1)}...) custom-call(s32[1,3]{1,0:T(1,128)S(1)} %copy-done.4, bf16[2,528,128]{2,1,0:T(8,128)(2,1)S(1)} %get-tuple-element.33.qa.q_ref, ...), custom_call_target="tpu_custom_call" | custom-call | flops 2147483648 | bytes 2097152 | tf_op jit(solution)/shard_map/pallas_call | solution.py:396
  42.5 1.9 %collective-permute-start.2 = (bf16[16,64,128]{2,1,0:T(8,128)(2,1)S(1)}, bf16[16,64,128]{2,1,0:T(8,128)(2,1)S(1)}, u32[]{:S(2)}, u32[]{:S(2)}) collective-permute-start(bf16[16,64,128]{2,1,0:T(8,128)(2,1)S(1)} %slice.3), channel_id=1, source_target_pairs={{0,32},{32,0},{1,33},{33,1},{2,34},{34,2},{3,35},{35,3},{4,36},{36... | collective-permute-start | bytes 786440 | tf_op jit(solution)/shard_map/ppermute | solution.py:377
  44.4 0.0 collective-permute-done.4.qb.q_ref
  44.4 0.0 collective-permute-done.3.qa.q_ref
  44.4 3.0 %shard_map.149 = (bf16[16,128,128]{2,1,0:T(8,128)(2,1)S(1)}, bf16[1024,128]{1,0:T(8,128)(2,1)S(1)}, bf16[1024,128]{1,0:T(8,128)(2,1)S(1)}, f32[4,256]{1,0:T(4,128)S(1)}, f32[4,256]{1,0:T(4,128)S(1)}) custom-call(s32[1,3]{1,0:T(1,128)S(1)} %copy-done.4, bf16[2,528,128]{2,1,0:T(8,128)(2,1)S(1)} %collective-permute-done.3.qa.q_ref, ...), custom_call_target="tpu_custom_call" | custom-call | flops 2147483648 | bytes 2097152 | tf_op jit(solution)/shard_map/pallas_call | solution.py:401
  47.4 0.0 collective-permute-done.2.side_ref
  47.4 0.0 copy-start.5
  47.4 3.1 %shard_map.150 = (bf16[16,256,128]{2,1,0:T(8,128)(2,1)}, f32[8,128]{1,0:T(8,128)S(1)}) custom-call(bf16[16,264,128]{2,1,0:T(8,128)(2,1)S(1)} %all-to-all-done.kv_ref, bf16[16,64,128]{2,1,0:T(8,128)(2,1)S(1)} %collective-permute-done.2.side_ref, bf16[16,128,128]{2,1,0:T(8,128)(2,1)S(1)} %get-tuple-element.39.prompt_ref, ...), custom_call_target="tpu_custom_call" | custom-call | flops 2147483648 | bytes 3145728 | tf_op jit(solution)/shard_map/pallas_call | solution.py:413
  50.6 0.0 copy-done.5
  50.6 6.5 %all-to-all-start.1 = ((bf16[16,256,128]{2,1,0:T(8,128)(2,1)}), bf16[16,256,128]{2,1,0:T(8,128)(2,1)S(1)}, u32[]{:S(2)}, u32[]{:S(2)}) async-start(bf16[16,256,128]{2,1,0:T(8,128)(2,1)} %get-tuple-element.49), calls=%async_computation.1 | async-start | bytes 2097152 | tf_op jit(solution)/shard_map/all_to_all | solution.py:373
  57.1 0.0 copy-start.6
  57.1 0.9 %copy-done.6 = bf16[16,64,128]{2,1,0:T(8,128)(2,1)S(1)} copy-done((bf16[16,64,128]{2,1,0:T(8,128)(2,1)S(1)}, bf16[16,64,128]{2,1,0:T(8,128)(2,1)}, u32[]{:S(2)}) %copy-start.6) | copy-done | bytes 262168
  58.0 2.0 %shard_map.154 = bf16[512,128]{1,0:T(8,128)(2,1)S(1)} custom-call(s32[1,3]{1,0:T(1,128)S(1)} %copy-done.4, f32[8,128]{1,0:T(8,128)S(1)} %get-tuple-element.48.margin_ref, bf16[2,528,128]{2,1,0:T(8,128)(2,1)S(1)} %collective-permute-done.3.qa.q_ref, bf16[16,264,128]{2,1,0:T(8,128)(2,1)S(1)} %all-to-all-done.kv_ref, bf16[16,64,128]{2,1,0:T(8,128)(2,1)S(1)} %copy-done.6), custom_call_target="tpu_custom_call" | custom-call | flops 1207959552 | bytes 3145728 | tf_op jit(solution)/shard_map/pallas_call | solution.py:434
  60.0 2.0 %collective-permute-start.6 = (bf16[512,128]{1,0:T(8,128)(2,1)S(1)}, bf16[512,128]{1,0:T(8,128)(2,1)S(1)}, u32[]{:S(2)}, u32[]{:S(2)}) collective-permute-start(bf16[512,128]{1,0:T(8,128)(2,1)S(1)} %shard_map.154), channel_id=1, source_target_pairs={{0,3},{1,0},{2,1},{3,2},{4,7},{5,4},{6,5},{7,6},{8,11},{9,8},{10,9... | collective-permute-start | bytes 393224 | tf_op jit(solution)/shard_map/ppermute | solution.py:381
  62.0 2.0 %shard_map.151 = bf16[528,128]{1,0:T(8,128)(2,1)S(1)} custom-call(s32[1,3]{1,0:T(1,128)S(1)} %copy-done.4, f32[8,128]{1,0:T(8,128)S(1)} %get-tuple-element.48.margin_ref, bf16[2,528,128]{2,1,0:T(8,128)(2,1)S(1)} %collective-permute-done.1.qb.q_ref, bf16[16,264,128]{2,1,0:T(8,128)(2,1)S(1)} %all-to-all-done.kv_ref, bf16[16,64,128]{2,1,0:T(8,128)(2,1)S(1)} %copy-done.6), custom_call_target="tpu_custom_call" | custom-call | flops 1207959552 | bytes 3145728 | tf_op jit(solution)/shard_map/pallas_call | solution.py:434
  64.0 4.6 %collective-permute-start.5 = (bf16[528,128]{1,0:T(8,128)(2,1)S(1)}, bf16[528,128]{1,0:T(8,128)(2,1)S(1)}, u32[]{:S(2)}, u32[]{:S(2)}) collective-permute-start(bf16[528,128]{1,0:T(8,128)(2,1)S(1)} %shard_map.151), channel_id=1, source_target_pairs={{0,2},{1,3},{2,0},{3,1},{4,6},{5,7},{6,4},{7,5},{8,10},{9,11},{10,... | collective-permute-start | bytes 405512 | tf_op jit(solution)/shard_map/ppermute | solution.py:381
  68.6 2.0 %shard_map.155 = bf16[512,128]{1,0:T(8,128)(2,1)S(1)} custom-call(s32[1,3]{1,0:T(1,128)S(1)} %copy-done.4, f32[8,128]{1,0:T(8,128)S(1)} %get-tuple-element.48.margin_ref, bf16[2,528,128]{2,1,0:T(8,128)(2,1)S(1)} %collective-permute-done.4.qb.q_ref, bf16[16,264,128]{2,1,0:T(8,128)(2,1)S(1)} %all-to-all-done.kv_ref, bf16[16,64,128]{2,1,0:T(8,128)(2,1)S(1)} %copy-done.6), custom_call_target="tpu_custom_call" | custom-call | flops 1207959552 | bytes 3145728 | tf_op jit(solution)/shard_map/pallas_call | solution.py:434
  70.6 4.4 %collective-permute-start.7 = (bf16[512,128]{1,0:T(8,128)(2,1)S(1)}, bf16[512,128]{1,0:T(8,128)(2,1)S(1)}, u32[]{:S(2)}, u32[]{:S(2)}) collective-permute-start(bf16[512,128]{1,0:T(8,128)(2,1)S(1)} %shard_map.155), channel_id=1, source_target_pairs={{0,1},{1,2},{2,3},{3,0},{4,5},{5,6},{6,7},{7,4},{8,9},{9,10},{10,1... | collective-permute-start | bytes 393224 | tf_op jit(solution)/shard_map/ppermute | solution.py:381
  75.0 2.0 %shard_map.153.d0 = bf16[512,128]{1,0:T(8,128)(2,1)S(1)} custom-call(s32[1,3]{1,0:T(1,128)S(1)} %copy-done.4, f32[8,128]{1,0:T(8,128)S(1)} %get-tuple-element.48.margin_ref, bf16[2,528,128]{2,1,0:T(8,128)(2,1)S(1)} %get-tuple-element.33.qa.q_ref, bf16[16,264,128]{2,1,0:T(8,128)(2,1)S(1)} %all-to-all-done.kv_ref, bf16[16,64,128]{2,1,0:T(8,128)(2,1)S(1)} %copy-done.6), custom_call_target="tpu_custom_call" | custom-call | flops 1207959552 | bytes 3145728 | tf_op jit(solution)/shard_map/pallas_call | solution.py:434
  77.0 0.0 collective-permute-done.6.d1
  77.0 7.6 %collective-permute-done.7.d3 = bf16[512,128]{1,0:T(8,128)(2,1)S(1)} collective-permute-done((bf16[512,128]{1,0:T(8,128)(2,1)S(1)}, bf16[512,128]{1,0:T(8,128)(2,1)S(1)}, u32[]{:S(2)}, u32[]{:S(2)}) %collective-permute-start.7) | collective-permute-done | bytes 131104 | tf_op jit(solution)/shard_map/ppermute | solution.py:381
  84.6 0.0 collective-permute-done.5.d2
  84.6 0.9 %shard_map.156 = (bf16[1,2,32,2048]{3,2,1,0:T(8,128)(2,1)}, f32[1]{0:T(128)}) custom-call(f32[8,128]{1,0:T(8,128)S(1)} %get-tuple-element.48.margin_ref, bf16[512,128]{1,0:T(8,128)(2,1)S(1)} %shard_map.153.d0, bf16[512,128]{1,0:T(8,128)(2,1)S(1)} %collective-permute-done.6.d1, bf16[528,128]{1,0:T(8,128)(2,1)S(1)} %collective-permute-done.5.d2, ...), custom_call_target="tpu_custom_call" | custom-call | bytes 1048576 | tf_op jit(solution)/shard_map/pallas_call | solution.py:498
  85.6 0.0 all-to-all-done.1.part_ref
  85.6 1.4 %shard_map.152 = (bf16[1,64,256]{2,1,0:T(8,128)(2,1)}, bf16[1,64,256]{2,1,0:T(8,128)(2,1)}, bf16[1,2,32,256]{3,2,1,0:T(8,128)(2,1)}, bf16[1,2,32,256]{3,2,1,0:T(8,128)(2,1)}) custom-call(s32[1,3]{1,0:T(1,128)S(1)} %copy-done.4, f32[8,128]{1,0:T(8,128)S(1)} %get-tuple-element.48.margin_ref, bf16[528,128]{1,0:T(8,128)(2,1)S(1)} %collective-permute-done.5.d2, ...), custom_call_target="tpu_custom_call" | custom-call | bytes 1048576 | tf_op jit(solution)/shard_map/pallas_call | solution.py:506
  (2 shorter events, 0.1 us)
Async XLA Ops:
  2.7 8.8 %copy-start = (bf16[1,1,32,4096]{3,2,1,0:T(8,128)(2,1)S(1)}, bf16[1,1,32,4096]{3,2,1,0:T(8,128)(2,1)}, u32[]{:S(2)}) copy-start(bf16[1,1,32,4096]{3,2,1,0:T(8,128)(2,1)} %q_hbm.1) | copy-start | bytes 786436
  2.7 8.8 %copy-start.1 = (bf16[1,1,32,4096]{3,2,1,0:T(8,128)(2,1)S(1)}, bf16[1,1,32,4096]{3,2,1,0:T(8,128)(2,1)}, u32[]{:S(2)}) copy-start(bf16[1,1,32,4096]{3,2,1,0:T(8,128)(2,1)} %g_hbm.1) | copy-start | bytes 786436
  2.7 8.8 %copy-start.2 = (bf16[1,1,32,32]{3,2,1,0:T(8,128)(2,1)S(1)}, bf16[1,1,32,32]{3,2,1,0:T(8,128)(2,1)}, u32[]{:S(2)}) copy-start(bf16[1,1,32,32]{3,2,1,0:T(8,128)(2,1)} %lse_hbm.1) | copy-start | bytes 6148
  2.7 8.8 %copy-start.3 = (bf16[1,1,32,32]{3,2,1,0:T(8,128)(2,1)S(1)}, bf16[1,1,32,32]{3,2,1,0:T(8,128)(2,1)}, u32[]{:S(2)}) copy-start(bf16[1,1,32,32]{3,2,1,0:T(8,128)(2,1)} %delta_hbm.1) | copy-start | bytes 6148
  2.8 36.7 %all-to-all-start = ((bf16[16,264,128]{2,1,0:T(8,128)(2,1)}), bf16[16,264,128]{2,1,0:T(8,128)(2,1)S(1)}, u32[]{:S(2)}, u32[]{:S(2)}) async-start(bf16[16,264,128]{2,1,0:T(8,128)(2,1)} %shard_map.145), calls=%async_computation | async-start | bytes 2162688 | tf_op jit(solution)/shard_map/all_to_all | solution.py:373
  11.5 27.9 %copy-start.4 = (s32[1,3]{1,0:T(1,128)S(1)}, s32[1,3]{1,0:T(1,128)}, u32[]{:S(2)}) copy-start(s32[1,3]{1,0:T(1,128)} %lengths_ref.13) | copy-start | bytes 40
  12.1 3.4 %collective-permute-start = (bf16[2,528,128]{2,1,0:T(8,128)(2,1)S(1)}, bf16[2,528,128]{2,1,0:T(8,128)(2,1)S(1)}, u32[]{:S(2)}, u32[]{:S(2)}) collective-permute-start(bf16[2,528,128]{2,1,0:T(8,128)(2,1)S(1)} %get-tuple-element.32), channel_id=1, source_target_pairs={{0,32},{32,0},{1,33},{33,1},{2,34},{34,2},{3,35},{35,3},{4,36},{36... | collective-permute-start | bytes 811016 | tf_op jit(solution)/shard_map/ppermute | solution.py:377
  15.6 16.8 %collective-permute-start.1 = (bf16[2,528,128]{2,1,0:T(8,128)(2,1)S(1)}, bf16[2,528,128]{2,1,0:T(8,128)(2,1)S(1)}, u32[]{:S(2)}, u32[]{:S(2)}) collective-permute-start(bf16[2,528,128]{2,1,0:T(8,128)(2,1)S(1)} %get-tuple-element.33.qa.q_ref), channel_id=1, source_target_pairs={{0,2},{1,3},{2,0},{3,1},{4,6},{5,7},{6,4},{7,5},{8,10},{9,11},{10,... | collective-permute-start | bytes 811016 | tf_op jit(solution)/shard_map/ppermute | solution.py:381
  19.7 24.7 %collective-permute-start.4 = (bf16[2,528,128]{2,1,0:T(8,128)(2,1)S(1)}, bf16[2,528,128]{2,1,0:T(8,128)(2,1)S(1)}, u32[]{:S(2)}, u32[]{:S(2)}) collective-permute-start(bf16[2,528,128]{2,1,0:T(8,128)(2,1)S(1)} %get-tuple-element.36), channel_id=1, source_target_pairs={{0,3},{1,0},{2,1},{3,2},{4,7},{5,4},{6,5},{7,6},{8,11},{9,8},{10,9... | collective-permute-start | bytes 811016 | tf_op jit(solution)/shard_map/ppermute | solution.py:381
  21.6 22.8 %collective-permute-start.3 = (bf16[2,528,128]{2,1,0:T(8,128)(2,1)S(1)}, bf16[2,528,128]{2,1,0:T(8,128)(2,1)S(1)}, u32[]{:S(2)}, u32[]{:S(2)}) collective-permute-start(bf16[2,528,128]{2,1,0:T(8,128)(2,1)S(1)} %get-tuple-element.36), channel_id=1, source_target_pairs={{0,1},{1,2},{2,3},{3,0},{4,5},{5,6},{6,7},{7,4},{8,9},{9,10},{10,1... | collective-permute-start | bytes 811016 | tf_op jit(solution)/shard_map/ppermute | solution.py:381
  42.5 5.0 %collective-permute-start.2 = (bf16[16,64,128]{2,1,0:T(8,128)(2,1)S(1)}, bf16[16,64,128]{2,1,0:T(8,128)(2,1)S(1)}, u32[]{:S(2)}, u32[]{:S(2)}) collective-permute-start(bf16[16,64,128]{2,1,0:T(8,128)(2,1)S(1)} %slice.3), channel_id=1, source_target_pairs={{0,32},{32,0},{1,33},{33,1},{2,34},{34,2},{3,35},{35,3},{4,36},{36... | collective-permute-start | bytes 786440 | tf_op jit(solution)/shard_map/ppermute | solution.py:377
  47.4 3.2 %copy-start.5 = (bf16[16,64,128]{2,1,0:T(8,128)(2,1)}, bf16[16,64,128]{2,1,0:T(8,128)(2,1)S(1)}, u32[]{:S(2)}) copy-start(bf16[16,64,128]{2,1,0:T(8,128)(2,1)S(1)} %collective-permute-done.2.side_ref) | copy-start | bytes 786436
  50.6 35.0 %all-to-all-start.1 = ((bf16[16,256,128]{2,1,0:T(8,128)(2,1)}), bf16[16,256,128]{2,1,0:T(8,128)(2,1)S(1)}, u32[]{:S(2)}, u32[]{:S(2)}) async-start(bf16[16,256,128]{2,1,0:T(8,128)(2,1)} %get-tuple-element.49), calls=%async_computation.1 | async-start | bytes 2097152 | tf_op jit(solution)/shard_map/all_to_all | solution.py:373
  57.1 0.9 %copy-start.6 = (bf16[16,64,128]{2,1,0:T(8,128)(2,1)S(1)}, bf16[16,64,128]{2,1,0:T(8,128)(2,1)}, u32[]{:S(2)}) copy-start(bf16[16,64,128]{2,1,0:T(8,128)(2,1)} %copy-done.5) | copy-start | bytes 786436
  60.0 17.0 %collective-permute-start.6 = (bf16[512,128]{1,0:T(8,128)(2,1)S(1)}, bf16[512,128]{1,0:T(8,128)(2,1)S(1)}, u32[]{:S(2)}, u32[]{:S(2)}) collective-permute-start(bf16[512,128]{1,0:T(8,128)(2,1)S(1)} %shard_map.154), channel_id=1, source_target_pairs={{0,3},{1,0},{2,1},{3,2},{4,7},{5,4},{6,5},{7,6},{8,11},{9,8},{10,9... | collective-permute-start | bytes 393224 | tf_op jit(solution)/shard_map/ppermute | solution.py:381
  64.0 20.6 %collective-permute-start.5 = (bf16[528,128]{1,0:T(8,128)(2,1)S(1)}, bf16[528,128]{1,0:T(8,128)(2,1)S(1)}, u32[]{:S(2)}, u32[]{:S(2)}) collective-permute-start(bf16[528,128]{1,0:T(8,128)(2,1)S(1)} %shard_map.151), channel_id=1, source_target_pairs={{0,2},{1,3},{2,0},{3,1},{4,6},{5,7},{6,4},{7,5},{8,10},{9,11},{10,... | collective-permute-start | bytes 405512 | tf_op jit(solution)/shard_map/ppermute | solution.py:381
  70.6 14.0 %collective-permute-start.7 = (bf16[512,128]{1,0:T(8,128)(2,1)S(1)}, bf16[512,128]{1,0:T(8,128)(2,1)S(1)}, u32[]{:S(2)}, u32[]{:S(2)}) collective-permute-start(bf16[512,128]{1,0:T(8,128)(2,1)S(1)} %shard_map.155), channel_id=1, source_target_pairs={{0,1},{1,2},{2,3},{3,0},{4,5},{5,6},{6,7},{7,4},{8,9},{9,10},{10,1... | collective-permute-start | bytes 393224 | tf_op jit(solution)/shard_map/ppermute | solution.py:381

commit v11 on v6

--- a/solution.py
+++ b/solution.py
@@ -77,7 +77,7 @@
 
 
 def kv_pack_kernel(
-    lengths_hbm, logratio_hbm, pk_hbm, pv_hbm, rk_hbm, rv_hbm, kv_ref, lengths, logratio, pk, pv, rk, rv, sems
+    lengths_hbm, logratio_hbm, pk_hbm, pv_hbm, rk_hbm, rv_hbm, kv_hbm, lengths, logratio, pk, pv, rk, rv, kv_ref, sems
 ):
     pairs = (
         (lengths_hbm, lengths),
@@ -105,11 +105,17 @@
         parts += [jnp.where(first_core, a, b).astype(bf16) for a, b in zip(low_head, high_head)]
         parts += [jnp.where(first_core, b, a).astype(bf16) for a, b in zip(low_head, high_head)]
         parts += [block]
-        for y in range(ROWS_Y):
-            at = 0
-            for part in parts:
-                kv_ref[y * 2 + xl, at : at + part.shape[0], :] = part
-                at += part.shape[0]
+        at = 0
+        for part in parts:
+            kv_ref[xl, at : at + part.shape[0], :] = part
+            at += part.shape[0]
+    copies = [
+        pltpu.make_async_copy(kv_ref, kv_hbm.at[2 * y : 2 * y + 2], sems.at[6 + y]) for y in range(ROWS_Y)
+    ]
+    for copy in copies:
+        copy.start()
+    for copy in copies:
+        copy.wait()
 
 
 def query_pack_kernel(q_hbm, g_hbm, lse_hbm, delta_hbm, own_ref, other_ref, q, g, lse, delta, sems):
@@ -281,25 +287,32 @@
         copy.wait()
 
 
-def query_kernel(k, margin_ref, kv_ref, side_ref, query_rows, grad_rows, lse_ref, delta_ref, out_ref):
+def query_kernel(k, lengths_ref, margin_ref, q_ref, kv_ref, side_ref, out_ref):
+    items = []
     for j in range(2):
-        t = j * X + k
-        query, grad = query_rows[tile_rows(t), :], grad_rows[tile_rows(t), :]
-        lse, delta = lse_ref[t : t + 1, :], delta_ref[t : t + 1, :]
-        total = None
         resp, start = ((kv_ref, 2 * PROMPT), (side_ref, 0))[j]
-        parts = [(kv_ref, c, PROMPT, 0, None) for c in range(PEERS_N * PROMPT // BLOCK)]
-        for c in range(PEERS_N * POS // BLOCK):
-            parts.append((resp, c, POS, start, key_positions(c, BLOCK) <= row_position(k)))
-        for ref, c, count, start, allowed in parts:
+        items += [(j, kv_ref, c, PROMPT, 0) for c in range(PEERS_N * PROMPT // BLOCK)]
+        items += [(j, resp, c, POS, start) for c in range(PEERS_N * POS // BLOCK)]
+    totals, waiting = [None, None], None
+    for item in items + [None]:
+        if item:
+            j, ref, c, count, start = item
             per = BLOCK // count
             rows = slice(c * per, (c + 1) * per)
             key = ref[rows, start : start + count, :].reshape(BLOCK, LANES)
             value = ref[rows, start + count : start + 2 * count, :].reshape(BLOCK, LANES)
-            _, score_grads = cell(key, value, query, grad, lse, delta, allowed)
-            term = dot(score_grads, key, ((0,), (0,)))
-            total = term if total is None else total + term
-        out_ref[tile_rows(j), :] = (total * SCALE).astype(bf16)
+            allowed = key_positions(c, BLOCK) <= row_position(k) if count == POS else None
+            lse, delta = row_stats(lengths_ref, q_ref[j, 2 * TILE :, :], k, j)
+            _, score_grads = cell(
+                key, value, q_ref[j, 0:TILE, :], q_ref[j, TILE : 2 * TILE, :], lse, delta, allowed
+            )
+        if waiting:
+            n, grads, keys = waiting
+            term = dot(keys, grads, ((0,), (0,)))
+            totals[n] = term if totals[n] is None else totals[n] + term
+        waiting = (j, score_grads, key)
+    for j in range(2):
+        out_ref[tile_rows(j), :] = jnp.transpose(totals[j] * SCALE).astype(bf16)
     if k == 2:
         out_ref[2 * TILE :, :] = split_margin(margin_ref[0:1, 0:1], STAT_ROWS)
 
@@ -325,7 +338,7 @@
 
 def query_final_kernel(margin_ref, d0, d1, d2, d3, out_ref, gate_ref):
     gate = gate_of(margin_ref[0:1, 0:1], d2[2 * TILE :, :])
-    gate_ref[...] = jnp.broadcast_to(gate, gate_ref.shape)
+    gate_ref[0] = gate[0, 0]
     core = lax.axis_index("pair")
     even = lax.axis_index("xl") == 0
     for j in range(2):
@@ -392,15 +405,15 @@
     )(kv, side, prompt_part, *rows)
 
 
-def query_call(k, margin, kv, side, *rows):
+def query_call(k, lengths, margin, rows, kv, side):
     extra = STAT_ROWS if k == 2 else 0
     return call(
         functools.partial(query_kernel, k),
         jax.ShapeDtypeStruct((2 * TILE + extra, LANES), bf16),
-        "vvvvvvv",
+        "svvvv",
         flops=3 * 2 * 512 * 1536 * 128 * 2,
         size=3 * 2**20,
-    )(margin, kv, side, *rows)
+    )(lengths, margin, rows, kv, side)
 
 
 def per_device(
@@ -420,6 +433,7 @@
         kv_pack_kernel,
         shape((PEERS_N, KV_ROWS + MARGIN_ROWS, LANES), bf16),
         "aaaaaa",
+        out_spaces="a",
         size=2 * 2**20,
         limit=60,
         scratch=(
@@ -429,7 +443,8 @@
             pltpu.VMEM((PROMPT, 2 * LANES), bf16),
             pltpu.VMEM((POS, X * LANES), bf16),
             pltpu.VMEM((POS, X * LANES), bf16),
-            pltpu.SemaphoreType.DMA((6,)),
+            pltpu.VMEM((2, KV_ROWS + MARGIN_ROWS, LANES), bf16),
+            pltpu.SemaphoreType.DMA((6 + ROWS_Y,)),
         ),
     )(lengths, logratio, prompt_keys, prompt_values, resp_keys, resp_values)
     kv = swap(kv)
@@ -449,25 +464,27 @@
         ),
     )(queries, resp_grads, resp_lse, resp_delta)
     same, odd = call(join_kernel, (block, block), "vv", size=2**20)(own, cross(other))
-    rows = (same, shift(odd, 1), shift(same, 2), shift(odd, 3))
+    far = shift(same, 2)
+    rows = (same, shift(odd, 1), far, shift(odd, 3))
 
     side = cross(kv[:, KV_ROWS - SIDE : KV_ROWS, :])
-    prompt_part, *rows = prompt_call(lengths, rows, kv)
-    part, margin = resp_call(kv, side, prompt_part, *rows)
-    grads = [query_call(k, margin, kv, side, *rows) for k in range(X)]
+    prompt_part, *tables = prompt_call(lengths, rows, kv)
+    part, margin = resp_call(kv, side, prompt_part, *tables)
+    grads = [query_call(k, lengths, margin, rows[k], kv, side) for k in range(X)]
     part = swap(part)
     back = [grads[0]] + [shift(grads[k], X - k) for k in range(1, X)]
     query_grad, gate = call(
         query_final_kernel,
-        (shape((1, 2, POS, 2 * GROUP * LANES), bf16), shape((8, LANES), f32)),
+        (shape((1, 2, POS, 2 * GROUP * LANES), bf16), shape((1,), f32)),
         "vvvvv",
+        out_spaces="vs",
         size=2**20,
     )(margin, *back)
     outs = (shape((1, PROMPT, 2 * LANES), bf16),) * 2 + (shape((1, 2, POS, 2 * LANES), bf16),) * 2
     pk_grad, pv_grad, key_grad, value_grad = call(kv_final_kernel, outs, "svvv", size=2**20)(
         lengths, margin, back[2], part
     )
-    return pk_grad, pv_grad, query_grad, key_grad, value_grad, gate[0, 0:1]
+    return pk_grad, pv_grad, query_grad, key_grad, value_grad, gate
 
 
 def solution(mesh):

time: 91.4 us -> 90.7 us (level)
  the two profiles are of different devices: /device:TPU:1 before, /device:TPU:6 now
where the time goes in v11:
time: 90.7 us; the launch traced here: 89.5 us
  starting transfers between devices  43.3 us (48%)
  waiting for transfers between devices  23 us (25%)
  Pallas kernels  21.3 us (23%)
  local copies, waits for them, and re-layouts  1 us (1%)
    ppermute x6, starting transfers between devices, shift(): return lax.ppermute(values, ROW, [(i, (i + by) % X) for i in range(X)])  20.9 us
    all_to_all x2, starting transfers between devices, swap(): lax.all_to_all(values, PEERS, split_axis=0, concat_axis=0, tiled=True)  18.6 us
    all_to_all x2, waiting for transfers between devices, swap(): lax.all_to_all(values, PEERS, split_axis=0, concat_axis=0, tiled=True)  13.9 us
    pallas_call x4, Pallas kernels, query_call(): call(functools.partial(query_kernel, k), jax.ShapeDtypeStruct((2 * TILE +...  8.01 us
    ppermute x6, waiting for transfers between devices, shift(): return lax.ppermute(values, ROW, [(i, (i + by) % X) for i in range(X)])  7.58 us
    pallas_call x1, Pallas kernels, prompt_call(): call(prompt_kernel, (shape((PEERS_N, 2 * PROMPT, LANES), bf16), shape((co...  5.15 us
    ppermute x2, starting transfers between devices, cross(): return lax.ppermute(values, 'pair', [(0, 1), (1, 0)])  3.84 us
    pallas_call x1, Pallas kernels, resp_call(): call(resp_kernel, (shape((PEERS_N, KV_ROWS, LANES), bf16), shape((8, LANE...  3.16 us
  transfers between devices with their start and end apart: 10, of which 4 were waited for; matrix products, arithmetic and copies ran while one was open for 0% of the time, Pallas kernels for 16%

profile of v11, /device:TPU:6, one launch (start us, length us, event | category | flops | bytes accessed | tf_op | source)
XLA Modules:
  0.0 89.5 jit_solution(15406719985848464870)
XLA Ops:
  0.6 2.1 %shard_map.145 = bf16[16,264,128]{2,1,0:T(8,128)(2,1)} custom-call(s32[1,3]{1,0:T(1,128)} %lengths_ref.11, f32[1,2,32]{2,1,0:T(2,128)} %logratio_hbm.1, bf16[1,64,256]{2,1,0:T(8,128)(2,1)} %pk_hbm.1, bf16[1,64,256]{2,1,0:T(8,128)(2,1)} %pv_hbm.1, bf16[1,1,32,512]{3,2,1,0:T(8,128)(2,1)} %rk_hbm.1, bf16[1,1,32,512]{3,2,1,0:T(8,128)(2,1)} %rv_hbm.1), custom_call_target="tpu_custom_call" | custom-call | bytes 2097152 | tf_op jit(solution)/shard_map/pallas_call | solution.py:432
  2.7 0.0 copy-start
  2.7 0.0 copy-start.1
  2.7 0.0 copy-start.2
  2.7 0.0 copy-start.3
  2.8 8.7 %all-to-all-start = ((bf16[16,264,128]{2,1,0:T(8,128)(2,1)}), bf16[16,264,128]{2,1,0:T(8,128)(2,1)S(1)}, u32[]{:S(2)}, u32[]{:S(2)}) async-start(bf16[16,264,128]{2,1,0:T(8,128)(2,1)} %shard_map.145), calls=%async_computation | async-start | bytes 2162688 | tf_op jit(solution)/shard_map/all_to_all | solution.py:356
  11.5 0.0 copy-done
  11.5 0.0 copy-done.1
  11.5 0.0 copy-done.2
  11.5 0.0 copy-done.3
  11.5 0.0 copy-start.4
  11.5 0.6 shard_map.146
  12.1 1.9 %collective-permute-start.1 = (bf16[2,528,128]{2,1,0:T(8,128)(2,1)S(1)}, bf16[2,528,128]{2,1,0:T(8,128)(2,1)S(1)}, u32[]{:S(2)}, u32[]{:S(2)}) collective-permute-start(bf16[2,528,128]{2,1,0:T(8,128)(2,1)S(1)} %get-tuple-element.24), channel_id=1, source_target_pairs={{0,32},{32,0},{1,33},{33,1},{2,34},{34,2},{3,35},{35,3},{4,36},{36... | collective-permute-start | bytes 811016 | tf_op jit(solution)/shard_map/ppermute | solution.py:360
  14.0 1.5 %collective-permute-done.1.other_ref = bf16[2,528,128]{2,1,0:T(8,128)(2,1)S(1)} collective-permute-done((bf16[2,528,128]{2,1,0:T(8,128)(2,1)S(1)}, bf16[2,528,128]{2,1,0:T(8,128)(2,1)S(1)}, u32[]{:S(2)}, u32[]{:S(2)}) %collective-permute-start.1) | collective-permute-done | bytes 270368 | tf_op jit(solution)/shard_map/ppermute | solution.py:360
  15.6 2.0 %collective-permute-start.4 = (bf16[2,528,128]{2,1,0:T(8,128)(2,1)S(1)}, bf16[2,528,128]{2,1,0:T(8,128)(2,1)S(1)}, u32[]{:S(2)}, u32[]{:S(2)}) collective-permute-start(bf16[2,528,128]{2,1,0:T(8,128)(2,1)S(1)} %get-tuple-element.26), channel_id=1, source_target_pairs={{0,3},{1,0},{2,1},{3,2},{4,7},{5,4},{6,5},{7,6},{8,11},{9,8},{10,9... | collective-permute-start | bytes 811016 | tf_op jit(solution)/shard_map/ppermute | solution.py:364
  17.6 5.0 %collective-permute-start.2 = (bf16[2,528,128]{2,1,0:T(8,128)(2,1)S(1)}, bf16[2,528,128]{2,1,0:T(8,128)(2,1)S(1)}, u32[]{:S(2)}, u32[]{:S(2)}) collective-permute-start(bf16[2,528,128]{2,1,0:T(8,128)(2,1)S(1)} %get-tuple-element.26), channel_id=1, source_target_pairs={{0,1},{1,2},{2,3},{3,0},{4,5},{5,6},{6,7},{7,4},{8,9},{9,10},{10,1... | collective-permute-start | bytes 811016 | tf_op jit(solution)/shard_map/ppermute | solution.py:364
  22.7 2.9 %collective-permute-start.3 = (bf16[2,528,128]{2,1,0:T(8,128)(2,1)S(1)}, bf16[2,528,128]{2,1,0:T(8,128)(2,1)S(1)}, u32[]{:S(2)}, u32[]{:S(2)}) collective-permute-start(bf16[2,528,128]{2,1,0:T(8,128)(2,1)S(1)} %get-tuple-element.25.q0.q_ref), channel_id=1, source_target_pairs={{0,2},{1,3},{2,0},{3,1},{4,6},{5,7},{6,4},{7,5},{8,10},{9,11},{10,... | collective-permute-start | bytes 811016 | tf_op jit(solution)/shard_map/ppermute | solution.py:364
  25.6 13.9 %all-to-all-done.kv_ref = bf16[16,264,128]{2,1,0:T(8,128)(2,1)S(1)} async-done(((bf16[16,264,128]{2,1,0:T(8,128)(2,1)}), bf16[16,264,128]{2,1,0:T(8,128)(2,1)S(1)}, u32[]{:S(2)}, u32[]{:S(2)}) %all-to-all-start) | async-done | bytes 1081376 | tf_op jit(solution)/shard_map/all_to_all | solution.py:356
  39.5 1.9 %collective-permute-start = (bf16[16,64,128]{2,1,0:T(8,128)(2,1)S(1)}, bf16[16,64,128]{2,1,0:T(8,128)(2,1)S(1)}, u32[]{:S(2)}, u32[]{:S(2)}) collective-permute-start(bf16[16,64,128]{2,1,0:T(8,128)(2,1)S(1)} %slice.4), channel_id=1, source_target_pairs={{0,32},{32,0},{1,33},{33,1},{2,34},{34,2},{3,35},{35,3},{4,36},{36... | collective-permute-start | bytes 786440 | tf_op jit(solution)/shard_map/ppermute | solution.py:360
  41.4 0.0 collective-permute-done.4.q3.q_ref
  41.4 0.0 collective-permute-done.2.q1.q_ref
  41.4 0.5 collective-permute-done.3.q2.q_ref
  41.9 0.0 copy-done.4
  41.9 5.1 %shard_map.148 = (bf16[16,128,128]{2,1,0:T(8,128)(2,1)S(1)}, bf16[2048,128]{1,0:T(8,128)(2,1)S(1)}, bf16[2048,128]{1,0:T(8,128)(2,1)S(1)}, f32[8,256]{1,0:T(8,128)S(1)}, f32[8,256]{1,0:T(8,128)S(1)}) custom-call(s32[1,3]{1,0:T(1,128)S(1)} %copy-done.4, bf16[2,528,128]{2,1,0:T(8,128)(2,1)S(1)} %get-tuple-element.25.q0.q_ref, ...), custom_call_target="tpu_custom_call" | custom-call | flops 4294967296 | bytes 3145728 | tf_op jit(solution)/shard_map/pallas_call | solution.py:370
  47.1 0.0 collective-permute-done.side_ref
  47.1 0.0 copy-start.5
  47.1 3.2 %shard_map.149 = (bf16[16,256,128]{2,1,0:T(8,128)(2,1)}, f32[8,128]{1,0:T(8,128)S(1)}) custom-call(bf16[16,264,128]{2,1,0:T(8,128)(2,1)S(1)} %all-to-all-done.kv_ref, bf16[16,64,128]{2,1,0:T(8,128)(2,1)S(1)} %collective-permute-done.side_ref, bf16[16,128,128]{2,1,0:T(8,128)(2,1)S(1)} %get-tuple-element.27.prompt_ref, ...), custom_call_target="tpu_custom_call" | custom-call | flops 2147483648 | bytes 3145728 | tf_op jit(solution)/shard_map/pallas_call | solution.py:389
  50.3 0.0 copy-done.5
  50.3 9.9 %all-to-all-start.1 = ((bf16[16,256,128]{2,1,0:T(8,128)(2,1)}), bf16[16,256,128]{2,1,0:T(8,128)(2,1)S(1)}, u32[]{:S(2)}, u32[]{:S(2)}) async-start(bf16[16,256,128]{2,1,0:T(8,128)(2,1)} %get-tuple-element.33), calls=%async_computation.1 | async-start | bytes 2097152 | tf_op jit(solution)/shard_map/all_to_all | solution.py:356
  60.1 0.0 copy-start.6
  60.1 0.9 %copy-done.6 = bf16[16,64,128]{2,1,0:T(8,128)(2,1)S(1)} copy-done((bf16[16,64,128]{2,1,0:T(8,128)(2,1)S(1)}, bf16[16,64,128]{2,1,0:T(8,128)(2,1)}, u32[]{:S(2)}) %copy-start.6) | copy-done | bytes 262168
  61.1 2.0 %shard_map.153 = bf16[512,128]{1,0:T(8,128)(2,1)S(1)} custom-call(s32[1,3]{1,0:T(1,128)S(1)} %copy-done.4, f32[8,128]{1,0:T(8,128)S(1)} %get-tuple-element.32.margin_ref, bf16[2,528,128]{2,1,0:T(8,128)(2,1)S(1)} %collective-permute-done.2.q1.q_ref, bf16[16,264,128]{2,1,0:T(8,128)(2,1)S(1)} %all-to-all-done.kv_ref, bf16[16,64,128]{2,1,0:T(8,128)(2,1)S(1)} %copy-done.6), custom_call_target="tpu_custom_call" | custom-call | flops 1207959552 | bytes 3145728 | tf_op jit(solution)/shard_map/pallas_call | solution.py:410
  63.1 2.0 %collective-permute-start.6 = (bf16[512,128]{1,0:T(8,128)(2,1)S(1)}, bf16[512,128]{1,0:T(8,128)(2,1)S(1)}, u32[]{:S(2)}, u32[]{:S(2)}) collective-permute-start(bf16[512,128]{1,0:T(8,128)(2,1)S(1)} %shard_map.153), channel_id=1, source_target_pairs={{0,3},{1,0},{2,1},{3,2},{4,7},{5,4},{6,5},{7,6},{8,11},{9,8},{10,9... | collective-permute-start | bytes 393224 | tf_op jit(solution)/shard_map/ppermute | solution.py:364
  65.1 2.0 %shard_map.150 = bf16[528,128]{1,0:T(8,128)(2,1)S(1)} custom-call(s32[1,3]{1,0:T(1,128)S(1)} %copy-done.4, f32[8,128]{1,0:T(8,128)S(1)} %get-tuple-element.32.margin_ref, bf16[2,528,128]{2,1,0:T(8,128)(2,1)S(1)} %collective-permute-done.3.q2.q_ref, bf16[16,264,128]{2,1,0:T(8,128)(2,1)S(1)} %all-to-all-done.kv_ref, bf16[16,64,128]{2,1,0:T(8,128)(2,1)S(1)} %copy-done.6), custom_call_target="tpu_custom_call" | custom-call | flops 1207959552 | bytes 3145728 | tf_op jit(solution)/shard_map/pallas_call | solution.py:410
  67.1 4.5 %collective-permute-start.5 = (bf16[528,128]{1,0:T(8,128)(2,1)S(1)}, bf16[528,128]{1,0:T(8,128)(2,1)S(1)}, u32[]{:S(2)}, u32[]{:S(2)}) collective-permute-start(bf16[528,128]{1,0:T(8,128)(2,1)S(1)} %shard_map.150), channel_id=1, source_target_pairs={{0,2},{1,3},{2,0},{3,1},{4,6},{5,7},{6,4},{7,5},{8,10},{9,11},{10,... | collective-permute-start | bytes 405512 | tf_op jit(solution)/shard_map/ppermute | solution.py:364
  71.6 2.0 %shard_map.154 = bf16[512,128]{1,0:T(8,128)(2,1)S(1)} custom-call(s32[1,3]{1,0:T(1,128)S(1)} %copy-done.4, f32[8,128]{1,0:T(8,128)S(1)} %get-tuple-element.32.margin_ref, bf16[2,528,128]{2,1,0:T(8,128)(2,1)S(1)} %collective-permute-done.4.q3.q_ref, bf16[16,264,128]{2,1,0:T(8,128)(2,1)S(1)} %all-to-all-done.kv_ref, bf16[16,64,128]{2,1,0:T(8,128)(2,1)S(1)} %copy-done.6), custom_call_target="tpu_custom_call" | custom-call | flops 1207959552 | bytes 3145728 | tf_op jit(solution)/shard_map/pallas_call | solution.py:410
  73.6 4.4 %collective-permute-start.7 = (bf16[512,128]{1,0:T(8,128)(2,1)S(1)}, bf16[512,128]{1,0:T(8,128)(2,1)S(1)}, u32[]{:S(2)}, u32[]{:S(2)}) collective-permute-start(bf16[512,128]{1,0:T(8,128)(2,1)S(1)} %shard_map.154), channel_id=1, source_target_pairs={{0,1},{1,2},{2,3},{3,0},{4,5},{5,6},{6,7},{7,4},{8,9},{9,10},{10,1... | collective-permute-start | bytes 393224 | tf_op jit(solution)/shard_map/ppermute | solution.py:364
  78.1 2.0 %shard_map.152.d0 = bf16[512,128]{1,0:T(8,128)(2,1)S(1)} custom-call(s32[1,3]{1,0:T(1,128)S(1)} %copy-done.4, f32[8,128]{1,0:T(8,128)S(1)} %get-tuple-element.32.margin_ref, bf16[2,528,128]{2,1,0:T(8,128)(2,1)S(1)} %get-tuple-element.25.q0.q_ref, bf16[16,264,128]{2,1,0:T(8,128)(2,1)S(1)} %all-to-all-done.kv_ref, bf16[16,64,128]{2,1,0:T(8,128)(2,1)S(1)} %copy-done.6), custom_call_target="tpu_custom_call" | custom-call | flops 1207959552 | bytes 3145728 | tf_op jit(solution)/shard_map/pallas_call | solution.py:410
  80.1 0.0 collective-permute-done.6.d1
  80.1 7.1 %collective-permute-done.7.d3 = bf16[512,128]{1,0:T(8,128)(2,1)S(1)} collective-permute-done((bf16[512,128]{1,0:T(8,128)(2,1)S(1)}, bf16[512,128]{1,0:T(8,128)(2,1)S(1)}, u32[]{:S(2)}, u32[]{:S(2)}) %collective-permute-start.7) | collective-permute-done | bytes 131104 | tf_op jit(solution)/shard_map/ppermute | solution.py:364
  87.2 0.0 collective-permute-done.5.d2
  87.2 0.9 %shard_map.155 = (bf16[1,2,32,2048]{3,2,1,0:T(8,128)(2,1)}, f32[1]{0:T(128)}) custom-call(f32[8,128]{1,0:T(8,128)S(1)} %get-tuple-element.32.margin_ref, bf16[512,128]{1,0:T(8,128)(2,1)S(1)} %shard_map.152.d0, bf16[512,128]{1,0:T(8,128)(2,1)S(1)} %collective-permute-done.6.d1, bf16[528,128]{1,0:T(8,128)(2,1)S(1)} %collective-permute-done.5.d2, ...), custom_call_target="tpu_custom_call" | custom-call | bytes 1048576 | tf_op jit(solution)/shard_map/pallas_call | solution.py:476
  88.1 0.0 all-to-all-done.1.part_ref
  88.1 1.4 %shard_map.151 = (bf16[1,64,256]{2,1,0:T(8,128)(2,1)}, bf16[1,64,256]{2,1,0:T(8,128)(2,1)}, bf16[1,2,32,256]{3,2,1,0:T(8,128)(2,1)}, bf16[1,2,32,256]{3,2,1,0:T(8,128)(2,1)}) custom-call(s32[1,3]{1,0:T(1,128)S(1)} %copy-done.4, f32[8,128]{1,0:T(8,128)S(1)} %get-tuple-element.32.margin_ref, bf16[528,128]{1,0:T(8,128)(2,1)S(1)} %collective-permute-done.5.d2, ...), custom_call_target="tpu_custom_call" | custom-call | bytes 1048576 | tf_op jit(solution)/shard_map/pallas_call | solution.py:484
  (2 shorter events, 0.1 us)
Async XLA Ops:
  2.7 8.8 %copy-start = (bf16[1,1,32,4096]{3,2,1,0:T(8,128)(2,1)S(1)}, bf16[1,1,32,4096]{3,2,1,0:T(8,128)(2,1)}, u32[]{:S(2)}) copy-start(bf16[1,1,32,4096]{3,2,1,0:T(8,128)(2,1)} %q_hbm.1) | copy-start | bytes 786436
  2.7 8.8 %copy-start.1 = (bf16[1,1,32,4096]{3,2,1,0:T(8,128)(2,1)S(1)}, bf16[1,1,32,4096]{3,2,1,0:T(8,128)(2,1)}, u32[]{:S(2)}) copy-start(bf16[1,1,32,4096]{3,2,1,0:T(8,128)(2,1)} %g_hbm.1) | copy-start | bytes 786436
  2.7 8.8 %copy-start.2 = (bf16[1,1,32,32]{3,2,1,0:T(8,128)(2,1)S(1)}, bf16[1,1,32,32]{3,2,1,0:T(8,128)(2,1)}, u32[]{:S(2)}) copy-start(bf16[1,1,32,32]{3,2,1,0:T(8,128)(2,1)} %lse_hbm.1) | copy-start | bytes 6148
  2.7 8.8 %copy-start.3 = (bf16[1,1,32,32]{3,2,1,0:T(8,128)(2,1)S(1)}, bf16[1,1,32,32]{3,2,1,0:T(8,128)(2,1)}, u32[]{:S(2)}) copy-start(bf16[1,1,32,32]{3,2,1,0:T(8,128)(2,1)} %delta_hbm.1) | copy-start | bytes 6148
  2.8 36.7 %all-to-all-start = ((bf16[16,264,128]{2,1,0:T(8,128)(2,1)}), bf16[16,264,128]{2,1,0:T(8,128)(2,1)S(1)}, u32[]{:S(2)}, u32[]{:S(2)}) async-start(bf16[16,264,128]{2,1,0:T(8,128)(2,1)} %shard_map.145), calls=%async_computation | async-start | bytes 2162688 | tf_op jit(solution)/shard_map/all_to_all | solution.py:356
  11.5 30.4 %copy-start.4 = (s32[1,3]{1,0:T(1,128)S(1)}, s32[1,3]{1,0:T(1,128)}, u32[]{:S(2)}) copy-start(s32[1,3]{1,0:T(1,128)} %lengths_ref.11) | copy-start | bytes 40
  12.1 3.4 %collective-permute-start.1 = (bf16[2,528,128]{2,1,0:T(8,128)(2,1)S(1)}, bf16[2,528,128]{2,1,0:T(8,128)(2,1)S(1)}, u32[]{:S(2)}, u32[]{:S(2)}) collective-permute-start(bf16[2,528,128]{2,1,0:T(8,128)(2,1)S(1)} %get-tuple-element.24), channel_id=1, source_target_pairs={{0,32},{32,0},{1,33},{33,1},{2,34},{34,2},{3,35},{35,3},{4,36},{36... | collective-permute-start | bytes 811016 | tf_op jit(solution)/shard_map/ppermute | solution.py:360
  15.6 25.8 %collective-permute-start.4 = (bf16[2,528,128]{2,1,0:T(8,128)(2,1)S(1)}, bf16[2,528,128]{2,1,0:T(8,128)(2,1)S(1)}, u32[]{:S(2)}, u32[]{:S(2)}) collective-permute-start(bf16[2,528,128]{2,1,0:T(8,128)(2,1)S(1)} %get-tuple-element.26), channel_id=1, source_target_pairs={{0,3},{1,0},{2,1},{3,2},{4,7},{5,4},{6,5},{7,6},{8,11},{9,8},{10,9... | collective-permute-start | bytes 811016 | tf_op jit(solution)/shard_map/ppermute | solution.py:364
  17.6 23.8 %collective-permute-start.2 = (bf16[2,528,128]{2,1,0:T(8,128)(2,1)S(1)}, bf16[2,528,128]{2,1,0:T(8,128)(2,1)S(1)}, u32[]{:S(2)}, u32[]{:S(2)}) collective-permute-start(bf16[2,528,128]{2,1,0:T(8,128)(2,1)S(1)} %get-tuple-element.26), channel_id=1, source_target_pairs={{0,1},{1,2},{2,3},{3,0},{4,5},{5,6},{6,7},{7,4},{8,9},{9,10},{10,1... | collective-permute-start | bytes 811016 | tf_op jit(solution)/shard_map/ppermute | solution.py:364
  22.7 19.3 %collective-permute-start.3 = (bf16[2,528,128]{2,1,0:T(8,128)(2,1)S(1)}, bf16[2,528,128]{2,1,0:T(8,128)(2,1)S(1)}, u32[]{:S(2)}, u32[]{:S(2)}) collective-permute-start(bf16[2,528,128]{2,1,0:T(8,128)(2,1)S(1)} %get-tuple-element.25.q0.q_ref), channel_id=1, source_target_pairs={{0,2},{1,3},{2,0},{3,1},{4,6},{5,7},{6,4},{7,5},{8,10},{9,11},{10,... | collective-permute-start | bytes 811016 | tf_op jit(solution)/shard_map/ppermute | solution.py:364
  39.5 7.6 %collective-permute-start = (bf16[16,64,128]{2,1,0:T(8,128)(2,1)S(1)}, bf16[16,64,128]{2,1,0:T(8,128)(2,1)S(1)}, u32[]{:S(2)}, u32[]{:S(2)}) collective-permute-start(bf16[16,64,128]{2,1,0:T(8,128)(2,1)S(1)} %slice.4), channel_id=1, source_target_pairs={{0,32},{32,0},{1,33},{33,1},{2,34},{34,2},{3,35},{35,3},{4,36},{36... | collective-permute-start | bytes 786440 | tf_op jit(solution)/shard_map/ppermute | solution.py:360
  47.1 3.2 %copy-start.5 = (bf16[16,64,128]{2,1,0:T(8,128)(2,1)}, bf16[16,64,128]{2,1,0:T(8,128)(2,1)S(1)}, u32[]{:S(2)}) copy-start(bf16[16,64,128]{2,1,0:T(8,128)(2,1)S(1)} %collective-permute-done.side_ref) | copy-start | bytes 786436
  50.3 37.8 %all-to-all-start.1 = ((bf16[16,256,128]{2,1,0:T(8,128)(2,1)}), bf16[16,256,128]{2,1,0:T(8,128)(2,1)S(1)}, u32[]{:S(2)}, u32[]{:S(2)}) async-start(bf16[16,256,128]{2,1,0:T(8,128)(2,1)} %get-tuple-element.33), calls=%async_computation.1 | async-start | bytes 2097152 | tf_op jit(solution)/shard_map/all_to_all | solution.py:356
  60.1 0.9 %copy-start.6 = (bf16[16,64,128]{2,1,0:T(8,128)(2,1)S(1)}, bf16[16,64,128]{2,1,0:T(8,128)(2,1)}, u32[]{:S(2)}) copy-start(bf16[16,64,128]{2,1,0:T(8,128)(2,1)} %copy-done.5) | copy-start | bytes 786436
  63.1 17.0 %collective-permute-start.6 = (bf16[512,128]{1,0:T(8,128)(2,1)S(1)}, bf16[512,128]{1,0:T(8,128)(2,1)S(1)}, u32[]{:S(2)}, u32[]{:S(2)}) collective-permute-start(bf16[512,128]{1,0:T(8,128)(2,1)S(1)} %shard_map.153), channel_id=1, source_target_pairs={{0,3},{1,0},{2,1},{3,2},{4,7},{5,4},{6,5},{7,6},{8,11},{9,8},{10,9... | collective-permute-start | bytes 393224 | tf_op jit(solution)/shard_map/ppermute | solution.py:364
  67.1 20.1 %collective-permute-start.5 = (bf16[528,128]{1,0:T(8,128)(2,1)S(1)}, bf16[528,128]{1,0:T(8,128)(2,1)S(1)}, u32[]{:S(2)}, u32[]{:S(2)}) collective-permute-start(bf16[528,128]{1,0:T(8,128)(2,1)S(1)} %shard_map.150), channel_id=1, source_target_pairs={{0,2},{1,3},{2,0},{3,1},{4,6},{5,7},{6,4},{7,5},{8,10},{9,11},{10,... | collective-permute-start | bytes 405512 | tf_op jit(solution)/shard_map/ppermute | solution.py:364
  73.6 13.5 %collective-permute-start.7 = (bf16[512,128]{1,0:T(8,128)(2,1)S(1)}, bf16[512,128]{1,0:T(8,128)(2,1)S(1)}, u32[]{:S(2)}, u32[]{:S(2)}) collective-permute-start(bf16[512,128]{1,0:T(8,128)(2,1)S(1)} %shard_map.154), channel_id=1, source_target_pairs={{0,1},{1,2},{2,3},{3,0},{4,5},{5,6},{6,7},{7,4},{8,9},{9,10},{10,1... | collective-permute-start | bytes 393224 | tf_op jit(solution)/shard_map/ppermute | solution.py:364

commit v12 on v10

--- a/solution.py
+++ b/solution.py
@@ -204,13 +204,8 @@
     return slice(tile * TILE, (tile + 1) * TILE)
 
 
-def prompt_kernel(first_half, lengths_ref, qa, qb, kv_ref, *refs):
-    if first_half:
-        key_sum, value_sum = refs[:2]
-    else:
-        key_sum, value_sum, out_ref = refs[:3]
-    query_rows, grad_rows, lse_ref, delta_ref, weights, score_grads = refs[-6:]
-    for n, ref in enumerate((qa, qb)):
+def fill_tables(first_half, lengths_ref, sources, query_rows, grad_rows, lse_ref, delta_ref):
+    for n, ref in enumerate(sources):
         for j in range(2):
             t = j * 2 + n
             at = tile_rows(t)
@@ -219,6 +214,19 @@
             k = 2 * n if first_half else 2 * n + 1
             lse, delta = row_stats(lengths_ref, ref[j, 2 * TILE :, :], k, j)
             lse_ref[t : t + 1, :], delta_ref[t : t + 1, :] = lse, delta
+
+
+def tables_kernel(lengths_ref, qa, qb, *tables):
+    fill_tables(True, lengths_ref, (qa, qb), *tables)
+
+
+def prompt_kernel(first_half, *refs):
+    if first_half:
+        query_rows, grad_rows, lse_ref, delta_ref, kv_ref, key_sum, value_sum, weights, score_grads = refs
+    else:
+        lengths_ref, qa, qb, kv_ref, key_sum, value_sum, out_ref = refs[:7]
+        query_rows, grad_rows, lse_ref, delta_ref, weights, score_grads = refs[7:]
+        fill_tables(False, lengths_ref, (qa, qb), query_rows, grad_rows, lse_ref, delta_ref)
     per = PROMPT_BLOCK // PROMPT
 
     def first(c, slot):
@@ -393,9 +401,8 @@
     sums = (shape((PEERS_N * PROMPT, LANES), f32),) * 2
     scratch = (pltpu.VMEM((2, PROMPT_BLOCK, count), bf16), pltpu.VMEM((2, PROMPT_BLOCK, count), bf16))
     cost = dict(flops=2 * 2 * 2048 * 1024 * 128 * 2, size=2 * 2**20, scratch=scratch)
-    key_sum, value_sum, *first = call(functools.partial(prompt_kernel, True), sums + tables, "svvv", **cost)(
-        lengths, rows[0], rows[2], kv
-    )
+    first = call(tables_kernel, tables, "svv", size=2**20)(lengths, rows[0], rows[2])
+    key_sum, value_sum = call(functools.partial(prompt_kernel, True), sums, "vvvvv", **cost)(*first, kv)
     key_sum, source = lax.optimization_barrier((key_sum, kv))
     side = cross(source[:, KV_ROWS - SIDE : KV_ROWS, :])
     part, *second = call(

time: 88.6 us -> 88.6 us (level)
    pallas_call x1 -> x2, Pallas kernels: 2.97 us -> 3 us  [the longest x1 2.42 us: prompt_call(): call(functools.partial(prompt_kernel, True), sums, 'vvvvv', **cost)]
where the time goes in v12:
time: 88.6 us; the launch traced here: 87 us
  starting transfers between devices  41.8 us (47%)
  Pallas kernels  22.1 us (25%)
  waiting for transfers between devices  21.2 us (24%)
  local copies, waits for them, and re-layouts  1 us (1%)
  between operations  0.91 us (1%)
    ppermute x6, starting transfers between devices, shift(): return lax.ppermute(values, ROW, [(i, (i + by) % X) for i in range(X)])  22.2 us
    all_to_all x2, starting transfers between devices, swap(): lax.all_to_all(values, PEERS, split_axis=0, concat_axis=0, tiled=True)  15.8 us
    ppermute x6, waiting for transfers between devices, shift(): return lax.ppermute(values, ROW, [(i, (i + by) % X) for i in range(X)])  13.2 us
    pallas_call x4, Pallas kernels, query_call(): call(functools.partial(query_kernel, k), jax.ShapeDtypeStruct((2 * TILE +...  7.95 us
    all_to_all x2, waiting for transfers between devices, swap(): lax.all_to_all(values, PEERS, split_axis=0, concat_axis=0, tiled=True)  6.5 us
    ppermute x2, starting transfers between devices, cross(): return lax.ppermute(values, 'pair', [(0, 1), (1, 0)])  3.84 us
    pallas_call x1, Pallas kernels, resp_call(): call(resp_kernel, (shape((PEERS_N, KV_ROWS, LANES), bf16), shape((8, LANE...  3.18 us
    pallas_call x1, Pallas kernels, prompt_call(): call(functools.partial(prompt_kernel, False), (shape((PEERS_N, 2 * PROMPT...  3.01 us
  transfers between devices with their start and end apart: 10, of which 4 were waited for; matrix products, arithmetic and copies ran while one was open for 0% of the time, Pallas kernels for 18%

profile of v12, /device:TPU:6, one launch (start us, length us, event | category | flops | bytes accessed | tf_op | source)
XLA Modules:
  0.0 87.0 jit_solution(10606331425090470055)
XLA Ops:
  0.6 2.1 %shard_map.145 = bf16[16,264,128]{2,1,0:T(8,128)(2,1)} custom-call(s32[1,3]{1,0:T(1,128)} %lengths_ref.11, f32[1,2,32]{2,1,0:T(2,128)} %logratio_hbm.1, bf16[1,64,256]{2,1,0:T(8,128)(2,1)} %pk_hbm.1, bf16[1,64,256]{2,1,0:T(8,128)(2,1)} %pv_hbm.1, bf16[1,1,32,512]{3,2,1,0:T(8,128)(2,1)} %rk_hbm.1, bf16[1,1,32,512]{3,2,1,0:T(8,128)(2,1)} %rv_hbm.1), custom_call_target="tpu_custom_call" | custom-call | bytes 2097152 | tf_op jit(solution)/shard_map/pallas_call | solution.py:463
  2.7 0.0 copy-start
  2.7 0.0 copy-start.1
  2.7 0.0 copy-start.2
  2.7 0.0 copy-start.3
  2.7 8.7 %all-to-all-start = ((bf16[16,264,128]{2,1,0:T(8,128)(2,1)}), bf16[16,264,128]{2,1,0:T(8,128)(2,1)S(1)}, u32[]{:S(2)}, u32[]{:S(2)}) async-start(bf16[16,264,128]{2,1,0:T(8,128)(2,1)} %shard_map.145), calls=%async_computation | async-start | bytes 2162688 | tf_op jit(solution)/shard_map/all_to_all | solution.py:381
  11.5 0.0 copy-done
  11.5 0.0 copy-done.1
  11.5 0.0 copy-done.2
  11.5 0.0 copy-done.3
  11.5 0.0 copy-start.4
  11.5 0.6 shard_map.146
  12.1 1.9 %collective-permute-start = (bf16[2,528,128]{2,1,0:T(8,128)(2,1)S(1)}, bf16[2,528,128]{2,1,0:T(8,128)(2,1)S(1)}, u32[]{:S(2)}, u32[]{:S(2)}) collective-permute-start(bf16[2,528,128]{2,1,0:T(8,128)(2,1)S(1)} %get-tuple-element.32), channel_id=1, source_target_pairs={{0,32},{32,0},{1,33},{33,1},{2,34},{34,2},{3,35},{35,3},{4,36},{36... | collective-permute-start | bytes 811016 | tf_op jit(solution)/shard_map/ppermute | solution.py:385
  14.0 1.5 %collective-permute-done.other_ref = bf16[2,528,128]{2,1,0:T(8,128)(2,1)S(1)} collective-permute-done((bf16[2,528,128]{2,1,0:T(8,128)(2,1)S(1)}, bf16[2,528,128]{2,1,0:T(8,128)(2,1)S(1)}, u32[]{:S(2)}, u32[]{:S(2)}) %collective-permute-start) | collective-permute-done | bytes 270368 | tf_op jit(solution)/shard_map/ppermute | solution.py:385
  15.6 4.1 %collective-permute-start.1 = (bf16[2,528,128]{2,1,0:T(8,128)(2,1)S(1)}, bf16[2,528,128]{2,1,0:T(8,128)(2,1)S(1)}, u32[]{:S(2)}, u32[]{:S(2)}) collective-permute-start(bf16[2,528,128]{2,1,0:T(8,128)(2,1)S(1)} %get-tuple-element.33.qa.q_ref), channel_id=1, source_target_pairs={{0,2},{1,3},{2,0},{3,1},{4,6},{5,7},{6,4},{7,5},{8,10},{9,11},{10,... | collective-permute-start | bytes 811016 | tf_op jit(solution)/shard_map/ppermute | solution.py:389
  19.7 1.9 %collective-permute-start.4 = (bf16[2,528,128]{2,1,0:T(8,128)(2,1)S(1)}, bf16[2,528,128]{2,1,0:T(8,128)(2,1)S(1)}, u32[]{:S(2)}, u32[]{:S(2)}) collective-permute-start(bf16[2,528,128]{2,1,0:T(8,128)(2,1)S(1)} %get-tuple-element.40), channel_id=1, source_target_pairs={{0,3},{1,0},{2,1},{3,2},{4,7},{5,4},{6,5},{7,6},{8,11},{9,8},{10,9... | collective-permute-start | bytes 811016 | tf_op jit(solution)/shard_map/ppermute | solution.py:389
  21.6 5.1 %collective-permute-start.3 = (bf16[2,528,128]{2,1,0:T(8,128)(2,1)S(1)}, bf16[2,528,128]{2,1,0:T(8,128)(2,1)S(1)}, u32[]{:S(2)}, u32[]{:S(2)}) collective-permute-start(bf16[2,528,128]{2,1,0:T(8,128)(2,1)S(1)} %get-tuple-element.40), channel_id=1, source_target_pairs={{0,1},{1,2},{2,3},{3,0},{4,5},{5,6},{6,7},{7,4},{8,9},{9,10},{10,1... | collective-permute-start | bytes 811016 | tf_op jit(solution)/shard_map/ppermute | solution.py:389
  26.8 5.6 %collective-permute-done.1.qb.q_ref = bf16[2,528,128]{2,1,0:T(8,128)(2,1)S(1)} collective-permute-done((bf16[2,528,128]{2,1,0:T(8,128)(2,1)S(1)}, bf16[2,528,128]{2,1,0:T(8,128)(2,1)S(1)}, u32[]{:S(2)}, u32[]{:S(2)}) %collective-permute-start.1) | collective-permute-done | bytes 270368 | tf_op jit(solution)/shard_map/ppermute | solution.py:389
  32.3 0.0 copy-done.4
  32.3 0.6 shard_map.148
  32.9 6.5 %all-to-all-done.refs_4_.refs_3_.kv_ref = bf16[16,264,128]{2,1,0:T(8,128)(2,1)S(1)} async-done(((bf16[16,264,128]{2,1,0:T(8,128)(2,1)}), bf16[16,264,128]{2,1,0:T(8,128)(2,1)S(1)}, u32[]{:S(2)}, u32[]{:S(2)}) %all-to-all-start) | async-done | bytes 1081376 | tf_op jit(solution)/shard_map/all_to_all | solution.py:381
  39.4 2.4 %shard_map.149 = (f32[1024,128]{1,0:T(8,128)S(1)}, f32[1024,128]{1,0:T(8,128)S(1)}) custom-call(bf16[1024,128]{1,0:T(8,128)(2,1)S(1)} %get-tuple-element.34.refs_0_.query_a, bf16[1024,128]{1,0:T(8,128)(2,1)S(1)} %get-tuple-element.35.refs_1_.grad_a, f32[4,256]{1,0:T(4,128)S(1)} %get-tuple-element.36.refs_2_.lse_a, ...), custom_call_target="tpu_custom_call" | custom-call | flops 2147483648 | bytes 2097152 | tf_op jit(solution)/shard_map/pallas_call | solution.py:405
  41.9 1.9 %collective-permute-start.2 = (bf16[16,64,128]{2,1,0:T(8,128)(2,1)S(1)}, bf16[16,64,128]{2,1,0:T(8,128)(2,1)S(1)}, u32[]{:S(2)}, u32[]{:S(2)}) collective-permute-start(bf16[16,64,128]{2,1,0:T(8,128)(2,1)S(1)} %slice.3), channel_id=1, source_target_pairs={{0,32},{32,0},{1,33},{33,1},{2,34},{34,2},{3,35},{35,3},{4,36},{36... | collective-permute-start | bytes 786440 | tf_op jit(solution)/shard_map/ppermute | solution.py:385
  43.8 0.0 collective-permute-done.4.refs_2_.q_ref
  43.8 0.0 collective-permute-done.3.refs_1_.q_ref
  43.8 3.0 %shard_map.150 = (bf16[16,128,128]{2,1,0:T(8,128)(2,1)S(1)}, bf16[1024,128]{1,0:T(8,128)(2,1)S(1)}, bf16[1024,128]{1,0:T(8,128)(2,1)S(1)}, f32[4,256]{1,0:T(4,128)S(1)}, f32[4,256]{1,0:T(4,128)S(1)}) custom-call(s32[1,3]{1,0:T(1,128)S(1)} %copy-done.4, bf16[2,528,128]{2,1,0:T(8,128)(2,1)S(1)} %collective-permute-done.3.refs_1_.q_ref, ...), custom_call_target="tpu_custom_call" | custom-call | flops 2147483648 | bytes 2097152 | tf_op jit(solution)/shard_map/pallas_call | solution.py:408
  46.9 0.0 collective-permute-done.2.side_ref
  46.9 0.0 copy-start.5
  46.9 3.2 %shard_map.151 = (bf16[16,256,128]{2,1,0:T(8,128)(2,1)}, f32[8,128]{1,0:T(8,128)S(1)}) custom-call(bf16[16,264,128]{2,1,0:T(8,128)(2,1)S(1)} %all-to-all-done.refs_4_.refs_3_.kv_ref, bf16[16,64,128]{2,1,0:T(8,128)(2,1)S(1)} %collective-permute-done.2.side_ref, bf16[16,128,128]{2,1,0:T(8,128)(2,1)S(1)} %get-tuple-element.43.prompt_ref, ...), custom_call_target="tpu_custom_call" | custom-call | flops 2147483648 | bytes 3145728 | tf_op jit(solution)/shard_map/pallas_call | solution.py:420
  50.1 0.0 copy-done.5
  50.1 7.1 %all-to-all-start.1 = ((bf16[16,256,128]{2,1,0:T(8,128)(2,1)}), bf16[16,256,128]{2,1,0:T(8,128)(2,1)S(1)}, u32[]{:S(2)}, u32[]{:S(2)}) async-start(bf16[16,256,128]{2,1,0:T(8,128)(2,1)} %get-tuple-element.49), calls=%async_computation.1 | async-start | bytes 2097152 | tf_op jit(solution)/shard_map/all_to_all | solution.py:381
  57.1 0.0 copy-start.6
  57.1 0.9 %copy-done.6 = bf16[16,64,128]{2,1,0:T(8,128)(2,1)S(1)} copy-done((bf16[16,64,128]{2,1,0:T(8,128)(2,1)S(1)}, bf16[16,64,128]{2,1,0:T(8,128)(2,1)}, u32[]{:S(2)}) %copy-start.6) | copy-done | bytes 262168
  58.1 0.0 copy-start.7
  58.1 2.0 %shard_map.155 = bf16[512,128]{1,0:T(8,128)(2,1)S(1)} custom-call(s32[1,3]{1,0:T(1,128)S(1)} %copy-done.4, f32[8,128]{1,0:T(8,128)S(1)} %get-tuple-element.48.margin_ref, bf16[2,528,128]{2,1,0:T(8,128)(2,1)S(1)} %collective-permute-done.3.refs_1_.q_ref, bf16[16,264,128]{2,1,0:T(8,128)(2,1)S(1)} %all-to-all-done.refs_4_.refs_3_.kv_ref, ...), custom_call_target="tpu_custom_call" | custom-call | flops 1207959552 | bytes 3145728 | tf_op jit(solution)/shard_map/pallas_call | solution.py:441
  60.1 2.0 %collective-permute-start.6 = (bf16[512,128]{1,0:T(8,128)(2,1)S(1)}, bf16[512,128]{1,0:T(8,128)(2,1)S(1)}, u32[]{:S(2)}, u32[]{:S(2)}) collective-permute-start(bf16[512,128]{1,0:T(8,128)(2,1)S(1)} %shard_map.155), channel_id=1, source_target_pairs={{0,3},{1,0},{2,1},{3,2},{4,7},{5,4},{6,5},{7,6},{8,11},{9,8},{10,9... | collective-permute-start | bytes 393224 | tf_op jit(solution)/shard_map/ppermute | solution.py:389
  62.1 0.0 copy-done.7
  62.1 2.0 %shard_map.152 = bf16[528,128]{1,0:T(8,128)(2,1)S(1)} custom-call(s32[1,3]{1,0:T(1,128)S(1)} %copy-done.4, f32[8,128]{1,0:T(8,128)S(1)} %get-tuple-element.48.margin_ref, bf16[2,528,128]{2,1,0:T(8,128)(2,1)S(1)} %collective-permute-done.1.qb.q_ref, bf16[16,264,128]{2,1,0:T(8,128)(2,1)S(1)} %all-to-all-done.refs_4_.refs_3_.kv_ref, ...), custom_call_target="tpu_custom_call" | custom-call | flops 1207959552 | bytes 3145728 | tf_op jit(solution)/shard_map/pallas_call | solution.py:441
  64.1 4.6 %collective-permute-start.5 = (bf16[528,128]{1,0:T(8,128)(2,1)S(1)}, bf16[528,128]{1,0:T(8,128)(2,1)S(1)}, u32[]{:S(2)}, u32[]{:S(2)}) collective-permute-start(bf16[528,128]{1,0:T(8,128)(2,1)S(1)} %shard_map.152), channel_id=1, source_target_pairs={{0,2},{1,3},{2,0},{3,1},{4,6},{5,7},{6,4},{7,5},{8,10},{9,11},{10,... | collective-permute-start | bytes 405512 | tf_op jit(solution)/shard_map/ppermute | solution.py:389
  68.7 2.0 %shard_map.156 = bf16[512,128]{1,0:T(8,128)(2,1)S(1)} custom-call(s32[1,3]{1,0:T(1,128)S(1)} %copy-done.4, f32[8,128]{1,0:T(8,128)S(1)} %get-tuple-element.48.margin_ref, bf16[2,528,128]{2,1,0:T(8,128)(2,1)S(1)} %collective-permute-done.4.refs_2_.q_ref, bf16[16,264,128]{2,1,0:T(8,128)(2,1)S(1)} %all-to-all-done.refs_4_.refs_3_.kv_ref, ...), custom_call_target="tpu_custom_call" | custom-call | flops 1207959552 | bytes 3145728 | tf_op jit(solution)/shard_map/pallas_call | solution.py:441
  70.7 4.4 %collective-permute-start.7 = (bf16[512,128]{1,0:T(8,128)(2,1)S(1)}, bf16[512,128]{1,0:T(8,128)(2,1)S(1)}, u32[]{:S(2)}, u32[]{:S(2)}) collective-permute-start(bf16[512,128]{1,0:T(8,128)(2,1)S(1)} %shard_map.156), channel_id=1, source_target_pairs={{0,1},{1,2},{2,3},{3,0},{4,5},{5,6},{6,7},{7,4},{8,9},{9,10},{10,1... | collective-permute-start | bytes 393224 | tf_op jit(solution)/shard_map/ppermute | solution.py:389
  75.1 2.0 %shard_map.154.d0 = bf16[512,128]{1,0:T(8,128)(2,1)S(1)} custom-call(s32[1,3]{1,0:T(1,128)S(1)} %copy-done.4, f32[8,128]{1,0:T(8,128)S(1)} %get-tuple-element.48.margin_ref, bf16[2,528,128]{2,1,0:T(8,128)(2,1)S(1)} %get-tuple-element.33.qa.q_ref, bf16[16,264,128]{2,1,0:T(8,128)(2,1)S(1)} %all-to-all-done.refs_4_.refs_3_.kv_ref, ...), custom_call_target="tpu_custom_call" | custom-call | flops 1207959552 | bytes 3145728 | tf_op jit(solution)/shard_map/pallas_call | solution.py:441
  77.1 0.0 collective-permute-done.6.d1
  77.1 7.6 %collective-permute-done.7.d3 = bf16[512,128]{1,0:T(8,128)(2,1)S(1)} collective-permute-done((bf16[512,128]{1,0:T(8,128)(2,1)S(1)}, bf16[512,128]{1,0:T(8,128)(2,1)S(1)}, u32[]{:S(2)}, u32[]{:S(2)}) %collective-permute-start.7) | collective-permute-done | bytes 131104 | tf_op jit(solution)/shard_map/ppermute | solution.py:389
  84.7 0.0 collective-permute-done.5.d2
  84.7 0.9 %shard_map.157 = (bf16[1,2,32,2048]{3,2,1,0:T(8,128)(2,1)}, f32[1]{0:T(128)}) custom-call(f32[8,128]{1,0:T(8,128)S(1)} %get-tuple-element.48.margin_ref, bf16[512,128]{1,0:T(8,128)(2,1)S(1)} %shard_map.154.d0, bf16[512,128]{1,0:T(8,128)(2,1)S(1)} %collective-permute-done.6.d1, bf16[528,128]{1,0:T(8,128)(2,1)S(1)} %collective-permute-done.5.d2, ...), custom_call_target="tpu_custom_call" | custom-call | bytes 1048576 | tf_op jit(solution)/shard_map/pallas_call | solution.py:505
  85.6 0.0 all-to-all-done.1.part_ref
  85.6 1.4 %shard_map.153 = (bf16[1,64,256]{2,1,0:T(8,128)(2,1)}, bf16[1,64,256]{2,1,0:T(8,128)(2,1)}, bf16[1,2,32,256]{3,2,1,0:T(8,128)(2,1)}, bf16[1,2,32,256]{3,2,1,0:T(8,128)(2,1)}) custom-call(s32[1,3]{1,0:T(1,128)S(1)} %copy-done.4, f32[8,128]{1,0:T(8,128)S(1)} %get-tuple-element.48.margin_ref, bf16[528,128]{1,0:T(8,128)(2,1)S(1)} %collective-permute-done.5.d2, ...), custom_call_target="tpu_custom_call" | custom-call | bytes 1048576 | tf_op jit(solution)/shard_map/pallas_call | solution.py:513
  (2 shorter events, 0.1 us)
Async XLA Ops:
  2.7 8.8 %copy-start = (bf16[1,1,32,4096]{3,2,1,0:T(8,128)(2,1)S(1)}, bf16[1,1,32,4096]{3,2,1,0:T(8,128)(2,1)}, u32[]{:S(2)}) copy-start(bf16[1,1,32,4096]{3,2,1,0:T(8,128)(2,1)} %q_hbm.1) | copy-start | bytes 786436
  2.7 8.8 %copy-start.1 = (bf16[1,1,32,4096]{3,2,1,0:T(8,128)(2,1)S(1)}, bf16[1,1,32,4096]{3,2,1,0:T(8,128)(2,1)}, u32[]{:S(2)}) copy-start(bf16[1,1,32,4096]{3,2,1,0:T(8,128)(2,1)} %g_hbm.1) | copy-start | bytes 786436
  2.7 8.8 %copy-start.2 = (bf16[1,1,32,32]{3,2,1,0:T(8,128)(2,1)S(1)}, bf16[1,1,32,32]{3,2,1,0:T(8,128)(2,1)}, u32[]{:S(2)}) copy-start(bf16[1,1,32,32]{3,2,1,0:T(8,128)(2,1)} %lse_hbm.1) | copy-start | bytes 6148
  2.7 8.8 %copy-start.3 = (bf16[1,1,32,32]{3,2,1,0:T(8,128)(2,1)S(1)}, bf16[1,1,32,32]{3,2,1,0:T(8,128)(2,1)}, u32[]{:S(2)}) copy-start(bf16[1,1,32,32]{3,2,1,0:T(8,128)(2,1)} %delta_hbm.1) | copy-start | bytes 6148
  2.7 36.7 %all-to-all-start = ((bf16[16,264,128]{2,1,0:T(8,128)(2,1)}), bf16[16,264,128]{2,1,0:T(8,128)(2,1)S(1)}, u32[]{:S(2)}, u32[]{:S(2)}) async-start(bf16[16,264,128]{2,1,0:T(8,128)(2,1)} %shard_map.145), calls=%async_computation | async-start | bytes 2162688 | tf_op jit(solution)/shard_map/all_to_all | solution.py:381
  11.5 20.9 %copy-start.4 = (s32[1,3]{1,0:T(1,128)S(1)}, s32[1,3]{1,0:T(1,128)}, u32[]{:S(2)}) copy-start(s32[1,3]{1,0:T(1,128)} %lengths_ref.11) | copy-start | bytes 40
  12.1 3.4 %collective-permute-start = (bf16[2,528,128]{2,1,0:T(8,128)(2,1)S(1)}, bf16[2,528,128]{2,1,0:T(8,128)(2,1)S(1)}, u32[]{:S(2)}, u32[]{:S(2)}) collective-permute-start(bf16[2,528,128]{2,1,0:T(8,128)(2,1)S(1)} %get-tuple-element.32), channel_id=1, source_target_pairs={{0,32},{32,0},{1,33},{33,1},{2,34},{34,2},{3,35},{35,3},{4,36},{36... | collective-permute-start | bytes 811016 | tf_op jit(solution)/shard_map/ppermute | solution.py:385
  15.6 16.8 %collective-permute-start.1 = (bf16[2,528,128]{2,1,0:T(8,128)(2,1)S(1)}, bf16[2,528,128]{2,1,0:T(8,128)(2,1)S(1)}, u32[]{:S(2)}, u32[]{:S(2)}) collective-permute-start(bf16[2,528,128]{2,1,0:T(8,128)(2,1)S(1)} %get-tuple-element.33.qa.q_ref), channel_id=1, source_target_pairs={{0,2},{1,3},{2,0},{3,1},{4,6},{5,7},{6,4},{7,5},{8,10},{9,11},{10,... | collective-permute-start | bytes 811016 | tf_op jit(solution)/shard_map/ppermute | solution.py:389
  19.7 24.1 %collective-permute-start.4 = (bf16[2,528,128]{2,1,0:T(8,128)(2,1)S(1)}, bf16[2,528,128]{2,1,0:T(8,128)(2,1)S(1)}, u32[]{:S(2)}, u32[]{:S(2)}) collective-permute-start(bf16[2,528,128]{2,1,0:T(8,128)(2,1)S(1)} %get-tuple-element.40), channel_id=1, source_target_pairs={{0,3},{1,0},{2,1},{3,2},{4,7},{5,4},{6,5},{7,6},{8,11},{9,8},{10,9... | collective-permute-start | bytes 811016 | tf_op jit(solution)/shard_map/ppermute | solution.py:389
  21.6 22.2 %collective-permute-start.3 = (bf16[2,528,128]{2,1,0:T(8,128)(2,1)S(1)}, bf16[2,528,128]{2,1,0:T(8,128)(2,1)S(1)}, u32[]{:S(2)}, u32[]{:S(2)}) collective-permute-start(bf16[2,528,128]{2,1,0:T(8,128)(2,1)S(1)} %get-tuple-element.40), channel_id=1, source_target_pairs={{0,1},{1,2},{2,3},{3,0},{4,5},{5,6},{6,7},{7,4},{8,9},{9,10},{10,1... | collective-permute-start | bytes 811016 | tf_op jit(solution)/shard_map/ppermute | solution.py:389
  41.9 5.0 %collective-permute-start.2 = (bf16[16,64,128]{2,1,0:T(8,128)(2,1)S(1)}, bf16[16,64,128]{2,1,0:T(8,128)(2,1)S(1)}, u32[]{:S(2)}, u32[]{:S(2)}) collective-permute-start(bf16[16,64,128]{2,1,0:T(8,128)(2,1)S(1)} %slice.3), channel_id=1, source_target_pairs={{0,32},{32,0},{1,33},{33,1},{2,34},{34,2},{3,35},{35,3},{4,36},{36... | collective-permute-start | bytes 786440 | tf_op jit(solution)/shard_map/ppermute | solution.py:385
  46.9 3.2 %copy-start.5 = (bf16[16,64,128]{2,1,0:T(8,128)(2,1)}, bf16[16,64,128]{2,1,0:T(8,128)(2,1)S(1)}, u32[]{:S(2)}) copy-start(bf16[16,64,128]{2,1,0:T(8,128)(2,1)S(1)} %collective-permute-done.2.side_ref) | copy-start | bytes 786436
  50.1 35.5 %all-to-all-start.1 = ((bf16[16,256,128]{2,1,0:T(8,128)(2,1)}), bf16[16,256,128]{2,1,0:T(8,128)(2,1)S(1)}, u32[]{:S(2)}, u32[]{:S(2)}) async-start(bf16[16,256,128]{2,1,0:T(8,128)(2,1)} %get-tuple-element.49), calls=%async_computation.1 | async-start | bytes 2097152 | tf_op jit(solution)/shard_map/all_to_all | solution.py:381
  57.1 0.9 %copy-start.6 = (bf16[16,64,128]{2,1,0:T(8,128)(2,1)S(1)}, bf16[16,64,128]{2,1,0:T(8,128)(2,1)}, u32[]{:S(2)}) copy-start(bf16[16,64,128]{2,1,0:T(8,128)(2,1)} %copy-done.5) | copy-start | bytes 786436
  58.1 4.0 %copy-start.7 = (bf16[16,64,128]{2,1,0:T(8,128)(2,1)S(1)}, bf16[16,64,128]{2,1,0:T(8,128)(2,1)}, u32[]{:S(2)}) copy-start(bf16[16,64,128]{2,1,0:T(8,128)(2,1)} %copy-done.5) | copy-start | bytes 786436
  60.1 17.0 %collective-permute-start.6 = (bf16[512,128]{1,0:T(8,128)(2,1)S(1)}, bf16[512,128]{1,0:T(8,128)(2,1)S(1)}, u32[]{:S(2)}, u32[]{:S(2)}) collective-permute-start(bf16[512,128]{1,0:T(8,128)(2,1)S(1)} %shard_map.155), channel_id=1, source_target_pairs={{0,3},{1,0},{2,1},{3,2},{4,7},{5,4},{6,5},{7,6},{8,11},{9,8},{10,9... | collective-permute-start | bytes 393224 | tf_op jit(solution)/shard_map/ppermute | solution.py:389
  64.1 20.6 %collective-permute-start.5 = (bf16[528,128]{1,0:T(8,128)(2,1)S(1)}, bf16[528,128]{1,0:T(8,128)(2,1)S(1)}, u32[]{:S(2)}, u32[]{:S(2)}) collective-permute-start(bf16[528,128]{1,0:T(8,128)(2,1)S(1)} %shard_map.152), channel_id=1, source_target_pairs={{0,2},{1,3},{2,0},{3,1},{4,6},{5,7},{6,4},{7,5},{8,10},{9,11},{10,... | collective-permute-start | bytes 405512 | tf_op jit(solution)/shard_map/ppermute | solution.py:389
  70.7 14.0 %collective-permute-start.7 = (bf16[512,128]{1,0:T(8,128)(2,1)S(1)}, bf16[512,128]{1,0:T(8,128)(2,1)S(1)}, u32[]{:S(2)}, u32[]{:S(2)}) collective-permute-start(bf16[512,128]{1,0:T(8,128)(2,1)S(1)} %shard_map.156), channel_id=1, source_target_pairs={{0,1},{1,2},{2,3},{3,0},{4,5},{5,6},{6,7},{7,4},{8,9},{9,10},{10,1... | collective-permute-start | bytes 393224 | tf_op jit(solution)/shard_map/ppermute | solution.py:389

commit v13 on v12

--- a/solution.py
+++ b/solution.py
@@ -29,7 +29,7 @@
 SCALE = LANES**-0.5
 DEAD = 1e30
 BLOCK = 512
-PROMPT_BLOCK = 256
+PROMPT_BLOCK = 512
 MARGIN_ROWS = 8
 
 
@@ -78,7 +78,7 @@
 
 
 def kv_pack_kernel(
-    lengths_hbm, logratio_hbm, pk_hbm, pv_hbm, rk_hbm, rv_hbm, kv_hbm, lengths, logratio, pk, pv, rk, rv, kv_ref, sems
+    lengths_hbm, logratio_hbm, pk_hbm, pv_hbm, rk_hbm, rv_hbm, kv_ref, lengths, logratio, pk, pv, rk, rv, sems
 ):
     pairs = (
         (lengths_hbm, lengths),
@@ -106,17 +106,11 @@
         parts += [jnp.where(first_core, a, b).astype(bf16) for a, b in zip(low_head, high_head)]
         parts += [jnp.where(first_core, b, a).astype(bf16) for a, b in zip(low_head, high_head)]
         parts += [block]
-        at = 0
-        for part in parts:
-            kv_ref[xl, at : at + part.shape[0], :] = part
-            at += part.shape[0]
-    copies = [
-        pltpu.make_async_copy(kv_ref, kv_hbm.at[2 * y : 2 * y + 2], sems.at[6 + y]) for y in range(ROWS_Y)
-    ]
-    for copy in copies:
-        copy.start()
-    for copy in copies:
-        copy.wait()
+        for y in range(ROWS_Y):
+            at = 0
+            for part in parts:
+                kv_ref[y * 2 + xl, at : at + part.shape[0], :] = part
+                at += part.shape[0]
 
 
 def query_pack_kernel(q_hbm, g_hbm, lse_hbm, delta_hbm, own_ref, other_ref, q, g, lse, delta, sems):
@@ -464,7 +458,6 @@
         kv_pack_kernel,
         shape((PEERS_N, KV_ROWS + MARGIN_ROWS, LANES), bf16),
         "aaaaaa",
-        out_spaces="a",
         size=2 * 2**20,
         limit=60,
         scratch=(
@@ -474,8 +467,7 @@
             pltpu.VMEM((PROMPT, 2 * LANES), bf16),
             pltpu.VMEM((POS, X * LANES), bf16),
             pltpu.VMEM((POS, X * LANES), bf16),
-            pltpu.VMEM((2, KV_ROWS + MARGIN_ROWS, LANES), bf16),
-            pltpu.SemaphoreType.DMA((6 + ROWS_Y,)),
+            pltpu.SemaphoreType.DMA((6,)),
         ),
     )(lengths, logratio, prompt_keys, prompt_values, resp_keys, resp_values)
     kv = swap(kv)

time: 88.6 us -> 88.5 us (level)
  no operation moved by 1% of the time
where the time goes in v13:
time: 88.5 us; the launch traced here: 86.9 us
  starting transfers between devices  41.8 us (47%)
  Pallas kernels  21.9 us (25%)
  waiting for transfers between devices  21.2 us (24%)
  local copies, waits for them, and re-layouts  1 us (1%)
  between operations  0.91 us (1%)
    ppermute x6, starting transfers between devices, shift(): return lax.ppermute(values, ROW, [(i, (i + by) % X) for i in range(X)])  22.2 us
    all_to_all x2, starting transfers between devices, swap(): lax.all_to_all(values, PEERS, split_axis=0, concat_axis=0, tiled=True)  15.8 us
    ppermute x6, waiting for transfers between devices, shift(): return lax.ppermute(values, ROW, [(i, (i + by) % X) for i in range(X)])  13.2 us
    pallas_call x4, Pallas kernels, query_call(): call(functools.partial(query_kernel, k), jax.ShapeDtypeStruct((2 * TILE +...  7.95 us
    all_to_all x2, waiting for transfers between devices, swap(): lax.all_to_all(values, PEERS, split_axis=0, concat_axis=0, tiled=True)  6.5 us
    ppermute x2, starting transfers between devices, cross(): return lax.ppermute(values, 'pair', [(0, 1), (1, 0)])  3.84 us
    pallas_call x1, Pallas kernels, resp_call(): call(resp_kernel, (shape((PEERS_N, KV_ROWS, LANES), bf16), shape((8, LANE...  3.17 us
    pallas_call x1, Pallas kernels, prompt_call(): call(functools.partial(prompt_kernel, False), (shape((PEERS_N, 2 * PROMPT...  2.98 us
  transfers between devices with their start and end apart: 10, of which 4 were waited for; matrix products, arithmetic and copies ran while one was open for 0% of the time, Pallas kernels for 18%

profile of v13, /device:TPU:6, one launch (start us, length us, event | category | flops | bytes accessed | tf_op | source)
XLA Modules:
  0.0 86.9 jit_solution(117764999577238762)
XLA Ops:
  0.6 2.0 %shard_map.145 = bf16[16,264,128]{2,1,0:T(8,128)(2,1)} custom-call(s32[1,3]{1,0:T(1,128)} %lengths_ref.11, f32[1,2,32]{2,1,0:T(2,128)} %logratio_hbm.1, bf16[1,64,256]{2,1,0:T(8,128)(2,1)} %pk_hbm.1, bf16[1,64,256]{2,1,0:T(8,128)(2,1)} %pv_hbm.1, bf16[1,1,32,512]{3,2,1,0:T(8,128)(2,1)} %rk_hbm.1, bf16[1,1,32,512]{3,2,1,0:T(8,128)(2,1)} %rv_hbm.1), custom_call_target="tpu_custom_call" | custom-call | bytes 2097152 | tf_op jit(solution)/shard_map/pallas_call | solution.py:457
  2.6 0.0 copy-start
  2.6 0.0 copy-start.1
  2.7 0.0 copy-start.2
  2.7 0.0 copy-start.3
  2.7 8.7 %all-to-all-start = ((bf16[16,264,128]{2,1,0:T(8,128)(2,1)}), bf16[16,264,128]{2,1,0:T(8,128)(2,1)S(1)}, u32[]{:S(2)}, u32[]{:S(2)}) async-start(bf16[16,264,128]{2,1,0:T(8,128)(2,1)} %shard_map.145), calls=%async_computation | async-start | bytes 2162688 | tf_op jit(solution)/shard_map/all_to_all | solution.py:375
  11.4 0.0 copy-done
  11.4 0.0 copy-done.1
  11.4 0.0 copy-done.2
  11.4 0.0 copy-done.3
  11.4 0.0 copy-start.4
  11.5 0.6 shard_map.146
  12.0 1.9 %collective-permute-start = (bf16[2,528,128]{2,1,0:T(8,128)(2,1)S(1)}, bf16[2,528,128]{2,1,0:T(8,128)(2,1)S(1)}, u32[]{:S(2)}, u32[]{:S(2)}) collective-permute-start(bf16[2,528,128]{2,1,0:T(8,128)(2,1)S(1)} %get-tuple-element.32), channel_id=1, source_target_pairs={{0,32},{32,0},{1,33},{33,1},{2,34},{34,2},{3,35},{35,3},{4,36},{36... | collective-permute-start | bytes 811016 | tf_op jit(solution)/shard_map/ppermute | solution.py:379
  14.0 1.5 %collective-permute-done.other_ref = bf16[2,528,128]{2,1,0:T(8,128)(2,1)S(1)} collective-permute-done((bf16[2,528,128]{2,1,0:T(8,128)(2,1)S(1)}, bf16[2,528,128]{2,1,0:T(8,128)(2,1)S(1)}, u32[]{:S(2)}, u32[]{:S(2)}) %collective-permute-start) | collective-permute-done | bytes 270368 | tf_op jit(solution)/shard_map/ppermute | solution.py:379
  15.5 4.1 %collective-permute-start.1 = (bf16[2,528,128]{2,1,0:T(8,128)(2,1)S(1)}, bf16[2,528,128]{2,1,0:T(8,128)(2,1)S(1)}, u32[]{:S(2)}, u32[]{:S(2)}) collective-permute-start(bf16[2,528,128]{2,1,0:T(8,128)(2,1)S(1)} %get-tuple-element.33.qa.q_ref), channel_id=1, source_target_pairs={{0,2},{1,3},{2,0},{3,1},{4,6},{5,7},{6,4},{7,5},{8,10},{9,11},{10,... | collective-permute-start | bytes 811016 | tf_op jit(solution)/shard_map/ppermute | solution.py:383
  19.6 1.9 %collective-permute-start.4 = (bf16[2,528,128]{2,1,0:T(8,128)(2,1)S(1)}, bf16[2,528,128]{2,1,0:T(8,128)(2,1)S(1)}, u32[]{:S(2)}, u32[]{:S(2)}) collective-permute-start(bf16[2,528,128]{2,1,0:T(8,128)(2,1)S(1)} %get-tuple-element.40), channel_id=1, source_target_pairs={{0,3},{1,0},{2,1},{3,2},{4,7},{5,4},{6,5},{7,6},{8,11},{9,8},{10,9... | collective-permute-start | bytes 811016 | tf_op jit(solution)/shard_map/ppermute | solution.py:383
  21.6 5.1 %collective-permute-start.3 = (bf16[2,528,128]{2,1,0:T(8,128)(2,1)S(1)}, bf16[2,528,128]{2,1,0:T(8,128)(2,1)S(1)}, u32[]{:S(2)}, u32[]{:S(2)}) collective-permute-start(bf16[2,528,128]{2,1,0:T(8,128)(2,1)S(1)} %get-tuple-element.40), channel_id=1, source_target_pairs={{0,1},{1,2},{2,3},{3,0},{4,5},{5,6},{6,7},{7,4},{8,9},{9,10},{10,1... | collective-permute-start | bytes 811016 | tf_op jit(solution)/shard_map/ppermute | solution.py:383
  26.7 5.6 %collective-permute-done.1.qb.q_ref = bf16[2,528,128]{2,1,0:T(8,128)(2,1)S(1)} collective-permute-done((bf16[2,528,128]{2,1,0:T(8,128)(2,1)S(1)}, bf16[2,528,128]{2,1,0:T(8,128)(2,1)S(1)}, u32[]{:S(2)}, u32[]{:S(2)}) %collective-permute-start.1) | collective-permute-done | bytes 270368 | tf_op jit(solution)/shard_map/ppermute | solution.py:383
  32.3 0.0 copy-done.4
  32.3 0.6 shard_map.148
  32.9 6.5 %all-to-all-done.refs_4_.refs_3_.kv_ref = bf16[16,264,128]{2,1,0:T(8,128)(2,1)S(1)} async-done(((bf16[16,264,128]{2,1,0:T(8,128)(2,1)}), bf16[16,264,128]{2,1,0:T(8,128)(2,1)S(1)}, u32[]{:S(2)}, u32[]{:S(2)}) %all-to-all-start) | async-done | bytes 1081376 | tf_op jit(solution)/shard_map/all_to_all | solution.py:375
  39.4 2.4 %shard_map.149 = (f32[1024,128]{1,0:T(8,128)S(1)}, f32[1024,128]{1,0:T(8,128)S(1)}) custom-call(bf16[1024,128]{1,0:T(8,128)(2,1)S(1)} %get-tuple-element.34.refs_0_.query_a, bf16[1024,128]{1,0:T(8,128)(2,1)S(1)} %get-tuple-element.35.refs_1_.grad_a, f32[4,256]{1,0:T(4,128)S(1)} %get-tuple-element.36.refs_2_.lse_a, ...), custom_call_target="tpu_custom_call" | custom-call | flops 2147483648 | bytes 2097152 | tf_op jit(solution)/shard_map/pallas_call | solution.py:399
  41.8 1.9 %collective-permute-start.2 = (bf16[16,64,128]{2,1,0:T(8,128)(2,1)S(1)}, bf16[16,64,128]{2,1,0:T(8,128)(2,1)S(1)}, u32[]{:S(2)}, u32[]{:S(2)}) collective-permute-start(bf16[16,64,128]{2,1,0:T(8,128)(2,1)S(1)} %slice.3), channel_id=1, source_target_pairs={{0,32},{32,0},{1,33},{33,1},{2,34},{34,2},{3,35},{35,3},{4,36},{36... | collective-permute-start | bytes 786440 | tf_op jit(solution)/shard_map/ppermute | solution.py:379
  43.7 0.0 collective-permute-done.4.refs_2_.q_ref
  43.7 0.0 collective-permute-done.3.refs_1_.q_ref
  43.7 3.0 %shard_map.150 = (bf16[16,128,128]{2,1,0:T(8,128)(2,1)S(1)}, bf16[1024,128]{1,0:T(8,128)(2,1)S(1)}, bf16[1024,128]{1,0:T(8,128)(2,1)S(1)}, f32[4,256]{1,0:T(4,128)S(1)}, f32[4,256]{1,0:T(4,128)S(1)}) custom-call(s32[1,3]{1,0:T(1,128)S(1)} %copy-done.4, bf16[2,528,128]{2,1,0:T(8,128)(2,1)S(1)} %collective-permute-done.3.refs_1_.q_ref, ...), custom_call_target="tpu_custom_call" | custom-call | flops 2147483648 | bytes 2097152 | tf_op jit(solution)/shard_map/pallas_call | solution.py:402
  46.7 0.0 collective-permute-done.2.side_ref
  46.7 0.0 copy-start.5
  46.7 3.2 %shard_map.151 = (bf16[16,256,128]{2,1,0:T(8,128)(2,1)}, f32[8,128]{1,0:T(8,128)S(1)}) custom-call(bf16[16,264,128]{2,1,0:T(8,128)(2,1)S(1)} %all-to-all-done.refs_4_.refs_3_.kv_ref, bf16[16,64,128]{2,1,0:T(8,128)(2,1)S(1)} %collective-permute-done.2.side_ref, bf16[16,128,128]{2,1,0:T(8,128)(2,1)S(1)} %get-tuple-element.43.prompt_ref, ...), custom_call_target="tpu_custom_call" | custom-call | flops 2147483648 | bytes 3145728 | tf_op jit(solution)/shard_map/pallas_call | solution.py:414
  49.9 0.0 copy-done.5
  49.9 7.1 %all-to-all-start.1 = ((bf16[16,256,128]{2,1,0:T(8,128)(2,1)}), bf16[16,256,128]{2,1,0:T(8,128)(2,1)S(1)}, u32[]{:S(2)}, u32[]{:S(2)}) async-start(bf16[16,256,128]{2,1,0:T(8,128)(2,1)} %get-tuple-element.49), calls=%async_computation.1 | async-start | bytes 2097152 | tf_op jit(solution)/shard_map/all_to_all | solution.py:375
  57.0 0.0 copy-start.6
  57.0 0.9 %copy-done.6 = bf16[16,64,128]{2,1,0:T(8,128)(2,1)S(1)} copy-done((bf16[16,64,128]{2,1,0:T(8,128)(2,1)S(1)}, bf16[16,64,128]{2,1,0:T(8,128)(2,1)}, u32[]{:S(2)}) %copy-start.6) | copy-done | bytes 262168
  57.9 0.0 copy-start.7
  57.9 2.0 %shard_map.155 = bf16[512,128]{1,0:T(8,128)(2,1)S(1)} custom-call(s32[1,3]{1,0:T(1,128)S(1)} %copy-done.4, f32[8,128]{1,0:T(8,128)S(1)} %get-tuple-element.48.margin_ref, bf16[2,528,128]{2,1,0:T(8,128)(2,1)S(1)} %collective-permute-done.3.refs_1_.q_ref, bf16[16,264,128]{2,1,0:T(8,128)(2,1)S(1)} %all-to-all-done.refs_4_.refs_3_.kv_ref, ...), custom_call_target="tpu_custom_call" | custom-call | flops 1207959552 | bytes 3145728 | tf_op jit(solution)/shard_map/pallas_call | solution.py:435
  59.9 2.0 %collective-permute-start.6 = (bf16[512,128]{1,0:T(8,128)(2,1)S(1)}, bf16[512,128]{1,0:T(8,128)(2,1)S(1)}, u32[]{:S(2)}, u32[]{:S(2)}) collective-permute-start(bf16[512,128]{1,0:T(8,128)(2,1)S(1)} %shard_map.155), channel_id=1, source_target_pairs={{0,3},{1,0},{2,1},{3,2},{4,7},{5,4},{6,5},{7,6},{8,11},{9,8},{10,9... | collective-permute-start | bytes 393224 | tf_op jit(solution)/shard_map/ppermute | solution.py:383
  62.0 0.0 copy-done.7
  62.0 2.0 %shard_map.152 = bf16[528,128]{1,0:T(8,128)(2,1)S(1)} custom-call(s32[1,3]{1,0:T(1,128)S(1)} %copy-done.4, f32[8,128]{1,0:T(8,128)S(1)} %get-tuple-element.48.margin_ref, bf16[2,528,128]{2,1,0:T(8,128)(2,1)S(1)} %collective-permute-done.1.qb.q_ref, bf16[16,264,128]{2,1,0:T(8,128)(2,1)S(1)} %all-to-all-done.refs_4_.refs_3_.kv_ref, ...), custom_call_target="tpu_custom_call" | custom-call | flops 1207959552 | bytes 3145728 | tf_op jit(solution)/shard_map/pallas_call | solution.py:435
  64.0 4.6 %collective-permute-start.5 = (bf16[528,128]{1,0:T(8,128)(2,1)S(1)}, bf16[528,128]{1,0:T(8,128)(2,1)S(1)}, u32[]{:S(2)}, u32[]{:S(2)}) collective-permute-start(bf16[528,128]{1,0:T(8,128)(2,1)S(1)} %shard_map.152), channel_id=1, source_target_pairs={{0,2},{1,3},{2,0},{3,1},{4,6},{5,7},{6,4},{7,5},{8,10},{9,11},{10,... | collective-permute-start | bytes 405512 | tf_op jit(solution)/shard_map/ppermute | solution.py:383
  68.5 2.0 %shard_map.156 = bf16[512,128]{1,0:T(8,128)(2,1)S(1)} custom-call(s32[1,3]{1,0:T(1,128)S(1)} %copy-done.4, f32[8,128]{1,0:T(8,128)S(1)} %get-tuple-element.48.margin_ref, bf16[2,528,128]{2,1,0:T(8,128)(2,1)S(1)} %collective-permute-done.4.refs_2_.q_ref, bf16[16,264,128]{2,1,0:T(8,128)(2,1)S(1)} %all-to-all-done.refs_4_.refs_3_.kv_ref, ...), custom_call_target="tpu_custom_call" | custom-call | flops 1207959552 | bytes 3145728 | tf_op jit(solution)/shard_map/pallas_call | solution.py:435
  70.5 4.4 %collective-permute-start.7 = (bf16[512,128]{1,0:T(8,128)(2,1)S(1)}, bf16[512,128]{1,0:T(8,128)(2,1)S(1)}, u32[]{:S(2)}, u32[]{:S(2)}) collective-permute-start(bf16[512,128]{1,0:T(8,128)(2,1)S(1)} %shard_map.156), channel_id=1, source_target_pairs={{0,1},{1,2},{2,3},{3,0},{4,5},{5,6},{6,7},{7,4},{8,9},{9,10},{10,1... | collective-permute-start | bytes 393224 | tf_op jit(solution)/shard_map/ppermute | solution.py:383
  74.9 2.0 %shard_map.154.d0 = bf16[512,128]{1,0:T(8,128)(2,1)S(1)} custom-call(s32[1,3]{1,0:T(1,128)S(1)} %copy-done.4, f32[8,128]{1,0:T(8,128)S(1)} %get-tuple-element.48.margin_ref, bf16[2,528,128]{2,1,0:T(8,128)(2,1)S(1)} %get-tuple-element.33.qa.q_ref, bf16[16,264,128]{2,1,0:T(8,128)(2,1)S(1)} %all-to-all-done.refs_4_.refs_3_.kv_ref, ...), custom_call_target="tpu_custom_call" | custom-call | flops 1207959552 | bytes 3145728 | tf_op jit(solution)/shard_map/pallas_call | solution.py:435
  76.9 0.0 collective-permute-done.6.d1
  76.9 7.6 %collective-permute-done.7.d3 = bf16[512,128]{1,0:T(8,128)(2,1)S(1)} collective-permute-done((bf16[512,128]{1,0:T(8,128)(2,1)S(1)}, bf16[512,128]{1,0:T(8,128)(2,1)S(1)}, u32[]{:S(2)}, u32[]{:S(2)}) %collective-permute-start.7) | collective-permute-done | bytes 131104 | tf_op jit(solution)/shard_map/ppermute | solution.py:383
  84.6 0.0 collective-permute-done.5.d2
  84.6 0.9 %shard_map.157 = (bf16[1,2,32,2048]{3,2,1,0:T(8,128)(2,1)}, f32[1]{0:T(128)}) custom-call(f32[8,128]{1,0:T(8,128)S(1)} %get-tuple-element.48.margin_ref, bf16[512,128]{1,0:T(8,128)(2,1)S(1)} %shard_map.154.d0, bf16[512,128]{1,0:T(8,128)(2,1)S(1)} %collective-permute-done.6.d1, bf16[528,128]{1,0:T(8,128)(2,1)S(1)} %collective-permute-done.5.d2, ...), custom_call_target="tpu_custom_call" | custom-call | bytes 1048576 | tf_op jit(solution)/shard_map/pallas_call | solution.py:497
  85.5 0.0 all-to-all-done.1.part_ref
  85.5 1.4 %shard_map.153 = (bf16[1,64,256]{2,1,0:T(8,128)(2,1)}, bf16[1,64,256]{2,1,0:T(8,128)(2,1)}, bf16[1,2,32,256]{3,2,1,0:T(8,128)(2,1)}, bf16[1,2,32,256]{3,2,1,0:T(8,128)(2,1)}) custom-call(s32[1,3]{1,0:T(1,128)S(1)} %copy-done.4, f32[8,128]{1,0:T(8,128)S(1)} %get-tuple-element.48.margin_ref, bf16[528,128]{1,0:T(8,128)(2,1)S(1)} %collective-permute-done.5.d2, ...), custom_call_target="tpu_custom_call" | custom-call | bytes 1048576 | tf_op jit(solution)/shard_map/pallas_call | solution.py:505
  (2 shorter events, 0.1 us)
Async XLA Ops:
  2.6 8.8 %copy-start = (bf16[1,1,32,4096]{3,2,1,0:T(8,128)(2,1)S(1)}, bf16[1,1,32,4096]{3,2,1,0:T(8,128)(2,1)}, u32[]{:S(2)}) copy-start(bf16[1,1,32,4096]{3,2,1,0:T(8,128)(2,1)} %q_hbm.1) | copy-start | bytes 786436
  2.6 8.8 %copy-start.1 = (bf16[1,1,32,4096]{3,2,1,0:T(8,128)(2,1)S(1)}, bf16[1,1,32,4096]{3,2,1,0:T(8,128)(2,1)}, u32[]{:S(2)}) copy-start(bf16[1,1,32,4096]{3,2,1,0:T(8,128)(2,1)} %g_hbm.1) | copy-start | bytes 786436
  2.7 8.8 %copy-start.2 = (bf16[1,1,32,32]{3,2,1,0:T(8,128)(2,1)S(1)}, bf16[1,1,32,32]{3,2,1,0:T(8,128)(2,1)}, u32[]{:S(2)}) copy-start(bf16[1,1,32,32]{3,2,1,0:T(8,128)(2,1)} %lse_hbm.1) | copy-start | bytes 6148
  2.7 8.8 %copy-start.3 = (bf16[1,1,32,32]{3,2,1,0:T(8,128)(2,1)S(1)}, bf16[1,1,32,32]{3,2,1,0:T(8,128)(2,1)}, u32[]{:S(2)}) copy-start(bf16[1,1,32,32]{3,2,1,0:T(8,128)(2,1)} %delta_hbm.1) | copy-start | bytes 6148
  2.7 36.7 %all-to-all-start = ((bf16[16,264,128]{2,1,0:T(8,128)(2,1)}), bf16[16,264,128]{2,1,0:T(8,128)(2,1)S(1)}, u32[]{:S(2)}, u32[]{:S(2)}) async-start(bf16[16,264,128]{2,1,0:T(8,128)(2,1)} %shard_map.145), calls=%async_computation | async-start | bytes 2162688 | tf_op jit(solution)/shard_map/all_to_all | solution.py:375
  11.4 20.9 %copy-start.4 = (s32[1,3]{1,0:T(1,128)S(1)}, s32[1,3]{1,0:T(1,128)}, u32[]{:S(2)}) copy-start(s32[1,3]{1,0:T(1,128)} %lengths_ref.11) | copy-start | bytes 40
  12.0 3.4 %collective-permute-start = (bf16[2,528,128]{2,1,0:T(8,128)(2,1)S(1)}, bf16[2,528,128]{2,1,0:T(8,128)(2,1)S(1)}, u32[]{:S(2)}, u32[]{:S(2)}) collective-permute-start(bf16[2,528,128]{2,1,0:T(8,128)(2,1)S(1)} %get-tuple-element.32), channel_id=1, source_target_pairs={{0,32},{32,0},{1,33},{33,1},{2,34},{34,2},{3,35},{35,3},{4,36},{36... | collective-permute-start | bytes 811016 | tf_op jit(solution)/shard_map/ppermute | solution.py:379
  15.5 16.8 %collective-permute-start.1 = (bf16[2,528,128]{2,1,0:T(8,128)(2,1)S(1)}, bf16[2,528,128]{2,1,0:T(8,128)(2,1)S(1)}, u32[]{:S(2)}, u32[]{:S(2)}) collective-permute-start(bf16[2,528,128]{2,1,0:T(8,128)(2,1)S(1)} %get-tuple-element.33.qa.q_ref), channel_id=1, source_target_pairs={{0,2},{1,3},{2,0},{3,1},{4,6},{5,7},{6,4},{7,5},{8,10},{9,11},{10,... | collective-permute-start | bytes 811016 | tf_op jit(solution)/shard_map/ppermute | solution.py:383
  19.6 24.1 %collective-permute-start.4 = (bf16[2,528,128]{2,1,0:T(8,128)(2,1)S(1)}, bf16[2,528,128]{2,1,0:T(8,128)(2,1)S(1)}, u32[]{:S(2)}, u32[]{:S(2)}) collective-permute-start(bf16[2,528,128]{2,1,0:T(8,128)(2,1)S(1)} %get-tuple-element.40), channel_id=1, source_target_pairs={{0,3},{1,0},{2,1},{3,2},{4,7},{5,4},{6,5},{7,6},{8,11},{9,8},{10,9... | collective-permute-start | bytes 811016 | tf_op jit(solution)/shard_map/ppermute | solution.py:383
  21.6 22.1 %collective-permute-start.3 = (bf16[2,528,128]{2,1,0:T(8,128)(2,1)S(1)}, bf16[2,528,128]{2,1,0:T(8,128)(2,1)S(1)}, u32[]{:S(2)}, u32[]{:S(2)}) collective-permute-start(bf16[2,528,128]{2,1,0:T(8,128)(2,1)S(1)} %get-tuple-element.40), channel_id=1, source_target_pairs={{0,1},{1,2},{2,3},{3,0},{4,5},{5,6},{6,7},{7,4},{8,9},{9,10},{10,1... | collective-permute-start | bytes 811016 | tf_op jit(solution)/shard_map/ppermute | solution.py:383
  41.8 4.9 %collective-permute-start.2 = (bf16[16,64,128]{2,1,0:T(8,128)(2,1)S(1)}, bf16[16,64,128]{2,1,0:T(8,128)(2,1)S(1)}, u32[]{:S(2)}, u32[]{:S(2)}) collective-permute-start(bf16[16,64,128]{2,1,0:T(8,128)(2,1)S(1)} %slice.3), channel_id=1, source_target_pairs={{0,32},{32,0},{1,33},{33,1},{2,34},{34,2},{3,35},{35,3},{4,36},{36... | collective-permute-start | bytes 786440 | tf_op jit(solution)/shard_map/ppermute | solution.py:379
  46.7 3.2 %copy-start.5 = (bf16[16,64,128]{2,1,0:T(8,128)(2,1)}, bf16[16,64,128]{2,1,0:T(8,128)(2,1)S(1)}, u32[]{:S(2)}) copy-start(bf16[16,64,128]{2,1,0:T(8,128)(2,1)S(1)} %collective-permute-done.2.side_ref) | copy-start | bytes 786436
  49.9 35.6 %all-to-all-start.1 = ((bf16[16,256,128]{2,1,0:T(8,128)(2,1)}), bf16[16,256,128]{2,1,0:T(8,128)(2,1)S(1)}, u32[]{:S(2)}, u32[]{:S(2)}) async-start(bf16[16,256,128]{2,1,0:T(8,128)(2,1)} %get-tuple-element.49), calls=%async_computation.1 | async-start | bytes 2097152 | tf_op jit(solution)/shard_map/all_to_all | solution.py:375
  57.0 0.9 %copy-start.6 = (bf16[16,64,128]{2,1,0:T(8,128)(2,1)S(1)}, bf16[16,64,128]{2,1,0:T(8,128)(2,1)}, u32[]{:S(2)}) copy-start(bf16[16,64,128]{2,1,0:T(8,128)(2,1)} %copy-done.5) | copy-start | bytes 786436
  57.9 4.0 %copy-start.7 = (bf16[16,64,128]{2,1,0:T(8,128)(2,1)S(1)}, bf16[16,64,128]{2,1,0:T(8,128)(2,1)}, u32[]{:S(2)}) copy-start(bf16[16,64,128]{2,1,0:T(8,128)(2,1)} %copy-done.5) | copy-start | bytes 786436
  59.9 17.0 %collective-permute-start.6 = (bf16[512,128]{1,0:T(8,128)(2,1)S(1)}, bf16[512,128]{1,0:T(8,128)(2,1)S(1)}, u32[]{:S(2)}, u32[]{:S(2)}) collective-permute-start(bf16[512,128]{1,0:T(8,128)(2,1)S(1)} %shard_map.155), channel_id=1, source_target_pairs={{0,3},{1,0},{2,1},{3,2},{4,7},{5,4},{6,5},{7,6},{8,11},{9,8},{10,9... | collective-permute-start | bytes 393224 | tf_op jit(solution)/shard_map/ppermute | solution.py:383
  64.0 20.6 %collective-permute-start.5 = (bf16[528,128]{1,0:T(8,128)(2,1)S(1)}, bf16[528,128]{1,0:T(8,128)(2,1)S(1)}, u32[]{:S(2)}, u32[]{:S(2)}) collective-permute-start(bf16[528,128]{1,0:T(8,128)(2,1)S(1)} %shard_map.152), channel_id=1, source_target_pairs={{0,2},{1,3},{2,0},{3,1},{4,6},{5,7},{6,4},{7,5},{8,10},{9,11},{10,... | collective-permute-start | bytes 405512 | tf_op jit(solution)/shard_map/ppermute | solution.py:383
  70.5 14.1 %collective-permute-start.7 = (bf16[512,128]{1,0:T(8,128)(2,1)S(1)}, bf16[512,128]{1,0:T(8,128)(2,1)S(1)}, u32[]{:S(2)}, u32[]{:S(2)}) collective-permute-start(bf16[512,128]{1,0:T(8,128)(2,1)S(1)} %shard_map.156), channel_id=1, source_target_pairs={{0,1},{1,2},{2,3},{3,0},{4,5},{5,6},{6,7},{7,4},{8,9},{9,10},{10,1... | collective-permute-start | bytes 393224 | tf_op jit(solution)/shard_map/ppermute | solution.py:383
